TPU v7x, 32 devices: a whole 2x2x4 slice. The times are simulated.
32 devices in a mesh: dom: 8 (over y, x, core), band: 4 (over z).
Axes of the slice: x: 2, y: 2, z: 4, core: 2. Of those that a mesh axis runs over, the one named last changes fastest.
Arguments:
- states: float32 [1536, 1536], P('dom', 'band'), may hold values from -6 to 6
- inv_mass: float32 [1536], P('dom'), may hold values from 0.5 to 2
- cell_ham: float32 [40, 343, 343], P('dom'), as said below
- cell_nodes: int32 [40, 343], P('dom'), may hold values from 0 to 287, as said below
- send_up: int32 [384], P('dom'), may hold values from 0 to 191, as said below
- send_down: int32 [384], P('dom'), may hold values from 0 to 191, as said below
- owner: int32 [8], replicated, may hold values from 0 to 7, each once
- rotation_store: float32 [1536, 1536], P('dom'), may hold values from -0.15625 to 0.15625
Outputs:
- rotated: float32 [1536, 1536], P('dom', 'band')
Inputs may be any that keep to these rules, and one draw needn't show every extreme that they name: `cell_ham`: each cell's matrix is symmetric. `cell_nodes`: each domain's cells name every one of its extended nodes at least once. `send_up`: the 48 entries of one domain are distinct. `send_down`: the 48 entries of one domain are distinct. `owner`: a permutation.
All inputs are finite; a program needn't handle non-finite values.
Results may differ from a plain program's by a relative error of at most 0.00007.
Values sent between devices are 32-bit elements; how exact they have to be, the bound alone decides.
No kernel may reach another device: no remote copies, remote signals or barrier semaphores. Data moves between devices by JAX's collectives and lax.ppermute only.
A program may use at most 64 MiB of HBM per device.

v0:
```python
import jax
import jax.numpy as jnp
from jax import lax
from jax.sharding import PartitionSpec as P

filter_center = 2.5
filter_half = 3.5
spectrum_floor = -4.0
sigma_one = filter_half / (spectrum_floor - filter_center)
sigma_two = 1.0 / (2.0 / sigma_one - sigma_one)


def with_halo(block, sides, width):
    for axis, dim in sides:
        count = lax.axis_size(axis)
        forward = [(i, i + 1) for i in range(count - 1)]
        forward.append((count - 1, 0))
        backward = [(target, source) for source, target in forward]
        low = lax.ppermute(
            lax.slice_in_dim(block, block.shape[dim] - width, None, axis=dim), axis, forward
        )
        high = lax.ppermute(lax.slice_in_dim(block, 0, width, axis=dim), axis, backward)
        block = jnp.concatenate([low, block, high], axis=dim)
    return block


def apply_operator(values, inv_mass, cell_ham, cell_nodes, send_up, send_down):
    owned_count = values.shape[0]
    ghost_count = send_up.shape[0]
    block_cols = values.shape[1]
    scaled = values * inv_mass[:, None]
    outgoing = jnp.concatenate([scaled[send_down], scaled[send_up]], axis=0)
    padded = with_halo(outgoing, (("dom", 0),), ghost_count)
    extended = jnp.concatenate([scaled, padded[:ghost_count], padded[3 * ghost_count :]], axis=0)
    gathered = extended[cell_nodes]
    products = jnp.einsum(
        "cij,cjs->cis",
        cell_ham,
        gathered,
        precision=lax.Precision.HIGHEST,
        preferred_element_type=jnp.float32,
    )
    empty = jnp.zeros((owned_count + 2 * ghost_count, block_cols), jnp.float32)
    assembled = empty.at[cell_nodes.reshape(-1)].add(products.reshape(-1, block_cols))
    returning = assembled[owned_count:]
    returned = with_halo(returning, (("dom", 0),), ghost_count)
    result = assembled[:owned_count].at[send_down].add(returned[:ghost_count])
    result = result.at[send_up].add(returned[3 * ghost_count :])
    return result * inv_mass[:, None]


def shards(states, inv_mass, cell_ham, cell_nodes, send_up, send_down, owner, rotation_store):
    block_cols = states.shape[1]
    panel_rows = rotation_store.shape[0]
    filtered_one = (
        sigma_one
        / filter_half
        * (
            apply_operator(states, inv_mass, cell_ham, cell_nodes, send_up, send_down)
            - filter_center * states
        )
    )
    applied = apply_operator(filtered_one, inv_mass, cell_ham, cell_nodes, send_up, send_down)
    filtered_two = (
        2.0 * sigma_two / filter_half * (applied - filter_center * filtered_one)
        - sigma_one * sigma_two * states
    )
    row_index = (
        owner[:, None] * panel_rows + jnp.arange(panel_rows, dtype=jnp.int32)[None, :]
    ).reshape(-1)
    band_index = lax.axis_index("band")
    own_columns = lax.dynamic_slice_in_dim(rotation_store, band_index * block_cols, block_cols, 1)
    columns = lax.all_gather(own_columns, "dom", axis=0, tiled=True)
    ordered = columns[row_index]
    return jnp.dot(
        lax.all_gather(filtered_two, "band", axis=1, tiled=True),
        ordered,
        precision=lax.Precision.HIGHEST,
        preferred_element_type=jnp.float32,
    )


def solution(mesh):
    in_specs = (
        P("dom", "band"),
        P("dom"),
        P("dom", None, None),
        P("dom", None),
        P("dom"),
        P("dom"),
        P(),
        P("dom", None),
    )
    out_specs = P("dom", "band")
    return jax.shard_map(shards, mesh=mesh, in_specs=in_specs, out_specs=out_specs, check_vma=False)
```

profile of v0, /device:TPU:0, one launch (start us, length us, event | category | flops | bytes accessed | tf_op | source)
XLA Modules:
  0.0 159.8 jit_solution(5527315448965602357)
XLA Ops:
  6.5 0.0 copy-start
  6.5 0.0 all-gather.5.cloned.1.call-start
  6.5 1.9 %constant_dynamic-slice_fusion = f32[192,384]{1,0:T(8,128)} fusion(f32[192,1536]{1,0:T(8,128)} %param.15, s32[]{:T(128)S(6)} %select_n.44), kind=kLoop, calls=%fused_computation.39 | loop fusion | bytes 589828 | tf_op jit(solution)/shard_map/dynamic_slice | solution.py:72
  8.4 0.0 all-gather.5.cloned.1.call-update
  8.4 0.0 all-gather.3.cloned.1.call-start
  8.5 0.7 compare_select_fusion.4
  9.1 1.1 broadcast_multiply_fusion
  10.2 0.6 gather_fusion
  10.8 0.5 collective-permute-start
  11.3 0.7 compare_select_fusion.3
  12.0 0.6 gather_fusion.1
  12.6 2.9 %collective-permute-start.1 = (f32[48,384]{1,0:T(8,128)S(1)}, f32[48,384]{1,0:T(8,128)}, u32[]{:S(2)}, u32[]{:S(2)}) collective-permute-start(f32[48,384]{1,0:T(8,128)S(1)} %gather_fusion.1), channel_id=1, source_target_pairs={{4,0},{8,4},{12,8},{16,12},{20,16},{24,20},{28,24},{0,28},{5,1},{9... | collective-permute-start | bytes 221192 | tf_op jit(solution)/shard_map/ppermute | solution.py:22
  15.6 0.0 copy-done.7
  15.6 0.1 reshape.71
  15.7 0.1 reshape.92
  15.8 0.0 copy-done.9
  15.8 0.4 collective-permute-done
  16.3 1.3 collective-permute-done.1
  17.6 0.9 pad_maximum_fusion
  18.5 5.5 %gather_fusion.2 = f32[1715,384]{1,0:T(8,128)} fusion(f32[288,384]{1,0:T(8,128)S(1)} %pad_maximum_fusion, s32[2048]{0:T(1024)S(1)} %pad_clamp_fusion.1), kind=kCustom, calls=%fused_computation.2 | custom fusion | bytes 5275340 | tf_op jit(solution)/shard_map/gather | solution.py:35
  24.0 3.6 %reshape.91 = f32[5,343,384]{2,1,0:T(8,128)} reshape(f32[1715,384]{1,0:T(8,128)} %gather_fusion.2) | data formatting | bytes 5268480 | tf_op jit(solution)/shard_map/gather | solution.py:35
  27.6 8.9 %convolution_bitcast_fusion.1 = f32[5,343,384]{2,1,0:T(8,128)} fusion(f32[5,343,384]{2,1,0:T(8,128)} %reshape.91, f32[5,343,343]{2,1,0:T(8,128)S(1)} %copy-done), kind=kOutput, calls=%fused_computation.14 | convolution fusion | flops 2710632960 | bytes 7621460 | tf_op jit(solution)/shard_map/cij,cjs->cis/dot_general | solution.py:36
  36.5 3.6 %reshape.134 = f32[1715,384]{1,0:T(8,128)} reshape(f32[5,343,384]{2,1,0:T(8,128)} %convolution_bitcast_fusion.1) | data formatting | bytes 5268480 | tf_op jit(solution)/shard_map/reshape | solution.py:44
  40.1 13.3 %scatter_custom_fusion = f32[288,384]{1,0:T(8,128)S(1)} fusion(s32[1715]{0:T(1024)S(1)} %fusion.5, f32[1715,384]{1,0:T(8,128)} %reshape.134, f32[]{:T(128)} %constant.12.clone.1), kind=kCustom, calls=%fused_computation.22 | custom fusion | flops 658560 | bytes 442880 | tf_op jit(solution)/shard_map/scatter-add | solution.py:44
  53.4 0.7 fusion.8
  54.1 1.6 collective-permute-start.2
  55.7 1.2 collective-permute-start.3
  56.9 0.0 copy-done.4
  56.9 0.6 broadcast_multiply_fusion.1
  57.5 1.0 slice.44
  58.5 0.4 collective-permute-done.2
  58.9 1.1 scatter_fusion
  60.0 0.0 collective-permute-done.3
  60.1 1.3 scatter_fusion.1
  61.4 0.8 fusion
  62.2 0.0 copy-start.1
  62.2 0.6 gather_fusion.3
  62.8 0.6 gather_fusion.4
  63.5 0.6 collective-permute-start.4
  64.1 2.1 %collective-permute-start.5 = (f32[48,384]{1,0:T(8,128)S(1)}, f32[48,384]{1,0:T(8,128)S(1)}, u32[]{:S(2)}, u32[]{:S(2)}) collective-permute-start(f32[48,384]{1,0:T(8,128)S(1)} %gather_fusion.4), channel_id=1, source_target_pairs={{4,0},{8,4},{12,8},{16,12},{20,16},{24,20},{28,24},{0,28},{5,1},{9... | collective-permute-start | bytes 221192 | tf_op jit(solution)/shard_map/ppermute | solution.py:22
  66.2 2.0 %collective-permute-done.4 = f32[48,384]{1,0:T(8,128)S(1)} collective-permute-done((f32[48,384]{1,0:T(8,128)S(1)}, f32[48,384]{1,0:T(8,128)S(1)}, u32[]{:S(2)}, u32[]{:S(2)}) %collective-permute-start.4) | collective-permute-done | bytes 73760 | tf_op jit(solution)/shard_map/ppermute | solution.py:19
  68.2 0.0 collective-permute-done.5
  68.2 1.0 pad_maximum_fusion.1
  69.2 5.5 %gather_fusion.5 = f32[1715,384]{1,0:T(8,128)} fusion(f32[288,384]{1,0:T(8,128)S(1)} %pad_maximum_fusion.1, s32[2048]{0:T(1024)S(1)} %pad_clamp_fusion.1), kind=kCustom, calls=%fused_computation.5 | custom fusion | bytes 5275340 | tf_op jit(solution)/shard_map/gather | solution.py:35
  74.7 3.6 %reshape.115 = f32[5,343,384]{2,1,0:T(8,128)} reshape(f32[1715,384]{1,0:T(8,128)} %gather_fusion.5) | data formatting | bytes 5268480 | tf_op jit(solution)/shard_map/gather | solution.py:35
  78.3 8.9 %convolution_bitcast_fusion = f32[5,343,384]{2,1,0:T(8,128)} fusion(f32[5,343,384]{2,1,0:T(8,128)} %reshape.115, f32[5,343,343]{2,1,0:T(8,128)S(1)} %copy-done), kind=kOutput, calls=%fused_computation.13 | convolution fusion | flops 2710632960 | bytes 7621460 | tf_op jit(solution)/shard_map/cij,cjs->cis/dot_general | solution.py:36
  87.2 3.6 %reshape.158 = f32[1715,384]{1,0:T(8,128)} reshape(f32[5,343,384]{2,1,0:T(8,128)} %convolution_bitcast_fusion) | data formatting | bytes 5268480 | tf_op jit(solution)/shard_map/reshape | solution.py:44
  90.8 13.9 %scatter_custom_fusion.3 = f32[288,384]{1,0:T(8,128)} fusion(s32[1715]{0:T(1024)S(1)} %fusion.5, f32[1715,384]{1,0:T(8,128)} %reshape.158, f32[]{:T(128)} %constant.12.clone.1), kind=kCustom, calls=%fused_computation.20 | custom fusion | flops 658560 | bytes 442880 | tf_op jit(solution)/shard_map/scatter-add | solution.py:44
  104.7 1.6 fusion.7
  106.3 1.1 collective-permute-start.6
  107.3 1.6 collective-permute-start.7
  108.9 1.0 slice.47
  109.9 1.2 collective-permute-done.6
  111.1 1.4 scatter_fusion.2
  112.4 0.0 collective-permute-done.7
  112.5 1.6 scatter_fusion.3
  114.1 0.9 multiply_subtract_fusion
  114.9 0.0 all-gather.3.cloned.1.call-update
  115.0 0.1 iota_add_fusion
  115.1 0.1 add.87
  115.2 0.0 all-gather.5.cloned.1.call-done
  115.2 6.9 %gather_fusion.6 = f32[1536,384]{1,0:T(8,128)} fusion(f32[1536,384]{1,0:T(8,128)} %all-gather.5.cloned.1.call-done, s32[2048]{0:T(1024)S(1)} %pad_clamp_fusion), kind=kCustom, calls=%fused_computation.6 | custom fusion | bytes 4724736 | tf_op jit(solution)/shard_map/gather | solution.py:74
  122.1 25.9 %all-gather.3.cloned.1.call-done = f32[192,1536]{1,0:T(8,128)} async-done(((f32[192,384]{1,0:T(8,128)}), f32[192,1536]{1,0:T(8,128)}) %all-gather.3.cloned.1.call-update) | async-done | bytes 1179664 | tf_op jit(solution)/shard_map/all_gather | solution.py:76
  148.1 4.9 %fusion.9 = f32[192,384]{1,0:T(8,128)} fusion(f32[192,1536]{1,0:T(8,128)} %all-gather.3.cloned.1.call-done, f32[1536,384]{1,0:T(8,128)} %gather_fusion.6), kind=kOutput, calls=%fused_computation.42 | convolution fusion | flops 1358954496 | bytes 3833856 | tf_op jit(solution)/shard_map/dot_general | solution.py:75
  (27 shorter events, 0.1 us)
Async XLA Ops:
  6.5 21.0 %copy-start = (f32[5,343,343]{2,1,0:T(8,128)S(1)}, f32[5,343,343]{2,1,0:T(8,128)}, u32[]{:S(2)}) copy-start(f32[5,343,343]{2,1,0:T(8,128)} %param.10) | copy-start | bytes 7058944
  6.5 9.1 %copy-start.5 = (s32[5,343]{1,0:T(8,128)S(1)}, s32[5,343]{1,0:T(8,128)}, u32[]{:S(2)}) copy-start(s32[5,343]{1,0:T(8,128)} %param.11) | copy-start | bytes 20584
  6.5 108.7 %all-gather.5.cloned.1.call-start = ((), (), s32[]{:S(2)}) async-start(), calls=%async_computation.1 | async-start | bytes 2654208 | tf_op jit(solution)/shard_map/all_gather | solution.py:73
  8.4 139.7 %all-gather.3.cloned.1.call-start = ((), (), s32[]{:S(2)}) async-start(), calls=%async_computation | async-start | bytes 1474560 | tf_op jit(solution)/shard_map/all_gather | solution.py:76
  9.1 6.5 %copy-start.7 = (s32[48]{0:T(128)}, s32[48]{0:T(128)S(1)}, u32[]{:S(2)}) copy-start(s32[48]{0:T(128)S(1)} %compare_select_fusion.4) | copy-start | bytes 580
  10.8 5.4 %collective-permute-start = (f32[48,384]{1,0:T(8,128)S(1)}, f32[48,384]{1,0:T(8,128)S(1)}, u32[]{:S(2)}, u32[]{:S(2)}) collective-permute-start(f32[48,384]{1,0:T(8,128)S(1)} %gather_fusion), channel_id=1, source_target_pairs={{0,4},{4,8},{8,12},{12,16},{16,20},{20,24},{24,28},{28,0},{1,5},{5... | collective-permute-start | bytes 221192 | tf_op jit(solution)/shard_map/ppermute | solution.py:19
  12.0 3.8 %copy-start.9 = (s32[48]{0:T(128)}, s32[48]{0:T(128)S(1)}, u32[]{:S(2)}) copy-start(s32[48]{0:T(128)S(1)} %compare_select_fusion.3) | copy-start | bytes 580
  12.6 4.9 %collective-permute-start.1 = (f32[48,384]{1,0:T(8,128)S(1)}, f32[48,384]{1,0:T(8,128)}, u32[]{:S(2)}, u32[]{:S(2)}) collective-permute-start(f32[48,384]{1,0:T(8,128)S(1)} %gather_fusion.1), channel_id=1, source_target_pairs={{4,0},{8,4},{12,8},{16,12},{20,16},{24,20},{28,24},{0,28},{5,1},{9... | collective-permute-start | bytes 221192 | tf_op jit(solution)/shard_map/ppermute | solution.py:22
  36.5 20.4 %copy-start.6 = (f32[192]{0:T(256)S(1)}, f32[192]{0:T(256)}, u32[]{:S(2)}) copy-start(f32[192]{0:T(256)} %param.9) | copy-start | bytes 2308
  40.1 21.3 %copy-start.2 = (f32[192,384]{1,0:T(8,128)S(1)}, f32[192,384]{1,0:T(8,128)}, u32[]{:S(2)}) copy-start(f32[192,384]{1,0:T(8,128)} %param.8) | copy-start | bytes 884740
  53.4 3.5 %copy-start.4 = (f32[288,384]{1,0:T(8,128)}, f32[288,384]{1,0:T(8,128)S(1)}, u32[]{:S(2)}) copy-start(f32[288,384]{1,0:T(8,128)S(1)} %scatter_custom_fusion) | copy-start | bytes 1327108
  54.1 4.8 %collective-permute-start.2 = (f32[48,384]{1,0:T(8,128)S(1)}, f32[48,384]{1,0:T(8,128)S(1)}, u32[]{:S(2)}, u32[]{:S(2)}) collective-permute-start(f32[48,384]{1,0:T(8,128)S(1)} %get-tuple-element.8), channel_id=1, source_target_pairs={{0,4},{4,8},{8,12},{12,16},{16,20},{20,24},{24,28},{28,0},{1,5},{5... | collective-permute-start | bytes 221192 | tf_op jit(solution)/shard_map/ppermute | solution.py:19
  55.7 4.4 %collective-permute-start.3 = (f32[48,384]{1,0:T(8,128)}, f32[48,384]{1,0:T(8,128)S(1)}, u32[]{:S(2)}, u32[]{:S(2)}) collective-permute-start(f32[48,384]{1,0:T(8,128)} %get-tuple-element.7), channel_id=1, source_target_pairs={{4,0},{8,4},{12,8},{16,12},{20,16},{24,20},{28,24},{0,28},{5,1},{9... | collective-permute-start | bytes 221192 | tf_op jit(solution)/shard_map/ppermute | solution.py:22
  62.2 6.0 %copy-start.1 = (f32[192,384]{1,0:T(8,128)}, f32[192,384]{1,0:T(8,128)S(1)}, u32[]{:S(2)}) copy-start(f32[192,384]{1,0:T(8,128)S(1)} %fusion) | copy-start | bytes 884740
  63.5 4.7 %collective-permute-start.4 = (f32[48,384]{1,0:T(8,128)S(1)}, f32[48,384]{1,0:T(8,128)S(1)}, u32[]{:S(2)}, u32[]{:S(2)}) collective-permute-start(f32[48,384]{1,0:T(8,128)S(1)} %gather_fusion.3), channel_id=1, source_target_pairs={{0,4},{4,8},{8,12},{12,16},{16,20},{20,24},{24,28},{28,0},{1,5},{5... | collective-permute-start | bytes 221192 | tf_op jit(solution)/shard_map/ppermute | solution.py:19
  64.1 4.2 %collective-permute-start.5 = (f32[48,384]{1,0:T(8,128)S(1)}, f32[48,384]{1,0:T(8,128)S(1)}, u32[]{:S(2)}, u32[]{:S(2)}) collective-permute-start(f32[48,384]{1,0:T(8,128)S(1)} %gather_fusion.4), channel_id=1, source_target_pairs={{4,0},{8,4},{12,8},{16,12},{20,16},{24,20},{28,24},{0,28},{5,1},{9... | collective-permute-start | bytes 221192 | tf_op jit(solution)/shard_map/ppermute | solution.py:22
  87.2 23.9 %copy-start.10 = (s32[48]{0:T(128)S(1)}, s32[48]{0:T(128)}, u32[]{:S(2)}) copy-start(s32[48]{0:T(128)} %copy-done.9) | copy-start | bytes 580
  87.2 25.2 %copy-start.8 = (s32[48]{0:T(128)S(1)}, s32[48]{0:T(128)}, u32[]{:S(2)}) copy-start(s32[48]{0:T(128)} %copy-done.7) | copy-start | bytes 580
  90.8 23.3 %copy-start.3 = (f32[192,384]{1,0:T(8,128)S(1)}, f32[192,384]{1,0:T(8,128)}, u32[]{:S(2)}) copy-start(f32[192,384]{1,0:T(8,128)} %param.8) | copy-start | bytes 884740
  90.8 24.2 %copy-start.11 = (s32[8]{0:T(128)S(1)}, s32[8]{0:T(128)}, u32[]{:S(2)}) copy-start(s32[8]{0:T(128)} %param.14) | copy-start | bytes 100
  106.3 4.8 %collective-permute-start.6 = (f32[48,384]{1,0:T(8,128)S(1)}, f32[48,384]{1,0:T(8,128)}, u32[]{:S(2)}, u32[]{:S(2)}) collective-permute-start(f32[48,384]{1,0:T(8,128)S(1)} %get-tuple-element.6), channel_id=1, source_target_pairs={{0,4},{4,8},{8,12},{12,16},{16,20},{20,24},{24,28},{28,0},{1,5},{5... | collective-permute-start | bytes 221192 | tf_op jit(solution)/shard_map/ppermute | solution.py:19
  107.3 5.1 %collective-permute-start.7 = (f32[48,384]{1,0:T(8,128)}, f32[48,384]{1,0:T(8,128)}, u32[]{:S(2)}, u32[]{:S(2)}) collective-permute-start(f32[48,384]{1,0:T(8,128)} %get-tuple-element.5), channel_id=1, source_target_pairs={{4,0},{8,4},{12,8},{16,12},{20,16},{24,20},{28,24},{0,28},{5,1},{9... | collective-permute-start | bytes 221192 | tf_op jit(solution)/shard_map/ppermute | solution.py:22
Sparse Core Ops, SparseCore 0:
  9.2 31.7 all-gather.4
  115.1 32.9 all-gather.2
where the time goes:
time: 161 us; the launch traced here: 160 us
  local copies, waits for them, and re-layouts  41.1 us (26%)
  other arithmetic  39.3 us (24%)
  waiting for transfers between devices  31.4 us (20%)
  matrix products  22.8 us (14%)
  between operations  13.6 us (8%)
  starting transfers between devices  11.6 us (7%)
    scatter-add x2, other arithmetic, apply_operator(): empty.at[cell_nodes.reshape(-1)].add(products.reshape(-1, block_cols))  27.2 us
    all_gather x1, waiting for transfers between devices, shards(): lax.all_gather(filtered_two, 'band', axis=1, tiled=True)  25.9 us
    gather x4, local copies, waits for them, and re-layouts, apply_operator(): gathered = extended[cell_nodes]  18.1 us
    dot_general x2, matrix products, apply_operator(): jnp.einsum('cij,cjs->cis', cell_ham, gathered, precision=lax.Precision.HI...  17.9 us
    ppermute x4, starting transfers between devices, with_halo(): lax.ppermute(lax.slice_in_dim(block, 0, width, axis=dim), axis, backward)  7.83 us
    reshape x2, local copies, waits for them, and re-layouts, apply_operator(): products.reshape(-1, block_cols)  7.19 us
    gather x1, local copies, waits for them, and re-layouts, shards(): ordered = columns[row_index]  6.91 us
    dot_general x1, matrix products, shards(): jnp.dot(lax.all_gather(filtered_two, 'band', axis=1, tiled=True), ordered...  4.88 us
  transfers between devices with their start and end apart: 10, of which 6 were waited for; matrix products, arithmetic and copies ran while one was open for 60% of the time, Pallas kernels for 0%

commit v1 on v0

v1 whole, which is shorter than its diff:
```python
import functools

import jax
import jax.numpy as jnp
from jax import lax
from jax.experimental import pallas as pl
from jax.experimental.pallas import tpu as pltpu
from jax.sharding import PartitionSpec as P

filter_center = 2.5
filter_half = 3.5
spectrum_floor = -4.0
sigma_one = filter_half / (spectrum_floor - filter_center)
sigma_two = 1.0 / (2.0 / sigma_one - sigma_one)

f32 = jnp.float32
bf16 = jnp.bfloat16
VMEM_LIMIT = 48 * 1024 * 1024


def split(x):
    hi = x.astype(bf16)
    lo = (x - hi.astype(f32)).astype(bf16)
    return hi, lo


def mm(a, b, dims=((1,), (0,))):
    return lax.dot_general(a, b, (dims, ((), ())), preferred_element_type=f32)


def select(onehot, x):
    hi, lo = split(x)
    rest = (x - hi.astype(f32) - lo.astype(f32)).astype(bf16)
    return mm(onehot, hi) + mm(onehot, lo) + mm(onehot, rest)


def as_column(row):
    n = row.shape[1]
    here = lax.broadcasted_iota(jnp.int32, (n, n), 0) == lax.broadcasted_iota(jnp.int32, (n, n), 1)
    return jnp.sum(jnp.where(here, row, jnp.zeros_like(row)), axis=1, keepdims=True)


def pick_rows(list_row, owned):
    column = as_column(list_row.astype(f32)).astype(jnp.int32)
    shape = (list_row.shape[1], owned)
    return (lax.broadcasted_iota(jnp.int32, shape, 1) == column).astype(f32).astype(bf16)


def put_rows(list_row, owned):
    shape = (owned, list_row.shape[1])
    return (lax.broadcasted_iota(jnp.int32, shape, 0) == list_row).astype(f32).astype(bf16)


def call(kernel, out_shape, args, cost, scalars=(), **kwargs):
    vmem = pl.BlockSpec(memory_space=pltpu.VMEM)
    smem = pl.BlockSpec(memory_space=pltpu.SMEM)
    specs = [smem if i in scalars else vmem for i in range(len(args))]
    return pl.pallas_call(
        kernel,
        out_shape=out_shape,
        in_specs=specs,
        out_specs=jax.tree.map(lambda _: vmem, out_shape),
        compiler_params=pltpu.CompilerParams(vmem_limit_bytes=VMEM_LIMIT),
        cost_estimate=pl.CostEstimate(flops=cost, bytes_accessed=1 << 20, transcendentals=0),
        **kwargs,
    )(*args)


def shape(*dims, dtype=f32):
    return jax.ShapeDtypeStruct(dims, dtype)


def send_kernel(s, m, up, dn, up_out, dn_out):
    owned = s.shape[0]
    x = s[...] * as_column(m[...])
    up_out[...] = select(pick_rows(up[...], owned), x)
    dn_out[...] = select(pick_rows(dn[...], owned), x)


def assemble_kernel(ham, nodes, out, total):
    cell = pl.program_id(0)
    ext = total.shape[0]
    row = nodes[pl.ds(cell, 1), :]
    spread = (lax.broadcasted_iota(jnp.int32, (ext, row.shape[1]), 0) == row).astype(f32).astype(bf16)
    hi, lo = split(ham[0])
    left_hi, left_lo = split(mm(spread, hi) + mm(spread, lo))
    both = mm(jnp.concatenate([left_hi, left_lo], axis=0), spread, ((1,), (1,)))
    term = both[:ext] + both[ext:]

    @pl.when(cell == 0)
    def _():
        total[...] = term

    @pl.when(cell > 0)
    def _():
        total[...] += term

    @pl.when(cell == pl.num_programs(0) - 1)
    def _():
        full = total[...]
        hi = full.astype(bf16).astype(f32)
        out[...] = jnp.concatenate([hi, full - hi, hi], axis=1).astype(bf16)


def assemble(cell_ham, cell_nodes, ext):
    cells, n, _ = cell_ham.shape
    return pl.pallas_call(
        assemble_kernel,
        grid=(cells,),
        out_shape=shape(ext, 3 * ext, dtype=bf16),
        in_specs=[
            pl.BlockSpec((1, n, n), lambda c: (c, 0, 0)),
            pl.BlockSpec((cells, n), lambda c: (0, 0)),
        ],
        out_specs=pl.BlockSpec((ext, 3 * ext), lambda c: (0, 0)),
        scratch_shapes=[pltpu.VMEM((ext, ext), f32)],
        compiler_params=pltpu.CompilerParams(vmem_limit_bytes=VMEM_LIMIT),
        cost_estimate=pl.CostEstimate(
            flops=cells * 8 * n * n * ext, bytes_accessed=cells * n * n * 4, transcendentals=0
        ),
    )(cell_ham, cell_nodes)


def apply_kernel(v, m, lower, upper, ham, own, to_lower, to_upper):
    owned = v.shape[0]
    ghost = lower.shape[0]
    x = jnp.concatenate([v[...] * as_column(m[...]), lower[...], upper[...]], axis=0)
    hi, lo = split(x)
    z = mm(ham[...], jnp.concatenate([hi, hi, lo], axis=0))
    own[...] = z[:owned]
    to_lower[...] = z[owned : owned + ghost]
    to_upper[...] = z[owned + ghost :]


def collect(own, from_upper, from_lower, up, dn):
    owned = own.shape[0]
    return (
        own[...]
        + select(put_rows(up[...], owned), from_upper[...])
        + select(put_rows(dn[...], owned), from_lower[...])
    )


def middle_kernel(own, from_upper, from_lower, s, m, up, dn, one, up_out, dn_out):
    owned = s.shape[0]
    column = as_column(m[...])
    r = collect(own, from_upper, from_lower, up, dn)
    filtered = (sigma_one / filter_half) * (r * column - filter_center * s[...])
    one[...] = filtered
    x = filtered * column
    up_out[...] = select(pick_rows(up[...], owned), x)
    dn_out[...] = select(pick_rows(dn[...], owned), x)


def last_kernel(own, from_upper, from_lower, s, one, m, up, dn, two):
    column = as_column(m[...])
    r = collect(own, from_upper, from_lower, up, dn)
    two[...] = (
        2.0 * sigma_two / filter_half * (r * column - filter_center * one[...])
        - sigma_one * sigma_two * s[...]
    )


def order_kernel(owner, *refs):
    parts, (hi_out, lo_out) = refs[:-2], refs[-2:]
    here = lax.axis_index("dom")
    for b, part in enumerate(parts):
        slot = here ^ b
        place = jnp.int32(0)
        for p in range(len(parts)):
            place = place + jnp.where(owner[p] == slot, p, 0)
        hi, lo = split(part[...])
        hi_out[place] = hi
        lo_out[place] = lo


def rotate_kernel(hi_ref, lo_ref, *refs):
    parts, out = refs[:-1], refs[-1]
    here = lax.axis_index("band")
    bands = hi_ref.shape[0]
    total = None
    for r, part in enumerate(parts):
        k = lax.rem(here + r, bands)
        hi, lo = split(part[...])
        rhi, rlo = hi_ref[k], lo_ref[k]
        term = mm(
            jnp.concatenate([hi, lo, hi], axis=1), jnp.concatenate([rhi, rhi, rlo], axis=0)
        )
        total = term if total is None else total + term
    out[...] = total


def cyclic(count, step):
    return [(i, (i + step) % count) for i in range(count)]


def flip(count, bits):
    return [(i, i ^ bits) for i in range(count)]


def ordered_rotation(own_columns, owner, bands):
    doms = lax.axis_size("dom")
    rows, cols = own_columns.shape
    if doms == 8 and rows % 16 == 0:
        parts = [own_columns] + [
            lax.ppermute(own_columns, "dom", flip(doms, bits)) for bits in (2, 4, 6)
        ]
        other = [lax.ppermute(part, "dom", flip(doms, 1)) for part in parts]
        slots = [part for pair in zip(parts, other) for part in pair]
        hi, lo = call(
            order_kernel,
            (shape(doms, rows, cols, dtype=bf16),) * 2,
            [owner, *slots],
            rows * doms * cols * 16,
            scalars=(0,),
        )
    else:
        columns = lax.all_gather(own_columns, "dom", axis=0, tiled=True)
        hi, lo = split(columns.reshape(doms, rows, cols)[owner])
    total = doms * rows
    return hi.reshape(bands, total // bands, cols), lo.reshape(bands, total // bands, cols)


def shards(states, inv_mass, cell_ham, cell_nodes, send_up, send_down, owner, rotation_store):
    owned, cols = states.shape
    ghost = send_up.shape[0]
    ext = owned + 2 * ghost
    doms, bands = lax.axis_size("dom"), lax.axis_size("band")
    m = inv_mass[None, :]
    up = send_up[None, :]
    dn = send_down[None, :]
    upward, downward = cyclic(doms, 1), cyclic(doms, -1)
    halo = shape(ghost, cols)
    block = shape(owned, cols)
    small = 4 * ghost * owned * cols * 3

    def exchange(to_upper, to_lower):
        from_lower = lax.ppermute(to_upper, "dom", upward)
        from_upper = lax.ppermute(to_lower, "dom", downward)
        return from_lower, from_upper

    def apply(v, lower, upper, ham):
        own, to_lower, to_upper = call(
            apply_kernel, (block, halo, halo), [v, m, lower, upper, ham], 6 * ext * ext * cols
        )
        from_lower, from_upper = exchange(to_upper, to_lower)
        return own, from_upper, from_lower

    to_upper, to_lower = call(send_kernel, (halo, halo), [states, m, up, dn], small)
    lower, upper = exchange(to_upper, to_lower)
    ham = assemble(cell_ham, cell_nodes, ext)
    band = lax.axis_index("band")
    own_columns = lax.dynamic_slice_in_dim(rotation_store, band * cols, cols, 1)
    rot_hi, rot_lo = ordered_rotation(own_columns, owner, bands)
    first = apply(states, lower, upper, ham)
    one, to_upper, to_lower = call(
        middle_kernel, (block, halo, halo), [*first, states, m, up, dn], 2 * small
    )
    lower, upper = exchange(to_upper, to_lower)
    second = apply(one, lower, upper, ham)
    two = call(last_kernel, block, [*second, states, one, m, up, dn], small)
    parts = [two] + [lax.ppermute(two, "band", cyclic(bands, -r)) for r in range(1, bands)]
    return call(
        rotate_kernel, block, [rot_hi, rot_lo, *parts], 6 * owned * cols * cols * bands
    )


def solution(mesh):
    in_specs = (
        P("dom", "band"),
        P("dom"),
        P("dom", None, None),
        P("dom", None),
        P("dom"),
        P("dom"),
        P(),
        P("dom", None),
    )
    out_specs = P("dom", "band")
    return jax.shard_map(shards, mesh=mesh, in_specs=in_specs, out_specs=out_specs, check_vma=False)
```

time: 161 us -> 71.1 us (0.44)
  other arithmetic: 39.3 us -> 0 us
  local copies, waits for them, and re-layouts: 41.1 us -> 6.73 us
  matrix products: 22.8 us -> 0 us
  between operations: 13.6 us -> 0.16 us
  Pallas kernels: 0 us -> 10.4 us
  waiting for transfers between devices: 31.4 us -> 37.6 us
  starting transfers between devices: 11.6 us -> 15.9 us
    scatter-add x6 -> x0, other arithmetic: 32.6 us -> none  [the longest x2 27.2 us: apply_operator(): empty.at[cell_nodes.reshape(-1)].add(products.reshape(-1, block_cols))]
    ppermute x8 -> x18, waiting for transfers between devices: 5.38 us -> 37.6 us  [the longest x3 21.1 us: shards(): lax.ppermute(two, 'band', cyclic(bands, -r))]
    gather x9 -> x0, local copies, waits for them, and re-layouts: 27.5 us -> none  [the longest x4 18.1 us: apply_operator(): gathered = extended[cell_nodes]]
    all_gather x2 -> x0, waiting for transfers between devices: 26 us -> none  [the longest x1 25.9 us: shards(): lax.all_gather(filtered_two, 'band', axis=1, tiled=True)]
    dot_general x3 -> x0, matrix products: 22.8 us -> none  [the longest x2 17.9 us: apply_operator(): jnp.einsum('cij,cjs->cis', cell_ham, gathered, precision=lax.Precision.HI...]
    pallas_call x0 -> x8, Pallas kernels: none -> 10.4 us  [the longest x7 5.65 us: call(): pl.pallas_call(kernel, out_shape=out_shape, in_specs=specs, out_specs=jax...]
    reshape x3 -> x0, local copies, waits for them, and re-layouts: 7.27 us -> none  [the longest x2 7.19 us: apply_operator(): products.reshape(-1, block_cols)]
    unnamed x24, local copies, waits for them, and re-layouts: 0.05 us -> 6.7 us
  transfers between devices with their start and end apart: 10 -> 18, of which waited for: 6 -> 8; matrix products, arithmetic and copies ran while one was open for 60% -> 0% of each run, Pallas kernels for 0% -> 12%
where the time goes in v1:
time: 71.1 us; the launch traced here: 70.8 us
  waiting for transfers between devices  37.6 us (53%)
  starting transfers between devices  15.9 us (22%)
  Pallas kernels  10.4 us (15%)
  local copies, waits for them, and re-layouts  6.73 us (9%)
    ppermute x3, waiting for transfers between devices, shards(): lax.ppermute(two, 'band', cyclic(bands, -r))  21.1 us
    ppermute x4, waiting for transfers between devices, exchange(): from_lower = lax.ppermute(to_upper, 'dom', upward)  10.7 us
    unnamed x24, local copies, waits for them, and re-layouts  6.7 us
    ppermute x4, waiting for transfers between devices, exchange(): from_upper = lax.ppermute(to_lower, 'dom', downward)  5.82 us
    pallas_call x7, Pallas kernels, call(): pl.pallas_call(kernel, out_shape=out_shape, in_specs=specs, out_specs=jax...  5.65 us
    ppermute x4, starting transfers between devices, exchange(): from_upper = lax.ppermute(to_lower, 'dom', downward)  5.52 us
    pallas_call x1, Pallas kernels, assemble(): pl.pallas_call(assemble_kernel, grid=(cells,), out_shape=shape(ext, 3 * e...  4.77 us
    ppermute x3, starting transfers between devices, shards(): lax.ppermute(two, 'band', cyclic(bands, -r))  4.67 us
  transfers between devices with their start and end apart: 18, of which 8 were waited for; matrix products, arithmetic and copies ran while one was open for 0% of the time, Pallas kernels for 12%

profile of v1, /device:TPU:0, one launch (start us, length us, event | category | flops | bytes accessed | tf_op | source)
XLA Modules:
  0.0 70.8 jit_solution(11575217824702518940)
XLA Ops:
  0.0 0.0 copy-start
  0.0 1.3 %copy-done = f32[192,1536]{1,0:T(8,128)S(1)} copy-done((f32[192,1536]{1,0:T(8,128)S(1)}, f32[192,1536]{1,0:T(8,128)}, u32[]{:S(2)}) %copy-start) | copy-done | bytes 1179672
  1.3 3.0 %collective-permute-start.1 = (f32[192,384]{1,0:T(8,128)S(1)}, f32[192,384]{1,0:T(8,128)S(1)}, u32[]{:S(2)}, u32[]{:S(2)}) collective-permute-start(f32[192,384]{1,0:T(8,128)S(1)} %constant_dynamic-slice_fusion.refs_0_), channel_id=1, source_target_pairs={{0,8},{4,12},{8,0},{12,4},{16,24},{20,28},{24,16},{28,20},{1,9},{5... | collective-permute-start | bytes 884744 | tf_op jit(solution)/shard_map/ppermute | solution.py:206
  4.3 1.5 %collective-permute-start.3 = (f32[192,384]{1,0:T(8,128)S(1)}, f32[192,384]{1,0:T(8,128)S(1)}, u32[]{:S(2)}, u32[]{:S(2)}) collective-permute-start(f32[192,384]{1,0:T(8,128)S(1)} %constant_dynamic-slice_fusion.refs_0_), channel_id=1, source_target_pairs={{0,16},{4,20},{8,24},{12,28},{16,0},{20,4},{24,8},{28,12},{1,17},{... | collective-permute-start | bytes 884744 | tf_op jit(solution)/shard_map/ppermute | solution.py:206
  5.8 0.0 copy-start.1
  5.8 1.0 %copy-done.1 = f32[192,384]{1,0:T(8,128)S(1)} copy-done((f32[192,384]{1,0:T(8,128)S(1)}, f32[192,384]{1,0:T(8,128)}, u32[]{:S(2)}) %copy-start.1) | copy-done | bytes 294936
  6.8 0.7 copy-done.3
  7.5 0.0 copy-start.5
  7.5 0.7 copy-done.5
  8.1 0.0 copy-start.7
  8.1 0.7 copy-done.7
  8.8 0.4 shard_map.83
  9.2 0.1 collective-permute-start.7
  9.3 0.0 copy-start.2
  9.3 0.0 copy-start.4
  9.3 0.0 copy-start.6
  9.3 0.0 copy-start.8
  9.3 2.6 %collective-permute-start.8 = (f32[48,384]{1,0:T(8,128)S(1)}, f32[48,384]{1,0:T(8,128)S(1)}, u32[]{:S(2)}, u32[]{:S(2)}) collective-permute-start(f32[48,384]{1,0:T(8,128)S(1)} %get-tuple-element.21), channel_id=1, source_target_pairs={{0,28},{4,0},{8,4},{12,8},{16,12},{20,16},{24,20},{28,24},{1,29},{... | collective-permute-start | bytes 221192 | tf_op jit(solution)/shard_map/ppermute | solution.py:239
  12.0 1.7 %copy-done.10 = f32[5,343,343]{2,1,0:T(8,128)S(1)} copy-done((f32[5,343,343]{2,1,0:T(8,128)S(1)}, f32[5,343,343]{2,1,0:T(8,128)}, u32[]{:S(2)}) %copy-start.10) | copy-done | bytes 2353004
  13.7 0.7 copy-done.11
  14.4 4.8 %shard_map.84.ham = bf16[288,864]{1,0:T(8,128)(2,1)S(1)} custom-call(f32[5,343,343]{2,1,0:T(8,128)S(1)} %copy-done.10, s32[5,343]{1,0:T(8,128)S(1)} %copy-done.11), custom_call_target="tpu_custom_call" | custom-call | flops 1355316480 | bytes 2352980 | tf_op jit(solution)/shard_map/pallas_call | solution.py:107
  19.2 0.0 collective-permute-done.7.lower
  19.2 0.0 collective-permute-done.8.upper
  19.2 0.0 copy-done.2
  19.2 0.0 copy-done.4
  19.2 0.6 shard_map.85
  19.8 0.1 collective-permute-start.9
  19.9 0.4 collective-permute-start.10
  20.4 0.0 collective-permute-start.5
  20.4 1.9 %collective-permute-done.9.from_upper = f32[48,384]{1,0:T(8,128)S(1)} collective-permute-done((f32[48,384]{1,0:T(8,128)S(1)}, f32[48,384]{1,0:T(8,128)S(1)}, u32[]{:S(2)}, u32[]{:S(2)}) %collective-permute-start.9) | collective-permute-done | bytes 73760 | tf_op jit(solution)/shard_map/ppermute | solution.py:239
  22.4 0.4 collective-permute-start
  22.7 0.0 collective-permute-done.1.refs_2_
  22.7 0.2 collective-permute-start.2
  22.9 1.8 %collective-permute-done.10.from_lower = f32[48,384]{1,0:T(8,128)S(1)} collective-permute-done((f32[48,384]{1,0:T(8,128)S(1)}, f32[48,384]{1,0:T(8,128)S(1)}, u32[]{:S(2)}, u32[]{:S(2)}) %collective-permute-start.10) | collective-permute-done | bytes 73760 | tf_op jit(solution)/shard_map/ppermute | solution.py:238
  24.6 0.0 copy-done.6
  24.6 0.0 copy-done.8
  24.6 0.8 %shard_map.86 = (f32[192,384]{1,0:T(8,128)S(1)}, f32[48,384]{1,0:T(8,128)S(1)}, f32[48,384]{1,0:T(8,128)S(1)}) custom-call(f32[192,384]{1,0:T(8,128)S(1)} %get-tuple-element.22.own, f32[48,384]{1,0:T(8,128)S(1)} %collective-permute-done.9.from_upper, f32[48,384]{1,0:T(8,128)S(1)} %collective-permute-done.10.from_lower, f32[192,384]{1,0:T(8,128)S(1)} %copy-done.2, ...), custom_call_target="tpu_custom_call" | custom-call | flops 84934656 | bytes 1048576 | tf_op jit(solution)/shard_map/pallas_call | solution.py:58
  25.4 0.0 collective-permute-start.11
  25.5 6.2 %collective-permute-done.11.lower = f32[48,384]{1,0:T(8,128)S(1)} collective-permute-done((f32[48,384]{1,0:T(8,128)S(1)}, f32[48,384]{1,0:T(8,128)S(1)}, u32[]{:S(2)}, u32[]{:S(2)}) %collective-permute-start.11) | collective-permute-done | bytes 73760 | tf_op jit(solution)/shard_map/ppermute | solution.py:238
  31.7 0.0 collective-permute-start.12
  31.7 2.0 %collective-permute-done.12.upper = f32[48,384]{1,0:T(8,128)S(1)} collective-permute-done((f32[48,384]{1,0:T(8,128)S(1)}, f32[48,384]{1,0:T(8,128)S(1)}, u32[]{:S(2)}, u32[]{:S(2)}) %collective-permute-start.12) | collective-permute-done | bytes 73760 | tf_op jit(solution)/shard_map/ppermute | solution.py:239
  33.7 0.6 shard_map.87
  34.3 2.7 %collective-permute-start.13 = (f32[48,384]{1,0:T(8,128)S(1)}, f32[48,384]{1,0:T(8,128)S(1)}, u32[]{:S(2)}, u32[]{:S(2)}) collective-permute-start(f32[48,384]{1,0:T(8,128)S(1)} %get-tuple-element.29), channel_id=1, source_target_pairs={{0,28},{4,0},{8,4},{12,8},{16,12},{20,16},{24,20},{28,24},{1,29},{... | collective-permute-start | bytes 221192 | tf_op jit(solution)/shard_map/ppermute | solution.py:239
  37.0 0.0 collective-permute-done.3.refs_4_
  37.0 0.0 collective-permute-start.14
  37.0 0.0 collective-permute-done.5.refs_6_
  37.0 0.1 collective-permute-start.4
  37.1 1.9 %collective-permute-done.13.from_upper = f32[48,384]{1,0:T(8,128)S(1)} collective-permute-done((f32[48,384]{1,0:T(8,128)S(1)}, f32[48,384]{1,0:T(8,128)S(1)}, u32[]{:S(2)}, u32[]{:S(2)}) %collective-permute-start.13) | collective-permute-done | bytes 73760 | tf_op jit(solution)/shard_map/ppermute | solution.py:239
  39.0 0.0 collective-permute-start.6
  39.0 2.7 %collective-permute-done.14.from_lower = f32[48,384]{1,0:T(8,128)S(1)} collective-permute-done((f32[48,384]{1,0:T(8,128)S(1)}, f32[48,384]{1,0:T(8,128)S(1)}, u32[]{:S(2)}, u32[]{:S(2)}) %collective-permute-start.14) | collective-permute-done | bytes 73760 | tf_op jit(solution)/shard_map/ppermute | solution.py:238
  41.7 0.4 shard_map.88.refs_0_
  42.1 3.7 %collective-permute-start.15 = (f32[192,384]{1,0:T(8,128)S(1)}, f32[192,384]{1,0:T(8,128)S(1)}, u32[]{:S(2)}, u32[]{:S(2)}) collective-permute-start(f32[192,384]{1,0:T(8,128)S(1)} %shard_map.88.refs_0_), channel_id=1, source_target_pairs={{0,3},{1,0},{2,1},{3,2},{4,7},{5,4},{6,5},{7,6},{8,11},{9,8},{10,9... | collective-permute-start | bytes 884744 | tf_op jit(solution)/shard_map/ppermute | solution.py:262
  45.8 0.0 collective-permute-done.refs_1_
  45.8 0.0 collective-permute-start.16
  45.8 0.0 collective-permute-done.2.refs_3_
  45.8 1.0 %collective-permute-start.17 = (f32[192,384]{1,0:T(8,128)S(1)}, f32[192,384]{1,0:T(8,128)S(1)}, u32[]{:S(2)}, u32[]{:S(2)}) collective-permute-start(f32[192,384]{1,0:T(8,128)S(1)} %shard_map.88.refs_0_), channel_id=1, source_target_pairs={{0,1},{1,2},{2,3},{3,0},{4,5},{5,6},{6,7},{7,4},{8,9},{9,10},{10,1... | collective-permute-start | bytes 884744 | tf_op jit(solution)/shard_map/ppermute | solution.py:262
  46.8 0.0 collective-permute-done.4.refs_5_
  46.8 0.0 collective-permute-done.6.refs_7_
  46.8 0.0 copy-done.9
  46.8 1.0 %shard_map.82 = (bf16[8,192,384]{2,1,0:T(8,128)(2,1)S(1)}, bf16[8,192,384]{2,1,0:T(8,128)(2,1)S(1)}) custom-call(s32[8]{0:T(128)S(1)} %copy-done.9, f32[192,384]{1,0:T(8,128)S(1)} %constant_dynamic-slice_fusion.refs_0_, f32[192,384]{1,0:T(8,128)S(1)} %collective-permute-done.refs_1_, f32[192,384]{1,0:T(8,128)S(1)} %collective-permute-done.1.refs_2_, ...), custom_call_target="tpu_custom_call" | custom-call | flops 9437184 | bytes 1048576 | tf_op jit(solution)/shard_map/pallas_call | solution.py:58
  47.8 5.4 %collective-permute-done.15.refs_1_ = f32[192,384]{1,0:T(8,128)S(1)} collective-permute-done((f32[192,384]{1,0:T(8,128)S(1)}, f32[192,384]{1,0:T(8,128)S(1)}, u32[]{:S(2)}, u32[]{:S(2)}) %collective-permute-start.15) | collective-permute-done | bytes 294944 | tf_op jit(solution)/shard_map/ppermute | solution.py:262
  53.2 15.6 %collective-permute-done.16.refs_2_ = f32[192,384]{1,0:T(8,128)S(1)} collective-permute-done((f32[192,384]{1,0:T(8,128)S(1)}, f32[192,384]{1,0:T(8,128)S(1)}, u32[]{:S(2)}, u32[]{:S(2)}) %collective-permute-start.16) | collective-permute-done | bytes 294944 | tf_op jit(solution)/shard_map/ppermute | solution.py:262
  68.9 0.0 collective-permute-done.17.refs_3_
  68.9 1.9 %shard_map.89 = f32[192,384]{1,0:T(8,128)} custom-call(bf16[4,384,384]{2,1,0:T(8,128)(2,1)S(1)} %bitcast.5, bf16[4,384,384]{2,1,0:T(8,128)(2,1)S(1)} %bitcast.6, f32[192,384]{1,0:T(8,128)S(1)} %shard_map.88.refs_0_, f32[192,384]{1,0:T(8,128)S(1)} %collective-permute-done.15.refs_1_, f32[192,384]{1,0:T(8,128)S(1)} %collective-permute-done.16.refs_2_, ...), custom_call_target="tpu_custom_call" | custom-call | flops 679477248 | bytes 1048576 | tf_op jit(solution)/shard_map/pallas_call | solution.py:58
  (5 shorter events, 0.0 us)
Async XLA Ops:
  0.0 1.3 %copy-start = (f32[192,1536]{1,0:T(8,128)S(1)}, f32[192,1536]{1,0:T(8,128)}, u32[]{:S(2)}) copy-start(f32[192,1536]{1,0:T(8,128)} %param.15) | copy-start | bytes 3538948
  1.3 21.4 %collective-permute-start.1 = (f32[192,384]{1,0:T(8,128)S(1)}, f32[192,384]{1,0:T(8,128)S(1)}, u32[]{:S(2)}, u32[]{:S(2)}) collective-permute-start(f32[192,384]{1,0:T(8,128)S(1)} %constant_dynamic-slice_fusion.refs_0_), channel_id=1, source_target_pairs={{0,8},{4,12},{8,0},{12,4},{16,24},{20,28},{24,16},{28,20},{1,9},{5... | collective-permute-start | bytes 884744 | tf_op jit(solution)/shard_map/ppermute | solution.py:206
  4.3 32.7 %collective-permute-start.3 = (f32[192,384]{1,0:T(8,128)S(1)}, f32[192,384]{1,0:T(8,128)S(1)}, u32[]{:S(2)}, u32[]{:S(2)}) collective-permute-start(f32[192,384]{1,0:T(8,128)S(1)} %constant_dynamic-slice_fusion.refs_0_), channel_id=1, source_target_pairs={{0,16},{4,20},{8,24},{12,28},{16,0},{20,4},{24,8},{28,12},{1,17},{... | collective-permute-start | bytes 884744 | tf_op jit(solution)/shard_map/ppermute | solution.py:206
  5.8 1.0 %copy-start.1 = (f32[192,384]{1,0:T(8,128)S(1)}, f32[192,384]{1,0:T(8,128)}, u32[]{:S(2)}) copy-start(f32[192,384]{1,0:T(8,128)} %s.5) | copy-start | bytes 884740
  6.8 0.7 copy-start.3
  7.5 0.7 copy-start.5
  8.1 0.7 copy-start.7
  9.2 10.0 %collective-permute-start.7 = (f32[48,384]{1,0:T(8,128)S(1)}, f32[48,384]{1,0:T(8,128)S(1)}, u32[]{:S(2)}, u32[]{:S(2)}) collective-permute-start(f32[48,384]{1,0:T(8,128)S(1)} %get-tuple-element.20), channel_id=1, source_target_pairs={{0,4},{4,8},{8,12},{12,16},{16,20},{20,24},{24,28},{28,0},{1,5},{5... | collective-permute-start | bytes 221192 | tf_op jit(solution)/shard_map/ppermute | solution.py:238
  9.3 10.0 %copy-start.2 = (f32[192,384]{1,0:T(8,128)S(1)}, f32[192,384]{1,0:T(8,128)}, u32[]{:S(2)}) copy-start(f32[192,384]{1,0:T(8,128)} %s.5) | copy-start | bytes 884740
  9.3 10.0 %copy-start.4 = (f32[192]{0:T(256)S(1)}, f32[192]{0:T(256)}, u32[]{:S(2)}) copy-start(f32[192]{0:T(256)} %param.9) | copy-start | bytes 2308
  9.3 15.3 %copy-start.6 = (s32[48]{0:T(128)S(1)}, s32[48]{0:T(128)}, u32[]{:S(2)}) copy-start(s32[48]{0:T(128)} %param.12) | copy-start | bytes 580
  9.3 15.3 %copy-start.8 = (s32[48]{0:T(128)S(1)}, s32[48]{0:T(128)}, u32[]{:S(2)}) copy-start(s32[48]{0:T(128)} %param.13) | copy-start | bytes 580
  9.3 9.9 %collective-permute-start.8 = (f32[48,384]{1,0:T(8,128)S(1)}, f32[48,384]{1,0:T(8,128)S(1)}, u32[]{:S(2)}, u32[]{:S(2)}) collective-permute-start(f32[48,384]{1,0:T(8,128)S(1)} %get-tuple-element.21), channel_id=1, source_target_pairs={{0,28},{4,0},{8,4},{12,8},{16,12},{20,16},{24,20},{28,24},{1,29},{... | collective-permute-start | bytes 221192 | tf_op jit(solution)/shard_map/ppermute | solution.py:239
  12.0 1.7 %copy-start.10 = (f32[5,343,343]{2,1,0:T(8,128)S(1)}, f32[5,343,343]{2,1,0:T(8,128)}, u32[]{:S(2)}) copy-start(f32[5,343,343]{2,1,0:T(8,128)} %ham.1) | copy-start | bytes 7058944
  13.7 0.7 copy-start.11
  19.8 2.5 %collective-permute-start.9 = (f32[48,384]{1,0:T(8,128)S(1)}, f32[48,384]{1,0:T(8,128)S(1)}, u32[]{:S(2)}, u32[]{:S(2)}) collective-permute-start(f32[48,384]{1,0:T(8,128)S(1)} %get-tuple-element.23), channel_id=1, source_target_pairs={{0,28},{4,0},{8,4},{12,8},{16,12},{20,16},{24,20},{28,24},{1,29},{... | collective-permute-start | bytes 221192 | tf_op jit(solution)/shard_map/ppermute | solution.py:239
  19.9 4.7 %collective-permute-start.10 = (f32[48,384]{1,0:T(8,128)S(1)}, f32[48,384]{1,0:T(8,128)S(1)}, u32[]{:S(2)}, u32[]{:S(2)}) collective-permute-start(f32[48,384]{1,0:T(8,128)S(1)} %get-tuple-element.24), channel_id=1, source_target_pairs={{0,4},{4,8},{8,12},{12,16},{16,20},{20,24},{24,28},{28,0},{1,5},{5... | collective-permute-start | bytes 221192 | tf_op jit(solution)/shard_map/ppermute | solution.py:238
  20.4 16.7 %collective-permute-start.5 = (f32[192,384]{1,0:T(8,128)S(1)}, f32[192,384]{1,0:T(8,128)S(1)}, u32[]{:S(2)}, u32[]{:S(2)}) collective-permute-start(f32[192,384]{1,0:T(8,128)S(1)} %constant_dynamic-slice_fusion.refs_0_), channel_id=1, source_target_pairs={{0,24},{4,28},{8,16},{12,20},{16,8},{20,12},{24,0},{28,4},{1,25},{... | collective-permute-start | bytes 884744 | tf_op jit(solution)/shard_map/ppermute | solution.py:206
  22.4 23.4 %collective-permute-start = (f32[192,384]{1,0:T(8,128)S(1)}, f32[192,384]{1,0:T(8,128)S(1)}, u32[]{:S(2)}, u32[]{:S(2)}) collective-permute-start(f32[192,384]{1,0:T(8,128)S(1)} %constant_dynamic-slice_fusion.refs_0_), channel_id=1, source_target_pairs={{0,4},{4,0},{8,12},{12,8},{16,20},{20,16},{24,28},{28,24},{1,5},{5... | collective-permute-start | bytes 884744 | tf_op jit(solution)/shard_map/ppermute | solution.py:208
  22.7 23.1 %collective-permute-start.2 = (f32[192,384]{1,0:T(8,128)S(1)}, f32[192,384]{1,0:T(8,128)S(1)}, u32[]{:S(2)}, u32[]{:S(2)}) collective-permute-start(f32[192,384]{1,0:T(8,128)S(1)} %collective-permute-done.1.refs_2_), channel_id=1, source_target_pairs={{0,4},{4,0},{8,12},{12,8},{16,20},{20,16},{24,28},{28,24},{1,5},{5... | collective-permute-start | bytes 884744 | tf_op jit(solution)/shard_map/ppermute | solution.py:208
  25.4 21.4 %copy-start.9 = (s32[8]{0:T(128)S(1)}, s32[8]{0:T(128)}, u32[]{:S(2)}) copy-start(s32[8]{0:T(128)} %owner.1) | copy-start | bytes 100
  25.4 6.3 %collective-permute-start.11 = (f32[48,384]{1,0:T(8,128)S(1)}, f32[48,384]{1,0:T(8,128)S(1)}, u32[]{:S(2)}, u32[]{:S(2)}) collective-permute-start(f32[48,384]{1,0:T(8,128)S(1)} %get-tuple-element.26), channel_id=1, source_target_pairs={{0,4},{4,8},{8,12},{12,16},{16,20},{20,24},{24,28},{28,0},{1,5},{5... | collective-permute-start | bytes 221192 | tf_op jit(solution)/shard_map/ppermute | solution.py:238
  31.7 2.0 %collective-permute-start.12 = (f32[48,384]{1,0:T(8,128)S(1)}, f32[48,384]{1,0:T(8,128)S(1)}, u32[]{:S(2)}, u32[]{:S(2)}) collective-permute-start(f32[48,384]{1,0:T(8,128)S(1)} %get-tuple-element.27), channel_id=1, source_target_pairs={{0,28},{4,0},{8,4},{12,8},{16,12},{20,16},{24,20},{28,24},{1,29},{... | collective-permute-start | bytes 221192 | tf_op jit(solution)/shard_map/ppermute | solution.py:239
  34.3 4.7 %collective-permute-start.13 = (f32[48,384]{1,0:T(8,128)S(1)}, f32[48,384]{1,0:T(8,128)S(1)}, u32[]{:S(2)}, u32[]{:S(2)}) collective-permute-start(f32[48,384]{1,0:T(8,128)S(1)} %get-tuple-element.29), channel_id=1, source_target_pairs={{0,28},{4,0},{8,4},{12,8},{16,12},{20,16},{24,20},{28,24},{1,29},{... | collective-permute-start | bytes 221192 | tf_op jit(solution)/shard_map/ppermute | solution.py:239
  37.0 4.7 %collective-permute-start.14 = (f32[48,384]{1,0:T(8,128)S(1)}, f32[48,384]{1,0:T(8,128)S(1)}, u32[]{:S(2)}, u32[]{:S(2)}) collective-permute-start(f32[48,384]{1,0:T(8,128)S(1)} %get-tuple-element.30), channel_id=1, source_target_pairs={{0,4},{4,8},{8,12},{12,16},{16,20},{20,24},{24,28},{28,0},{1,5},{5... | collective-permute-start | bytes 221192 | tf_op jit(solution)/shard_map/ppermute | solution.py:238
  37.0 9.8 %collective-permute-start.4 = (f32[192,384]{1,0:T(8,128)S(1)}, f32[192,384]{1,0:T(8,128)S(1)}, u32[]{:S(2)}, u32[]{:S(2)}) collective-permute-start(f32[192,384]{1,0:T(8,128)S(1)} %collective-permute-done.3.refs_4_), channel_id=1, source_target_pairs={{0,4},{4,0},{8,12},{12,8},{16,20},{20,16},{24,28},{28,24},{1,5},{5... | collective-permute-start | bytes 884744 | tf_op jit(solution)/shard_map/ppermute | solution.py:208
  39.0 7.8 %collective-permute-start.6 = (f32[192,384]{1,0:T(8,128)S(1)}, f32[192,384]{1,0:T(8,128)S(1)}, u32[]{:S(2)}, u32[]{:S(2)}) collective-permute-start(f32[192,384]{1,0:T(8,128)S(1)} %collective-permute-done.5.refs_6_), channel_id=1, source_target_pairs={{0,4},{4,0},{8,12},{12,8},{16,20},{20,16},{24,28},{28,24},{1,5},{5... | collective-permute-start | bytes 884744 | tf_op jit(solution)/shard_map/ppermute | solution.py:208
  42.1 11.1 %collective-permute-start.15 = (f32[192,384]{1,0:T(8,128)S(1)}, f32[192,384]{1,0:T(8,128)S(1)}, u32[]{:S(2)}, u32[]{:S(2)}) collective-permute-start(f32[192,384]{1,0:T(8,128)S(1)} %shard_map.88.refs_0_), channel_id=1, source_target_pairs={{0,3},{1,0},{2,1},{3,2},{4,7},{5,4},{6,5},{7,6},{8,11},{9,8},{10,9... | collective-permute-start | bytes 884744 | tf_op jit(solution)/shard_map/ppermute | solution.py:262
  45.8 23.1 %collective-permute-start.16 = (f32[192,384]{1,0:T(8,128)S(1)}, f32[192,384]{1,0:T(8,128)S(1)}, u32[]{:S(2)}, u32[]{:S(2)}) collective-permute-start(f32[192,384]{1,0:T(8,128)S(1)} %shard_map.88.refs_0_), channel_id=1, source_target_pairs={{0,2},{1,3},{2,0},{3,1},{4,6},{5,7},{6,4},{7,5},{8,10},{9,11},{10,... | collective-permute-start | bytes 884744 | tf_op jit(solution)/shard_map/ppermute | solution.py:262
  45.8 23.1 %collective-permute-start.17 = (f32[192,384]{1,0:T(8,128)S(1)}, f32[192,384]{1,0:T(8,128)S(1)}, u32[]{:S(2)}, u32[]{:S(2)}) collective-permute-start(f32[192,384]{1,0:T(8,128)S(1)} %shard_map.88.refs_0_), channel_id=1, source_target_pairs={{0,1},{1,2},{2,3},{3,0},{4,5},{5,6},{6,7},{7,4},{8,9},{9,10},{10,1... | collective-permute-start | bytes 884744 | tf_op jit(solution)/shard_map/ppermute | solution.py:262

commit v2 on v1

v2 whole, which is shorter than its diff:
```python
import functools

import jax
import jax.numpy as jnp
from jax import lax
from jax.experimental import pallas as pl
from jax.experimental.pallas import tpu as pltpu
from jax.sharding import PartitionSpec as P

filter_center = 2.5
filter_half = 3.5
spectrum_floor = -4.0
sigma_one = filter_half / (spectrum_floor - filter_center)
sigma_two = 1.0 / (2.0 / sigma_one - sigma_one)

f32 = jnp.float32
bf16 = jnp.bfloat16
VMEM_LIMIT = 32 * 1024 * 1024
VMEM_MOST = 56 * 1024 * 1024


def split(x):
    hi = x.astype(bf16)
    lo = (x - hi.astype(f32)).astype(bf16)
    return hi, lo


def mm(a, b, dims=((1,), (0,))):
    return lax.dot_general(a, b, (dims, ((), ())), preferred_element_type=f32)


def select(onehot, x):
    hi, lo = split(x)
    rest = (x - hi.astype(f32) - lo.astype(f32)).astype(bf16)
    return mm(onehot, hi) + mm(onehot, lo) + mm(onehot, rest)


def as_column(row):
    n = row.shape[1]
    here = lax.broadcasted_iota(jnp.int32, (n, n), 0) == lax.broadcasted_iota(jnp.int32, (n, n), 1)
    return jnp.sum(jnp.where(here, row, jnp.zeros_like(row)), axis=1, keepdims=True)


def pick_rows(list_row, owned):
    column = as_column(list_row.astype(f32)).astype(jnp.int32)
    shape = (list_row.shape[1], owned)
    return (lax.broadcasted_iota(jnp.int32, shape, 1) == column).astype(f32).astype(bf16)


def put_rows(list_row, owned):
    shape = (owned, list_row.shape[1])
    return (lax.broadcasted_iota(jnp.int32, shape, 0) == list_row).astype(f32).astype(bf16)


def call(kernel, out_shape, args, cost, scalars=(), **kwargs):
    vmem = pl.BlockSpec(memory_space=pltpu.VMEM)
    smem = pl.BlockSpec(memory_space=pltpu.SMEM)
    specs = [smem if i in scalars else vmem for i in range(len(args))]
    return pl.pallas_call(
        kernel,
        out_shape=out_shape,
        in_specs=specs,
        out_specs=jax.tree.map(lambda _: vmem, out_shape),
        compiler_params=pltpu.CompilerParams(vmem_limit_bytes=VMEM_LIMIT),
        cost_estimate=pl.CostEstimate(flops=cost, bytes_accessed=1 << 20, transcendentals=0),
        **kwargs,
    )(*args)


def shape(*dims, dtype=f32):
    return jax.ShapeDtypeStruct(dims, dtype)


def near_and_far(up, dn):
    even = lax.rem(lax.axis_index("dom"), 2) == 0
    up, dn = up[...], dn[...]
    return jnp.where(even, up, dn), jnp.where(even, dn, up)


def send_rows(x, up, dn, near_out, far_out):
    near, far = near_and_far(up, dn)
    near_out[...] = select(pick_rows(near, x.shape[0]), x)
    far_out[...] = select(pick_rows(far, x.shape[0]), x)


def cell_term(ham, row, ext):
    n = ham.shape[0]
    gap = -n % 16
    hi, lo = split(jnp.concatenate([ham, jnp.zeros((gap, n), f32)], axis=0))
    spread = lax.broadcasted_iota(jnp.int32, (ext, n), 0) == row
    spread = spread.astype(f32)
    twice = jnp.concatenate([spread, jnp.zeros((ext, gap), f32), spread, jnp.zeros((ext, gap), f32)], axis=1)
    spread = spread.astype(bf16)
    left_hi, left_lo = split(mm(twice.astype(bf16), jnp.concatenate([hi, lo], axis=0)))
    wide = ext // 256 * 256
    both = mm(jnp.concatenate([left_hi, left_lo], axis=0), spread[:wide], ((1,), (1,)))
    rest = mm(
        jnp.concatenate([left_hi[wide:], left_lo[wide:]], axis=0), spread[wide:], ((1,), (1,))
    )
    return both[:ext] + both[ext:], rest[: ext - wide] + rest[ext - wide :]


def assemble_kernel(ghost, nodes_any, ham_any, out, raw, ham, left, corner, sem):
    cells = ham.shape[0]
    ext, wide = left.shape
    owned = ext - 2 * ghost
    moves = [(nodes_any, raw)] + [(ham_any.at[c], ham.at[c]) for c in range(cells)]
    copies = [pltpu.make_async_copy(a, b, sem.at[i]) for i, (a, b) in enumerate(moves)]
    for copy in copies:
        copy.start()
    copies[0].wait()
    node = raw[...]
    lower = (node >= owned) & (node < owned + ghost)
    swapped = jnp.where(lower, node + ghost, jnp.where(node >= owned + ghost, node - ghost, node))
    nodes = jnp.where(lax.rem(lax.axis_index("dom"), 2) == 0, swapped, node)
    for c in range(cells):
        copies[1 + c].wait()
        term, rest = cell_term(ham[c], nodes[c : c + 1, :], ext)
        left[...] = term if c == 0 else left[...] + term
        corner[...] = rest if c == 0 else corner[...] + rest
    below = jnp.transpose(left[ext - 128 :, :])[:, 128 - (ext - wide) :]
    right = jnp.concatenate([below, corner[...]], axis=0)
    full = jnp.concatenate([left[...], right], axis=1)
    hi = full.astype(bf16).astype(f32)
    out[...] = jnp.concatenate([hi, full - hi, hi], axis=1).astype(bf16)


def assemble(cell_nodes, cell_ham, ext, ghost):
    cells, n, _ = cell_ham.shape
    wide = ext // 256 * 256
    return pl.pallas_call(
        functools.partial(assemble_kernel, ghost),
        out_shape=shape(ext, 3 * ext, dtype=bf16),
        in_specs=[pl.BlockSpec(memory_space=pl.ANY)] * 2,
        out_specs=pl.BlockSpec(memory_space=pltpu.VMEM),
        scratch_shapes=[
            pltpu.VMEM((cells, n), jnp.int32),
            pltpu.VMEM((cells, n, n), f32),
            pltpu.VMEM((ext, wide), f32),
            pltpu.VMEM((ext - wide, ext - wide), f32),
            pltpu.SemaphoreType.DMA((1 + cells,)),
        ],
        compiler_params=pltpu.CompilerParams(vmem_limit_bytes=VMEM_MOST),
        cost_estimate=pl.CostEstimate(
            flops=cells * 8 * n * n * ext, bytes_accessed=cells * n * n * 4, transcendentals=0
        ),
    )(cell_nodes, cell_ham)


def apply_kernel(v, m, near, far, ham, own, to_near, to_far):
    owned = v.shape[0]
    ghost = near.shape[0]
    x = jnp.concatenate([v[...] * as_column(m[...]), near[...], far[...]], axis=0)
    hi, lo = split(x)
    z = mm(ham[...], jnp.concatenate([hi, hi, lo], axis=0))
    own[...] = z[:owned]
    to_near[...] = z[owned : owned + ghost]
    to_far[...] = z[owned + ghost :]


def collect(own, from_near, from_far, up, dn):
    owned = own.shape[0]
    near, far = near_and_far(up, dn)
    return (
        own[...]
        + select(put_rows(near, owned), from_near[...])
        + select(put_rows(far, owned), from_far[...])
    )


def middle_kernel(own, from_near, from_far, s, m, up, dn, one, near_out, far_out):
    column = as_column(m[...])
    r = collect(own, from_near, from_far, up, dn)
    filtered = (sigma_one / filter_half) * (r * column - filter_center * s[...])
    one[...] = filtered
    send_rows(filtered * column, up, dn, near_out, far_out)


def last_kernel(own, from_near, from_far, s, one, m, up, dn, two):
    column = as_column(m[...])
    r = collect(own, from_near, from_far, up, dn)
    two[...] = (
        2.0 * sigma_two / filter_half * (r * column - filter_center * one[...])
        - sigma_one * sigma_two * s[...]
    )


def order_kernel(owner, *refs):
    parts, (hi_out, lo_out) = refs[:-2], refs[-2:]
    here = lax.axis_index("dom")
    for b, part in enumerate(parts):
        slot = here ^ b
        place = jnp.int32(0)
        for p in range(len(parts)):
            place = place + jnp.where(owner[p] == slot, p, 0)
        hi, lo = split(part[...])
        hi_out[place] = hi
        lo_out[place] = lo


def rotated_rows(hi_ref, lo_ref, parts):
    here = lax.axis_index("band")
    total = None
    for r, part in parts:
        k = here ^ r
        hi, lo = split(part)
        rhi, rlo = hi_ref[k], lo_ref[k]
        term = mm(
            jnp.concatenate([hi, lo, hi], axis=1), jnp.concatenate([rhi, rhi, rlo], axis=0)
        )
        total = term if total is None else total + term
    return total


def rotate_kernel(hi_ref, lo_ref, own, one, two, out):
    out[...] = rotated_rows(hi_ref, lo_ref, [(0, own[...]), (1, one[...]), (2, two[...])])


def rotate_last_kernel(hi_ref, lo_ref, total, inner, outer, m, up, dn, out, near_out, far_out):
    rows = total[...] + rotated_rows(hi_ref, lo_ref, [(3, inner[...] + outer[...])])
    out[...] = rows
    send_rows(rows * as_column(m[...]), up, dn, near_out, far_out)


def flip(count, bits):
    return [(i, i ^ bits) for i in range(count)]


def ordered_rotation(slots, owner, bands):
    rows, cols = slots[0].shape
    total = len(slots) * rows
    hi, lo = call(
        order_kernel,
        (shape(len(slots), rows, cols, dtype=bf16),) * 2,
        [owner, *slots],
        total * cols * 16,
        scalars=(0,),
    )
    return hi.reshape(bands, total // bands, cols), lo.reshape(bands, total // bands, cols)


def shards(states, inv_mass, cell_ham, cell_nodes, send_up, send_down, owner, rotation_store):
    owned, cols = states.shape
    ghost = send_up.shape[0]
    ext = owned + 2 * ghost
    doms, bands = lax.axis_size("dom"), lax.axis_size("band")
    m = inv_mass[None, :]
    up = send_up[None, :]
    dn = send_down[None, :]
    near_pairs = flip(doms, 1)
    far_pairs = [(i, (i - 1 if i % 2 == 0 else i + 1) % doms) for i in range(doms)]
    halo = shape(ghost, cols)
    block = shape(owned, cols)
    small = 4 * ghost * owned * cols * 3

    def exchange(to_near, to_far):
        from_far = lax.ppermute(to_far, "dom", far_pairs)
        from_near = lax.ppermute(to_near, "dom", near_pairs)
        return from_near, from_far

    def apply(v, near, far, ham):
        own, to_near, to_far = call(
            apply_kernel, (block, halo, halo), [v, m, near, far, ham], 6 * ext * ext * cols
        )
        return (own, *exchange(to_near, to_far))

    ham = assemble(cell_nodes, cell_ham, ext, ghost)
    band = lax.axis_index("band")
    own_columns = lax.dynamic_slice_in_dim(rotation_store, band * cols, cols, 1)
    one = lax.ppermute(states, "band", flip(4, 1))
    two = lax.ppermute(states, "band", flip(4, 2))
    paired = doms == 8 and rotation_store.shape[0] % 16 == 0
    parts = [own_columns]
    if paired:
        parts += [lax.ppermute(own_columns, "dom", flip(doms, b)) for b in (2, 4, 6)]
    held, one, two, ham, *parts = lax.optimization_barrier((states, one, two, ham, *parts))
    inner = lax.ppermute(held, "band", [(1, 2), (2, 1)])
    outer = lax.ppermute(two, "band", [(1, 0), (2, 3)])
    if paired:
        other = [lax.ppermute(part, "dom", near_pairs) for part in parts]
        slots = [part for pair in zip(parts, other) for part in pair]
        rotation = ordered_rotation(slots, owner, bands)
    else:
        columns = lax.all_gather(own_columns, "dom", axis=0, tiled=True)
        columns = columns.reshape(doms, -1, cols)[owner].reshape(bands, -1, cols)
        rotation = split(columns)
    work = 6 * owned * cols * cols
    total = call(rotate_kernel, block, [*rotation, held, one, two], 3 * work)
    turned, to_near, to_far = call(
        rotate_last_kernel,
        (block, halo, halo),
        [*rotation, total, inner, outer, m, up, dn],
        work,
    )
    near, far = exchange(to_near, to_far)
    first = apply(turned, near, far, ham)
    filtered, to_near, to_far = call(
        middle_kernel, (block, halo, halo), [*first, turned, m, up, dn], 2 * small
    )
    near, far = exchange(to_near, to_far)
    second = apply(filtered, near, far, ham)
    return call(last_kernel, block, [*second, turned, filtered, m, up, dn], small)


def solution(mesh):
    in_specs = (
        P("dom", "band"),
        P("dom"),
        P("dom", None, None),
        P("dom", None),
        P("dom"),
        P("dom"),
        P(),
        P("dom", None),
    )
    out_specs = P("dom", "band")
    return jax.shard_map(shards, mesh=mesh, in_specs=in_specs, out_specs=out_specs, check_vma=False)
```

time: 71.1 us -> 59 us (0.83)
  waiting for transfers between devices: 37.6 us -> 23.5 us
  starting transfers between devices: 15.9 us -> 22.2 us
  local copies, waits for them, and re-layouts: 6.73 us -> 1.33 us
  Pallas kernels: 10.4 us -> 11.6 us
    ppermute x18 -> x19, waiting for transfers between devices: 37.6 us -> 23.5 us  [the longest x4 9.37 us: exchange(): from_far = lax.ppermute(to_far, 'dom', far_pairs)]
    ppermute x18 -> x19, starting transfers between devices: 15.9 us -> 22.2 us  [the longest x4 9.6 us: exchange(): from_far = lax.ppermute(to_far, 'dom', far_pairs)]
    unnamed x24 -> x14, local copies, waits for them, and re-layouts: 6.7 us -> 1.31 us
    pallas_call x1, Pallas kernels: 4.77 us -> 5.92 us  [assemble(): pl.pallas_call(functools.partial(assemble_kernel, ghost), out_shape=shape...]
  transfers between devices with their start and end apart: 18 -> 19, of which waited for: 8 -> 9; matrix products, arithmetic and copies ran while one was open for 0% -> 0% of each run, Pallas kernels for 12% -> 13%
where the time goes in v2:
time: 59 us; the launch traced here: 58.9 us
  waiting for transfers between devices  23.5 us (40%)
  starting transfers between devices  22.2 us (38%)
  Pallas kernels  11.6 us (20%)
  local copies, waits for them, and re-layouts  1.33 us (2%)
    ppermute x4, starting transfers between devices, exchange(): from_far = lax.ppermute(to_far, 'dom', far_pairs)  9.6 us
    ppermute x4, waiting for transfers between devices, exchange(): from_far = lax.ppermute(to_far, 'dom', far_pairs)  9.37 us
    ppermute x1, waiting for transfers between devices, shards(): outer = lax.ppermute(two, 'band', [(1, 0), (2, 3)])  7.51 us
    pallas_call x1, Pallas kernels, assemble(): pl.pallas_call(functools.partial(assemble_kernel, ghost), out_shape=shape...  5.92 us
    pallas_call x7, Pallas kernels, call(): pl.pallas_call(kernel, out_shape=out_shape, in_specs=specs, out_specs=jax...  5.72 us
    ppermute x3, starting transfers between devices, shards(): lax.ppermute(own_columns, 'dom', flip(doms, b))  4.6 us
    ppermute x1, starting transfers between devices, shards(): two = lax.ppermute(states, 'band', flip(4, 2))  2.59 us
    ppermute x1, waiting for transfers between devices, shards(): two = lax.ppermute(states, 'band', flip(4, 2))  2.51 us
  transfers between devices with their start and end apart: 19, of which 9 were waited for; matrix products, arithmetic and copies ran while one was open for 0% of the time, Pallas kernels for 13%

profile of v2, /device:TPU:0, one launch (start us, length us, event | category | flops | bytes accessed | tf_op | source)
XLA Modules:
  0.0 58.9 jit_solution(16097322277382798625)
XLA Ops:
  0.0 0.0 copy-start
  0.0 1.3 %copy-done = f32[192,1536]{1,0:T(8,128)S(1)} copy-done((f32[192,1536]{1,0:T(8,128)S(1)}, f32[192,1536]{1,0:T(8,128)}, u32[]{:S(2)}) %copy-start) | copy-done | bytes 1179672
  1.3 0.0 copy-start.2
  1.3 0.0 copy-start.6
  1.3 4.0 %collective-permute-start.4 = (f32[192,384]{1,0:T(8,128)S(1)}, f32[192,384]{1,0:T(8,128)S(1)}, u32[]{:S(2)}, u32[]{:S(2)}) collective-permute-start(f32[192,384]{1,0:T(8,128)S(1)} %constant_dynamic-slice_fusion.refs_0_), channel_id=1, source_target_pairs={{0,24},{4,28},{8,16},{12,20},{16,8},{20,12},{24,0},{28,4},{1,25},{... | collective-permute-start | bytes 884744 | tf_op jit(solution)/shard_map/ppermute | solution.py:275
  5.3 0.5 collective-permute-start.3
  5.8 0.1 collective-permute-start.2
  5.9 2.0 %collective-permute-start = (f32[192,384]{1,0:T(8,128)}, f32[192,384]{1,0:T(8,128)S(1)}, u32[]{:S(2)}, u32[]{:S(2)}) collective-permute-start(f32[192,384]{1,0:T(8,128)} %own), channel_id=1, source_target_pairs={{0,1},{1,0},{2,3},{3,2},{4,5},{5,4},{6,7},{7,6},{8,9},{9,8},{10,11... | collective-permute-start | bytes 884744 | tf_op jit(solution)/shard_map/ppermute | solution.py:270
  7.9 2.6 %collective-permute-start.1 = (f32[192,384]{1,0:T(8,128)}, f32[192,384]{1,0:T(8,128)S(1)}, u32[]{:S(2)}, u32[]{:S(2)}) collective-permute-start(f32[192,384]{1,0:T(8,128)} %own), channel_id=1, source_target_pairs={{0,2},{1,3},{2,0},{3,1},{4,6},{5,7},{6,4},{7,5},{8,10},{9,11},{10,... | collective-permute-start | bytes 884744 | tf_op jit(solution)/shard_map/ppermute | solution.py:271
  10.5 5.9 %shard_map.82.ham = bf16[288,864]{1,0:T(8,128)(2,1)} custom-call(s32[5,343]{1,0:T(8,128)} %nodes_any.1, f32[5,343,343]{2,1,0:T(8,128)} %ham_any.1), custom_call_target="tpu_custom_call" | custom-call | flops 1355316480 | bytes 2352980 | tf_op jit(solution)/shard_map/pallas_call | solution.py:131
  16.4 0.0 collective-permute-done.4.refs_6_
  16.4 2.2 %collective-permute-done.3.refs_4_ = f32[192,384]{1,0:T(8,128)S(1)} collective-permute-done((f32[192,384]{1,0:T(8,128)S(1)}, f32[192,384]{1,0:T(8,128)S(1)}, u32[]{:S(2)}, u32[]{:S(2)}) %collective-permute-start.3) | collective-permute-done | bytes 294944 | tf_op jit(solution)/shard_map/ppermute | solution.py:275
  18.6 0.3 collective-permute-done.2.refs_2_
  18.9 1.6 %collective-permute-done.one = f32[192,384]{1,0:T(8,128)S(1)} collective-permute-done((f32[192,384]{1,0:T(8,128)}, f32[192,384]{1,0:T(8,128)S(1)}, u32[]{:S(2)}, u32[]{:S(2)}) %collective-permute-start) | collective-permute-done | bytes 294944 | tf_op jit(solution)/shard_map/ppermute | solution.py:270
  20.5 2.5 %collective-permute-done.1.two = f32[192,384]{1,0:T(8,128)S(1)} collective-permute-done((f32[192,384]{1,0:T(8,128)}, f32[192,384]{1,0:T(8,128)S(1)}, u32[]{:S(2)}, u32[]{:S(2)}) %collective-permute-start.1) | collective-permute-done | bytes 294944 | tf_op jit(solution)/shard_map/ppermute | solution.py:271
  23.0 0.0 collective-permute-start.5
  23.0 0.5 collective-permute-start.6
  23.5 0.0 collective-permute-start.7
  23.5 0.5 collective-permute-start.8
  24.0 0.0 copy-done.2
  24.1 0.7 %collective-permute-start.9 = (f32[192,384]{1,0:T(8,128)S(1)}, f32[192,384]{1,0:T(8,128)S(1)}, u32[]{:S(2)}, u32[]{:S(2)}) collective-permute-start(f32[192,384]{1,0:T(8,128)S(1)} %copy-done.2), channel_id=1, source_target_pairs={{1,2},{2,1},{5,6},{6,5},{9,10},{10,9},{13,14},{14,13},{17,18},{18,... | collective-permute-start | bytes 884744 | tf_op jit(solution)/shard_map/ppermute | solution.py:277
  24.7 0.0 collective-permute-done.5.refs_1_
  24.7 1.3 %collective-permute-start.10 = (f32[192,384]{1,0:T(8,128)S(1)}, f32[192,384]{1,0:T(8,128)S(1)}, u32[]{:S(2)}, u32[]{:S(2)}) collective-permute-start(f32[192,384]{1,0:T(8,128)S(1)} %collective-permute-done.1.two), channel_id=1, source_target_pairs={{1,0},{2,3},{5,4},{6,7},{9,8},{10,11},{13,12},{14,15},{17,16},{18,... | collective-permute-start | bytes 884744 | tf_op jit(solution)/shard_map/ppermute | solution.py:278
  26.0 0.0 collective-permute-done.6.refs_3_
  26.0 0.0 collective-permute-done.7.refs_5_
  26.1 0.0 collective-permute-done.8.refs_7_
  26.1 0.0 copy-done.6
  26.1 1.0 %shard_map.83 = (bf16[8,192,384]{2,1,0:T(8,128)(2,1)S(1)}, bf16[8,192,384]{2,1,0:T(8,128)(2,1)S(1)}) custom-call(s32[8]{0:T(128)S(1)} %copy-done.6, f32[192,384]{1,0:T(8,128)S(1)} %constant_dynamic-slice_fusion.refs_0_, f32[192,384]{1,0:T(8,128)S(1)} %collective-permute-done.5.refs_1_, f32[192,384]{1,0:T(8,128)S(1)} %collective-permute-done.2.refs_2_, ...), custom_call_target="tpu_custom_call" | custom-call | flops 9437184 | bytes 1048576 | tf_op jit(solution)/shard_map/pallas_call | solution.py:59
  27.1 0.0 copy-start.3
  27.1 0.0 copy-start.4
  27.1 0.0 copy-start.5
  27.1 0.9 %shard_map.84.total = f32[192,384]{1,0:T(8,128)S(1)} custom-call(bf16[4,384,384]{2,1,0:T(8,128)(2,1)S(1)} %bitcast.5, bf16[4,384,384]{2,1,0:T(8,128)(2,1)S(1)} %bitcast.7, f32[192,384]{1,0:T(8,128)S(1)} %copy-done.2, f32[192,384]{1,0:T(8,128)S(1)} %collective-permute-done.one, f32[192,384]{1,0:T(8,128)S(1)} %collective-permute-done.1.two), custom_call_target="tpu_custom_call" | custom-call | flops 509607936 | bytes 1048576 | tf_op jit(solution)/shard_map/pallas_call | solution.py:59
  28.0 0.0 collective-permute-done.9.inner
  28.0 7.5 %collective-permute-done.10.outer = f32[192,384]{1,0:T(8,128)S(1)} collective-permute-done((f32[192,384]{1,0:T(8,128)S(1)}, f32[192,384]{1,0:T(8,128)S(1)}, u32[]{:S(2)}, u32[]{:S(2)}) %collective-permute-start.10) | collective-permute-done | bytes 294944 | tf_op jit(solution)/shard_map/ppermute | solution.py:278
  35.5 0.0 copy-done.3
  35.6 0.0 copy-done.4
  35.6 0.0 copy-done.5
  35.6 0.0 copy-start.1
  35.6 0.7 %shard_map.85 = (f32[192,384]{1,0:T(8,128)S(1)}, f32[48,384]{1,0:T(8,128)S(1)}, f32[48,384]{1,0:T(8,128)S(1)}) custom-call(bf16[4,384,384]{2,1,0:T(8,128)(2,1)S(1)} %bitcast.6, bf16[4,384,384]{2,1,0:T(8,128)(2,1)S(1)} %bitcast.8, f32[192,384]{1,0:T(8,128)S(1)} %shard_map.84.total, f32[192,384]{1,0:T(8,128)S(1)} %collective-permute-done.9.inner, ...), custom_call_target="tpu_custom_call" | custom-call | flops 169869312 | bytes 1048576 | tf_op jit(solution)/shard_map/pallas_call | solution.py:59
  36.3 0.1 collective-permute-start.11
  36.4 2.5 %collective-permute-start.12 = (f32[48,384]{1,0:T(8,128)S(1)}, f32[48,384]{1,0:T(8,128)S(1)}, u32[]{:S(2)}, u32[]{:S(2)}) collective-permute-start(f32[48,384]{1,0:T(8,128)S(1)} %get-tuple-element.38), channel_id=1, source_target_pairs={{0,28},{4,8},{8,4},{12,16},{16,12},{20,24},{24,20},{28,0},{1,29},{... | collective-permute-start | bytes 221192 | tf_op jit(solution)/shard_map/ppermute | solution.py:257
  38.9 0.0 collective-permute-done.11.near
  38.9 2.4 %collective-permute-done.12.far = f32[48,384]{1,0:T(8,128)S(1)} collective-permute-done((f32[48,384]{1,0:T(8,128)S(1)}, f32[48,384]{1,0:T(8,128)S(1)}, u32[]{:S(2)}, u32[]{:S(2)}) %collective-permute-start.12) | collective-permute-done | bytes 73760 | tf_op jit(solution)/shard_map/ppermute | solution.py:257
  41.3 0.0 copy-done.1
  41.3 0.6 shard_map.86
  41.9 0.2 collective-permute-start.13
  42.0 2.3 %collective-permute-start.14 = (f32[48,384]{1,0:T(8,128)S(1)}, f32[48,384]{1,0:T(8,128)S(1)}, u32[]{:S(2)}, u32[]{:S(2)}) collective-permute-start(f32[48,384]{1,0:T(8,128)S(1)} %get-tuple-element.42), channel_id=1, source_target_pairs={{0,28},{4,8},{8,4},{12,16},{16,12},{20,24},{24,20},{28,0},{1,29},{... | collective-permute-start | bytes 221192 | tf_op jit(solution)/shard_map/ppermute | solution.py:257
  44.3 0.0 collective-permute-done.13.from_near
  44.3 2.4 %collective-permute-done.14.from_far = f32[48,384]{1,0:T(8,128)S(1)} collective-permute-done((f32[48,384]{1,0:T(8,128)S(1)}, f32[48,384]{1,0:T(8,128)S(1)}, u32[]{:S(2)}, u32[]{:S(2)}) %collective-permute-start.14) | collective-permute-done | bytes 73760 | tf_op jit(solution)/shard_map/ppermute | solution.py:257
  46.7 0.8 %shard_map.87 = (f32[192,384]{1,0:T(8,128)S(1)}, f32[48,384]{1,0:T(8,128)S(1)}, f32[48,384]{1,0:T(8,128)S(1)}) custom-call(f32[192,384]{1,0:T(8,128)S(1)} %get-tuple-element.40.own, f32[48,384]{1,0:T(8,128)S(1)} %collective-permute-done.13.from_near, f32[48,384]{1,0:T(8,128)S(1)} %collective-permute-done.14.from_far, f32[192,384]{1,0:T(8,128)S(1)} %get-tuple-element.36.v.s, ...), custom_call_target="tpu_custom_call" | custom-call | flops 84934656 | bytes 1048576 | tf_op jit(solution)/shard_map/pallas_call | solution.py:59
  47.5 0.1 collective-permute-start.15
  47.6 2.3 %collective-permute-start.16 = (f32[48,384]{1,0:T(8,128)S(1)}, f32[48,384]{1,0:T(8,128)S(1)}, u32[]{:S(2)}, u32[]{:S(2)}) collective-permute-start(f32[48,384]{1,0:T(8,128)S(1)} %get-tuple-element.45), channel_id=1, source_target_pairs={{0,28},{4,8},{8,4},{12,16},{16,12},{20,24},{24,20},{28,0},{1,29},{... | collective-permute-start | bytes 221192 | tf_op jit(solution)/shard_map/ppermute | solution.py:257
  49.9 0.0 collective-permute-done.15.near
  49.9 2.4 %collective-permute-done.16.far = f32[48,384]{1,0:T(8,128)S(1)} collective-permute-done((f32[48,384]{1,0:T(8,128)S(1)}, f32[48,384]{1,0:T(8,128)S(1)}, u32[]{:S(2)}, u32[]{:S(2)}) %collective-permute-start.16) | collective-permute-done | bytes 73760 | tf_op jit(solution)/shard_map/ppermute | solution.py:257
  52.3 0.6 shard_map.88
  52.9 0.2 collective-permute-start.17
  53.0 2.4 %collective-permute-start.18 = (f32[48,384]{1,0:T(8,128)S(1)}, f32[48,384]{1,0:T(8,128)S(1)}, u32[]{:S(2)}, u32[]{:S(2)}) collective-permute-start(f32[48,384]{1,0:T(8,128)S(1)} %get-tuple-element.48), channel_id=1, source_target_pairs={{0,28},{4,8},{8,4},{12,16},{16,12},{20,24},{24,20},{28,0},{1,29},{... | collective-permute-start | bytes 221192 | tf_op jit(solution)/shard_map/ppermute | solution.py:257
  55.5 0.0 collective-permute-done.17.from_near
  55.5 2.2 %collective-permute-done.18.from_far = f32[48,384]{1,0:T(8,128)S(1)} collective-permute-done((f32[48,384]{1,0:T(8,128)S(1)}, f32[48,384]{1,0:T(8,128)S(1)}, u32[]{:S(2)}, u32[]{:S(2)}) %collective-permute-start.18) | collective-permute-done | bytes 73760 | tf_op jit(solution)/shard_map/ppermute | solution.py:257
  57.7 1.1 %shard_map.89 = f32[192,384]{1,0:T(8,128)} custom-call(f32[192,384]{1,0:T(8,128)S(1)} %get-tuple-element.46.own, f32[48,384]{1,0:T(8,128)S(1)} %collective-permute-done.17.from_near, f32[48,384]{1,0:T(8,128)S(1)} %collective-permute-done.18.from_far, f32[192,384]{1,0:T(8,128)S(1)} %get-tuple-element.36.v.s, f32[192,384]{1,0:T(8,128)S(1)} %get-tuple-element.43.v.one, ...), custom_call_target="tpu_custom_call" | custom-call | flops 42467328 | bytes 1048576 | tf_op jit(solution)/shard_map/pallas_call | solution.py:59
  (1 shorter events, 0.0 us)
Async XLA Ops:
  0.0 1.3 %copy-start = (f32[192,1536]{1,0:T(8,128)S(1)}, f32[192,1536]{1,0:T(8,128)}, u32[]{:S(2)}) copy-start(f32[192,1536]{1,0:T(8,128)} %param.15) | copy-start | bytes 3538948
  1.3 22.8 %copy-start.2 = (f32[192,384]{1,0:T(8,128)S(1)}, f32[192,384]{1,0:T(8,128)}, u32[]{:S(2)}) copy-start(f32[192,384]{1,0:T(8,128)} %own) | copy-start | bytes 884740
  1.3 24.8 %copy-start.6 = (s32[8]{0:T(128)S(1)}, s32[8]{0:T(128)}, u32[]{:S(2)}) copy-start(s32[8]{0:T(128)} %owner.1) | copy-start | bytes 100
  1.3 15.1 %collective-permute-start.4 = (f32[192,384]{1,0:T(8,128)S(1)}, f32[192,384]{1,0:T(8,128)S(1)}, u32[]{:S(2)}, u32[]{:S(2)}) collective-permute-start(f32[192,384]{1,0:T(8,128)S(1)} %constant_dynamic-slice_fusion.refs_0_), channel_id=1, source_target_pairs={{0,24},{4,28},{8,16},{12,20},{16,8},{20,12},{24,0},{28,4},{1,25},{... | collective-permute-start | bytes 884744 | tf_op jit(solution)/shard_map/ppermute | solution.py:275
  5.3 13.3 %collective-permute-start.3 = (f32[192,384]{1,0:T(8,128)S(1)}, f32[192,384]{1,0:T(8,128)S(1)}, u32[]{:S(2)}, u32[]{:S(2)}) collective-permute-start(f32[192,384]{1,0:T(8,128)S(1)} %constant_dynamic-slice_fusion.refs_0_), channel_id=1, source_target_pairs={{0,16},{4,20},{8,24},{12,28},{16,0},{20,4},{24,8},{28,12},{1,17},{... | collective-permute-start | bytes 884744 | tf_op jit(solution)/shard_map/ppermute | solution.py:275
  5.8 13.1 %collective-permute-start.2 = (f32[192,384]{1,0:T(8,128)S(1)}, f32[192,384]{1,0:T(8,128)S(1)}, u32[]{:S(2)}, u32[]{:S(2)}) collective-permute-start(f32[192,384]{1,0:T(8,128)S(1)} %constant_dynamic-slice_fusion.refs_0_), channel_id=1, source_target_pairs={{0,8},{4,12},{8,0},{12,4},{16,24},{20,28},{24,16},{28,20},{1,9},{5... | collective-permute-start | bytes 884744 | tf_op jit(solution)/shard_map/ppermute | solution.py:275
  5.9 14.6 %collective-permute-start = (f32[192,384]{1,0:T(8,128)}, f32[192,384]{1,0:T(8,128)S(1)}, u32[]{:S(2)}, u32[]{:S(2)}) collective-permute-start(f32[192,384]{1,0:T(8,128)} %own), channel_id=1, source_target_pairs={{0,1},{1,0},{2,3},{3,2},{4,5},{5,4},{6,7},{7,6},{8,9},{9,8},{10,11... | collective-permute-start | bytes 884744 | tf_op jit(solution)/shard_map/ppermute | solution.py:270
  7.9 15.1 %collective-permute-start.1 = (f32[192,384]{1,0:T(8,128)}, f32[192,384]{1,0:T(8,128)S(1)}, u32[]{:S(2)}, u32[]{:S(2)}) collective-permute-start(f32[192,384]{1,0:T(8,128)} %own), channel_id=1, source_target_pairs={{0,2},{1,3},{2,0},{3,1},{4,6},{5,7},{6,4},{7,5},{8,10},{9,11},{10,... | collective-permute-start | bytes 884744 | tf_op jit(solution)/shard_map/ppermute | solution.py:271
  23.0 1.7 %collective-permute-start.5 = (f32[192,384]{1,0:T(8,128)S(1)}, f32[192,384]{1,0:T(8,128)S(1)}, u32[]{:S(2)}, u32[]{:S(2)}) collective-permute-start(f32[192,384]{1,0:T(8,128)S(1)} %constant_dynamic-slice_fusion.refs_0_), channel_id=1, source_target_pairs={{0,4},{4,0},{8,12},{12,8},{16,20},{20,16},{24,28},{28,24},{1,5},{5... | collective-permute-start | bytes 884744 | tf_op jit(solution)/shard_map/ppermute | solution.py:280
  23.0 3.0 %collective-permute-start.6 = (f32[192,384]{1,0:T(8,128)S(1)}, f32[192,384]{1,0:T(8,128)S(1)}, u32[]{:S(2)}, u32[]{:S(2)}) collective-permute-start(f32[192,384]{1,0:T(8,128)S(1)} %collective-permute-done.2.refs_2_), channel_id=1, source_target_pairs={{0,4},{4,0},{8,12},{12,8},{16,20},{20,16},{24,28},{28,24},{1,5},{5... | collective-permute-start | bytes 884744 | tf_op jit(solution)/shard_map/ppermute | solution.py:280
  23.5 2.5 %collective-permute-start.7 = (f32[192,384]{1,0:T(8,128)S(1)}, f32[192,384]{1,0:T(8,128)S(1)}, u32[]{:S(2)}, u32[]{:S(2)}) collective-permute-start(f32[192,384]{1,0:T(8,128)S(1)} %collective-permute-done.3.refs_4_), channel_id=1, source_target_pairs={{0,4},{4,0},{8,12},{12,8},{16,20},{20,16},{24,28},{28,24},{1,5},{5... | collective-permute-start | bytes 884744 | tf_op jit(solution)/shard_map/ppermute | solution.py:280
  23.5 2.5 %collective-permute-start.8 = (f32[192,384]{1,0:T(8,128)S(1)}, f32[192,384]{1,0:T(8,128)S(1)}, u32[]{:S(2)}, u32[]{:S(2)}) collective-permute-start(f32[192,384]{1,0:T(8,128)S(1)} %collective-permute-done.4.refs_6_), channel_id=1, source_target_pairs={{0,4},{4,0},{8,12},{12,8},{16,20},{20,16},{24,28},{28,24},{1,5},{5... | collective-permute-start | bytes 884744 | tf_op jit(solution)/shard_map/ppermute | solution.py:280
  24.1 4.0 %collective-permute-start.9 = (f32[192,384]{1,0:T(8,128)S(1)}, f32[192,384]{1,0:T(8,128)S(1)}, u32[]{:S(2)}, u32[]{:S(2)}) collective-permute-start(f32[192,384]{1,0:T(8,128)S(1)} %copy-done.2), channel_id=1, source_target_pairs={{1,2},{2,1},{5,6},{6,5},{9,10},{10,9},{13,14},{14,13},{17,18},{18,... | collective-permute-start | bytes 884744 | tf_op jit(solution)/shard_map/ppermute | solution.py:277
  24.7 10.8 %collective-permute-start.10 = (f32[192,384]{1,0:T(8,128)S(1)}, f32[192,384]{1,0:T(8,128)S(1)}, u32[]{:S(2)}, u32[]{:S(2)}) collective-permute-start(f32[192,384]{1,0:T(8,128)S(1)} %collective-permute-done.1.two), channel_id=1, source_target_pairs={{1,0},{2,3},{5,4},{6,7},{9,8},{10,11},{13,12},{14,15},{17,16},{18,... | collective-permute-start | bytes 884744 | tf_op jit(solution)/shard_map/ppermute | solution.py:278
  27.1 8.5 %copy-start.3 = (f32[192]{0:T(256)S(1)}, f32[192]{0:T(256)}, u32[]{:S(2)}) copy-start(f32[192]{0:T(256)} %param.9) | copy-start | bytes 2308
  27.1 8.5 %copy-start.4 = (s32[48]{0:T(128)S(1)}, s32[48]{0:T(128)}, u32[]{:S(2)}) copy-start(s32[48]{0:T(128)} %param.12) | copy-start | bytes 580
  27.1 8.5 %copy-start.5 = (s32[48]{0:T(128)S(1)}, s32[48]{0:T(128)}, u32[]{:S(2)}) copy-start(s32[48]{0:T(128)} %param.13) | copy-start | bytes 580
  35.6 5.7 %copy-start.1 = (bf16[288,864]{1,0:T(8,128)(2,1)S(1)}, bf16[288,864]{1,0:T(8,128)(2,1)}, u32[]{:S(2)}) copy-start(bf16[288,864]{1,0:T(8,128)(2,1)} %shard_map.82.ham) | copy-start | bytes 1492996
  36.3 2.6 %collective-permute-start.11 = (f32[48,384]{1,0:T(8,128)S(1)}, f32[48,384]{1,0:T(8,128)S(1)}, u32[]{:S(2)}, u32[]{:S(2)}) collective-permute-start(f32[48,384]{1,0:T(8,128)S(1)} %get-tuple-element.37), channel_id=1, source_target_pairs={{0,4},{4,0},{8,12},{12,8},{16,20},{20,16},{24,28},{28,24},{1,5},{5... | collective-permute-start | bytes 221192 | tf_op jit(solution)/shard_map/ppermute | solution.py:258
  36.4 4.9 %collective-permute-start.12 = (f32[48,384]{1,0:T(8,128)S(1)}, f32[48,384]{1,0:T(8,128)S(1)}, u32[]{:S(2)}, u32[]{:S(2)}) collective-permute-start(f32[48,384]{1,0:T(8,128)S(1)} %get-tuple-element.38), channel_id=1, source_target_pairs={{0,28},{4,8},{8,4},{12,16},{16,12},{20,24},{24,20},{28,0},{1,29},{... | collective-permute-start | bytes 221192 | tf_op jit(solution)/shard_map/ppermute | solution.py:257
  41.9 2.5 %collective-permute-start.13 = (f32[48,384]{1,0:T(8,128)S(1)}, f32[48,384]{1,0:T(8,128)S(1)}, u32[]{:S(2)}, u32[]{:S(2)}) collective-permute-start(f32[48,384]{1,0:T(8,128)S(1)} %get-tuple-element.41), channel_id=1, source_target_pairs={{0,4},{4,0},{8,12},{12,8},{16,20},{20,16},{24,28},{28,24},{1,5},{5... | collective-permute-start | bytes 221192 | tf_op jit(solution)/shard_map/ppermute | solution.py:258
  42.0 4.7 %collective-permute-start.14 = (f32[48,384]{1,0:T(8,128)S(1)}, f32[48,384]{1,0:T(8,128)S(1)}, u32[]{:S(2)}, u32[]{:S(2)}) collective-permute-start(f32[48,384]{1,0:T(8,128)S(1)} %get-tuple-element.42), channel_id=1, source_target_pairs={{0,28},{4,8},{8,4},{12,16},{16,12},{20,24},{24,20},{28,0},{1,29},{... | collective-permute-start | bytes 221192 | tf_op jit(solution)/shard_map/ppermute | solution.py:257
  47.5 2.4 %collective-permute-start.15 = (f32[48,384]{1,0:T(8,128)S(1)}, f32[48,384]{1,0:T(8,128)S(1)}, u32[]{:S(2)}, u32[]{:S(2)}) collective-permute-start(f32[48,384]{1,0:T(8,128)S(1)} %get-tuple-element.44), channel_id=1, source_target_pairs={{0,4},{4,0},{8,12},{12,8},{16,20},{20,16},{24,28},{28,24},{1,5},{5... | collective-permute-start | bytes 221192 | tf_op jit(solution)/shard_map/ppermute | solution.py:258
  47.6 4.7 %collective-permute-start.16 = (f32[48,384]{1,0:T(8,128)S(1)}, f32[48,384]{1,0:T(8,128)S(1)}, u32[]{:S(2)}, u32[]{:S(2)}) collective-permute-start(f32[48,384]{1,0:T(8,128)S(1)} %get-tuple-element.45), channel_id=1, source_target_pairs={{0,28},{4,8},{8,4},{12,16},{16,12},{20,24},{24,20},{28,0},{1,29},{... | collective-permute-start | bytes 221192 | tf_op jit(solution)/shard_map/ppermute | solution.py:257
  52.9 2.6 %collective-permute-start.17 = (f32[48,384]{1,0:T(8,128)S(1)}, f32[48,384]{1,0:T(8,128)S(1)}, u32[]{:S(2)}, u32[]{:S(2)}) collective-permute-start(f32[48,384]{1,0:T(8,128)S(1)} %get-tuple-element.47), channel_id=1, source_target_pairs={{0,4},{4,0},{8,12},{12,8},{16,20},{20,16},{24,28},{28,24},{1,5},{5... | collective-permute-start | bytes 221192 | tf_op jit(solution)/shard_map/ppermute | solution.py:258
  53.0 4.7 %collective-permute-start.18 = (f32[48,384]{1,0:T(8,128)S(1)}, f32[48,384]{1,0:T(8,128)S(1)}, u32[]{:S(2)}, u32[]{:S(2)}) collective-permute-start(f32[48,384]{1,0:T(8,128)S(1)} %get-tuple-element.48), channel_id=1, source_target_pairs={{0,28},{4,8},{8,4},{12,16},{16,12},{20,24},{24,20},{28,0},{1,29},{... | collective-permute-start | bytes 221192 | tf_op jit(solution)/shard_map/ppermute | solution.py:257

commit v3 on v2

--- a/solution.py
+++ b/solution.py
@@ -71,16 +71,28 @@
     return jax.ShapeDtypeStruct(dims, dtype)
 
 
-def near_and_far(up, dn):
+def lists_kernel(m, up, dn, column, pick, put):
+    owned = m.shape[1]
+    column[...] = jnp.broadcast_to(as_column(m[...]), column.shape)
     even = lax.rem(lax.axis_index("dom"), 2) == 0
     up, dn = up[...], dn[...]
-    return jnp.where(even, up, dn), jnp.where(even, dn, up)
-
-
-def send_rows(x, up, dn, near_out, far_out):
-    near, far = near_and_far(up, dn)
-    near_out[...] = select(pick_rows(near, x.shape[0]), x)
-    far_out[...] = select(pick_rows(far, x.shape[0]), x)
+    near, far = jnp.where(even, up, dn), jnp.where(even, dn, up)
+    rows = jnp.concatenate([pick_rows(near, owned), pick_rows(far, owned)], axis=0)
+    pick[...] = jnp.concatenate([rows.astype(f32)] * 3, axis=1).astype(bf16)
+    lanes = [put_rows(near, owned).astype(f32), put_rows(far, owned).astype(f32)]
+    put[...] = jnp.concatenate(lanes * 3, axis=1).astype(bf16)
+
+
+def split_three(x):
+    hi, lo = split(x)
+    return hi, lo, (x - hi.astype(f32) - lo.astype(f32)).astype(bf16)
+
+
+def send_rows(x, pick, near_out, far_out):
+    rows = mm(pick[...], jnp.concatenate(split_three(x), axis=0))
+    ghost = near_out.shape[0]
+    near_out[...] = rows[:ghost]
+    far_out[...] = rows[ghost:]
 
 
 def cell_term(ham, row, ext):
@@ -100,7 +112,7 @@
     return both[:ext] + both[ext:], rest[: ext - wide] + rest[ext - wide :]
 
 
-def assemble_kernel(ghost, nodes_any, ham_any, out, raw, ham, left, corner, sem):
+def assemble_kernel(ghost, nodes_any, ham_any, own, halo, raw, ham, left, corner, sem):
     cells = ham.shape[0]
     ext, wide = left.shape
     owned = ext - 2 * ghost
@@ -122,7 +134,10 @@
     right = jnp.concatenate([below, corner[...]], axis=0)
     full = jnp.concatenate([left[...], right], axis=1)
     hi = full.astype(bf16).astype(f32)
-    out[...] = jnp.concatenate([hi, full - hi, hi], axis=1).astype(bf16)
+    lo = full - hi
+    for out, start, stop in ((own, 0, owned), (halo, owned, ext)):
+        high = hi[:, start:stop]
+        out[...] = jnp.concatenate([high, lo[:, start:stop], high], axis=1).astype(bf16)
 
 
 def assemble(cell_nodes, cell_ham, ext, ghost):
@@ -130,9 +145,12 @@
     wide = ext // 256 * 256
     return pl.pallas_call(
         functools.partial(assemble_kernel, ghost),
-        out_shape=shape(ext, 3 * ext, dtype=bf16),
+        out_shape=(
+            shape(ext, 3 * (ext - 2 * ghost), dtype=bf16),
+            shape(ext, 6 * ghost, dtype=bf16),
+        ),
         in_specs=[pl.BlockSpec(memory_space=pl.ANY)] * 2,
-        out_specs=pl.BlockSpec(memory_space=pltpu.VMEM),
+        out_specs=(pl.BlockSpec(memory_space=pltpu.VMEM),) * 2,
         scratch_shapes=[
             pltpu.VMEM((cells, n), jnp.int32),
             pltpu.VMEM((cells, n, n), f32),
@@ -147,42 +165,48 @@
     )(cell_nodes, cell_ham)
 
 
-def apply_kernel(v, m, near, far, ham, own, to_near, to_far):
-    owned = v.shape[0]
+def own_kernel(v, column, ham, out):
+    hi, lo = split(v[...] * column[:, :1])
+    out[...] = mm(ham[...], jnp.concatenate([hi, hi, lo], axis=0))
+
+
+def add_halo(partial, near, far, ham, to_near, to_far):
     ghost = near.shape[0]
-    x = jnp.concatenate([v[...] * as_column(m[...]), near[...], far[...]], axis=0)
-    hi, lo = split(x)
-    z = mm(ham[...], jnp.concatenate([hi, hi, lo], axis=0))
-    own[...] = z[:owned]
+    owned = partial.shape[0] - 2 * ghost
+    hi, lo = split(jnp.concatenate([near[...], far[...]], axis=0))
+    z = partial[...] + mm(ham[...], jnp.concatenate([hi, hi, lo], axis=0))
     to_near[...] = z[owned : owned + ghost]
     to_far[...] = z[owned + ghost :]
-
-
-def collect(own, from_near, from_far, up, dn):
-    owned = own.shape[0]
-    near, far = near_and_far(up, dn)
-    return (
-        own[...]
-        + select(put_rows(near, owned), from_near[...])
-        + select(put_rows(far, owned), from_far[...])
-    )
-
-
-def middle_kernel(own, from_near, from_far, s, m, up, dn, one, near_out, far_out):
-    column = as_column(m[...])
-    r = collect(own, from_near, from_far, up, dn)
-    filtered = (sigma_one / filter_half) * (r * column - filter_center * s[...])
+    return z[:owned]
+
+
+def first_kernel(partial, near, far, ham, column, s, base, to_near, to_far):
+    z = add_halo(partial, near, far, ham, to_near, to_far)
+    base[...] = (sigma_one / filter_half) * (z * column[:, :1] - filter_center * s[...])
+
+
+def second_kernel(partial, near, far, ham, column, one, s, base, to_near, to_far):
+    z = add_halo(partial, near, far, ham, to_near, to_far)
+    base[...] = (
+        2.0 * sigma_two / filter_half * (z * column[:, :1] - filter_center * one[...])
+        - sigma_one * sigma_two * s[...]
+    )
+
+
+def collect(factor, base, from_near, from_far, column, put):
+    parts = zip(split_three(from_near[...]), split_three(from_far[...]))
+    rows = jnp.concatenate([part for pair in parts for part in pair], axis=0)
+    return base[...] + factor * column[:, :1] * mm(put[...], rows)
+
+
+def middle_kernel(base, from_near, from_far, column, put, pick, one, near_out, far_out):
+    filtered = collect(sigma_one / filter_half, base, from_near, from_far, column, put)
     one[...] = filtered
-    send_rows(filtered * column, up, dn, near_out, far_out)
-
-
-def last_kernel(own, from_near, from_far, s, one, m, up, dn, two):
-    column = as_column(m[...])
-    r = collect(own, from_near, from_far, up, dn)
-    two[...] = (
-        2.0 * sigma_two / filter_half * (r * column - filter_center * one[...])
-        - sigma_one * sigma_two * s[...]
-    )
+    send_rows(filtered * column[:, :1], pick, near_out, far_out)
+
+
+def last_kernel(base, from_near, from_far, column, put, two):
+    two[...] = collect(2.0 * sigma_two / filter_half, base, from_near, from_far, column, put)
 
 
 def order_kernel(owner, *refs):
@@ -216,10 +240,12 @@
     out[...] = rotated_rows(hi_ref, lo_ref, [(0, own[...]), (1, one[...]), (2, two[...])])
 
 
-def rotate_last_kernel(hi_ref, lo_ref, total, inner, outer, m, up, dn, out, near_out, far_out):
-    rows = total[...] + rotated_rows(hi_ref, lo_ref, [(3, inner[...] + outer[...])])
+def rotate_last_kernel(hi_ref, lo_ref, total, inner, outer, column, pick, out, near_out, far_out):
+    here = lax.axis_index("band")
+    third = jnp.where((here == 1) | (here == 2), inner[...], outer[...])
+    rows = total[...] + rotated_rows(hi_ref, lo_ref, [(3, third)])
     out[...] = rows
-    send_rows(rows * as_column(m[...]), up, dn, near_out, far_out)
+    send_rows(rows * column[:, :1], pick, near_out, far_out)
 
 
 def flip(count, bits):
@@ -258,13 +284,17 @@
         from_near = lax.ppermute(to_near, "dom", near_pairs)
         return from_near, from_far
 
-    def apply(v, near, far, ham):
-        own, to_near, to_far = call(
-            apply_kernel, (block, halo, halo), [v, m, near, far, ham], 6 * ext * ext * cols
-        )
-        return (own, *exchange(to_near, to_far))
-
-    ham = assemble(cell_nodes, cell_ham, ext, ghost)
+    ham_own, ham_halo = assemble(cell_nodes, cell_ham, ext, ghost)
+    column, pick, put = call(
+        lists_kernel,
+        (
+            shape(owned, 128),
+            shape(2 * ghost, 3 * owned, dtype=bf16),
+            shape(owned, 6 * ghost, dtype=bf16),
+        ),
+        [m, up, dn],
+        owned * owned,
+    )
     band = lax.axis_index("band")
     own_columns = lax.dynamic_slice_in_dim(rotation_store, band * cols, cols, 1)
     one = lax.ppermute(states, "band", flip(4, 1))
@@ -273,9 +303,10 @@
     parts = [own_columns]
     if paired:
         parts += [lax.ppermute(own_columns, "dom", flip(doms, b)) for b in (2, 4, 6)]
-    held, one, two, ham, *parts = lax.optimization_barrier((states, one, two, ham, *parts))
-    inner = lax.ppermute(held, "band", [(1, 2), (2, 1)])
-    outer = lax.ppermute(two, "band", [(1, 0), (2, 3)])
+    ham_own, *parts = lax.optimization_barrier((ham_own, *parts))
+    held, one, two, ham_own = lax.optimization_barrier((states, one, two, ham_own))
+    inner = lax.ppermute(held, "band", [(0, 0), (1, 2), (2, 1), (3, 3)])
+    outer = lax.ppermute(two, "band", flip(4, 1))
     if paired:
         other = [lax.ppermute(part, "dom", near_pairs) for part in parts]
         slots = [part for pair in zip(parts, other) for part in pair]
@@ -289,17 +320,33 @@
     turned, to_near, to_far = call(
         rotate_last_kernel,
         (block, halo, halo),
-        [*rotation, total, inner, outer, m, up, dn],
+        [*rotation, total, inner, outer, column, pick],
         work,
     )
+    wide = shape(ext, cols)
+    work = 6 * ext * ext * cols
     near, far = exchange(to_near, to_far)
-    first = apply(turned, near, far, ham)
+    partial = call(own_kernel, wide, [turned, column, ham_own], work)
+    base, to_near, to_far = call(
+        first_kernel,
+        (block, halo, halo),
+        [partial, near, far, ham_halo, column, turned],
+        work,
+    )
+    near, far = exchange(to_near, to_far)
     filtered, to_near, to_far = call(
-        middle_kernel, (block, halo, halo), [*first, turned, m, up, dn], 2 * small
+        middle_kernel, (block, halo, halo), [base, near, far, column, put, pick], small
     )
     near, far = exchange(to_near, to_far)
-    second = apply(filtered, near, far, ham)
-    return call(last_kernel, block, [*second, turned, filtered, m, up, dn], small)
+    partial = call(own_kernel, wide, [filtered, column, ham_own], work)
+    base, to_near, to_far = call(
+        second_kernel,
+        (block, halo, halo),
+        [partial, near, far, ham_halo, column, filtered, turned],
+        work,
+    )
+    near, far = exchange(to_near, to_far)
+    return call(last_kernel, block, [base, near, far, column, put], small)
 
 
 def solution(mesh):

time: 59 us -> 54.3 us (0.920)
  the two profiles are of different devices: /device:TPU:0 before, /device:TPU:19 now
where the time goes in v3:
time: 54.3 us; the launch traced here: 54.2 us
  waiting for transfers between devices  21.5 us (40%)
  starting transfers between devices  19.5 us (36%)
  Pallas kernels  11.6 us (21%)
  local copies, waits for them, and re-layouts  1.34 us (2%)
    ppermute x4, waiting for transfers between devices, exchange(): from_far = lax.ppermute(to_far, 'dom', far_pairs)  12.8 us
    ppermute x4, starting transfers between devices, exchange(): from_far = lax.ppermute(to_far, 'dom', far_pairs)  5.9 us
    pallas_call x10, Pallas kernels, call(): pl.pallas_call(kernel, out_shape=out_shape, in_specs=specs, out_specs=jax...  5.78 us
    pallas_call x1, Pallas kernels, assemble(): pl.pallas_call(functools.partial(assemble_kernel, ghost), out_shape=(shap...  5.78 us
    ppermute x3, waiting for transfers between devices, shards(): lax.ppermute(own_columns, 'dom', flip(doms, b))  5.35 us
    ppermute x4, starting transfers between devices, exchange(): from_near = lax.ppermute(to_near, 'dom', near_pairs)  3.94 us
    ppermute x3, starting transfers between devices, shards(): lax.ppermute(own_columns, 'dom', flip(doms, b))  2.71 us
    ppermute x1, waiting for transfers between devices, shards(): inner = lax.ppermute(held, 'band', [(0, 0), (1, 2), (2, 1), (3, 3)])  2.51 us
  transfers between devices with their start and end apart: 19, of which 7 were waited for; matrix products, arithmetic and copies ran while one was open for 0% of the time, Pallas kernels for 16%

profile of v3, /device:TPU:19, one launch (start us, length us, event | category | flops | bytes accessed | tf_op | source)
XLA Modules:
  0.0 54.2 jit_solution(14383434762224688650)
XLA Ops:
  0.0 0.0 copy-start
  0.0 1.3 %copy-done = f32[192,1536]{1,0:T(8,128)S(1)} copy-done((f32[192,1536]{1,0:T(8,128)S(1)}, f32[192,1536]{1,0:T(8,128)}, u32[]{:S(2)}) %copy-start) | copy-done | bytes 1179672
  1.3 0.0 copy-start.3
  1.3 0.0 copy-start.4
  1.3 0.0 copy-start.6
  1.3 0.0 copy-start.7
  1.3 0.0 copy-start.5
  1.4 0.3 collective-permute-start
  1.7 1.2 %collective-permute-start.1 = (f32[192,384]{1,0:T(8,128)S(1)}, f32[192,384]{1,0:T(8,128)S(1)}, u32[]{:S(2)}, u32[]{:S(2)}) collective-permute-start(f32[192,384]{1,0:T(8,128)S(1)} %constant_dynamic-slice_fusion.refs_0_), channel_id=1, source_target_pairs={{0,16},{4,20},{8,24},{12,28},{16,0},{20,4},{24,8},{28,12},{1,17},{... | collective-permute-start | bytes 884744 | tf_op jit(solution)/shard_map/ppermute | solution.py:305
  2.9 1.2 %collective-permute-start.2 = (f32[192,384]{1,0:T(8,128)S(1)}, f32[192,384]{1,0:T(8,128)S(1)}, u32[]{:S(2)}, u32[]{:S(2)}) collective-permute-start(f32[192,384]{1,0:T(8,128)S(1)} %constant_dynamic-slice_fusion.refs_0_), channel_id=1, source_target_pairs={{0,24},{4,28},{8,16},{12,20},{16,8},{20,12},{24,0},{28,4},{1,25},{... | collective-permute-start | bytes 884744 | tf_op jit(solution)/shard_map/ppermute | solution.py:305
  4.1 1.3 %collective-permute-start.7 = (f32[192,384]{1,0:T(8,128)}, f32[192,384]{1,0:T(8,128)S(1)}, u32[]{:S(2)}, u32[]{:S(2)}) collective-permute-start(f32[192,384]{1,0:T(8,128)} %own), channel_id=1, source_target_pairs={{0,1},{1,0},{2,3},{3,2},{4,5},{5,4},{6,7},{7,6},{8,9},{9,8},{10,11... | collective-permute-start | bytes 884744 | tf_op jit(solution)/shard_map/ppermute | solution.py:300
  5.4 0.1 collective-permute-start.8
  5.4 5.8 %shard_map.82 = (bf16[288,576]{1,0:T(8,128)(2,1)}, bf16[288,288]{1,0:T(8,128)(2,1)}) custom-call(s32[5,343]{1,0:T(8,128)} %nodes_any.1, f32[5,343,343]{2,1,0:T(8,128)} %ham_any.1), custom_call_target="tpu_custom_call" | custom-call | flops 1355316480 | bytes 2352980 | tf_op jit(solution)/shard_map/pallas_call | solution.py:146
  11.2 0.0 collective-permute-done.refs_2_
  11.2 0.0 collective-permute-done.1.refs_4_
  11.2 5.3 %collective-permute-done.2.refs_6_ = f32[192,384]{1,0:T(8,128)S(1)} collective-permute-done((f32[192,384]{1,0:T(8,128)S(1)}, f32[192,384]{1,0:T(8,128)S(1)}, u32[]{:S(2)}, u32[]{:S(2)}) %collective-permute-start.2) | collective-permute-done | bytes 294944 | tf_op jit(solution)/shard_map/ppermute | solution.py:305
  16.6 1.5 %collective-permute-start.3 = (f32[192,384]{1,0:T(8,128)S(1)}, f32[192,384]{1,0:T(8,128)S(1)}, u32[]{:S(2)}, u32[]{:S(2)}) collective-permute-start(f32[192,384]{1,0:T(8,128)S(1)} %constant_dynamic-slice_fusion.refs_0_), channel_id=1, source_target_pairs={{0,4},{4,0},{8,12},{12,8},{16,20},{20,16},{24,28},{28,24},{1,5},{5... | collective-permute-start | bytes 884744 | tf_op jit(solution)/shard_map/ppermute | solution.py:311
  18.1 0.0 collective-permute-start.4
  18.1 0.5 collective-permute-start.5
  18.6 0.0 collective-permute-done.7.one
  18.6 0.0 collective-permute-start.6
  18.6 0.0 collective-permute-done.8.two
  18.7 1.4 %collective-permute-start.10 = (f32[192,384]{1,0:T(8,128)S(1)}, f32[192,384]{1,0:T(8,128)S(1)}, u32[]{:S(2)}, u32[]{:S(2)}) collective-permute-start(f32[192,384]{1,0:T(8,128)S(1)} %collective-permute-done.8.two), channel_id=1, source_target_pairs={{0,1},{1,0},{2,3},{3,2},{4,5},{5,4},{6,7},{7,6},{8,9},{9,8},{10,11... | collective-permute-start | bytes 884744 | tf_op jit(solution)/shard_map/ppermute | solution.py:309
  20.1 0.0 collective-permute-done.3.refs_1_
  20.1 0.0 copy-done.3
  20.1 2.0 %collective-permute-start.9 = (f32[192,384]{1,0:T(8,128)S(1)}, f32[192,384]{1,0:T(8,128)S(1)}, u32[]{:S(2)}, u32[]{:S(2)}) collective-permute-start(f32[192,384]{1,0:T(8,128)S(1)} %copy-done.3), channel_id=1, source_target_pairs={{0,0},{1,2},{2,1},{3,3},{4,4},{5,6},{6,5},{7,7},{8,8},{9,10},{10,9... | collective-permute-start | bytes 884744 | tf_op jit(solution)/shard_map/ppermute | solution.py:308
  22.2 0.0 copy-done.4
  22.2 0.0 copy-done.6
  22.2 0.0 copy-done.7
  22.2 0.2 shard_map.85
  22.4 0.0 collective-permute-done.4.refs_3_
  22.4 0.0 collective-permute-done.5.refs_5_
  22.4 0.0 collective-permute-done.6.refs_7_
  22.4 0.0 copy-done.5
  22.4 1.0 %shard_map.83 = (bf16[8,192,384]{2,1,0:T(8,128)(2,1)S(1)}, bf16[8,192,384]{2,1,0:T(8,128)(2,1)S(1)}) custom-call(s32[8]{0:T(128)S(1)} %copy-done.5, f32[192,384]{1,0:T(8,128)S(1)} %constant_dynamic-slice_fusion.refs_0_, f32[192,384]{1,0:T(8,128)S(1)} %collective-permute-done.3.refs_1_, f32[192,384]{1,0:T(8,128)S(1)} %collective-permute-done.refs_2_, ...), custom_call_target="tpu_custom_call" | custom-call | flops 9437184 | bytes 1048576 | tf_op jit(solution)/shard_map/pallas_call | solution.py:59
  23.4 0.9 %shard_map.84.total = f32[192,384]{1,0:T(8,128)S(1)} custom-call(bf16[4,384,384]{2,1,0:T(8,128)(2,1)S(1)} %bitcast.5, bf16[4,384,384]{2,1,0:T(8,128)(2,1)S(1)} %bitcast.7, f32[192,384]{1,0:T(8,128)S(1)} %copy-done.3, f32[192,384]{1,0:T(8,128)S(1)} %collective-permute-done.7.one, f32[192,384]{1,0:T(8,128)S(1)} %collective-permute-done.8.two), custom_call_target="tpu_custom_call" | custom-call | flops 509607936 | bytes 1048576 | tf_op jit(solution)/shard_map/pallas_call | solution.py:59
  24.4 0.9 %collective-permute-done.10.outer = f32[192,384]{1,0:T(8,128)S(1)} collective-permute-done((f32[192,384]{1,0:T(8,128)S(1)}, f32[192,384]{1,0:T(8,128)S(1)}, u32[]{:S(2)}, u32[]{:S(2)}) %collective-permute-start.10) | collective-permute-done | bytes 294944 | tf_op jit(solution)/shard_map/ppermute | solution.py:309
  25.2 2.5 %collective-permute-done.9.inner = f32[192,384]{1,0:T(8,128)S(1)} collective-permute-done((f32[192,384]{1,0:T(8,128)S(1)}, f32[192,384]{1,0:T(8,128)S(1)}, u32[]{:S(2)}, u32[]{:S(2)}) %collective-permute-start.9) | collective-permute-done | bytes 294944 | tf_op jit(solution)/shard_map/ppermute | solution.py:308
  27.7 0.7 %shard_map.86 = (f32[192,384]{1,0:T(8,128)S(1)}, f32[48,384]{1,0:T(8,128)S(1)}, f32[48,384]{1,0:T(8,128)S(1)}) custom-call(bf16[4,384,384]{2,1,0:T(8,128)(2,1)S(1)} %bitcast.6, bf16[4,384,384]{2,1,0:T(8,128)(2,1)S(1)} %bitcast.8, f32[192,384]{1,0:T(8,128)S(1)} %shard_map.84.total, f32[192,384]{1,0:T(8,128)S(1)} %collective-permute-done.9.inner, ...), custom_call_target="tpu_custom_call" | custom-call | flops 169869312 | bytes 1048576 | tf_op jit(solution)/shard_map/pallas_call | solution.py:59
  28.4 0.0 copy-start.2
  28.4 3.7 %collective-permute-start.11 = (f32[48,384]{1,0:T(8,128)S(1)}, f32[48,384]{1,0:T(8,128)S(1)}, u32[]{:S(2)}, u32[]{:S(2)}) collective-permute-start(f32[48,384]{1,0:T(8,128)S(1)} %get-tuple-element.48), channel_id=1, source_target_pairs={{0,4},{4,0},{8,12},{12,8},{16,20},{20,16},{24,28},{28,24},{1,5},{5... | collective-permute-start | bytes 221192 | tf_op jit(solution)/shard_map/ppermute | solution.py:284
  32.1 1.4 %collective-permute-start.12 = (f32[48,384]{1,0:T(8,128)S(1)}, f32[48,384]{1,0:T(8,128)S(1)}, u32[]{:S(2)}, u32[]{:S(2)}) collective-permute-start(f32[48,384]{1,0:T(8,128)S(1)} %get-tuple-element.49), channel_id=1, source_target_pairs={{0,28},{4,8},{8,4},{12,16},{16,12},{20,24},{24,20},{28,0},{1,29},{... | collective-permute-start | bytes 221192 | tf_op jit(solution)/shard_map/ppermute | solution.py:283
  33.5 0.0 copy-done.1
  33.5 0.5 shard_map.87.partial
  34.0 0.0 collective-permute-done.11.near
  34.0 3.1 %collective-permute-done.12.far = f32[48,384]{1,0:T(8,128)S(1)} collective-permute-done((f32[48,384]{1,0:T(8,128)S(1)}, f32[48,384]{1,0:T(8,128)S(1)}, u32[]{:S(2)}, u32[]{:S(2)}) %collective-permute-start.12) | collective-permute-done | bytes 73760 | tf_op jit(solution)/shard_map/ppermute | solution.py:283
  37.1 0.0 copy-done.2
  37.1 0.3 shard_map.88
  37.4 0.1 collective-permute-start.13
  37.5 1.6 %collective-permute-start.14 = (f32[48,384]{1,0:T(8,128)S(1)}, f32[48,384]{1,0:T(8,128)S(1)}, u32[]{:S(2)}, u32[]{:S(2)}) collective-permute-start(f32[48,384]{1,0:T(8,128)S(1)} %get-tuple-element.53), channel_id=1, source_target_pairs={{0,28},{4,8},{8,4},{12,16},{16,12},{20,24},{24,20},{28,0},{1,29},{... | collective-permute-start | bytes 221192 | tf_op jit(solution)/shard_map/ppermute | solution.py:283
  39.1 0.0 collective-permute-done.13.from_near
  39.1 3.5 %collective-permute-done.14.from_far = f32[48,384]{1,0:T(8,128)S(1)} collective-permute-done((f32[48,384]{1,0:T(8,128)S(1)}, f32[48,384]{1,0:T(8,128)S(1)}, u32[]{:S(2)}, u32[]{:S(2)}) %collective-permute-start.14) | collective-permute-done | bytes 73760 | tf_op jit(solution)/shard_map/ppermute | solution.py:283
  42.6 0.5 shard_map.89
  43.1 0.1 collective-permute-start.15
  43.1 1.5 %collective-permute-start.16 = (f32[48,384]{1,0:T(8,128)S(1)}, f32[48,384]{1,0:T(8,128)S(1)}, u32[]{:S(2)}, u32[]{:S(2)}) collective-permute-start(f32[48,384]{1,0:T(8,128)S(1)} %get-tuple-element.57), channel_id=1, source_target_pairs={{0,28},{4,8},{8,4},{12,16},{16,12},{20,24},{24,20},{28,0},{1,29},{... | collective-permute-start | bytes 221192 | tf_op jit(solution)/shard_map/ppermute | solution.py:283
  44.6 0.5 shard_map.90.partial
  45.1 0.0 collective-permute-done.15.near
  45.1 2.8 %collective-permute-done.16.far = f32[48,384]{1,0:T(8,128)S(1)} collective-permute-done((f32[48,384]{1,0:T(8,128)S(1)}, f32[48,384]{1,0:T(8,128)S(1)}, u32[]{:S(2)}, u32[]{:S(2)}) %collective-permute-start.16) | collective-permute-done | bytes 73760 | tf_op jit(solution)/shard_map/ppermute | solution.py:283
  47.9 0.3 shard_map.91
  48.2 0.1 collective-permute-start.17
  48.3 1.5 %collective-permute-start.18 = (f32[48,384]{1,0:T(8,128)S(1)}, f32[48,384]{1,0:T(8,128)S(1)}, u32[]{:S(2)}, u32[]{:S(2)}) collective-permute-start(f32[48,384]{1,0:T(8,128)S(1)} %get-tuple-element.60), channel_id=1, source_target_pairs={{0,28},{4,8},{8,4},{12,16},{16,12},{20,24},{24,20},{28,0},{1,29},{... | collective-permute-start | bytes 221192 | tf_op jit(solution)/shard_map/ppermute | solution.py:283
  49.8 0.0 collective-permute-done.17.from_near
  49.8 3.4 %collective-permute-done.18.from_far = f32[48,384]{1,0:T(8,128)S(1)} collective-permute-done((f32[48,384]{1,0:T(8,128)S(1)}, f32[48,384]{1,0:T(8,128)S(1)}, u32[]{:S(2)}, u32[]{:S(2)}) %collective-permute-start.18) | collective-permute-done | bytes 73760 | tf_op jit(solution)/shard_map/ppermute | solution.py:283
  53.2 1.0 %shard_map.92 = f32[192,384]{1,0:T(8,128)} custom-call(f32[192,384]{1,0:T(8,128)S(1)} %get-tuple-element.58.base, f32[48,384]{1,0:T(8,128)S(1)} %collective-permute-done.17.from_near, f32[48,384]{1,0:T(8,128)S(1)} %collective-permute-done.18.from_far, f32[192,128]{1,0:T(8,128)S(1)} %get-tuple-element.44.column, bf16[192,288]{1,0:T(8,128)(2,1)S(1)} %get-tuple-element.54.put), custom_call_target="tpu_custom_call" | custom-call | flops 42467328 | bytes 1048576 | tf_op jit(solution)/shard_map/pallas_call | solution.py:59
  (2 shorter events, 0.0 us)
Async XLA Ops:
  0.0 1.3 %copy-start = (f32[192,1536]{1,0:T(8,128)S(1)}, f32[192,1536]{1,0:T(8,128)}, u32[]{:S(2)}) copy-start(f32[192,1536]{1,0:T(8,128)} %param.15) | copy-start | bytes 3538948
  1.3 18.8 %copy-start.3 = (f32[192,384]{1,0:T(8,128)S(1)}, f32[192,384]{1,0:T(8,128)}, u32[]{:S(2)}) copy-start(f32[192,384]{1,0:T(8,128)} %own) | copy-start | bytes 884740
  1.3 20.8 %copy-start.4 = (f32[192]{0:T(256)S(1)}, f32[192]{0:T(256)}, u32[]{:S(2)}) copy-start(f32[192]{0:T(256)} %param.9) | copy-start | bytes 2308
  1.3 20.8 %copy-start.6 = (s32[48]{0:T(128)S(1)}, s32[48]{0:T(128)}, u32[]{:S(2)}) copy-start(s32[48]{0:T(128)} %param.12) | copy-start | bytes 580
  1.3 20.8 %copy-start.7 = (s32[48]{0:T(128)S(1)}, s32[48]{0:T(128)}, u32[]{:S(2)}) copy-start(s32[48]{0:T(128)} %param.13) | copy-start | bytes 580
  1.3 21.1 %copy-start.5 = (s32[8]{0:T(128)S(1)}, s32[8]{0:T(128)}, u32[]{:S(2)}) copy-start(s32[8]{0:T(128)} %owner.1) | copy-start | bytes 100
  1.4 9.9 %collective-permute-start = (f32[192,384]{1,0:T(8,128)S(1)}, f32[192,384]{1,0:T(8,128)S(1)}, u32[]{:S(2)}, u32[]{:S(2)}) collective-permute-start(f32[192,384]{1,0:T(8,128)S(1)} %constant_dynamic-slice_fusion.refs_0_), channel_id=1, source_target_pairs={{0,8},{4,12},{8,0},{12,4},{16,24},{20,28},{24,16},{28,20},{1,9},{5... | collective-permute-start | bytes 884744 | tf_op jit(solution)/shard_map/ppermute | solution.py:305
  1.7 9.5 %collective-permute-start.1 = (f32[192,384]{1,0:T(8,128)S(1)}, f32[192,384]{1,0:T(8,128)S(1)}, u32[]{:S(2)}, u32[]{:S(2)}) collective-permute-start(f32[192,384]{1,0:T(8,128)S(1)} %constant_dynamic-slice_fusion.refs_0_), channel_id=1, source_target_pairs={{0,16},{4,20},{8,24},{12,28},{16,0},{20,4},{24,8},{28,12},{1,17},{... | collective-permute-start | bytes 884744 | tf_op jit(solution)/shard_map/ppermute | solution.py:305
  2.9 13.7 %collective-permute-start.2 = (f32[192,384]{1,0:T(8,128)S(1)}, f32[192,384]{1,0:T(8,128)S(1)}, u32[]{:S(2)}, u32[]{:S(2)}) collective-permute-start(f32[192,384]{1,0:T(8,128)S(1)} %constant_dynamic-slice_fusion.refs_0_), channel_id=1, source_target_pairs={{0,24},{4,28},{8,16},{12,20},{16,8},{20,12},{24,0},{28,4},{1,25},{... | collective-permute-start | bytes 884744 | tf_op jit(solution)/shard_map/ppermute | solution.py:305
  4.1 14.6 %collective-permute-start.7 = (f32[192,384]{1,0:T(8,128)}, f32[192,384]{1,0:T(8,128)S(1)}, u32[]{:S(2)}, u32[]{:S(2)}) collective-permute-start(f32[192,384]{1,0:T(8,128)} %own), channel_id=1, source_target_pairs={{0,1},{1,0},{2,3},{3,2},{4,5},{5,4},{6,7},{7,6},{8,9},{9,8},{10,11... | collective-permute-start | bytes 884744 | tf_op jit(solution)/shard_map/ppermute | solution.py:300
  5.4 13.3 %collective-permute-start.8 = (f32[192,384]{1,0:T(8,128)}, f32[192,384]{1,0:T(8,128)S(1)}, u32[]{:S(2)}, u32[]{:S(2)}) collective-permute-start(f32[192,384]{1,0:T(8,128)} %own), channel_id=1, source_target_pairs={{0,2},{1,3},{2,0},{3,1},{4,6},{5,7},{6,4},{7,5},{8,10},{9,11},{10,... | collective-permute-start | bytes 884744 | tf_op jit(solution)/shard_map/ppermute | solution.py:301
  16.6 3.5 %collective-permute-start.3 = (f32[192,384]{1,0:T(8,128)S(1)}, f32[192,384]{1,0:T(8,128)S(1)}, u32[]{:S(2)}, u32[]{:S(2)}) collective-permute-start(f32[192,384]{1,0:T(8,128)S(1)} %constant_dynamic-slice_fusion.refs_0_), channel_id=1, source_target_pairs={{0,4},{4,0},{8,12},{12,8},{16,20},{20,16},{24,28},{28,24},{1,5},{5... | collective-permute-start | bytes 884744 | tf_op jit(solution)/shard_map/ppermute | solution.py:311
  18.1 4.3 %collective-permute-start.4 = (f32[192,384]{1,0:T(8,128)S(1)}, f32[192,384]{1,0:T(8,128)S(1)}, u32[]{:S(2)}, u32[]{:S(2)}) collective-permute-start(f32[192,384]{1,0:T(8,128)S(1)} %collective-permute-done.refs_2_), channel_id=1, source_target_pairs={{0,4},{4,0},{8,12},{12,8},{16,20},{20,16},{24,28},{28,24},{1,5},{5... | collective-permute-start | bytes 884744 | tf_op jit(solution)/shard_map/ppermute | solution.py:311
  18.1 4.3 %collective-permute-start.5 = (f32[192,384]{1,0:T(8,128)S(1)}, f32[192,384]{1,0:T(8,128)S(1)}, u32[]{:S(2)}, u32[]{:S(2)}) collective-permute-start(f32[192,384]{1,0:T(8,128)S(1)} %collective-permute-done.1.refs_4_), channel_id=1, source_target_pairs={{0,4},{4,0},{8,12},{12,8},{16,20},{20,16},{24,28},{28,24},{1,5},{5... | collective-permute-start | bytes 884744 | tf_op jit(solution)/shard_map/ppermute | solution.py:311
  18.6 3.8 %collective-permute-start.6 = (f32[192,384]{1,0:T(8,128)S(1)}, f32[192,384]{1,0:T(8,128)S(1)}, u32[]{:S(2)}, u32[]{:S(2)}) collective-permute-start(f32[192,384]{1,0:T(8,128)S(1)} %collective-permute-done.2.refs_6_), channel_id=1, source_target_pairs={{0,4},{4,0},{8,12},{12,8},{16,20},{20,16},{24,28},{28,24},{1,5},{5... | collective-permute-start | bytes 884744 | tf_op jit(solution)/shard_map/ppermute | solution.py:311
  18.7 6.6 %collective-permute-start.10 = (f32[192,384]{1,0:T(8,128)S(1)}, f32[192,384]{1,0:T(8,128)S(1)}, u32[]{:S(2)}, u32[]{:S(2)}) collective-permute-start(f32[192,384]{1,0:T(8,128)S(1)} %collective-permute-done.8.two), channel_id=1, source_target_pairs={{0,1},{1,0},{2,3},{3,2},{4,5},{5,4},{6,7},{7,6},{8,9},{9,8},{10,11... | collective-permute-start | bytes 884744 | tf_op jit(solution)/shard_map/ppermute | solution.py:309
  20.1 7.6 %collective-permute-start.9 = (f32[192,384]{1,0:T(8,128)S(1)}, f32[192,384]{1,0:T(8,128)S(1)}, u32[]{:S(2)}, u32[]{:S(2)}) collective-permute-start(f32[192,384]{1,0:T(8,128)S(1)} %copy-done.3), channel_id=1, source_target_pairs={{0,0},{1,2},{2,1},{3,3},{4,4},{5,6},{6,5},{7,7},{8,8},{9,10},{10,9... | collective-permute-start | bytes 884744 | tf_op jit(solution)/shard_map/ppermute | solution.py:308
  27.7 5.8 %copy-start.1 = (bf16[288,576]{1,0:T(8,128)(2,1)S(1)}, bf16[288,576]{1,0:T(8,128)(2,1)}, u32[]{:S(2)}) copy-start(bf16[288,576]{1,0:T(8,128)(2,1)} %get-tuple-element.47.ham) | copy-start | bytes 995332
  28.4 8.7 %copy-start.2 = (bf16[288,288]{1,0:T(8,128)(2,1)S(1)}, bf16[288,288]{1,0:T(8,128)(2,1)}, u32[]{:S(2)}) copy-start(bf16[288,288]{1,0:T(8,128)(2,1)} %get-tuple-element.50.ham) | copy-start | bytes 497668
  28.4 5.6 %collective-permute-start.11 = (f32[48,384]{1,0:T(8,128)S(1)}, f32[48,384]{1,0:T(8,128)S(1)}, u32[]{:S(2)}, u32[]{:S(2)}) collective-permute-start(f32[48,384]{1,0:T(8,128)S(1)} %get-tuple-element.48), channel_id=1, source_target_pairs={{0,4},{4,0},{8,12},{12,8},{16,20},{20,16},{24,28},{28,24},{1,5},{5... | collective-permute-start | bytes 221192 | tf_op jit(solution)/shard_map/ppermute | solution.py:284
  32.1 4.9 %collective-permute-start.12 = (f32[48,384]{1,0:T(8,128)S(1)}, f32[48,384]{1,0:T(8,128)S(1)}, u32[]{:S(2)}, u32[]{:S(2)}) collective-permute-start(f32[48,384]{1,0:T(8,128)S(1)} %get-tuple-element.49), channel_id=1, source_target_pairs={{0,28},{4,8},{8,4},{12,16},{16,12},{20,24},{24,20},{28,0},{1,29},{... | collective-permute-start | bytes 221192 | tf_op jit(solution)/shard_map/ppermute | solution.py:283
  37.4 1.7 %collective-permute-start.13 = (f32[48,384]{1,0:T(8,128)S(1)}, f32[48,384]{1,0:T(8,128)S(1)}, u32[]{:S(2)}, u32[]{:S(2)}) collective-permute-start(f32[48,384]{1,0:T(8,128)S(1)} %get-tuple-element.52), channel_id=1, source_target_pairs={{0,4},{4,0},{8,12},{12,8},{16,20},{20,16},{24,28},{28,24},{1,5},{5... | collective-permute-start | bytes 221192 | tf_op jit(solution)/shard_map/ppermute | solution.py:284
  37.5 5.1 %collective-permute-start.14 = (f32[48,384]{1,0:T(8,128)S(1)}, f32[48,384]{1,0:T(8,128)S(1)}, u32[]{:S(2)}, u32[]{:S(2)}) collective-permute-start(f32[48,384]{1,0:T(8,128)S(1)} %get-tuple-element.53), channel_id=1, source_target_pairs={{0,28},{4,8},{8,4},{12,16},{16,12},{20,24},{24,20},{28,0},{1,29},{... | collective-permute-start | bytes 221192 | tf_op jit(solution)/shard_map/ppermute | solution.py:283
  43.1 2.0 %collective-permute-start.15 = (f32[48,384]{1,0:T(8,128)S(1)}, f32[48,384]{1,0:T(8,128)S(1)}, u32[]{:S(2)}, u32[]{:S(2)}) collective-permute-start(f32[48,384]{1,0:T(8,128)S(1)} %get-tuple-element.56), channel_id=1, source_target_pairs={{0,4},{4,0},{8,12},{12,8},{16,20},{20,16},{24,28},{28,24},{1,5},{5... | collective-permute-start | bytes 221192 | tf_op jit(solution)/shard_map/ppermute | solution.py:284
  43.1 4.7 %collective-permute-start.16 = (f32[48,384]{1,0:T(8,128)S(1)}, f32[48,384]{1,0:T(8,128)S(1)}, u32[]{:S(2)}, u32[]{:S(2)}) collective-permute-start(f32[48,384]{1,0:T(8,128)S(1)} %get-tuple-element.57), channel_id=1, source_target_pairs={{0,28},{4,8},{8,4},{12,16},{16,12},{20,24},{24,20},{28,0},{1,29},{... | collective-permute-start | bytes 221192 | tf_op jit(solution)/shard_map/ppermute | solution.py:283
  48.2 1.6 %collective-permute-start.17 = (f32[48,384]{1,0:T(8,128)S(1)}, f32[48,384]{1,0:T(8,128)S(1)}, u32[]{:S(2)}, u32[]{:S(2)}) collective-permute-start(f32[48,384]{1,0:T(8,128)S(1)} %get-tuple-element.59), channel_id=1, source_target_pairs={{0,4},{4,0},{8,12},{12,8},{16,20},{20,16},{24,28},{28,24},{1,5},{5... | collective-permute-start | bytes 221192 | tf_op jit(solution)/shard_map/ppermute | solution.py:284
  48.3 4.9 %collective-permute-start.18 = (f32[48,384]{1,0:T(8,128)S(1)}, f32[48,384]{1,0:T(8,128)S(1)}, u32[]{:S(2)}, u32[]{:S(2)}) collective-permute-start(f32[48,384]{1,0:T(8,128)S(1)} %get-tuple-element.60), channel_id=1, source_target_pairs={{0,28},{4,8},{8,4},{12,16},{16,12},{20,24},{24,20},{28,0},{1,29},{... | collective-permute-start | bytes 221192 | tf_op jit(solution)/shard_map/ppermute | solution.py:283

commit v4 on v3

--- a/solution.py
+++ b/solution.py
@@ -180,12 +180,12 @@
     return z[:owned]
 
 
-def first_kernel(partial, near, far, ham, column, s, base, to_near, to_far):
+def first_kernel(far, partial, near, ham, column, s, base, to_near, to_far):
     z = add_halo(partial, near, far, ham, to_near, to_far)
     base[...] = (sigma_one / filter_half) * (z * column[:, :1] - filter_center * s[...])
 
 
-def second_kernel(partial, near, far, ham, column, one, s, base, to_near, to_far):
+def second_kernel(far, partial, near, ham, column, one, s, base, to_near, to_far):
     z = add_halo(partial, near, far, ham, to_near, to_far)
     base[...] = (
         2.0 * sigma_two / filter_half * (z * column[:, :1] - filter_center * one[...])
@@ -199,13 +199,13 @@
     return base[...] + factor * column[:, :1] * mm(put[...], rows)
 
 
-def middle_kernel(base, from_near, from_far, column, put, pick, one, near_out, far_out):
+def middle_kernel(from_far, base, from_near, column, put, pick, one, near_out, far_out):
     filtered = collect(sigma_one / filter_half, base, from_near, from_far, column, put)
     one[...] = filtered
     send_rows(filtered * column[:, :1], pick, near_out, far_out)
 
 
-def last_kernel(base, from_near, from_far, column, put, two):
+def last_kernel(from_far, base, from_near, column, put, two):
     two[...] = collect(2.0 * sigma_two / filter_half, base, from_near, from_far, column, put)
 
 
@@ -280,8 +280,8 @@
     small = 4 * ghost * owned * cols * 3
 
     def exchange(to_near, to_far):
+        from_near = lax.ppermute(to_near, "dom", near_pairs)
         from_far = lax.ppermute(to_far, "dom", far_pairs)
-        from_near = lax.ppermute(to_near, "dom", near_pairs)
         return from_near, from_far
 
     ham_own, ham_halo = assemble(cell_nodes, cell_ham, ext, ghost)
@@ -330,23 +330,23 @@
     base, to_near, to_far = call(
         first_kernel,
         (block, halo, halo),
-        [partial, near, far, ham_halo, column, turned],
+        [far, partial, near, ham_halo, column, turned],
         work,
     )
     near, far = exchange(to_near, to_far)
     filtered, to_near, to_far = call(
-        middle_kernel, (block, halo, halo), [base, near, far, column, put, pick], small
+        middle_kernel, (block, halo, halo), [far, base, near, column, put, pick], small
     )
     near, far = exchange(to_near, to_far)
     partial = call(own_kernel, wide, [filtered, column, ham_own], work)
     base, to_near, to_far = call(
         second_kernel,
         (block, halo, halo),
-        [partial, near, far, ham_halo, column, filtered, turned],
+        [far, partial, near, ham_halo, column, filtered, turned],
         work,
     )
     near, far = exchange(to_near, to_far)
-    return call(last_kernel, block, [base, near, far, column, put], small)
+    return call(last_kernel, block, [far, base, near, column, put], small)
 
 
 def solution(mesh):

time: 54.3 us -> 53.7 us (0.989)
  the two profiles are of different devices: /device:TPU:19 before, /device:TPU:0 now
where the time goes in v4:
time: 53.7 us; the launch traced here: 52.7 us
  waiting for transfers between devices  26.2 us (49%)
  starting transfers between devices  13.3 us (25%)
  Pallas kernels  11.6 us (22%)
  local copies, waits for them, and re-layouts  1.34 us (2%)
    ppermute x4, waiting for transfers between devices, exchange(): from_far = lax.ppermute(to_far, 'dom', far_pairs)  16.4 us
    pallas_call x10, Pallas kernels, call(): pl.pallas_call(kernel, out_shape=out_shape, in_specs=specs, out_specs=jax...  5.79 us
    pallas_call x1, Pallas kernels, assemble(): pl.pallas_call(functools.partial(assemble_kernel, ghost), out_shape=(shap...  5.78 us
    ppermute x3, starting transfers between devices, shards(): lax.ppermute(own_columns, 'dom', flip(doms, b))  4.54 us
    ppermute x1, waiting for transfers between devices, shards(): outer = lax.ppermute(two, 'band', flip(4, 1))  3.55 us
    ppermute x3, waiting for transfers between devices, shards(): lax.ppermute(own_columns, 'dom', flip(doms, b))  2.83 us
    ppermute x1, starting transfers between devices, shards(): two = lax.ppermute(states, 'band', flip(4, 2))  2.59 us
    ppermute x1, waiting for transfers between devices, shards(): two = lax.ppermute(states, 'band', flip(4, 2))  2.55 us
  transfers between devices with their start and end apart: 19, of which 8 were waited for; matrix products, arithmetic and copies ran while one was open for 0% of the time, Pallas kernels for 17%

profile of v4, /device:TPU:0, one launch (start us, length us, event | category | flops | bytes accessed | tf_op | source)
XLA Modules:
  0.0 52.7 jit_solution(9153345861620969146)
XLA Ops:
  0.0 0.0 copy-start
  0.0 1.3 %copy-done = f32[192,1536]{1,0:T(8,128)S(1)} copy-done((f32[192,1536]{1,0:T(8,128)S(1)}, f32[192,1536]{1,0:T(8,128)}, u32[]{:S(2)}) %copy-start) | copy-done | bytes 1179672
  1.3 0.0 copy-start.3
  1.3 0.0 copy-start.4
  1.3 0.0 copy-start.6
  1.3 0.0 copy-start.7
  1.3 0.0 copy-start.5
  1.4 3.0 %collective-permute-start = (f32[192,384]{1,0:T(8,128)S(1)}, f32[192,384]{1,0:T(8,128)S(1)}, u32[]{:S(2)}, u32[]{:S(2)}) collective-permute-start(f32[192,384]{1,0:T(8,128)S(1)} %constant_dynamic-slice_fusion.refs_0_), channel_id=1, source_target_pairs={{0,8},{4,12},{8,0},{12,4},{16,24},{20,28},{24,16},{28,20},{1,9},{5... | collective-permute-start | bytes 884744 | tf_op jit(solution)/shard_map/ppermute | solution.py:305
  4.4 1.5 %collective-permute-start.1 = (f32[192,384]{1,0:T(8,128)S(1)}, f32[192,384]{1,0:T(8,128)S(1)}, u32[]{:S(2)}, u32[]{:S(2)}) collective-permute-start(f32[192,384]{1,0:T(8,128)S(1)} %constant_dynamic-slice_fusion.refs_0_), channel_id=1, source_target_pairs={{0,16},{4,20},{8,24},{12,28},{16,0},{20,4},{24,8},{28,12},{1,17},{... | collective-permute-start | bytes 884744 | tf_op jit(solution)/shard_map/ppermute | solution.py:305
  5.9 0.0 collective-permute-start.2
  5.9 2.0 %collective-permute-start.7 = (f32[192,384]{1,0:T(8,128)}, f32[192,384]{1,0:T(8,128)S(1)}, u32[]{:S(2)}, u32[]{:S(2)}) collective-permute-start(f32[192,384]{1,0:T(8,128)} %own), channel_id=1, source_target_pairs={{0,1},{1,0},{2,3},{3,2},{4,5},{5,4},{6,7},{7,6},{8,9},{9,8},{10,11... | collective-permute-start | bytes 884744 | tf_op jit(solution)/shard_map/ppermute | solution.py:300
  7.9 2.6 %collective-permute-start.8 = (f32[192,384]{1,0:T(8,128)}, f32[192,384]{1,0:T(8,128)S(1)}, u32[]{:S(2)}, u32[]{:S(2)}) collective-permute-start(f32[192,384]{1,0:T(8,128)} %own), channel_id=1, source_target_pairs={{0,2},{1,3},{2,0},{3,1},{4,6},{5,7},{6,4},{7,5},{8,10},{9,11},{10,... | collective-permute-start | bytes 884744 | tf_op jit(solution)/shard_map/ppermute | solution.py:301
  10.5 5.8 %shard_map.82 = (bf16[288,576]{1,0:T(8,128)(2,1)}, bf16[288,288]{1,0:T(8,128)(2,1)}) custom-call(s32[5,343]{1,0:T(8,128)} %nodes_any.1, f32[5,343,343]{2,1,0:T(8,128)} %ham_any.1), custom_call_target="tpu_custom_call" | custom-call | flops 1355316480 | bytes 2352980 | tf_op jit(solution)/shard_map/pallas_call | solution.py:146
  16.3 0.0 collective-permute-done.refs_2_
  16.3 2.8 %collective-permute-done.1.refs_4_ = f32[192,384]{1,0:T(8,128)S(1)} collective-permute-done((f32[192,384]{1,0:T(8,128)S(1)}, f32[192,384]{1,0:T(8,128)S(1)}, u32[]{:S(2)}, u32[]{:S(2)}) %collective-permute-start.1) | collective-permute-done | bytes 294944 | tf_op jit(solution)/shard_map/ppermute | solution.py:305
  19.2 0.0 collective-permute-done.2.refs_6_
  19.2 0.0 collective-permute-start.3
  19.2 0.5 collective-permute-start.4
  19.7 0.0 collective-permute-start.5
  19.7 0.8 %collective-permute-done.7.one = f32[192,384]{1,0:T(8,128)S(1)} collective-permute-done((f32[192,384]{1,0:T(8,128)}, f32[192,384]{1,0:T(8,128)S(1)}, u32[]{:S(2)}, u32[]{:S(2)}) %collective-permute-start.7) | collective-permute-done | bytes 294944 | tf_op jit(solution)/shard_map/ppermute | solution.py:300
  20.5 0.0 collective-permute-start.6
  20.5 2.6 %collective-permute-done.8.two = f32[192,384]{1,0:T(8,128)S(1)} collective-permute-done((f32[192,384]{1,0:T(8,128)}, f32[192,384]{1,0:T(8,128)S(1)}, u32[]{:S(2)}, u32[]{:S(2)}) %collective-permute-start.8) | collective-permute-done | bytes 294944 | tf_op jit(solution)/shard_map/ppermute | solution.py:301
  23.1 0.4 collective-permute-start.10
  23.5 0.0 collective-permute-done.3.refs_1_
  23.5 0.0 copy-done.3
  23.5 0.7 %collective-permute-start.9 = (f32[192,384]{1,0:T(8,128)S(1)}, f32[192,384]{1,0:T(8,128)S(1)}, u32[]{:S(2)}, u32[]{:S(2)}) collective-permute-start(f32[192,384]{1,0:T(8,128)S(1)} %copy-done.3), channel_id=1, source_target_pairs={{0,0},{1,2},{2,1},{3,3},{4,4},{5,6},{6,5},{7,7},{8,8},{9,10},{10,9... | collective-permute-start | bytes 884744 | tf_op jit(solution)/shard_map/ppermute | solution.py:308
  24.2 0.0 copy-done.4
  24.2 0.0 copy-done.6
  24.2 0.0 copy-done.7
  24.2 0.2 shard_map.85
  24.4 0.0 collective-permute-done.4.refs_3_
  24.4 0.0 collective-permute-done.5.refs_5_
  24.4 0.0 collective-permute-done.6.refs_7_
  24.5 0.0 copy-done.5
  24.5 1.0 %shard_map.83 = (bf16[8,192,384]{2,1,0:T(8,128)(2,1)S(1)}, bf16[8,192,384]{2,1,0:T(8,128)(2,1)S(1)}) custom-call(s32[8]{0:T(128)S(1)} %copy-done.5, f32[192,384]{1,0:T(8,128)S(1)} %constant_dynamic-slice_fusion.refs_0_, f32[192,384]{1,0:T(8,128)S(1)} %collective-permute-done.3.refs_1_, f32[192,384]{1,0:T(8,128)S(1)} %collective-permute-done.refs_2_, ...), custom_call_target="tpu_custom_call" | custom-call | flops 9437184 | bytes 1048576 | tf_op jit(solution)/shard_map/pallas_call | solution.py:59
  25.5 0.9 %shard_map.84.total = f32[192,384]{1,0:T(8,128)S(1)} custom-call(bf16[4,384,384]{2,1,0:T(8,128)(2,1)S(1)} %bitcast.5, bf16[4,384,384]{2,1,0:T(8,128)(2,1)S(1)} %bitcast.7, f32[192,384]{1,0:T(8,128)S(1)} %copy-done.3, f32[192,384]{1,0:T(8,128)S(1)} %collective-permute-done.7.one, f32[192,384]{1,0:T(8,128)S(1)} %collective-permute-done.8.two), custom_call_target="tpu_custom_call" | custom-call | flops 509607936 | bytes 1048576 | tf_op jit(solution)/shard_map/pallas_call | solution.py:59
  26.4 3.6 %collective-permute-done.10.outer = f32[192,384]{1,0:T(8,128)S(1)} collective-permute-done((f32[192,384]{1,0:T(8,128)S(1)}, f32[192,384]{1,0:T(8,128)S(1)}, u32[]{:S(2)}, u32[]{:S(2)}) %collective-permute-start.10) | collective-permute-done | bytes 294944 | tf_op jit(solution)/shard_map/ppermute | solution.py:309
  29.9 0.0 collective-permute-done.9.inner
  29.9 0.7 %shard_map.86 = (f32[192,384]{1,0:T(8,128)S(1)}, f32[48,384]{1,0:T(8,128)S(1)}, f32[48,384]{1,0:T(8,128)S(1)}) custom-call(bf16[4,384,384]{2,1,0:T(8,128)(2,1)S(1)} %bitcast.6, bf16[4,384,384]{2,1,0:T(8,128)(2,1)S(1)} %bitcast.8, f32[192,384]{1,0:T(8,128)S(1)} %shard_map.84.total, f32[192,384]{1,0:T(8,128)S(1)} %collective-permute-done.9.inner, ...), custom_call_target="tpu_custom_call" | custom-call | flops 169869312 | bytes 1048576 | tf_op jit(solution)/shard_map/pallas_call | solution.py:59
  30.6 0.0 copy-start.2
  30.6 0.1 collective-permute-start.11
  30.7 1.8 %collective-permute-start.12 = (f32[48,384]{1,0:T(8,128)S(1)}, f32[48,384]{1,0:T(8,128)S(1)}, u32[]{:S(2)}, u32[]{:S(2)}) collective-permute-start(f32[48,384]{1,0:T(8,128)S(1)} %get-tuple-element.49), channel_id=1, source_target_pairs={{0,4},{4,0},{8,12},{12,8},{16,20},{20,16},{24,28},{28,24},{1,5},{5... | collective-permute-start | bytes 221192 | tf_op jit(solution)/shard_map/ppermute | solution.py:283
  32.5 0.0 copy-done.1
  32.5 0.5 shard_map.87.partial
  32.9 2.9 %collective-permute-done.11.far = f32[48,384]{1,0:T(8,128)S(1)} collective-permute-done((f32[48,384]{1,0:T(8,128)S(1)}, f32[48,384]{1,0:T(8,128)S(1)}, u32[]{:S(2)}, u32[]{:S(2)}) %collective-permute-start.11) | collective-permute-done | bytes 73760 | tf_op jit(solution)/shard_map/ppermute | solution.py:284
  35.9 0.0 collective-permute-done.12.near
  35.9 0.0 copy-done.2
  35.9 0.3 shard_map.88
  36.2 0.1 collective-permute-start.13
  36.3 0.3 collective-permute-start.14
  36.6 4.8 %collective-permute-done.13.from_far = f32[48,384]{1,0:T(8,128)S(1)} collective-permute-done((f32[48,384]{1,0:T(8,128)S(1)}, f32[48,384]{1,0:T(8,128)S(1)}, u32[]{:S(2)}, u32[]{:S(2)}) %collective-permute-start.13) | collective-permute-done | bytes 73760 | tf_op jit(solution)/shard_map/ppermute | solution.py:284
  41.4 0.0 collective-permute-done.14.from_near
  41.4 0.5 shard_map.89
  41.9 0.1 collective-permute-start.15
  42.0 0.1 collective-permute-start.16
  42.1 0.5 shard_map.90.partial
  42.5 4.1 %collective-permute-done.15.far = f32[48,384]{1,0:T(8,128)S(1)} collective-permute-done((f32[48,384]{1,0:T(8,128)S(1)}, f32[48,384]{1,0:T(8,128)S(1)}, u32[]{:S(2)}, u32[]{:S(2)}) %collective-permute-start.15) | collective-permute-done | bytes 73760 | tf_op jit(solution)/shard_map/ppermute | solution.py:284
  46.6 0.0 collective-permute-done.16.near
  46.6 0.3 shard_map.91
  47.0 0.1 collective-permute-start.17
  47.1 0.1 collective-permute-start.18
  47.1 4.6 %collective-permute-done.17.from_far = f32[48,384]{1,0:T(8,128)S(1)} collective-permute-done((f32[48,384]{1,0:T(8,128)S(1)}, f32[48,384]{1,0:T(8,128)S(1)}, u32[]{:S(2)}, u32[]{:S(2)}) %collective-permute-start.17) | collective-permute-done | bytes 73760 | tf_op jit(solution)/shard_map/ppermute | solution.py:284
  51.7 0.0 collective-permute-done.18.from_near
  51.7 1.0 %shard_map.92 = f32[192,384]{1,0:T(8,128)} custom-call(f32[48,384]{1,0:T(8,128)S(1)} %collective-permute-done.17.from_far, f32[192,384]{1,0:T(8,128)S(1)} %get-tuple-element.59.base, f32[48,384]{1,0:T(8,128)S(1)} %collective-permute-done.18.from_near, f32[192,128]{1,0:T(8,128)S(1)} %get-tuple-element.44.column, bf16[192,288]{1,0:T(8,128)(2,1)S(1)} %get-tuple-element.54.put), custom_call_target="tpu_custom_call" | custom-call | flops 42467328 | bytes 1048576 | tf_op jit(solution)/shard_map/pallas_call | solution.py:59
  (2 shorter events, 0.0 us)
Async XLA Ops:
  0.0 1.3 %copy-start = (f32[192,1536]{1,0:T(8,128)S(1)}, f32[192,1536]{1,0:T(8,128)}, u32[]{:S(2)}) copy-start(f32[192,1536]{1,0:T(8,128)} %param.15) | copy-start | bytes 3538948
  1.3 22.2 %copy-start.3 = (f32[192,384]{1,0:T(8,128)S(1)}, f32[192,384]{1,0:T(8,128)}, u32[]{:S(2)}) copy-start(f32[192,384]{1,0:T(8,128)} %own) | copy-start | bytes 884740
  1.3 22.9 %copy-start.4 = (f32[192]{0:T(256)S(1)}, f32[192]{0:T(256)}, u32[]{:S(2)}) copy-start(f32[192]{0:T(256)} %param.9) | copy-start | bytes 2308
  1.3 22.9 %copy-start.6 = (s32[48]{0:T(128)S(1)}, s32[48]{0:T(128)}, u32[]{:S(2)}) copy-start(s32[48]{0:T(128)} %param.12) | copy-start | bytes 580
  1.3 22.9 %copy-start.7 = (s32[48]{0:T(128)S(1)}, s32[48]{0:T(128)}, u32[]{:S(2)}) copy-start(s32[48]{0:T(128)} %param.13) | copy-start | bytes 580
  1.3 23.1 %copy-start.5 = (s32[8]{0:T(128)S(1)}, s32[8]{0:T(128)}, u32[]{:S(2)}) copy-start(s32[8]{0:T(128)} %owner.1) | copy-start | bytes 100
  1.4 15.0 %collective-permute-start = (f32[192,384]{1,0:T(8,128)S(1)}, f32[192,384]{1,0:T(8,128)S(1)}, u32[]{:S(2)}, u32[]{:S(2)}) collective-permute-start(f32[192,384]{1,0:T(8,128)S(1)} %constant_dynamic-slice_fusion.refs_0_), channel_id=1, source_target_pairs={{0,8},{4,12},{8,0},{12,4},{16,24},{20,28},{24,16},{28,20},{1,9},{5... | collective-permute-start | bytes 884744 | tf_op jit(solution)/shard_map/ppermute | solution.py:305
  4.4 14.8 %collective-permute-start.1 = (f32[192,384]{1,0:T(8,128)S(1)}, f32[192,384]{1,0:T(8,128)S(1)}, u32[]{:S(2)}, u32[]{:S(2)}) collective-permute-start(f32[192,384]{1,0:T(8,128)S(1)} %constant_dynamic-slice_fusion.refs_0_), channel_id=1, source_target_pairs={{0,16},{4,20},{8,24},{12,28},{16,0},{20,4},{24,8},{28,12},{1,17},{... | collective-permute-start | bytes 884744 | tf_op jit(solution)/shard_map/ppermute | solution.py:305
  5.9 13.3 %collective-permute-start.2 = (f32[192,384]{1,0:T(8,128)S(1)}, f32[192,384]{1,0:T(8,128)S(1)}, u32[]{:S(2)}, u32[]{:S(2)}) collective-permute-start(f32[192,384]{1,0:T(8,128)S(1)} %constant_dynamic-slice_fusion.refs_0_), channel_id=1, source_target_pairs={{0,24},{4,28},{8,16},{12,20},{16,8},{20,12},{24,0},{28,4},{1,25},{... | collective-permute-start | bytes 884744 | tf_op jit(solution)/shard_map/ppermute | solution.py:305
  5.9 14.6 %collective-permute-start.7 = (f32[192,384]{1,0:T(8,128)}, f32[192,384]{1,0:T(8,128)S(1)}, u32[]{:S(2)}, u32[]{:S(2)}) collective-permute-start(f32[192,384]{1,0:T(8,128)} %own), channel_id=1, source_target_pairs={{0,1},{1,0},{2,3},{3,2},{4,5},{5,4},{6,7},{7,6},{8,9},{9,8},{10,11... | collective-permute-start | bytes 884744 | tf_op jit(solution)/shard_map/ppermute | solution.py:300
  7.9 15.1 %collective-permute-start.8 = (f32[192,384]{1,0:T(8,128)}, f32[192,384]{1,0:T(8,128)S(1)}, u32[]{:S(2)}, u32[]{:S(2)}) collective-permute-start(f32[192,384]{1,0:T(8,128)} %own), channel_id=1, source_target_pairs={{0,2},{1,3},{2,0},{3,1},{4,6},{5,7},{6,4},{7,5},{8,10},{9,11},{10,... | collective-permute-start | bytes 884744 | tf_op jit(solution)/shard_map/ppermute | solution.py:301
  19.2 4.3 %collective-permute-start.3 = (f32[192,384]{1,0:T(8,128)S(1)}, f32[192,384]{1,0:T(8,128)S(1)}, u32[]{:S(2)}, u32[]{:S(2)}) collective-permute-start(f32[192,384]{1,0:T(8,128)S(1)} %constant_dynamic-slice_fusion.refs_0_), channel_id=1, source_target_pairs={{0,4},{4,0},{8,12},{12,8},{16,20},{20,16},{24,28},{28,24},{1,5},{5... | collective-permute-start | bytes 884744 | tf_op jit(solution)/shard_map/ppermute | solution.py:311
  19.2 5.3 %collective-permute-start.4 = (f32[192,384]{1,0:T(8,128)S(1)}, f32[192,384]{1,0:T(8,128)S(1)}, u32[]{:S(2)}, u32[]{:S(2)}) collective-permute-start(f32[192,384]{1,0:T(8,128)S(1)} %collective-permute-done.refs_2_), channel_id=1, source_target_pairs={{0,4},{4,0},{8,12},{12,8},{16,20},{20,16},{24,28},{28,24},{1,5},{5... | collective-permute-start | bytes 884744 | tf_op jit(solution)/shard_map/ppermute | solution.py:311
  19.7 4.8 %collective-permute-start.5 = (f32[192,384]{1,0:T(8,128)S(1)}, f32[192,384]{1,0:T(8,128)S(1)}, u32[]{:S(2)}, u32[]{:S(2)}) collective-permute-start(f32[192,384]{1,0:T(8,128)S(1)} %collective-permute-done.1.refs_4_), channel_id=1, source_target_pairs={{0,4},{4,0},{8,12},{12,8},{16,20},{20,16},{24,28},{28,24},{1,5},{5... | collective-permute-start | bytes 884744 | tf_op jit(solution)/shard_map/ppermute | solution.py:311
  20.5 3.9 %collective-permute-start.6 = (f32[192,384]{1,0:T(8,128)S(1)}, f32[192,384]{1,0:T(8,128)S(1)}, u32[]{:S(2)}, u32[]{:S(2)}) collective-permute-start(f32[192,384]{1,0:T(8,128)S(1)} %collective-permute-done.2.refs_6_), channel_id=1, source_target_pairs={{0,4},{4,0},{8,12},{12,8},{16,20},{20,16},{24,28},{28,24},{1,5},{5... | collective-permute-start | bytes 884744 | tf_op jit(solution)/shard_map/ppermute | solution.py:311
  23.1 6.9 %collective-permute-start.10 = (f32[192,384]{1,0:T(8,128)S(1)}, f32[192,384]{1,0:T(8,128)S(1)}, u32[]{:S(2)}, u32[]{:S(2)}) collective-permute-start(f32[192,384]{1,0:T(8,128)S(1)} %collective-permute-done.8.two), channel_id=1, source_target_pairs={{0,1},{1,0},{2,3},{3,2},{4,5},{5,4},{6,7},{7,6},{8,9},{9,8},{10,11... | collective-permute-start | bytes 884744 | tf_op jit(solution)/shard_map/ppermute | solution.py:309
  23.5 6.4 %collective-permute-start.9 = (f32[192,384]{1,0:T(8,128)S(1)}, f32[192,384]{1,0:T(8,128)S(1)}, u32[]{:S(2)}, u32[]{:S(2)}) collective-permute-start(f32[192,384]{1,0:T(8,128)S(1)} %copy-done.3), channel_id=1, source_target_pairs={{0,0},{1,2},{2,1},{3,3},{4,4},{5,6},{6,5},{7,7},{8,8},{9,10},{10,9... | collective-permute-start | bytes 884744 | tf_op jit(solution)/shard_map/ppermute | solution.py:308
  29.9 2.5 %copy-start.1 = (bf16[288,576]{1,0:T(8,128)(2,1)S(1)}, bf16[288,576]{1,0:T(8,128)(2,1)}, u32[]{:S(2)}) copy-start(bf16[288,576]{1,0:T(8,128)(2,1)} %get-tuple-element.48.ham) | copy-start | bytes 995332
  30.6 5.3 %copy-start.2 = (bf16[288,288]{1,0:T(8,128)(2,1)S(1)}, bf16[288,288]{1,0:T(8,128)(2,1)}, u32[]{:S(2)}) copy-start(bf16[288,288]{1,0:T(8,128)(2,1)} %get-tuple-element.50.ham) | copy-start | bytes 497668
  30.6 5.3 %collective-permute-start.11 = (f32[48,384]{1,0:T(8,128)S(1)}, f32[48,384]{1,0:T(8,128)S(1)}, u32[]{:S(2)}, u32[]{:S(2)}) collective-permute-start(f32[48,384]{1,0:T(8,128)S(1)} %get-tuple-element.46), channel_id=1, source_target_pairs={{0,28},{4,8},{8,4},{12,16},{16,12},{20,24},{24,20},{28,0},{1,29},{... | collective-permute-start | bytes 221192 | tf_op jit(solution)/shard_map/ppermute | solution.py:284
  30.7 5.2 %collective-permute-start.12 = (f32[48,384]{1,0:T(8,128)S(1)}, f32[48,384]{1,0:T(8,128)S(1)}, u32[]{:S(2)}, u32[]{:S(2)}) collective-permute-start(f32[48,384]{1,0:T(8,128)S(1)} %get-tuple-element.49), channel_id=1, source_target_pairs={{0,4},{4,0},{8,12},{12,8},{16,20},{20,16},{24,28},{28,24},{1,5},{5... | collective-permute-start | bytes 221192 | tf_op jit(solution)/shard_map/ppermute | solution.py:283
  36.2 5.2 %collective-permute-start.13 = (f32[48,384]{1,0:T(8,128)S(1)}, f32[48,384]{1,0:T(8,128)S(1)}, u32[]{:S(2)}, u32[]{:S(2)}) collective-permute-start(f32[48,384]{1,0:T(8,128)S(1)} %get-tuple-element.51), channel_id=1, source_target_pairs={{0,28},{4,8},{8,4},{12,16},{16,12},{20,24},{24,20},{28,0},{1,29},{... | collective-permute-start | bytes 221192 | tf_op jit(solution)/shard_map/ppermute | solution.py:284
  36.3 5.1 %collective-permute-start.14 = (f32[48,384]{1,0:T(8,128)S(1)}, f32[48,384]{1,0:T(8,128)S(1)}, u32[]{:S(2)}, u32[]{:S(2)}) collective-permute-start(f32[48,384]{1,0:T(8,128)S(1)} %get-tuple-element.53), channel_id=1, source_target_pairs={{0,4},{4,0},{8,12},{12,8},{16,20},{20,16},{24,28},{28,24},{1,5},{5... | collective-permute-start | bytes 221192 | tf_op jit(solution)/shard_map/ppermute | solution.py:283
  41.9 4.7 %collective-permute-start.15 = (f32[48,384]{1,0:T(8,128)S(1)}, f32[48,384]{1,0:T(8,128)S(1)}, u32[]{:S(2)}, u32[]{:S(2)}) collective-permute-start(f32[48,384]{1,0:T(8,128)S(1)} %get-tuple-element.55), channel_id=1, source_target_pairs={{0,28},{4,8},{8,4},{12,16},{16,12},{20,24},{24,20},{28,0},{1,29},{... | collective-permute-start | bytes 221192 | tf_op jit(solution)/shard_map/ppermute | solution.py:284
  42.0 4.7 %collective-permute-start.16 = (f32[48,384]{1,0:T(8,128)S(1)}, f32[48,384]{1,0:T(8,128)S(1)}, u32[]{:S(2)}, u32[]{:S(2)}) collective-permute-start(f32[48,384]{1,0:T(8,128)S(1)} %get-tuple-element.57), channel_id=1, source_target_pairs={{0,4},{4,0},{8,12},{12,8},{16,20},{20,16},{24,28},{28,24},{1,5},{5... | collective-permute-start | bytes 221192 | tf_op jit(solution)/shard_map/ppermute | solution.py:283
  47.0 4.7 %collective-permute-start.17 = (f32[48,384]{1,0:T(8,128)S(1)}, f32[48,384]{1,0:T(8,128)S(1)}, u32[]{:S(2)}, u32[]{:S(2)}) collective-permute-start(f32[48,384]{1,0:T(8,128)S(1)} %get-tuple-element.58), channel_id=1, source_target_pairs={{0,28},{4,8},{8,4},{12,16},{16,12},{20,24},{24,20},{28,0},{1,29},{... | collective-permute-start | bytes 221192 | tf_op jit(solution)/shard_map/ppermute | solution.py:284
  47.1 4.7 %collective-permute-start.18 = (f32[48,384]{1,0:T(8,128)S(1)}, f32[48,384]{1,0:T(8,128)S(1)}, u32[]{:S(2)}, u32[]{:S(2)}) collective-permute-start(f32[48,384]{1,0:T(8,128)S(1)} %get-tuple-element.60), channel_id=1, source_target_pairs={{0,4},{4,0},{8,12},{12,8},{16,20},{20,16},{24,28},{28,24},{1,5},{5... | collective-permute-start | bytes 221192 | tf_op jit(solution)/shard_map/ppermute | solution.py:283

commit v5 on v4

--- a/solution.py
+++ b/solution.py
@@ -62,7 +62,7 @@
         in_specs=specs,
         out_specs=jax.tree.map(lambda _: vmem, out_shape),
         compiler_params=pltpu.CompilerParams(vmem_limit_bytes=VMEM_LIMIT),
-        cost_estimate=pl.CostEstimate(flops=cost, bytes_accessed=1 << 20, transcendentals=0),
+        cost_estimate=pl.CostEstimate(flops=cost, bytes_accessed=min(cost, 1 << 20), transcendentals=0),
         **kwargs,
     )(*args)
 
@@ -71,7 +71,7 @@
     return jax.ShapeDtypeStruct(dims, dtype)
 
 
-def lists_kernel(m, up, dn, column, pick, put):
+def lists_kernel(m, up, dn, column, pick, put_near, put_far):
     owned = m.shape[1]
     column[...] = jnp.broadcast_to(as_column(m[...]), column.shape)
     even = lax.rem(lax.axis_index("dom"), 2) == 0
@@ -79,8 +79,8 @@
     near, far = jnp.where(even, up, dn), jnp.where(even, dn, up)
     rows = jnp.concatenate([pick_rows(near, owned), pick_rows(far, owned)], axis=0)
     pick[...] = jnp.concatenate([rows.astype(f32)] * 3, axis=1).astype(bf16)
-    lanes = [put_rows(near, owned).astype(f32), put_rows(far, owned).astype(f32)]
-    put[...] = jnp.concatenate(lanes * 3, axis=1).astype(bf16)
+    put_near[...] = jnp.concatenate([put_rows(near, owned).astype(f32)] * 3, axis=1).astype(bf16)
+    put_far[...] = jnp.concatenate([put_rows(far, owned).astype(f32)] * 3, axis=1).astype(bf16)
 
 
 def split_three(x):
@@ -88,11 +88,19 @@
     return hi, lo, (x - hi.astype(f32) - lo.astype(f32)).astype(bf16)
 
 
+def picked(x, pick):
+    return mm(pick, jnp.concatenate(split_three(x), axis=0))
+
+
 def send_rows(x, pick, near_out, far_out):
-    rows = mm(pick[...], jnp.concatenate(split_three(x), axis=0))
+    rows = picked(x, pick[...])
     ghost = near_out.shape[0]
     near_out[...] = rows[:ghost]
     far_out[...] = rows[ghost:]
+
+
+def placed(rows, put):
+    return mm(put[...], jnp.concatenate(split_three(rows[...]), axis=0))
 
 
 def cell_term(ham, row, ext):
@@ -173,7 +181,7 @@
 def add_halo(partial, near, far, ham, to_near, to_far):
     ghost = near.shape[0]
     owned = partial.shape[0] - 2 * ghost
-    hi, lo = split(jnp.concatenate([near[...], far[...]], axis=0))
+    hi, lo = split(jnp.concatenate([near, far], axis=0))
     z = partial[...] + mm(ham[...], jnp.concatenate([hi, hi, lo], axis=0))
     to_near[...] = z[owned : owned + ghost]
     to_far[...] = z[owned + ghost :]
@@ -181,32 +189,39 @@
 
 
 def first_kernel(far, partial, near, ham, column, s, base, to_near, to_far):
-    z = add_halo(partial, near, far, ham, to_near, to_far)
+    z = add_halo(partial, near[...], far[...], ham, to_near, to_far)
     base[...] = (sigma_one / filter_half) * (z * column[:, :1] - filter_center * s[...])
 
 
-def second_kernel(far, partial, near, ham, column, one, s, base, to_near, to_far):
-    z = add_halo(partial, near, far, ham, to_near, to_far)
+def near_sums_kernel(from_near, base, column, put_near, pick, out, to_far):
+    scale = column[:, :1]
+    rows = base[...] + (sigma_one / filter_half) * scale * placed(from_near, put_near)
+    out[...] = rows
+    wide = jnp.concatenate([rows * scale, column[...]], axis=1)
+    to_far[...] = picked(wide, pick[to_far.shape[0] :, :])
+
+
+def far_sums_kernel(from_far, base, column, put_far, pick, one, to_near):
+    scale = column[:, :1]
+    rows = base[...] + (sigma_one / filter_half) * scale * placed(from_far, put_far)
+    one[...] = rows
+    to_near[...] = picked(rows * scale, pick[: to_near.shape[0], :])
+
+
+def second_kernel(far, near, sent, partial, ham, column, one, s, base, to_near, to_far):
+    cols = sent.shape[1]
+    scale = far[:, cols : cols + 1]
+    whole = far[:, :cols] + (sigma_one / filter_half) * scale * scale * sent[...]
+    z = add_halo(partial, near[...], whole, ham, to_near, to_far)
     base[...] = (
         2.0 * sigma_two / filter_half * (z * column[:, :1] - filter_center * one[...])
         - sigma_one * sigma_two * s[...]
     )
 
 
-def collect(factor, base, from_near, from_far, column, put):
-    parts = zip(split_three(from_near[...]), split_three(from_far[...]))
-    rows = jnp.concatenate([part for pair in parts for part in pair], axis=0)
-    return base[...] + factor * column[:, :1] * mm(put[...], rows)
-
-
-def middle_kernel(from_far, base, from_near, column, put, pick, one, near_out, far_out):
-    filtered = collect(sigma_one / filter_half, base, from_near, from_far, column, put)
-    one[...] = filtered
-    send_rows(filtered * column[:, :1], pick, near_out, far_out)
-
-
-def last_kernel(from_far, base, from_near, column, put, two):
-    two[...] = collect(2.0 * sigma_two / filter_half, base, from_near, from_far, column, put)
+def last_kernel(from_far, base, from_near, column, put_near, put_far, two):
+    sums = placed(from_near, put_near) + placed(from_far, put_far)
+    two[...] = base[...] + 2.0 * sigma_two / filter_half * column[:, :1] * sums
 
 
 def order_kernel(owner, *refs):
@@ -279,19 +294,17 @@
     block = shape(owned, cols)
     small = 4 * ghost * owned * cols * 3
 
-    def exchange(to_near, to_far):
-        from_near = lax.ppermute(to_near, "dom", near_pairs)
-        from_far = lax.ppermute(to_far, "dom", far_pairs)
-        return from_near, from_far
+    def to_pair(rows):
+        return lax.ppermute(rows, "dom", near_pairs)
+
+    def to_other(rows):
+        return lax.ppermute(rows, "dom", far_pairs)
 
     ham_own, ham_halo = assemble(cell_nodes, cell_ham, ext, ghost)
-    column, pick, put = call(
+    put = shape(owned, 3 * ghost, dtype=bf16)
+    column, pick, put_near, put_far = call(
         lists_kernel,
-        (
-            shape(owned, 128),
-            shape(2 * ghost, 3 * owned, dtype=bf16),
-            shape(owned, 6 * ghost, dtype=bf16),
-        ),
+        (shape(owned, 128), shape(2 * ghost, 3 * owned, dtype=bf16), put, put),
         [m, up, dn],
         owned * owned,
     )
@@ -325,28 +338,32 @@
     )
     wide = shape(ext, cols)
     work = 6 * ext * ext * cols
-    near, far = exchange(to_near, to_far)
+    far, near = to_other(to_far), to_pair(to_near)
     partial = call(own_kernel, wide, [turned, column, ham_own], work)
-    base, to_near, to_far = call(
+    base, to_near, sent = call(
         first_kernel,
         (block, halo, halo),
         [far, partial, near, ham_halo, column, turned],
         work,
     )
-    near, far = exchange(to_near, to_far)
-    filtered, to_near, to_far = call(
-        middle_kernel, (block, halo, halo), [far, base, near, column, put, pick], small
-    )
-    near, far = exchange(to_near, to_far)
+    from_far, from_near = to_other(sent), to_pair(to_near)
+    base, to_far = call(
+        near_sums_kernel, (block, shape(ghost, cols + 128)), [from_near, base, column, put_near, pick], small
+    )
+    far = to_other(to_far)
+    filtered, to_near = call(
+        far_sums_kernel, (block, halo), [from_far, base, column, put_far, pick], 0
+    )
+    near = to_pair(to_near)
     partial = call(own_kernel, wide, [filtered, column, ham_own], work)
     base, to_near, to_far = call(
         second_kernel,
         (block, halo, halo),
-        [far, partial, near, ham_halo, column, filtered, turned],
+        [far, near, sent, partial, ham_halo, column, filtered, turned],
         work,
     )
-    near, far = exchange(to_near, to_far)
-    return call(last_kernel, block, [far, base, near, column, put], small)
+    far, near = to_other(to_far), to_pair(to_near)
+    return call(last_kernel, block, [far, base, near, column, put_near, put_far], small)
 
 
 def solution(mesh):

time: 53.7 us -> 51.3 us (0.955)
  waiting for transfers between devices: 26.2 us -> 20.9 us
  starting transfers between devices: 13.3 us -> 16.1 us
    ppermute x8, waiting for transfers between devices: 16.4 us -> 11.1 us  [the longest x4 10.4 us: to_other(): return lax.ppermute(rows, 'dom', far_pairs)]
    ppermute x8, starting transfers between devices: 2.53 us -> 5.29 us  [the longest x4 3.28 us: to_other(): return lax.ppermute(rows, 'dom', far_pairs)]
    pallas_call x10 -> x11, Pallas kernels: 5.79 us -> 6.18 us  [call(): pl.pallas_call(kernel, out_shape=out_shape, in_specs=specs, out_specs=jax...]
  transfers between devices with their start and end apart: 19 -> 19, of which waited for: 8 -> 9; matrix products, arithmetic and copies ran while one was open for 0% -> 0% of each run, Pallas kernels for 17% -> 19%
where the time goes in v5:
time: 51.3 us; the launch traced here: 50.5 us
  waiting for transfers between devices  20.9 us (41%)
  starting transfers between devices  16.1 us (31%)
  Pallas kernels  12 us (23%)
  local copies, waits for them, and re-layouts  1.34 us (3%)
    ppermute x4, waiting for transfers between devices, to_other(): return lax.ppermute(rows, 'dom', far_pairs)  10.4 us
    pallas_call x11, Pallas kernels, call(): pl.pallas_call(kernel, out_shape=out_shape, in_specs=specs, out_specs=jax...  6.18 us
    pallas_call x1, Pallas kernels, assemble(): pl.pallas_call(functools.partial(assemble_kernel, ghost), out_shape=(shap...  5.78 us
    ppermute x3, starting transfers between devices, shards(): lax.ppermute(own_columns, 'dom', flip(doms, b))  4.54 us
    ppermute x1, waiting for transfers between devices, shards(): outer = lax.ppermute(two, 'band', flip(4, 1))  3.56 us
    ppermute x4, starting transfers between devices, to_other(): return lax.ppermute(rows, 'dom', far_pairs)  3.28 us
    ppermute x3, waiting for transfers between devices, shards(): lax.ppermute(own_columns, 'dom', flip(doms, b))  2.83 us
    ppermute x1, starting transfers between devices, shards(): two = lax.ppermute(states, 'band', flip(4, 2))  2.59 us
  transfers between devices with their start and end apart: 19, of which 9 were waited for; matrix products, arithmetic and copies ran while one was open for 0% of the time, Pallas kernels for 19%

profile of v5, /device:TPU:0, one launch (start us, length us, event | category | flops | bytes accessed | tf_op | source)
XLA Modules:
  0.0 50.5 jit_solution(10211469442437391771)
XLA Ops:
  0.0 0.0 copy-start
  0.0 1.3 %copy-done = f32[192,1536]{1,0:T(8,128)S(1)} copy-done((f32[192,1536]{1,0:T(8,128)S(1)}, f32[192,1536]{1,0:T(8,128)}, u32[]{:S(2)}) %copy-start) | copy-done | bytes 1179672
  1.3 0.0 copy-start.3
  1.3 0.0 copy-start.4
  1.3 0.0 copy-start.6
  1.3 0.0 copy-start.7
  1.3 0.0 copy-start.5
  1.4 3.0 %collective-permute-start = (f32[192,384]{1,0:T(8,128)S(1)}, f32[192,384]{1,0:T(8,128)S(1)}, u32[]{:S(2)}, u32[]{:S(2)}) collective-permute-start(f32[192,384]{1,0:T(8,128)S(1)} %constant_dynamic-slice_fusion.refs_0_), channel_id=1, source_target_pairs={{0,8},{4,12},{8,0},{12,4},{16,24},{20,28},{24,16},{28,20},{1,9},{5... | collective-permute-start | bytes 884744 | tf_op jit(solution)/shard_map/ppermute | solution.py:318
  4.4 1.5 %collective-permute-start.1 = (f32[192,384]{1,0:T(8,128)S(1)}, f32[192,384]{1,0:T(8,128)S(1)}, u32[]{:S(2)}, u32[]{:S(2)}) collective-permute-start(f32[192,384]{1,0:T(8,128)S(1)} %constant_dynamic-slice_fusion.refs_0_), channel_id=1, source_target_pairs={{0,16},{4,20},{8,24},{12,28},{16,0},{20,4},{24,8},{28,12},{1,17},{... | collective-permute-start | bytes 884744 | tf_op jit(solution)/shard_map/ppermute | solution.py:318
  5.9 0.0 collective-permute-start.2
  5.9 2.0 %collective-permute-start.7 = (f32[192,384]{1,0:T(8,128)}, f32[192,384]{1,0:T(8,128)S(1)}, u32[]{:S(2)}, u32[]{:S(2)}) collective-permute-start(f32[192,384]{1,0:T(8,128)} %own), channel_id=1, source_target_pairs={{0,1},{1,0},{2,3},{3,2},{4,5},{5,4},{6,7},{7,6},{8,9},{9,8},{10,11... | collective-permute-start | bytes 884744 | tf_op jit(solution)/shard_map/ppermute | solution.py:313
  7.9 2.6 %collective-permute-start.8 = (f32[192,384]{1,0:T(8,128)}, f32[192,384]{1,0:T(8,128)S(1)}, u32[]{:S(2)}, u32[]{:S(2)}) collective-permute-start(f32[192,384]{1,0:T(8,128)} %own), channel_id=1, source_target_pairs={{0,2},{1,3},{2,0},{3,1},{4,6},{5,7},{6,4},{7,5},{8,10},{9,11},{10,... | collective-permute-start | bytes 884744 | tf_op jit(solution)/shard_map/ppermute | solution.py:314
  10.5 5.8 %shard_map.82 = (bf16[288,576]{1,0:T(8,128)(2,1)}, bf16[288,288]{1,0:T(8,128)(2,1)}) custom-call(s32[5,343]{1,0:T(8,128)} %nodes_any.1, f32[5,343,343]{2,1,0:T(8,128)} %ham_any.1), custom_call_target="tpu_custom_call" | custom-call | flops 1355316480 | bytes 2352980 | tf_op jit(solution)/shard_map/pallas_call | solution.py:154
  16.3 0.0 collective-permute-done.refs_2_
  16.3 2.8 %collective-permute-done.1.refs_4_ = f32[192,384]{1,0:T(8,128)S(1)} collective-permute-done((f32[192,384]{1,0:T(8,128)S(1)}, f32[192,384]{1,0:T(8,128)S(1)}, u32[]{:S(2)}, u32[]{:S(2)}) %collective-permute-start.1) | collective-permute-done | bytes 294944 | tf_op jit(solution)/shard_map/ppermute | solution.py:318
  19.2 0.0 collective-permute-done.2.refs_6_
  19.2 0.0 collective-permute-start.3
  19.2 0.5 %collective-permute-start.4 = (f32[192,384]{1,0:T(8,128)S(1)}, f32[192,384]{1,0:T(8,128)S(1)}, u32[]{:S(2)}, u32[]{:S(2)}) collective-permute-start(f32[192,384]{1,0:T(8,128)S(1)} %collective-permute-done.refs_2_), channel_id=1, source_target_pairs={{0,4},{4,0},{8,12},{12,8},{16,20},{20,16},{24,28},{28,24},{1,5},{5... | collective-permute-start | bytes 884744 | tf_op jit(solution)/shard_map/ppermute | solution.py:324
  19.7 0.0 collective-permute-start.5
  19.7 0.8 %collective-permute-done.7.one = f32[192,384]{1,0:T(8,128)S(1)} collective-permute-done((f32[192,384]{1,0:T(8,128)}, f32[192,384]{1,0:T(8,128)S(1)}, u32[]{:S(2)}, u32[]{:S(2)}) %collective-permute-start.7) | collective-permute-done | bytes 294944 | tf_op jit(solution)/shard_map/ppermute | solution.py:313
  20.5 0.0 collective-permute-start.6
  20.5 2.6 %collective-permute-done.8.two = f32[192,384]{1,0:T(8,128)S(1)} collective-permute-done((f32[192,384]{1,0:T(8,128)}, f32[192,384]{1,0:T(8,128)S(1)}, u32[]{:S(2)}, u32[]{:S(2)}) %collective-permute-start.8) | collective-permute-done | bytes 294944 | tf_op jit(solution)/shard_map/ppermute | solution.py:314
  23.1 0.4 collective-permute-start.10
  23.5 0.0 collective-permute-done.3.refs_1_
  23.5 0.0 copy-done.3
  23.5 0.7 %collective-permute-start.9 = (f32[192,384]{1,0:T(8,128)S(1)}, f32[192,384]{1,0:T(8,128)S(1)}, u32[]{:S(2)}, u32[]{:S(2)}) collective-permute-start(f32[192,384]{1,0:T(8,128)S(1)} %copy-done.3), channel_id=1, source_target_pairs={{0,0},{1,2},{2,1},{3,3},{4,4},{5,6},{6,5},{7,7},{8,8},{9,10},{10,9... | collective-permute-start | bytes 884744 | tf_op jit(solution)/shard_map/ppermute | solution.py:321
  24.2 0.0 copy-done.4
  24.2 0.0 copy-done.6
  24.2 0.0 copy-done.7
  24.2 0.2 shard_map.85
  24.4 0.0 collective-permute-done.4.refs_3_
  24.4 0.0 collective-permute-done.5.refs_5_
  24.4 0.0 collective-permute-done.6.refs_7_
  24.4 0.0 copy-done.5
  24.5 1.0 %shard_map.83 = (bf16[8,192,384]{2,1,0:T(8,128)(2,1)S(1)}, bf16[8,192,384]{2,1,0:T(8,128)(2,1)S(1)}) custom-call(s32[8]{0:T(128)S(1)} %copy-done.5, f32[192,384]{1,0:T(8,128)S(1)} %constant_dynamic-slice_fusion.refs_0_, f32[192,384]{1,0:T(8,128)S(1)} %collective-permute-done.3.refs_1_, f32[192,384]{1,0:T(8,128)S(1)} %collective-permute-done.refs_2_, ...), custom_call_target="tpu_custom_call" | custom-call | flops 9437184 | bytes 1048576 | tf_op jit(solution)/shard_map/pallas_call | solution.py:59
  25.4 0.9 %shard_map.84.total = f32[192,384]{1,0:T(8,128)S(1)} custom-call(bf16[4,384,384]{2,1,0:T(8,128)(2,1)S(1)} %bitcast.5, bf16[4,384,384]{2,1,0:T(8,128)(2,1)S(1)} %bitcast.7, f32[192,384]{1,0:T(8,128)S(1)} %copy-done.3, f32[192,384]{1,0:T(8,128)S(1)} %collective-permute-done.7.one, f32[192,384]{1,0:T(8,128)S(1)} %collective-permute-done.8.two), custom_call_target="tpu_custom_call" | custom-call | flops 509607936 | bytes 1048576 | tf_op jit(solution)/shard_map/pallas_call | solution.py:59
  26.4 3.6 %collective-permute-done.10.outer = f32[192,384]{1,0:T(8,128)S(1)} collective-permute-done((f32[192,384]{1,0:T(8,128)S(1)}, f32[192,384]{1,0:T(8,128)S(1)}, u32[]{:S(2)}, u32[]{:S(2)}) %collective-permute-start.10) | collective-permute-done | bytes 294944 | tf_op jit(solution)/shard_map/ppermute | solution.py:322
  29.9 0.0 collective-permute-done.9.inner
  29.9 0.7 %shard_map.86 = (f32[192,384]{1,0:T(8,128)S(1)}, f32[48,384]{1,0:T(8,128)S(1)}, f32[48,384]{1,0:T(8,128)S(1)}) custom-call(bf16[4,384,384]{2,1,0:T(8,128)(2,1)S(1)} %bitcast.6, bf16[4,384,384]{2,1,0:T(8,128)(2,1)S(1)} %bitcast.8, f32[192,384]{1,0:T(8,128)S(1)} %shard_map.84.total, f32[192,384]{1,0:T(8,128)S(1)} %collective-permute-done.9.inner, ...), custom_call_target="tpu_custom_call" | custom-call | flops 169869312 | bytes 1048576 | tf_op jit(solution)/shard_map/pallas_call | solution.py:59
  30.6 0.0 copy-start.2
  30.6 0.1 collective-permute-start.11
  30.7 1.8 %collective-permute-start.12 = (f32[48,384]{1,0:T(8,128)S(1)}, f32[48,384]{1,0:T(8,128)S(1)}, u32[]{:S(2)}, u32[]{:S(2)}) collective-permute-start(f32[48,384]{1,0:T(8,128)S(1)} %get-tuple-element.51), channel_id=1, source_target_pairs={{0,4},{4,0},{8,12},{12,8},{16,20},{20,16},{24,28},{28,24},{1,5},{5... | collective-permute-start | bytes 221192 | tf_op jit(solution)/shard_map/ppermute | solution.py:298
  32.5 0.0 copy-done.1
  32.5 0.5 shard_map.87.partial
  32.9 2.9 %collective-permute-done.11.far = f32[48,384]{1,0:T(8,128)S(1)} collective-permute-done((f32[48,384]{1,0:T(8,128)S(1)}, f32[48,384]{1,0:T(8,128)S(1)}, u32[]{:S(2)}, u32[]{:S(2)}) %collective-permute-start.11) | collective-permute-done | bytes 73760 | tf_op jit(solution)/shard_map/ppermute | solution.py:301
  35.9 0.0 collective-permute-done.12.near
  35.9 0.3 shard_map.88
  36.2 0.1 collective-permute-start.13
  36.3 1.3 %collective-permute-start.15 = (f32[48,384]{1,0:T(8,128)S(1)}, f32[48,384]{1,0:T(8,128)S(1)}, u32[]{:S(2)}, u32[]{:S(2)}) collective-permute-start(f32[48,384]{1,0:T(8,128)S(1)} %get-tuple-element.57.sent), channel_id=1, source_target_pairs={{0,28},{4,8},{8,4},{12,16},{16,12},{20,24},{24,20},{28,0},{1,29},{... | collective-permute-start | bytes 221192 | tf_op jit(solution)/shard_map/ppermute | solution.py:301
  37.6 0.0 collective-permute-done.13.from_near
  37.6 0.4 shard_map.89
  38.0 1.5 %collective-permute-start.14 = (f32[48,512]{1,0:T(8,128)S(1)}, f32[48,512]{1,0:T(8,128)S(1)}, u32[]{:S(2)}, u32[]{:S(2)}) collective-permute-start(f32[48,512]{1,0:T(8,128)S(1)} %get-tuple-element.56), channel_id=1, source_target_pairs={{0,28},{4,8},{8,4},{12,16},{16,12},{20,24},{24,20},{28,0},{1,29},{... | collective-permute-start | bytes 294920 | tf_op jit(solution)/shard_map/ppermute | solution.py:301
  39.5 2.0 %collective-permute-done.15.from_far = f32[48,384]{1,0:T(8,128)S(1)} collective-permute-done((f32[48,384]{1,0:T(8,128)S(1)}, f32[48,384]{1,0:T(8,128)S(1)}, u32[]{:S(2)}, u32[]{:S(2)}) %collective-permute-start.15) | collective-permute-done | bytes 73760 | tf_op jit(solution)/shard_map/ppermute | solution.py:301
  41.5 0.4 shard_map.90
  41.9 0.2 collective-permute-start.16
  42.1 0.5 shard_map.91.partial
  42.5 0.7 %collective-permute-done.16.near = f32[48,384]{1,0:T(8,128)S(1)} collective-permute-done((f32[48,384]{1,0:T(8,128)S(1)}, f32[48,384]{1,0:T(8,128)S(1)}, u32[]{:S(2)}, u32[]{:S(2)}) %collective-permute-start.16) | collective-permute-done | bytes 73760 | tf_op jit(solution)/shard_map/ppermute | solution.py:298
  43.2 0.8 %collective-permute-done.14.far = f32[48,512]{1,0:T(8,128)S(1)} collective-permute-done((f32[48,512]{1,0:T(8,128)S(1)}, f32[48,512]{1,0:T(8,128)S(1)}, u32[]{:S(2)}, u32[]{:S(2)}) %collective-permute-start.14) | collective-permute-done | bytes 98336 | tf_op jit(solution)/shard_map/ppermute | solution.py:301
  44.0 0.4 shard_map.92
  44.4 0.4 collective-permute-start.17
  44.9 0.0 collective-permute-start.18
  44.9 4.6 %collective-permute-done.17.from_far = f32[48,384]{1,0:T(8,128)S(1)} collective-permute-done((f32[48,384]{1,0:T(8,128)S(1)}, f32[48,384]{1,0:T(8,128)S(1)}, u32[]{:S(2)}, u32[]{:S(2)}) %collective-permute-start.17) | collective-permute-done | bytes 73760 | tf_op jit(solution)/shard_map/ppermute | solution.py:301
  49.5 0.0 collective-permute-done.18.from_near
  49.5 1.0 %shard_map.93 = f32[192,384]{1,0:T(8,128)} custom-call(f32[48,384]{1,0:T(8,128)S(1)} %collective-permute-done.17.from_far, f32[192,384]{1,0:T(8,128)S(1)} %get-tuple-element.63.base, f32[48,384]{1,0:T(8,128)S(1)} %collective-permute-done.18.from_near, f32[192,128]{1,0:T(8,128)S(1)} %get-tuple-element.46.column, ...), custom_call_target="tpu_custom_call" | custom-call | flops 42467328 | bytes 1048576 | tf_op jit(solution)/shard_map/pallas_call | solution.py:59
  (3 shorter events, 0.0 us)
Async XLA Ops:
  0.0 1.3 %copy-start = (f32[192,1536]{1,0:T(8,128)S(1)}, f32[192,1536]{1,0:T(8,128)}, u32[]{:S(2)}) copy-start(f32[192,1536]{1,0:T(8,128)} %param.15) | copy-start | bytes 3538948
  1.3 22.2 %copy-start.3 = (f32[192,384]{1,0:T(8,128)S(1)}, f32[192,384]{1,0:T(8,128)}, u32[]{:S(2)}) copy-start(f32[192,384]{1,0:T(8,128)} %own) | copy-start | bytes 884740
  1.3 22.9 %copy-start.4 = (f32[192]{0:T(256)S(1)}, f32[192]{0:T(256)}, u32[]{:S(2)}) copy-start(f32[192]{0:T(256)} %param.9) | copy-start | bytes 2308
  1.3 22.9 %copy-start.6 = (s32[48]{0:T(128)S(1)}, s32[48]{0:T(128)}, u32[]{:S(2)}) copy-start(s32[48]{0:T(128)} %param.12) | copy-start | bytes 580
  1.3 22.9 %copy-start.7 = (s32[48]{0:T(128)S(1)}, s32[48]{0:T(128)}, u32[]{:S(2)}) copy-start(s32[48]{0:T(128)} %param.13) | copy-start | bytes 580
  1.3 23.1 %copy-start.5 = (s32[8]{0:T(128)S(1)}, s32[8]{0:T(128)}, u32[]{:S(2)}) copy-start(s32[8]{0:T(128)} %owner.1) | copy-start | bytes 100
  1.4 15.0 %collective-permute-start = (f32[192,384]{1,0:T(8,128)S(1)}, f32[192,384]{1,0:T(8,128)S(1)}, u32[]{:S(2)}, u32[]{:S(2)}) collective-permute-start(f32[192,384]{1,0:T(8,128)S(1)} %constant_dynamic-slice_fusion.refs_0_), channel_id=1, source_target_pairs={{0,8},{4,12},{8,0},{12,4},{16,24},{20,28},{24,16},{28,20},{1,9},{5... | collective-permute-start | bytes 884744 | tf_op jit(solution)/shard_map/ppermute | solution.py:318
  4.4 14.8 %collective-permute-start.1 = (f32[192,384]{1,0:T(8,128)S(1)}, f32[192,384]{1,0:T(8,128)S(1)}, u32[]{:S(2)}, u32[]{:S(2)}) collective-permute-start(f32[192,384]{1,0:T(8,128)S(1)} %constant_dynamic-slice_fusion.refs_0_), channel_id=1, source_target_pairs={{0,16},{4,20},{8,24},{12,28},{16,0},{20,4},{24,8},{28,12},{1,17},{... | collective-permute-start | bytes 884744 | tf_op jit(solution)/shard_map/ppermute | solution.py:318
  5.9 13.3 %collective-permute-start.2 = (f32[192,384]{1,0:T(8,128)S(1)}, f32[192,384]{1,0:T(8,128)S(1)}, u32[]{:S(2)}, u32[]{:S(2)}) collective-permute-start(f32[192,384]{1,0:T(8,128)S(1)} %constant_dynamic-slice_fusion.refs_0_), channel_id=1, source_target_pairs={{0,24},{4,28},{8,16},{12,20},{16,8},{20,12},{24,0},{28,4},{1,25},{... | collective-permute-start | bytes 884744 | tf_op jit(solution)/shard_map/ppermute | solution.py:318
  5.9 14.6 %collective-permute-start.7 = (f32[192,384]{1,0:T(8,128)}, f32[192,384]{1,0:T(8,128)S(1)}, u32[]{:S(2)}, u32[]{:S(2)}) collective-permute-start(f32[192,384]{1,0:T(8,128)} %own), channel_id=1, source_target_pairs={{0,1},{1,0},{2,3},{3,2},{4,5},{5,4},{6,7},{7,6},{8,9},{9,8},{10,11... | collective-permute-start | bytes 884744 | tf_op jit(solution)/shard_map/ppermute | solution.py:313
  7.9 15.1 %collective-permute-start.8 = (f32[192,384]{1,0:T(8,128)}, f32[192,384]{1,0:T(8,128)S(1)}, u32[]{:S(2)}, u32[]{:S(2)}) collective-permute-start(f32[192,384]{1,0:T(8,128)} %own), channel_id=1, source_target_pairs={{0,2},{1,3},{2,0},{3,1},{4,6},{5,7},{6,4},{7,5},{8,10},{9,11},{10,... | collective-permute-start | bytes 884744 | tf_op jit(solution)/shard_map/ppermute | solution.py:314
  19.2 4.3 %collective-permute-start.3 = (f32[192,384]{1,0:T(8,128)S(1)}, f32[192,384]{1,0:T(8,128)S(1)}, u32[]{:S(2)}, u32[]{:S(2)}) collective-permute-start(f32[192,384]{1,0:T(8,128)S(1)} %constant_dynamic-slice_fusion.refs_0_), channel_id=1, source_target_pairs={{0,4},{4,0},{8,12},{12,8},{16,20},{20,16},{24,28},{28,24},{1,5},{5... | collective-permute-start | bytes 884744 | tf_op jit(solution)/shard_map/ppermute | solution.py:324
  19.2 5.3 %collective-permute-start.4 = (f32[192,384]{1,0:T(8,128)S(1)}, f32[192,384]{1,0:T(8,128)S(1)}, u32[]{:S(2)}, u32[]{:S(2)}) collective-permute-start(f32[192,384]{1,0:T(8,128)S(1)} %collective-permute-done.refs_2_), channel_id=1, source_target_pairs={{0,4},{4,0},{8,12},{12,8},{16,20},{20,16},{24,28},{28,24},{1,5},{5... | collective-permute-start | bytes 884744 | tf_op jit(solution)/shard_map/ppermute | solution.py:324
  19.7 4.8 %collective-permute-start.5 = (f32[192,384]{1,0:T(8,128)S(1)}, f32[192,384]{1,0:T(8,128)S(1)}, u32[]{:S(2)}, u32[]{:S(2)}) collective-permute-start(f32[192,384]{1,0:T(8,128)S(1)} %collective-permute-done.1.refs_4_), channel_id=1, source_target_pairs={{0,4},{4,0},{8,12},{12,8},{16,20},{20,16},{24,28},{28,24},{1,5},{5... | collective-permute-start | bytes 884744 | tf_op jit(solution)/shard_map/ppermute | solution.py:324
  20.5 3.9 %collective-permute-start.6 = (f32[192,384]{1,0:T(8,128)S(1)}, f32[192,384]{1,0:T(8,128)S(1)}, u32[]{:S(2)}, u32[]{:S(2)}) collective-permute-start(f32[192,384]{1,0:T(8,128)S(1)} %collective-permute-done.2.refs_6_), channel_id=1, source_target_pairs={{0,4},{4,0},{8,12},{12,8},{16,20},{20,16},{24,28},{28,24},{1,5},{5... | collective-permute-start | bytes 884744 | tf_op jit(solution)/shard_map/ppermute | solution.py:324
  23.1 6.9 %collective-permute-start.10 = (f32[192,384]{1,0:T(8,128)S(1)}, f32[192,384]{1,0:T(8,128)S(1)}, u32[]{:S(2)}, u32[]{:S(2)}) collective-permute-start(f32[192,384]{1,0:T(8,128)S(1)} %collective-permute-done.8.two), channel_id=1, source_target_pairs={{0,1},{1,0},{2,3},{3,2},{4,5},{5,4},{6,7},{7,6},{8,9},{9,8},{10,11... | collective-permute-start | bytes 884744 | tf_op jit(solution)/shard_map/ppermute | solution.py:322
  23.5 6.4 %collective-permute-start.9 = (f32[192,384]{1,0:T(8,128)S(1)}, f32[192,384]{1,0:T(8,128)S(1)}, u32[]{:S(2)}, u32[]{:S(2)}) collective-permute-start(f32[192,384]{1,0:T(8,128)S(1)} %copy-done.3), channel_id=1, source_target_pairs={{0,0},{1,2},{2,1},{3,3},{4,4},{5,6},{6,5},{7,7},{8,8},{9,10},{10,9... | collective-permute-start | bytes 884744 | tf_op jit(solution)/shard_map/ppermute | solution.py:321
  29.9 2.5 %copy-start.1 = (bf16[288,576]{1,0:T(8,128)(2,1)S(1)}, bf16[288,576]{1,0:T(8,128)(2,1)}, u32[]{:S(2)}) copy-start(bf16[288,576]{1,0:T(8,128)(2,1)} %get-tuple-element.50.ham) | copy-start | bytes 995332
  30.6 5.3 %copy-start.2 = (bf16[288,288]{1,0:T(8,128)(2,1)S(1)}, bf16[288,288]{1,0:T(8,128)(2,1)}, u32[]{:S(2)}) copy-start(bf16[288,288]{1,0:T(8,128)(2,1)} %get-tuple-element.52.ham) | copy-start | bytes 497668
  30.6 5.3 %collective-permute-start.11 = (f32[48,384]{1,0:T(8,128)S(1)}, f32[48,384]{1,0:T(8,128)S(1)}, u32[]{:S(2)}, u32[]{:S(2)}) collective-permute-start(f32[48,384]{1,0:T(8,128)S(1)} %get-tuple-element.48), channel_id=1, source_target_pairs={{0,28},{4,8},{8,4},{12,16},{16,12},{20,24},{24,20},{28,0},{1,29},{... | collective-permute-start | bytes 221192 | tf_op jit(solution)/shard_map/ppermute | solution.py:301
  30.7 5.2 %collective-permute-start.12 = (f32[48,384]{1,0:T(8,128)S(1)}, f32[48,384]{1,0:T(8,128)S(1)}, u32[]{:S(2)}, u32[]{:S(2)}) collective-permute-start(f32[48,384]{1,0:T(8,128)S(1)} %get-tuple-element.51), channel_id=1, source_target_pairs={{0,4},{4,0},{8,12},{12,8},{16,20},{20,16},{24,28},{28,24},{1,5},{5... | collective-permute-start | bytes 221192 | tf_op jit(solution)/shard_map/ppermute | solution.py:298
  36.2 1.4 %collective-permute-start.13 = (f32[48,384]{1,0:T(8,128)S(1)}, f32[48,384]{1,0:T(8,128)S(1)}, u32[]{:S(2)}, u32[]{:S(2)}) collective-permute-start(f32[48,384]{1,0:T(8,128)S(1)} %get-tuple-element.53), channel_id=1, source_target_pairs={{0,4},{4,0},{8,12},{12,8},{16,20},{20,16},{24,28},{28,24},{1,5},{5... | collective-permute-start | bytes 221192 | tf_op jit(solution)/shard_map/ppermute | solution.py:298
  36.3 5.2 %collective-permute-start.15 = (f32[48,384]{1,0:T(8,128)S(1)}, f32[48,384]{1,0:T(8,128)S(1)}, u32[]{:S(2)}, u32[]{:S(2)}) collective-permute-start(f32[48,384]{1,0:T(8,128)S(1)} %get-tuple-element.57.sent), channel_id=1, source_target_pairs={{0,28},{4,8},{8,4},{12,16},{16,12},{20,24},{24,20},{28,0},{1,29},{... | collective-permute-start | bytes 221192 | tf_op jit(solution)/shard_map/ppermute | solution.py:301
  38.0 6.0 %collective-permute-start.14 = (f32[48,512]{1,0:T(8,128)S(1)}, f32[48,512]{1,0:T(8,128)S(1)}, u32[]{:S(2)}, u32[]{:S(2)}) collective-permute-start(f32[48,512]{1,0:T(8,128)S(1)} %get-tuple-element.56), channel_id=1, source_target_pairs={{0,28},{4,8},{8,4},{12,16},{16,12},{20,24},{24,20},{28,0},{1,29},{... | collective-permute-start | bytes 294920 | tf_op jit(solution)/shard_map/ppermute | solution.py:301
  41.9 1.3 %collective-permute-start.16 = (f32[48,384]{1,0:T(8,128)S(1)}, f32[48,384]{1,0:T(8,128)S(1)}, u32[]{:S(2)}, u32[]{:S(2)}) collective-permute-start(f32[48,384]{1,0:T(8,128)S(1)} %get-tuple-element.60), channel_id=1, source_target_pairs={{0,4},{4,0},{8,12},{12,8},{16,20},{20,16},{24,28},{28,24},{1,5},{5... | collective-permute-start | bytes 221192 | tf_op jit(solution)/shard_map/ppermute | solution.py:298
  44.4 5.1 %collective-permute-start.17 = (f32[48,384]{1,0:T(8,128)S(1)}, f32[48,384]{1,0:T(8,128)S(1)}, u32[]{:S(2)}, u32[]{:S(2)}) collective-permute-start(f32[48,384]{1,0:T(8,128)S(1)} %get-tuple-element.62), channel_id=1, source_target_pairs={{0,28},{4,8},{8,4},{12,16},{16,12},{20,24},{24,20},{28,0},{1,29},{... | collective-permute-start | bytes 221192 | tf_op jit(solution)/shard_map/ppermute | solution.py:301
  44.9 4.6 %collective-permute-start.18 = (f32[48,384]{1,0:T(8,128)S(1)}, f32[48,384]{1,0:T(8,128)S(1)}, u32[]{:S(2)}, u32[]{:S(2)}) collective-permute-start(f32[48,384]{1,0:T(8,128)S(1)} %get-tuple-element.64), channel_id=1, source_target_pairs={{0,4},{4,0},{8,12},{12,8},{16,20},{20,16},{24,28},{28,24},{1,5},{5... | collective-permute-start | bytes 221192 | tf_op jit(solution)/shard_map/ppermute | solution.py:298

commit v6 on v5

--- a/solution.py
+++ b/solution.py
@@ -251,14 +251,18 @@
     return total
 
 
+def longer_kernel(block, out):
+    rows = block.shape[0]
+    out[:rows, :] = block[...]
+    out[rows:, :] = block[: out.shape[0] - rows, :]
+
+
 def rotate_kernel(hi_ref, lo_ref, own, one, two, out):
     out[...] = rotated_rows(hi_ref, lo_ref, [(0, own[...]), (1, one[...]), (2, two[...])])
 
 
-def rotate_last_kernel(hi_ref, lo_ref, total, inner, outer, column, pick, out, near_out, far_out):
-    here = lax.axis_index("band")
-    third = jnp.where((here == 1) | (here == 2), inner[...], outer[...])
-    rows = total[...] + rotated_rows(hi_ref, lo_ref, [(3, third)])
+def rotate_last_kernel(hi_ref, lo_ref, total, three, column, pick, out, near_out, far_out):
+    rows = total[...] + rotated_rows(hi_ref, lo_ref, [(3, three[: total.shape[0], :])])
     out[...] = rows
     send_rows(rows * column[:, :1], pick, near_out, far_out)
 
@@ -274,7 +278,7 @@
         order_kernel,
         (shape(len(slots), rows, cols, dtype=bf16),) * 2,
         [owner, *slots],
-        total * cols * 16,
+        0,
         scalars=(0,),
     )
     return hi.reshape(bands, total // bands, cols), lo.reshape(bands, total // bands, cols)
@@ -315,13 +319,17 @@
     paired = doms == 8 and rotation_store.shape[0] % 16 == 0
     parts = [own_columns]
     if paired:
-        parts += [lax.ppermute(own_columns, "dom", flip(doms, b)) for b in (2, 4, 6)]
+        parts += [lax.ppermute(own_columns, "dom", flip(doms, b)) for b in (2, 4)]
     ham_own, *parts = lax.optimization_barrier((ham_own, *parts))
-    held, one, two, ham_own = lax.optimization_barrier((states, one, two, ham_own))
-    inner = lax.ppermute(held, "band", [(0, 0), (1, 2), (2, 1), (3, 3)])
-    outer = lax.ppermute(two, "band", flip(4, 1))
     if paired:
-        other = [lax.ppermute(part, "dom", near_pairs) for part in parts]
+        parts.append(lax.ppermute(parts[1], "dom", flip(doms, 4)))
+        other = [lax.ppermute(part, "dom", near_pairs) for part in parts[:3]]
+    one, two, ham_own = lax.optimization_barrier((one, two, ham_own))
+    longer = call(longer_kernel, shape(owned + 8, cols), [two], 0)
+    three = lax.ppermute(longer, "band", flip(4, 1))
+    if paired:
+        two, parts[3] = lax.optimization_barrier((two, parts[3]))
+        other.append(lax.ppermute(parts[3], "dom", near_pairs))
         slots = [part for pair in zip(parts, other) for part in pair]
         rotation = ordered_rotation(slots, owner, bands)
     else:
@@ -329,11 +337,11 @@
         columns = columns.reshape(doms, -1, cols)[owner].reshape(bands, -1, cols)
         rotation = split(columns)
     work = 6 * owned * cols * cols
-    total = call(rotate_kernel, block, [*rotation, held, one, two], 3 * work)
+    total = call(rotate_kernel, block, [*rotation, states, one, two], 0)
     turned, to_near, to_far = call(
         rotate_last_kernel,
         (block, halo, halo),
-        [*rotation, total, inner, outer, column, pick],
+        [*rotation, total, three, column, pick],
         work,
     )
     wide = shape(ext, cols)

time: 51.3 us -> 49.3 us (0.961); the launches traced: 50.5 us -> 49.1 us
  starting transfers between devices: 16.1 us -> 14.8 us
    ppermute x1, waiting for transfers between devices: 0.83 us -> 4.05 us  [shards(): one = lax.ppermute(states, 'band', flip(4, 1))]
    ppermute x9 -> x8, waiting for transfers between devices: 6.4 us -> 3.36 us  [the longest x1 1.76 us: shards(): three = lax.ppermute(longer, 'band', flip(4, 1))]
    ppermute x4, starting transfers between devices: 2.01 us -> 0.79 us  [to_pair(): return lax.ppermute(rows, 'dom', near_pairs)]
    ppermute x4, waiting for transfers between devices: 10.4 us -> 9.73 us  [to_other(): return lax.ppermute(rows, 'dom', far_pairs)]
    ppermute x4, waiting for transfers between devices: 0.69 us -> 1.22 us  [to_pair(): return lax.ppermute(rows, 'dom', near_pairs)]
    ppermute x9 -> x8, starting transfers between devices: 6.16 us -> 6.5 us  [the longest x2 4.52 us: shards(): parts += [lax.ppermute(own_columns, 'dom', flip(doms, b)) for b in (2, 4)]]
    pallas_call x11 -> x12, Pallas kernels: 6.18 us -> 6.21 us  [call(): pl.pallas_call(kernel, out_shape=out_shape, in_specs=specs, out_specs=jax...]
  transfers between devices with their start and end apart: 19 -> 18, of which waited for: 9 -> 13; matrix products, arithmetic and copies ran while one was open for 0% -> 0% of each run, Pallas kernels for 19% -> 20%
where the time goes in v6:
time: 49.3 us; the launch traced here: 49.1 us
  waiting for transfers between devices  20.9 us (42%)
  starting transfers between devices  14.8 us (30%)
  Pallas kernels  12 us (24%)
  local copies, waits for them, and re-layouts  1.34 us (3%)
    ppermute x4, waiting for transfers between devices, to_other(): return lax.ppermute(rows, 'dom', far_pairs)  9.73 us
    pallas_call x12, Pallas kernels, call(): pl.pallas_call(kernel, out_shape=out_shape, in_specs=specs, out_specs=jax...  6.21 us
    pallas_call x1, Pallas kernels, assemble(): pl.pallas_call(functools.partial(assemble_kernel, ghost), out_shape=(shap...  5.78 us
    ppermute x2, starting transfers between devices, shards(): parts += [lax.ppermute(own_columns, 'dom', flip(doms, b)) for b in (2, 4)]  4.52 us
    ppermute x1, waiting for transfers between devices, shards(): one = lax.ppermute(states, 'band', flip(4, 1))  4.05 us
    ppermute x4, starting transfers between devices, to_other(): return lax.ppermute(rows, 'dom', far_pairs)  3.33 us
    ppermute x1, starting transfers between devices, shards(): two = lax.ppermute(states, 'band', flip(4, 2))  2.59 us
    ppermute x1, waiting for transfers between devices, shards(): two = lax.ppermute(states, 'band', flip(4, 2))  2.5 us
  transfers between devices with their start and end apart: 18, of which 13 were waited for; matrix products, arithmetic and copies ran while one was open for 0% of the time, Pallas kernels for 20%

profile of v6, /device:TPU:0, one launch (start us, length us, event | category | flops | bytes accessed | tf_op | source)
XLA Modules:
  0.0 49.1 jit_solution(645076336266697173)
XLA Ops:
  0.0 0.0 copy-start
  0.0 1.3 %copy-done = f32[192,1536]{1,0:T(8,128)S(1)} copy-done((f32[192,1536]{1,0:T(8,128)S(1)}, f32[192,1536]{1,0:T(8,128)}, u32[]{:S(2)}) %copy-start) | copy-done | bytes 1179672
  1.3 0.0 copy-start.4
  1.3 0.0 copy-start.6
  1.3 0.0 copy-start.7
  1.3 0.0 copy-start.5
  1.3 3.0 %collective-permute-start = (f32[192,384]{1,0:T(8,128)S(1)}, f32[192,384]{1,0:T(8,128)S(1)}, u32[]{:S(2)}, u32[]{:S(2)}) collective-permute-start(f32[192,384]{1,0:T(8,128)S(1)} %constant_dynamic-slice_fusion.refs_0_), channel_id=1, source_target_pairs={{0,8},{4,12},{8,0},{12,4},{16,24},{20,28},{24,16},{28,20},{1,9},{5... | collective-permute-start | bytes 884744 | tf_op jit(solution)/shard_map/ppermute | solution.py:322
  4.4 1.5 %collective-permute-start.1 = (f32[192,384]{1,0:T(8,128)S(1)}, f32[192,384]{1,0:T(8,128)S(1)}, u32[]{:S(2)}, u32[]{:S(2)}) collective-permute-start(f32[192,384]{1,0:T(8,128)S(1)} %constant_dynamic-slice_fusion.refs_0_), channel_id=1, source_target_pairs={{0,16},{4,20},{8,24},{12,28},{16,0},{20,4},{24,8},{28,12},{1,17},{... | collective-permute-start | bytes 884744 | tf_op jit(solution)/shard_map/ppermute | solution.py:322
  5.9 1.6 %collective-permute-start.5 = (f32[192,384]{1,0:T(8,128)}, f32[192,384]{1,0:T(8,128)S(1)}, u32[]{:S(2)}, u32[]{:S(2)}) collective-permute-start(f32[192,384]{1,0:T(8,128)} %own.1), channel_id=1, source_target_pairs={{0,1},{1,0},{2,3},{3,2},{4,5},{5,4},{6,7},{7,6},{8,9},{9,8},{10,11... | collective-permute-start | bytes 884744 | tf_op jit(solution)/shard_map/ppermute | solution.py:317
  7.5 2.6 %collective-permute-start.6 = (f32[192,384]{1,0:T(8,128)}, f32[192,384]{1,0:T(8,128)S(1)}, u32[]{:S(2)}, u32[]{:S(2)}) collective-permute-start(f32[192,384]{1,0:T(8,128)} %own.1), channel_id=1, source_target_pairs={{0,2},{1,3},{2,0},{3,1},{4,6},{5,7},{6,4},{7,5},{8,10},{9,11},{10,... | collective-permute-start | bytes 884744 | tf_op jit(solution)/shard_map/ppermute | solution.py:318
  10.0 5.8 %shard_map.82 = (bf16[288,576]{1,0:T(8,128)(2,1)}, bf16[288,288]{1,0:T(8,128)(2,1)}) custom-call(s32[5,343]{1,0:T(8,128)} %nodes_any.1, f32[5,343,343]{2,1,0:T(8,128)} %ham_any.1), custom_call_target="tpu_custom_call" | custom-call | flops 1355316480 | bytes 2352980 | tf_op jit(solution)/shard_map/pallas_call | solution.py:154
  15.8 0.0 collective-permute-done.refs_2_
  15.8 0.0 collective-permute-done.1.refs_4_
  15.8 0.6 %collective-permute-start.7 = (f32[192,384]{1,0:T(8,128)S(1)}, f32[192,384]{1,0:T(8,128)S(1)}, u32[]{:S(2)}, u32[]{:S(2)}) collective-permute-start(f32[192,384]{1,0:T(8,128)S(1)} %collective-permute-done.refs_2_), channel_id=1, source_target_pairs={{0,16},{4,20},{8,24},{12,28},{16,0},{20,4},{24,8},{28,12},{1,17},{... | collective-permute-start | bytes 884744 | tf_op jit(solution)/shard_map/ppermute | solution.py:325
  16.4 4.0 %collective-permute-done.5.one = f32[192,384]{1,0:T(8,128)S(1)} collective-permute-done((f32[192,384]{1,0:T(8,128)}, f32[192,384]{1,0:T(8,128)S(1)}, u32[]{:S(2)}, u32[]{:S(2)}) %collective-permute-start.5) | collective-permute-done | bytes 294944 | tf_op jit(solution)/shard_map/ppermute | solution.py:317
  20.5 2.5 %collective-permute-done.6.two.block = f32[192,384]{1,0:T(8,128)S(1)} collective-permute-done((f32[192,384]{1,0:T(8,128)}, f32[192,384]{1,0:T(8,128)S(1)}, u32[]{:S(2)}, u32[]{:S(2)}) %collective-permute-start.6) | collective-permute-done | bytes 294944 | tf_op jit(solution)/shard_map/ppermute | solution.py:318
  23.0 0.4 collective-permute-start.9
  23.4 0.0 collective-permute-start.3
  23.4 0.5 %collective-permute-start.2 = (f32[192,384]{1,0:T(8,128)S(1)}, f32[192,384]{1,0:T(8,128)S(1)}, u32[]{:S(2)}, u32[]{:S(2)}) collective-permute-start(f32[192,384]{1,0:T(8,128)S(1)} %constant_dynamic-slice_fusion.refs_0_), channel_id=1, source_target_pairs={{0,4},{4,0},{8,12},{12,8},{16,20},{20,16},{24,28},{28,24},{1,5},{5... | collective-permute-start | bytes 884744 | tf_op jit(solution)/shard_map/ppermute | solution.py:326
  23.9 0.0 collective-permute-start.4
  23.9 0.0 collective-permute-done.7.refs_6_
  23.9 0.5 %collective-permute-start.8 = (f32[192,384]{1,0:T(8,128)S(1)}, f32[192,384]{1,0:T(8,128)S(1)}, u32[]{:S(2)}, u32[]{:S(2)}) collective-permute-start(f32[192,384]{1,0:T(8,128)S(1)} %collective-permute-done.7.refs_6_), channel_id=1, source_target_pairs={{0,4},{4,0},{8,12},{12,8},{16,20},{20,16},{24,28},{28,24},{1,5},{5... | collective-permute-start | bytes 884744 | tf_op jit(solution)/shard_map/ppermute | solution.py:332
  24.4 0.0 copy-done.4
  24.4 0.0 copy-done.6
  24.4 0.0 copy-done.7
  24.4 0.2 shard_map.86
  24.6 0.0 copy-start.3
  24.6 0.3 collective-permute-done.3.refs_3_
  25.0 0.4 collective-permute-done.2.refs_1_
  25.4 0.4 collective-permute-done.4.refs_5_
  25.8 0.4 collective-permute-done.8.refs_7_
  26.2 0.0 copy-done.5
  26.2 1.0 %shard_map.83 = (bf16[8,192,384]{2,1,0:T(8,128)(2,1)S(1)}, bf16[8,192,384]{2,1,0:T(8,128)(2,1)S(1)}) custom-call(s32[8]{0:T(128)S(1)} %copy-done.5, f32[192,384]{1,0:T(8,128)S(1)} %constant_dynamic-slice_fusion.refs_0_, f32[192,384]{1,0:T(8,128)S(1)} %collective-permute-done.2.refs_1_, f32[192,384]{1,0:T(8,128)S(1)} %collective-permute-done.refs_2_, ...), custom_call_target="tpu_custom_call" | custom-call | tf_op jit(solution)/shard_map/pallas_call | solution.py:59
  27.2 0.0 copy-done.3
  27.2 0.9 %shard_map.84.total = f32[192,384]{1,0:T(8,128)S(1)} custom-call(bf16[4,384,384]{2,1,0:T(8,128)(2,1)S(1)} %bitcast.5, bf16[4,384,384]{2,1,0:T(8,128)(2,1)S(1)} %bitcast.7, f32[192,384]{1,0:T(8,128)S(1)} %copy-done.3, f32[192,384]{1,0:T(8,128)S(1)} %collective-permute-done.5.one, f32[192,384]{1,0:T(8,128)S(1)} %collective-permute-done.6.two.block), custom_call_target="tpu_custom_call" | custom-call | tf_op jit(solution)/shard_map/pallas_call | solution.py:59
  28.1 1.8 %collective-permute-done.9.three = f32[200,384]{1,0:T(8,128)S(1)} collective-permute-done((f32[200,384]{1,0:T(8,128)S(1)}, f32[200,384]{1,0:T(8,128)S(1)}, u32[]{:S(2)}, u32[]{:S(2)}) %collective-permute-start.9) | collective-permute-done | bytes 307232 | tf_op jit(solution)/shard_map/ppermute | solution.py:329
  29.9 0.0 copy-start.1
  29.9 0.7 %shard_map.87 = (f32[192,384]{1,0:T(8,128)S(1)}, f32[48,384]{1,0:T(8,128)S(1)}, f32[48,384]{1,0:T(8,128)S(1)}) custom-call(bf16[4,384,384]{2,1,0:T(8,128)(2,1)S(1)} %bitcast.6, bf16[4,384,384]{2,1,0:T(8,128)(2,1)S(1)} %bitcast.8, f32[192,384]{1,0:T(8,128)S(1)} %shard_map.84.total, f32[200,384]{1,0:T(8,128)S(1)} %collective-permute-done.9.three, ...), custom_call_target="tpu_custom_call" | custom-call | flops 169869312 | bytes 1048576 | tf_op jit(solution)/shard_map/pallas_call | solution.py:59
  30.6 0.0 copy-start.2
  30.6 0.1 collective-permute-start.10
  30.7 0.6 %collective-permute-start.11 = (f32[48,384]{1,0:T(8,128)S(1)}, f32[48,384]{1,0:T(8,128)S(1)}, u32[]{:S(2)}, u32[]{:S(2)}) collective-permute-start(f32[48,384]{1,0:T(8,128)S(1)} %get-tuple-element.51), channel_id=1, source_target_pairs={{0,4},{4,0},{8,12},{12,8},{16,20},{20,16},{24,28},{28,24},{1,5},{5... | collective-permute-start | bytes 221192 | tf_op jit(solution)/shard_map/ppermute | solution.py:302
  31.3 0.0 copy-done.1
  31.3 0.5 shard_map.88.partial
  31.8 3.5 %collective-permute-done.10.far = f32[48,384]{1,0:T(8,128)S(1)} collective-permute-done((f32[48,384]{1,0:T(8,128)S(1)}, f32[48,384]{1,0:T(8,128)S(1)}, u32[]{:S(2)}, u32[]{:S(2)}) %collective-permute-start.10) | collective-permute-done | bytes 73760 | tf_op jit(solution)/shard_map/ppermute | solution.py:305
  35.3 0.0 collective-permute-done.11.near
  35.3 0.0 copy-done.2
  35.3 0.3 shard_map.89
  35.6 0.1 collective-permute-start.12
  35.7 0.8 %collective-permute-start.14 = (f32[48,384]{1,0:T(8,128)S(1)}, f32[48,384]{1,0:T(8,128)S(1)}, u32[]{:S(2)}, u32[]{:S(2)}) collective-permute-start(f32[48,384]{1,0:T(8,128)S(1)} %get-tuple-element.57.sent), channel_id=1, source_target_pairs={{0,28},{4,8},{8,4},{12,16},{16,12},{20,24},{24,20},{28,0},{1,29},{... | collective-permute-start | bytes 221192 | tf_op jit(solution)/shard_map/ppermute | solution.py:305
  36.5 0.4 collective-permute-done.12.from_near
  37.0 0.4 shard_map.90
  37.4 1.5 %collective-permute-start.13 = (f32[48,512]{1,0:T(8,128)S(1)}, f32[48,512]{1,0:T(8,128)S(1)}, u32[]{:S(2)}, u32[]{:S(2)}) collective-permute-start(f32[48,512]{1,0:T(8,128)S(1)} %get-tuple-element.56), channel_id=1, source_target_pairs={{0,28},{4,8},{8,4},{12,16},{16,12},{20,24},{24,20},{28,0},{1,29},{... | collective-permute-start | bytes 294920 | tf_op jit(solution)/shard_map/ppermute | solution.py:305
  38.9 2.2 %collective-permute-done.14.from_far = f32[48,384]{1,0:T(8,128)S(1)} collective-permute-done((f32[48,384]{1,0:T(8,128)S(1)}, f32[48,384]{1,0:T(8,128)S(1)}, u32[]{:S(2)}, u32[]{:S(2)}) %collective-permute-start.14) | collective-permute-done | bytes 73760 | tf_op jit(solution)/shard_map/ppermute | solution.py:305
  41.1 0.4 shard_map.91
  41.5 0.1 collective-permute-start.15
  41.6 0.5 shard_map.92.partial
  42.0 0.8 %collective-permute-done.15.near = f32[48,384]{1,0:T(8,128)S(1)} collective-permute-done((f32[48,384]{1,0:T(8,128)S(1)}, f32[48,384]{1,0:T(8,128)S(1)}, u32[]{:S(2)}, u32[]{:S(2)}) %collective-permute-start.15) | collective-permute-done | bytes 73760 | tf_op jit(solution)/shard_map/ppermute | solution.py:302
  42.8 0.2 collective-permute-done.13.far
  43.0 0.4 shard_map.93
  43.4 0.9 %collective-permute-start.16 = (f32[48,384]{1,0:T(8,128)S(1)}, f32[48,384]{1,0:T(8,128)S(1)}, u32[]{:S(2)}, u32[]{:S(2)}) collective-permute-start(f32[48,384]{1,0:T(8,128)S(1)} %get-tuple-element.62), channel_id=1, source_target_pairs={{0,28},{4,8},{8,4},{12,16},{16,12},{20,24},{24,20},{28,0},{1,29},{... | collective-permute-start | bytes 221192 | tf_op jit(solution)/shard_map/ppermute | solution.py:305
  44.3 0.0 collective-permute-start.17
  44.3 3.8 %collective-permute-done.16.from_far = f32[48,384]{1,0:T(8,128)S(1)} collective-permute-done((f32[48,384]{1,0:T(8,128)S(1)}, f32[48,384]{1,0:T(8,128)S(1)}, u32[]{:S(2)}, u32[]{:S(2)}) %collective-permute-start.16) | collective-permute-done | bytes 73760 | tf_op jit(solution)/shard_map/ppermute | solution.py:305
  48.2 0.0 collective-permute-done.17.from_near
  48.2 1.0 %shard_map.94 = f32[192,384]{1,0:T(8,128)} custom-call(f32[48,384]{1,0:T(8,128)S(1)} %collective-permute-done.16.from_far, f32[192,384]{1,0:T(8,128)S(1)} %get-tuple-element.63.base, f32[48,384]{1,0:T(8,128)S(1)} %collective-permute-done.17.from_near, f32[192,128]{1,0:T(8,128)S(1)} %get-tuple-element.46.column, ...), custom_call_target="tpu_custom_call" | custom-call | flops 42467328 | bytes 1048576 | tf_op jit(solution)/shard_map/pallas_call | solution.py:59
  (2 shorter events, 0.0 us)
Async XLA Ops:
  0.0 1.3 %copy-start = (f32[192,1536]{1,0:T(8,128)S(1)}, f32[192,1536]{1,0:T(8,128)}, u32[]{:S(2)}) copy-start(f32[192,1536]{1,0:T(8,128)} %param.15) | copy-start | bytes 3538948
  1.3 23.1 %copy-start.4 = (f32[192]{0:T(256)S(1)}, f32[192]{0:T(256)}, u32[]{:S(2)}) copy-start(f32[192]{0:T(256)} %param.9) | copy-start | bytes 2308
  1.3 23.1 %copy-start.6 = (s32[48]{0:T(128)S(1)}, s32[48]{0:T(128)}, u32[]{:S(2)}) copy-start(s32[48]{0:T(128)} %param.12) | copy-start | bytes 580
  1.3 23.1 %copy-start.7 = (s32[48]{0:T(128)S(1)}, s32[48]{0:T(128)}, u32[]{:S(2)}) copy-start(s32[48]{0:T(128)} %param.13) | copy-start | bytes 580
  1.3 24.9 %copy-start.5 = (s32[8]{0:T(128)S(1)}, s32[8]{0:T(128)}, u32[]{:S(2)}) copy-start(s32[8]{0:T(128)} %owner.1) | copy-start | bytes 100
  1.3 14.5 %collective-permute-start = (f32[192,384]{1,0:T(8,128)S(1)}, f32[192,384]{1,0:T(8,128)S(1)}, u32[]{:S(2)}, u32[]{:S(2)}) collective-permute-start(f32[192,384]{1,0:T(8,128)S(1)} %constant_dynamic-slice_fusion.refs_0_), channel_id=1, source_target_pairs={{0,8},{4,12},{8,0},{12,4},{16,24},{20,28},{24,16},{28,20},{1,9},{5... | collective-permute-start | bytes 884744 | tf_op jit(solution)/shard_map/ppermute | solution.py:322
  4.4 11.5 %collective-permute-start.1 = (f32[192,384]{1,0:T(8,128)S(1)}, f32[192,384]{1,0:T(8,128)S(1)}, u32[]{:S(2)}, u32[]{:S(2)}) collective-permute-start(f32[192,384]{1,0:T(8,128)S(1)} %constant_dynamic-slice_fusion.refs_0_), channel_id=1, source_target_pairs={{0,16},{4,20},{8,24},{12,28},{16,0},{20,4},{24,8},{28,12},{1,17},{... | collective-permute-start | bytes 884744 | tf_op jit(solution)/shard_map/ppermute | solution.py:322
  5.9 14.6 %collective-permute-start.5 = (f32[192,384]{1,0:T(8,128)}, f32[192,384]{1,0:T(8,128)S(1)}, u32[]{:S(2)}, u32[]{:S(2)}) collective-permute-start(f32[192,384]{1,0:T(8,128)} %own.1), channel_id=1, source_target_pairs={{0,1},{1,0},{2,3},{3,2},{4,5},{5,4},{6,7},{7,6},{8,9},{9,8},{10,11... | collective-permute-start | bytes 884744 | tf_op jit(solution)/shard_map/ppermute | solution.py:317
  7.5 15.5 %collective-permute-start.6 = (f32[192,384]{1,0:T(8,128)}, f32[192,384]{1,0:T(8,128)S(1)}, u32[]{:S(2)}, u32[]{:S(2)}) collective-permute-start(f32[192,384]{1,0:T(8,128)} %own.1), channel_id=1, source_target_pairs={{0,2},{1,3},{2,0},{3,1},{4,6},{5,7},{6,4},{7,5},{8,10},{9,11},{10,... | collective-permute-start | bytes 884744 | tf_op jit(solution)/shard_map/ppermute | solution.py:318
  15.8 8.0 %collective-permute-start.7 = (f32[192,384]{1,0:T(8,128)S(1)}, f32[192,384]{1,0:T(8,128)S(1)}, u32[]{:S(2)}, u32[]{:S(2)}) collective-permute-start(f32[192,384]{1,0:T(8,128)S(1)} %collective-permute-done.refs_2_), channel_id=1, source_target_pairs={{0,16},{4,20},{8,24},{12,28},{16,0},{20,4},{24,8},{28,12},{1,17},{... | collective-permute-start | bytes 884744 | tf_op jit(solution)/shard_map/ppermute | solution.py:325
  23.0 6.9 %collective-permute-start.9 = (f32[200,384]{1,0:T(8,128)S(1)}, f32[200,384]{1,0:T(8,128)S(1)}, u32[]{:S(2)}, u32[]{:S(2)}) collective-permute-start(f32[200,384]{1,0:T(8,128)S(1)} %shard_map.85), channel_id=1, source_target_pairs={{0,1},{1,0},{2,3},{3,2},{4,5},{5,4},{6,7},{7,6},{8,9},{9,8},{10,11... | collective-permute-start | bytes 921608 | tf_op jit(solution)/shard_map/ppermute | solution.py:329
  23.4 1.6 %collective-permute-start.3 = (f32[192,384]{1,0:T(8,128)S(1)}, f32[192,384]{1,0:T(8,128)S(1)}, u32[]{:S(2)}, u32[]{:S(2)}) collective-permute-start(f32[192,384]{1,0:T(8,128)S(1)} %collective-permute-done.refs_2_), channel_id=1, source_target_pairs={{0,4},{4,0},{8,12},{12,8},{16,20},{20,16},{24,28},{28,24},{1,5},{5... | collective-permute-start | bytes 884744 | tf_op jit(solution)/shard_map/ppermute | solution.py:326
  23.4 2.0 %collective-permute-start.2 = (f32[192,384]{1,0:T(8,128)S(1)}, f32[192,384]{1,0:T(8,128)S(1)}, u32[]{:S(2)}, u32[]{:S(2)}) collective-permute-start(f32[192,384]{1,0:T(8,128)S(1)} %constant_dynamic-slice_fusion.refs_0_), channel_id=1, source_target_pairs={{0,4},{4,0},{8,12},{12,8},{16,20},{20,16},{24,28},{28,24},{1,5},{5... | collective-permute-start | bytes 884744 | tf_op jit(solution)/shard_map/ppermute | solution.py:326
  23.9 1.9 %collective-permute-start.4 = (f32[192,384]{1,0:T(8,128)S(1)}, f32[192,384]{1,0:T(8,128)S(1)}, u32[]{:S(2)}, u32[]{:S(2)}) collective-permute-start(f32[192,384]{1,0:T(8,128)S(1)} %collective-permute-done.1.refs_4_), channel_id=1, source_target_pairs={{0,4},{4,0},{8,12},{12,8},{16,20},{20,16},{24,28},{28,24},{1,5},{5... | collective-permute-start | bytes 884744 | tf_op jit(solution)/shard_map/ppermute | solution.py:326
  23.9 2.3 %collective-permute-start.8 = (f32[192,384]{1,0:T(8,128)S(1)}, f32[192,384]{1,0:T(8,128)S(1)}, u32[]{:S(2)}, u32[]{:S(2)}) collective-permute-start(f32[192,384]{1,0:T(8,128)S(1)} %collective-permute-done.7.refs_6_), channel_id=1, source_target_pairs={{0,4},{4,0},{8,12},{12,8},{16,20},{20,16},{24,28},{28,24},{1,5},{5... | collective-permute-start | bytes 884744 | tf_op jit(solution)/shard_map/ppermute | solution.py:332
  24.6 2.6 %copy-start.3 = (f32[192,384]{1,0:T(8,128)S(1)}, f32[192,384]{1,0:T(8,128)}, u32[]{:S(2)}) copy-start(f32[192,384]{1,0:T(8,128)} %own.1) | copy-start | bytes 884740
  29.9 1.4 %copy-start.1 = (bf16[288,576]{1,0:T(8,128)(2,1)S(1)}, bf16[288,576]{1,0:T(8,128)(2,1)}, u32[]{:S(2)}) copy-start(bf16[288,576]{1,0:T(8,128)(2,1)} %get-tuple-element.50.ham) | copy-start | bytes 995332
  30.6 4.8 %copy-start.2 = (bf16[288,288]{1,0:T(8,128)(2,1)S(1)}, bf16[288,288]{1,0:T(8,128)(2,1)}, u32[]{:S(2)}) copy-start(bf16[288,288]{1,0:T(8,128)(2,1)} %get-tuple-element.52.ham) | copy-start | bytes 497668
  30.6 4.7 %collective-permute-start.10 = (f32[48,384]{1,0:T(8,128)S(1)}, f32[48,384]{1,0:T(8,128)S(1)}, u32[]{:S(2)}, u32[]{:S(2)}) collective-permute-start(f32[48,384]{1,0:T(8,128)S(1)} %get-tuple-element.48), channel_id=1, source_target_pairs={{0,28},{4,8},{8,4},{12,16},{16,12},{20,24},{24,20},{28,0},{1,29},{... | collective-permute-start | bytes 221192 | tf_op jit(solution)/shard_map/ppermute | solution.py:305
  30.7 4.7 %collective-permute-start.11 = (f32[48,384]{1,0:T(8,128)S(1)}, f32[48,384]{1,0:T(8,128)S(1)}, u32[]{:S(2)}, u32[]{:S(2)}) collective-permute-start(f32[48,384]{1,0:T(8,128)S(1)} %get-tuple-element.51), channel_id=1, source_target_pairs={{0,4},{4,0},{8,12},{12,8},{16,20},{20,16},{24,28},{28,24},{1,5},{5... | collective-permute-start | bytes 221192 | tf_op jit(solution)/shard_map/ppermute | solution.py:302
  35.6 1.3 %collective-permute-start.12 = (f32[48,384]{1,0:T(8,128)S(1)}, f32[48,384]{1,0:T(8,128)S(1)}, u32[]{:S(2)}, u32[]{:S(2)}) collective-permute-start(f32[48,384]{1,0:T(8,128)S(1)} %get-tuple-element.53), channel_id=1, source_target_pairs={{0,4},{4,0},{8,12},{12,8},{16,20},{20,16},{24,28},{28,24},{1,5},{5... | collective-permute-start | bytes 221192 | tf_op jit(solution)/shard_map/ppermute | solution.py:302
  35.7 5.4 %collective-permute-start.14 = (f32[48,384]{1,0:T(8,128)S(1)}, f32[48,384]{1,0:T(8,128)S(1)}, u32[]{:S(2)}, u32[]{:S(2)}) collective-permute-start(f32[48,384]{1,0:T(8,128)S(1)} %get-tuple-element.57.sent), channel_id=1, source_target_pairs={{0,28},{4,8},{8,4},{12,16},{16,12},{20,24},{24,20},{28,0},{1,29},{... | collective-permute-start | bytes 221192 | tf_op jit(solution)/shard_map/ppermute | solution.py:305
  37.4 5.6 %collective-permute-start.13 = (f32[48,512]{1,0:T(8,128)S(1)}, f32[48,512]{1,0:T(8,128)S(1)}, u32[]{:S(2)}, u32[]{:S(2)}) collective-permute-start(f32[48,512]{1,0:T(8,128)S(1)} %get-tuple-element.56), channel_id=1, source_target_pairs={{0,28},{4,8},{8,4},{12,16},{16,12},{20,24},{24,20},{28,0},{1,29},{... | collective-permute-start | bytes 294920 | tf_op jit(solution)/shard_map/ppermute | solution.py:305
  41.5 1.3 %collective-permute-start.15 = (f32[48,384]{1,0:T(8,128)S(1)}, f32[48,384]{1,0:T(8,128)S(1)}, u32[]{:S(2)}, u32[]{:S(2)}) collective-permute-start(f32[48,384]{1,0:T(8,128)S(1)} %get-tuple-element.60), channel_id=1, source_target_pairs={{0,4},{4,0},{8,12},{12,8},{16,20},{20,16},{24,28},{28,24},{1,5},{5... | collective-permute-start | bytes 221192 | tf_op jit(solution)/shard_map/ppermute | solution.py:302
  43.4 4.7 %collective-permute-start.16 = (f32[48,384]{1,0:T(8,128)S(1)}, f32[48,384]{1,0:T(8,128)S(1)}, u32[]{:S(2)}, u32[]{:S(2)}) collective-permute-start(f32[48,384]{1,0:T(8,128)S(1)} %get-tuple-element.62), channel_id=1, source_target_pairs={{0,28},{4,8},{8,4},{12,16},{16,12},{20,24},{24,20},{28,0},{1,29},{... | collective-permute-start | bytes 221192 | tf_op jit(solution)/shard_map/ppermute | solution.py:305
  44.3 3.8 %collective-permute-start.17 = (f32[48,384]{1,0:T(8,128)S(1)}, f32[48,384]{1,0:T(8,128)S(1)}, u32[]{:S(2)}, u32[]{:S(2)}) collective-permute-start(f32[48,384]{1,0:T(8,128)S(1)} %get-tuple-element.64), channel_id=1, source_target_pairs={{0,4},{4,0},{8,12},{12,8},{16,20},{20,16},{24,28},{28,24},{1,5},{5... | collective-permute-start | bytes 221192 | tf_op jit(solution)/shard_map/ppermute | solution.py:302

commit v7 on v6

--- a/solution.py
+++ b/solution.py
@@ -319,17 +319,13 @@
     paired = doms == 8 and rotation_store.shape[0] % 16 == 0
     parts = [own_columns]
     if paired:
-        parts += [lax.ppermute(own_columns, "dom", flip(doms, b)) for b in (2, 4)]
-    ham_own, *parts = lax.optimization_barrier((ham_own, *parts))
-    if paired:
-        parts.append(lax.ppermute(parts[1], "dom", flip(doms, 4)))
-        other = [lax.ppermute(part, "dom", near_pairs) for part in parts[:3]]
+        parts += [lax.ppermute(own_columns, "dom", flip(doms, b)) for b in (2, 4, 6)]
     one, two, ham_own = lax.optimization_barrier((one, two, ham_own))
     longer = call(longer_kernel, shape(owned + 8, cols), [two], 0)
     three = lax.ppermute(longer, "band", flip(4, 1))
+    two, *parts = lax.optimization_barrier((two, *parts))
     if paired:
-        two, parts[3] = lax.optimization_barrier((two, parts[3]))
-        other.append(lax.ppermute(parts[3], "dom", near_pairs))
+        other = [lax.ppermute(part, "dom", near_pairs) for part in parts]
         slots = [part for pair in zip(parts, other) for part in pair]
         rotation = ordered_rotation(slots, owner, bands)
     else:
@@ -356,7 +352,7 @@
     )
     from_far, from_near = to_other(sent), to_pair(to_near)
     base, to_far = call(
-        near_sums_kernel, (block, shape(ghost, cols + 128)), [from_near, base, column, put_near, pick], small
+        near_sums_kernel, (block, shape(ghost, cols + 128)), [from_near, base, column, put_near, pick], 0
     )
     far = to_other(to_far)
     filtered, to_near = call(

time: 49.3 us -> 46.9 us (0.951)
  waiting for transfers between devices: 20.9 us -> 18.8 us
  local copies, waits for them, and re-layouts: 1.34 us -> 0.07 us
  starting transfers between devices: 14.8 us -> 15.7 us
    ppermute x1, waiting for transfers between devices: 4.05 us -> 1.38 us  [shards(): one = lax.ppermute(states, 'band', flip(4, 1))]
    ppermute x7, waiting for transfers between devices: 1.6 us -> 3.57 us  [the longest x3 1.97 us: shards(): lax.ppermute(own_columns, 'dom', flip(doms, b))]
    ppermute x1, waiting for transfers between devices: 1.76 us -> 0.01 us  [shards(): three = lax.ppermute(longer, 'band', flip(4, 1))]
    ppermute x7, starting transfers between devices: 6.11 us -> 4.57 us  [the longest x3 3.55 us: shards(): lax.ppermute(own_columns, 'dom', flip(doms, b))]
    ppermute x1, starting transfers between devices: 1.58 us -> 3.02 us  [shards(): one = lax.ppermute(states, 'band', flip(4, 1))]
    ppermute x4, starting transfers between devices: 3.33 us -> 4.69 us  [to_other(): return lax.ppermute(rows, 'dom', far_pairs)]
    unnamed x16, local copies, waits for them, and re-layouts: 1.31 us -> 0.05 us
    ppermute x4, waiting for transfers between devices: 9.73 us -> 10.6 us  [to_other(): return lax.ppermute(rows, 'dom', far_pairs)]
  transfers between devices with their start and end apart: 18 -> 18, of which waited for: 13 -> 12; matrix products, arithmetic and copies ran while one was open for 0% -> 0% of each run, Pallas kernels for 20% -> 21%
where the time goes in v7:
time: 46.9 us; the launch traced here: 46.8 us
  waiting for transfers between devices  18.8 us (40%)
  starting transfers between devices  15.7 us (33%)
  Pallas kernels  12 us (26%)
    ppermute x4, waiting for transfers between devices, to_other(): return lax.ppermute(rows, 'dom', far_pairs)  10.6 us
    pallas_call x12, Pallas kernels, call(): pl.pallas_call(kernel, out_shape=out_shape, in_specs=specs, out_specs=jax...  6.21 us
    pallas_call x1, Pallas kernels, assemble(): pl.pallas_call(functools.partial(assemble_kernel, ghost), out_shape=(shap...  5.79 us
    ppermute x4, starting transfers between devices, to_other(): return lax.ppermute(rows, 'dom', far_pairs)  4.69 us
    ppermute x3, starting transfers between devices, shards(): lax.ppermute(own_columns, 'dom', flip(doms, b))  3.55 us
    ppermute x1, starting transfers between devices, shards(): one = lax.ppermute(states, 'band', flip(4, 1))  3.02 us
    ppermute x1, starting transfers between devices, shards(): two = lax.ppermute(states, 'band', flip(4, 2))  2.59 us
    ppermute x1, waiting for transfers between devices, shards(): two = lax.ppermute(states, 'band', flip(4, 2))  2.56 us
  transfers between devices with their start and end apart: 18, of which 12 were waited for; matrix products, arithmetic and copies ran while one was open for 0% of the time, Pallas kernels for 21%

profile of v7, /device:TPU:0, one launch (start us, length us, event | category | flops | bytes accessed | tf_op | source)
XLA Modules:
  0.0 46.8 jit_solution(1013270723118969122)
XLA Ops:
  0.0 0.0 copy-start
  0.0 3.0 %collective-permute-start = (f32[192,384]{1,0:T(8,128)}, f32[192,384]{1,0:T(8,128)S(1)}, u32[]{:S(2)}, u32[]{:S(2)}) collective-permute-start(f32[192,384]{1,0:T(8,128)} %own.1), channel_id=1, source_target_pairs={{0,1},{1,0},{2,3},{3,2},{4,5},{5,4},{6,7},{7,6},{8,9},{9,8},{10,11... | collective-permute-start | bytes 884744 | tf_op jit(solution)/shard_map/ppermute | solution.py:317
  3.0 2.6 %collective-permute-start.1 = (f32[192,384]{1,0:T(8,128)}, f32[192,384]{1,0:T(8,128)S(1)}, u32[]{:S(2)}, u32[]{:S(2)}) collective-permute-start(f32[192,384]{1,0:T(8,128)} %own.1), channel_id=1, source_target_pairs={{0,2},{1,3},{2,0},{3,1},{4,6},{5,7},{6,4},{7,5},{8,10},{9,11},{10,... | collective-permute-start | bytes 884744 | tf_op jit(solution)/shard_map/ppermute | solution.py:318
  5.6 0.0 copy-done
  5.6 0.0 copy-start.4
  5.7 0.0 copy-start.6
  5.7 0.0 copy-start.7
  5.7 0.0 copy-start.5
  5.7 1.6 %collective-permute-start.2 = (f32[192,384]{1,0:T(8,128)S(1)}, f32[192,384]{1,0:T(8,128)S(1)}, u32[]{:S(2)}, u32[]{:S(2)}) collective-permute-start(f32[192,384]{1,0:T(8,128)S(1)} %constant_dynamic-slice_fusion.refs_0_), channel_id=1, source_target_pairs={{0,8},{4,12},{8,0},{12,4},{16,24},{20,28},{24,16},{28,20},{1,9},{5... | collective-permute-start | bytes 884744 | tf_op jit(solution)/shard_map/ppermute | solution.py:322
  7.3 1.5 %collective-permute-start.3 = (f32[192,384]{1,0:T(8,128)S(1)}, f32[192,384]{1,0:T(8,128)S(1)}, u32[]{:S(2)}, u32[]{:S(2)}) collective-permute-start(f32[192,384]{1,0:T(8,128)S(1)} %constant_dynamic-slice_fusion.refs_0_), channel_id=1, source_target_pairs={{0,16},{4,20},{8,24},{12,28},{16,0},{20,4},{24,8},{28,12},{1,17},{... | collective-permute-start | bytes 884744 | tf_op jit(solution)/shard_map/ppermute | solution.py:322
  8.8 0.5 %collective-permute-start.4 = (f32[192,384]{1,0:T(8,128)S(1)}, f32[192,384]{1,0:T(8,128)S(1)}, u32[]{:S(2)}, u32[]{:S(2)}) collective-permute-start(f32[192,384]{1,0:T(8,128)S(1)} %constant_dynamic-slice_fusion.refs_0_), channel_id=1, source_target_pairs={{0,24},{4,28},{8,16},{12,20},{16,8},{20,12},{24,0},{28,4},{1,25},{... | collective-permute-start | bytes 884744 | tf_op jit(solution)/shard_map/ppermute | solution.py:322
  9.3 5.8 %shard_map.82 = (bf16[288,576]{1,0:T(8,128)(2,1)}, bf16[288,288]{1,0:T(8,128)(2,1)}) custom-call(s32[5,343]{1,0:T(8,128)} %nodes_any.1, f32[5,343,343]{2,1,0:T(8,128)} %ham_any.1), custom_call_target="tpu_custom_call" | custom-call | flops 1355316480 | bytes 2352980 | tf_op jit(solution)/shard_map/pallas_call | solution.py:154
  15.0 1.4 %collective-permute-done.one = f32[192,384]{1,0:T(8,128)S(1)} collective-permute-done((f32[192,384]{1,0:T(8,128)}, f32[192,384]{1,0:T(8,128)S(1)}, u32[]{:S(2)}, u32[]{:S(2)}) %collective-permute-start) | collective-permute-done | bytes 294944 | tf_op jit(solution)/shard_map/ppermute | solution.py:317
  16.4 2.6 %collective-permute-done.1.two.block = f32[192,384]{1,0:T(8,128)S(1)} collective-permute-done((f32[192,384]{1,0:T(8,128)}, f32[192,384]{1,0:T(8,128)S(1)}, u32[]{:S(2)}, u32[]{:S(2)}) %collective-permute-start.1) | collective-permute-done | bytes 294944 | tf_op jit(solution)/shard_map/ppermute | solution.py:318
  19.0 0.5 %collective-permute-start.9 = (f32[200,384]{1,0:T(8,128)S(1)}, f32[200,384]{1,0:T(8,128)S(1)}, u32[]{:S(2)}, u32[]{:S(2)}) collective-permute-start(f32[200,384]{1,0:T(8,128)S(1)} %shard_map.85), channel_id=1, source_target_pairs={{0,1},{1,0},{2,3},{3,2},{4,5},{5,4},{6,7},{7,6},{8,9},{9,8},{10,11... | collective-permute-start | bytes 921608 | tf_op jit(solution)/shard_map/ppermute | solution.py:325
  19.5 0.0 collective-permute-done.2.refs_2_
  19.5 2.0 %collective-permute-done.3.refs_4_ = f32[192,384]{1,0:T(8,128)S(1)} collective-permute-done((f32[192,384]{1,0:T(8,128)S(1)}, f32[192,384]{1,0:T(8,128)S(1)}, u32[]{:S(2)}, u32[]{:S(2)}) %collective-permute-start.3) | collective-permute-done | bytes 294944 | tf_op jit(solution)/shard_map/ppermute | solution.py:322
  21.5 0.0 collective-permute-done.4.refs_6_
  21.5 0.0 collective-permute-start.5
  21.5 0.5 %collective-permute-start.6 = (f32[192,384]{1,0:T(8,128)S(1)}, f32[192,384]{1,0:T(8,128)S(1)}, u32[]{:S(2)}, u32[]{:S(2)}) collective-permute-start(f32[192,384]{1,0:T(8,128)S(1)} %collective-permute-done.2.refs_2_), channel_id=1, source_target_pairs={{0,4},{4,0},{8,12},{12,8},{16,20},{20,16},{24,28},{28,24},{1,5},{5... | collective-permute-start | bytes 884744 | tf_op jit(solution)/shard_map/ppermute | solution.py:328
  22.0 0.0 collective-permute-start.7
  22.0 0.5 %collective-permute-start.8 = (f32[192,384]{1,0:T(8,128)S(1)}, f32[192,384]{1,0:T(8,128)S(1)}, u32[]{:S(2)}, u32[]{:S(2)}) collective-permute-start(f32[192,384]{1,0:T(8,128)S(1)} %collective-permute-done.4.refs_6_), channel_id=1, source_target_pairs={{0,4},{4,0},{8,12},{12,8},{16,20},{20,16},{24,28},{28,24},{1,5},{5... | collective-permute-start | bytes 884744 | tf_op jit(solution)/shard_map/ppermute | solution.py:328
  22.5 0.0 copy-done.4
  22.5 0.0 copy-done.6
  22.5 0.0 copy-done.7
  22.5 0.2 shard_map.86
  22.7 0.0 copy-start.3
  22.7 0.3 collective-permute-done.5.refs_1_
  23.1 0.4 collective-permute-done.6.refs_3_
  23.5 0.4 collective-permute-done.7.refs_5_
  23.9 0.4 collective-permute-done.8.refs_7_
  24.3 0.0 copy-done.5
  24.3 1.0 %shard_map.83 = (bf16[8,192,384]{2,1,0:T(8,128)(2,1)S(1)}, bf16[8,192,384]{2,1,0:T(8,128)(2,1)S(1)}) custom-call(s32[8]{0:T(128)S(1)} %copy-done.5, f32[192,384]{1,0:T(8,128)S(1)} %constant_dynamic-slice_fusion.refs_0_, f32[192,384]{1,0:T(8,128)S(1)} %collective-permute-done.5.refs_1_, f32[192,384]{1,0:T(8,128)S(1)} %collective-permute-done.2.refs_2_, ...), custom_call_target="tpu_custom_call" | custom-call | tf_op jit(solution)/shard_map/pallas_call | solution.py:59
  25.3 0.0 copy-done.3
  25.3 0.9 %shard_map.84.total = f32[192,384]{1,0:T(8,128)S(1)} custom-call(bf16[4,384,384]{2,1,0:T(8,128)(2,1)S(1)} %bitcast.5, bf16[4,384,384]{2,1,0:T(8,128)(2,1)S(1)} %bitcast.7, f32[192,384]{1,0:T(8,128)S(1)} %copy-done.3, f32[192,384]{1,0:T(8,128)S(1)} %collective-permute-done.one, f32[192,384]{1,0:T(8,128)S(1)} %collective-permute-done.1.two.block), custom_call_target="tpu_custom_call" | custom-call | tf_op jit(solution)/shard_map/pallas_call | solution.py:59
  26.3 0.0 collective-permute-done.9.three
  26.3 0.0 copy-start.1
  26.3 0.7 %shard_map.87 = (f32[192,384]{1,0:T(8,128)S(1)}, f32[48,384]{1,0:T(8,128)S(1)}, f32[48,384]{1,0:T(8,128)S(1)}) custom-call(bf16[4,384,384]{2,1,0:T(8,128)(2,1)S(1)} %bitcast.6, bf16[4,384,384]{2,1,0:T(8,128)(2,1)S(1)} %bitcast.8, f32[192,384]{1,0:T(8,128)S(1)} %shard_map.84.total, f32[200,384]{1,0:T(8,128)S(1)} %collective-permute-done.9.three, ...), custom_call_target="tpu_custom_call" | custom-call | flops 169869312 | bytes 1048576 | tf_op jit(solution)/shard_map/pallas_call | solution.py:59
  27.0 0.0 copy-start.2
  27.0 1.3 %collective-permute-start.10 = (f32[48,384]{1,0:T(8,128)S(1)}, f32[48,384]{1,0:T(8,128)S(1)}, u32[]{:S(2)}, u32[]{:S(2)}) collective-permute-start(f32[48,384]{1,0:T(8,128)S(1)} %get-tuple-element.46), channel_id=1, source_target_pairs={{0,28},{4,8},{8,4},{12,16},{16,12},{20,24},{24,20},{28,0},{1,29},{... | collective-permute-start | bytes 221192 | tf_op jit(solution)/shard_map/ppermute | solution.py:305
  28.3 0.1 collective-permute-start.11
  28.4 0.0 copy-done.1
  28.4 0.5 %shard_map.88.partial = f32[288,384]{1,0:T(8,128)S(1)} custom-call(f32[192,384]{1,0:T(8,128)S(1)} %get-tuple-element.47.v.s, f32[192,128]{1,0:T(8,128)S(1)} %get-tuple-element.44.column, bf16[288,576]{1,0:T(8,128)(2,1)S(1)} %copy-done.1), custom_call_target="tpu_custom_call" | custom-call | flops 191102976 | bytes 1048576 | tf_op jit(solution)/shard_map/pallas_call | solution.py:59
  28.8 3.4 %collective-permute-done.10.far = f32[48,384]{1,0:T(8,128)S(1)} collective-permute-done((f32[48,384]{1,0:T(8,128)S(1)}, f32[48,384]{1,0:T(8,128)S(1)}, u32[]{:S(2)}, u32[]{:S(2)}) %collective-permute-start.10) | collective-permute-done | bytes 73760 | tf_op jit(solution)/shard_map/ppermute | solution.py:305
  32.2 0.0 collective-permute-done.11.near
  32.2 0.0 copy-done.2
  32.2 0.3 shard_map.89
  32.5 0.1 collective-permute-start.12
  32.6 1.2 %collective-permute-start.14 = (f32[48,384]{1,0:T(8,128)S(1)}, f32[48,384]{1,0:T(8,128)S(1)}, u32[]{:S(2)}, u32[]{:S(2)}) collective-permute-start(f32[48,384]{1,0:T(8,128)S(1)} %get-tuple-element.55.sent), channel_id=1, source_target_pairs={{0,28},{4,8},{8,4},{12,16},{16,12},{20,24},{24,20},{28,0},{1,29},{... | collective-permute-start | bytes 221192 | tf_op jit(solution)/shard_map/ppermute | solution.py:305
  33.9 0.0 collective-permute-done.12.from_near
  33.9 0.4 shard_map.90
  34.3 1.5 %collective-permute-start.13 = (f32[48,512]{1,0:T(8,128)S(1)}, f32[48,512]{1,0:T(8,128)S(1)}, u32[]{:S(2)}, u32[]{:S(2)}) collective-permute-start(f32[48,512]{1,0:T(8,128)S(1)} %get-tuple-element.54), channel_id=1, source_target_pairs={{0,28},{4,8},{8,4},{12,16},{16,12},{20,24},{24,20},{28,0},{1,29},{... | collective-permute-start | bytes 294920 | tf_op jit(solution)/shard_map/ppermute | solution.py:305
  35.8 2.0 %collective-permute-done.14.from_far = f32[48,384]{1,0:T(8,128)S(1)} collective-permute-done((f32[48,384]{1,0:T(8,128)S(1)}, f32[48,384]{1,0:T(8,128)S(1)}, u32[]{:S(2)}, u32[]{:S(2)}) %collective-permute-start.14) | collective-permute-done | bytes 73760 | tf_op jit(solution)/shard_map/ppermute | solution.py:305
  37.9 0.4 shard_map.91
  38.3 0.2 collective-permute-start.15
  38.4 0.5 shard_map.92.partial
  38.9 0.7 %collective-permute-done.15.near = f32[48,384]{1,0:T(8,128)S(1)} collective-permute-done((f32[48,384]{1,0:T(8,128)S(1)}, f32[48,384]{1,0:T(8,128)S(1)}, u32[]{:S(2)}, u32[]{:S(2)}) %collective-permute-start.15) | collective-permute-done | bytes 73760 | tf_op jit(solution)/shard_map/ppermute | solution.py:302
  39.6 0.8 %collective-permute-done.13.far = f32[48,512]{1,0:T(8,128)S(1)} collective-permute-done((f32[48,512]{1,0:T(8,128)S(1)}, f32[48,512]{1,0:T(8,128)S(1)}, u32[]{:S(2)}, u32[]{:S(2)}) %collective-permute-start.13) | collective-permute-done | bytes 98336 | tf_op jit(solution)/shard_map/ppermute | solution.py:305
  40.3 0.4 shard_map.93
  40.7 0.6 %collective-permute-start.16 = (f32[48,384]{1,0:T(8,128)S(1)}, f32[48,384]{1,0:T(8,128)S(1)}, u32[]{:S(2)}, u32[]{:S(2)}) collective-permute-start(f32[48,384]{1,0:T(8,128)S(1)} %get-tuple-element.60), channel_id=1, source_target_pairs={{0,28},{4,8},{8,4},{12,16},{16,12},{20,24},{24,20},{28,0},{1,29},{... | collective-permute-start | bytes 221192 | tf_op jit(solution)/shard_map/ppermute | solution.py:305
  41.4 0.0 collective-permute-start.17
  41.4 4.4 %collective-permute-done.16.from_far = f32[48,384]{1,0:T(8,128)S(1)} collective-permute-done((f32[48,384]{1,0:T(8,128)S(1)}, f32[48,384]{1,0:T(8,128)S(1)}, u32[]{:S(2)}, u32[]{:S(2)}) %collective-permute-start.16) | collective-permute-done | bytes 73760 | tf_op jit(solution)/shard_map/ppermute | solution.py:305
  45.8 0.0 collective-permute-done.17.from_near
  45.8 1.0 %shard_map.94 = f32[192,384]{1,0:T(8,128)} custom-call(f32[48,384]{1,0:T(8,128)S(1)} %collective-permute-done.16.from_far, f32[192,384]{1,0:T(8,128)S(1)} %get-tuple-element.61.base, f32[48,384]{1,0:T(8,128)S(1)} %collective-permute-done.17.from_near, f32[192,128]{1,0:T(8,128)S(1)} %get-tuple-element.44.column, ...), custom_call_target="tpu_custom_call" | custom-call | flops 42467328 | bytes 1048576 | tf_op jit(solution)/shard_map/pallas_call | solution.py:59
  (2 shorter events, 0.0 us)
Async XLA Ops:
  0.0 5.6 %copy-start = (f32[192,1536]{1,0:T(8,128)S(1)}, f32[192,1536]{1,0:T(8,128)}, u32[]{:S(2)}) copy-start(f32[192,1536]{1,0:T(8,128)} %param.15) | copy-start | bytes 3538948
  0.0 16.4 %collective-permute-start = (f32[192,384]{1,0:T(8,128)}, f32[192,384]{1,0:T(8,128)S(1)}, u32[]{:S(2)}, u32[]{:S(2)}) collective-permute-start(f32[192,384]{1,0:T(8,128)} %own.1), channel_id=1, source_target_pairs={{0,1},{1,0},{2,3},{3,2},{4,5},{5,4},{6,7},{7,6},{8,9},{9,8},{10,11... | collective-permute-start | bytes 884744 | tf_op jit(solution)/shard_map/ppermute | solution.py:317
  3.0 16.0 %collective-permute-start.1 = (f32[192,384]{1,0:T(8,128)}, f32[192,384]{1,0:T(8,128)S(1)}, u32[]{:S(2)}, u32[]{:S(2)}) collective-permute-start(f32[192,384]{1,0:T(8,128)} %own.1), channel_id=1, source_target_pairs={{0,2},{1,3},{2,0},{3,1},{4,6},{5,7},{6,4},{7,5},{8,10},{9,11},{10,... | collective-permute-start | bytes 884744 | tf_op jit(solution)/shard_map/ppermute | solution.py:318
  5.6 16.9 %copy-start.4 = (f32[192]{0:T(256)S(1)}, f32[192]{0:T(256)}, u32[]{:S(2)}) copy-start(f32[192]{0:T(256)} %param.9) | copy-start | bytes 2308
  5.7 16.9 %copy-start.6 = (s32[48]{0:T(128)S(1)}, s32[48]{0:T(128)}, u32[]{:S(2)}) copy-start(s32[48]{0:T(128)} %param.12) | copy-start | bytes 580
  5.7 16.8 %copy-start.7 = (s32[48]{0:T(128)S(1)}, s32[48]{0:T(128)}, u32[]{:S(2)}) copy-start(s32[48]{0:T(128)} %param.13) | copy-start | bytes 580
  5.7 18.7 %copy-start.5 = (s32[8]{0:T(128)S(1)}, s32[8]{0:T(128)}, u32[]{:S(2)}) copy-start(s32[8]{0:T(128)} %owner.1) | copy-start | bytes 100
  5.7 13.8 %collective-permute-start.2 = (f32[192,384]{1,0:T(8,128)S(1)}, f32[192,384]{1,0:T(8,128)S(1)}, u32[]{:S(2)}, u32[]{:S(2)}) collective-permute-start(f32[192,384]{1,0:T(8,128)S(1)} %constant_dynamic-slice_fusion.refs_0_), channel_id=1, source_target_pairs={{0,8},{4,12},{8,0},{12,4},{16,24},{20,28},{24,16},{28,20},{1,9},{5... | collective-permute-start | bytes 884744 | tf_op jit(solution)/shard_map/ppermute | solution.py:322
  7.3 14.2 %collective-permute-start.3 = (f32[192,384]{1,0:T(8,128)S(1)}, f32[192,384]{1,0:T(8,128)S(1)}, u32[]{:S(2)}, u32[]{:S(2)}) collective-permute-start(f32[192,384]{1,0:T(8,128)S(1)} %constant_dynamic-slice_fusion.refs_0_), channel_id=1, source_target_pairs={{0,16},{4,20},{8,24},{12,28},{16,0},{20,4},{24,8},{28,12},{1,17},{... | collective-permute-start | bytes 884744 | tf_op jit(solution)/shard_map/ppermute | solution.py:322
  8.8 12.7 %collective-permute-start.4 = (f32[192,384]{1,0:T(8,128)S(1)}, f32[192,384]{1,0:T(8,128)S(1)}, u32[]{:S(2)}, u32[]{:S(2)}) collective-permute-start(f32[192,384]{1,0:T(8,128)S(1)} %constant_dynamic-slice_fusion.refs_0_), channel_id=1, source_target_pairs={{0,24},{4,28},{8,16},{12,20},{16,8},{20,12},{24,0},{28,4},{1,25},{... | collective-permute-start | bytes 884744 | tf_op jit(solution)/shard_map/ppermute | solution.py:322
  19.0 7.2 %collective-permute-start.9 = (f32[200,384]{1,0:T(8,128)S(1)}, f32[200,384]{1,0:T(8,128)S(1)}, u32[]{:S(2)}, u32[]{:S(2)}) collective-permute-start(f32[200,384]{1,0:T(8,128)S(1)} %shard_map.85), channel_id=1, source_target_pairs={{0,1},{1,0},{2,3},{3,2},{4,5},{5,4},{6,7},{7,6},{8,9},{9,8},{10,11... | collective-permute-start | bytes 921608 | tf_op jit(solution)/shard_map/ppermute | solution.py:325
  21.5 1.6 %collective-permute-start.5 = (f32[192,384]{1,0:T(8,128)S(1)}, f32[192,384]{1,0:T(8,128)S(1)}, u32[]{:S(2)}, u32[]{:S(2)}) collective-permute-start(f32[192,384]{1,0:T(8,128)S(1)} %constant_dynamic-slice_fusion.refs_0_), channel_id=1, source_target_pairs={{0,4},{4,0},{8,12},{12,8},{16,20},{20,16},{24,28},{28,24},{1,5},{5... | collective-permute-start | bytes 884744 | tf_op jit(solution)/shard_map/ppermute | solution.py:328
  21.5 2.0 %collective-permute-start.6 = (f32[192,384]{1,0:T(8,128)S(1)}, f32[192,384]{1,0:T(8,128)S(1)}, u32[]{:S(2)}, u32[]{:S(2)}) collective-permute-start(f32[192,384]{1,0:T(8,128)S(1)} %collective-permute-done.2.refs_2_), channel_id=1, source_target_pairs={{0,4},{4,0},{8,12},{12,8},{16,20},{20,16},{24,28},{28,24},{1,5},{5... | collective-permute-start | bytes 884744 | tf_op jit(solution)/shard_map/ppermute | solution.py:328
  22.0 1.9 %collective-permute-start.7 = (f32[192,384]{1,0:T(8,128)S(1)}, f32[192,384]{1,0:T(8,128)S(1)}, u32[]{:S(2)}, u32[]{:S(2)}) collective-permute-start(f32[192,384]{1,0:T(8,128)S(1)} %collective-permute-done.3.refs_4_), channel_id=1, source_target_pairs={{0,4},{4,0},{8,12},{12,8},{16,20},{20,16},{24,28},{28,24},{1,5},{5... | collective-permute-start | bytes 884744 | tf_op jit(solution)/shard_map/ppermute | solution.py:328
  22.0 2.3 %collective-permute-start.8 = (f32[192,384]{1,0:T(8,128)S(1)}, f32[192,384]{1,0:T(8,128)S(1)}, u32[]{:S(2)}, u32[]{:S(2)}) collective-permute-start(f32[192,384]{1,0:T(8,128)S(1)} %collective-permute-done.4.refs_6_), channel_id=1, source_target_pairs={{0,4},{4,0},{8,12},{12,8},{16,20},{20,16},{24,28},{28,24},{1,5},{5... | collective-permute-start | bytes 884744 | tf_op jit(solution)/shard_map/ppermute | solution.py:328
  22.7 2.6 %copy-start.3 = (f32[192,384]{1,0:T(8,128)S(1)}, f32[192,384]{1,0:T(8,128)}, u32[]{:S(2)}) copy-start(f32[192,384]{1,0:T(8,128)} %own.1) | copy-start | bytes 884740
  26.3 2.1 %copy-start.1 = (bf16[288,576]{1,0:T(8,128)(2,1)S(1)}, bf16[288,576]{1,0:T(8,128)(2,1)}, u32[]{:S(2)}) copy-start(bf16[288,576]{1,0:T(8,128)(2,1)} %get-tuple-element.48.ham) | copy-start | bytes 995332
  27.0 5.3 %copy-start.2 = (bf16[288,288]{1,0:T(8,128)(2,1)S(1)}, bf16[288,288]{1,0:T(8,128)(2,1)}, u32[]{:S(2)}) copy-start(bf16[288,288]{1,0:T(8,128)(2,1)} %get-tuple-element.50.ham) | copy-start | bytes 497668
  27.0 5.3 %collective-permute-start.10 = (f32[48,384]{1,0:T(8,128)S(1)}, f32[48,384]{1,0:T(8,128)S(1)}, u32[]{:S(2)}, u32[]{:S(2)}) collective-permute-start(f32[48,384]{1,0:T(8,128)S(1)} %get-tuple-element.46), channel_id=1, source_target_pairs={{0,28},{4,8},{8,4},{12,16},{16,12},{20,24},{24,20},{28,0},{1,29},{... | collective-permute-start | bytes 221192 | tf_op jit(solution)/shard_map/ppermute | solution.py:305
  28.3 4.0 %collective-permute-start.11 = (f32[48,384]{1,0:T(8,128)S(1)}, f32[48,384]{1,0:T(8,128)S(1)}, u32[]{:S(2)}, u32[]{:S(2)}) collective-permute-start(f32[48,384]{1,0:T(8,128)S(1)} %get-tuple-element.49), channel_id=1, source_target_pairs={{0,4},{4,0},{8,12},{12,8},{16,20},{20,16},{24,28},{28,24},{1,5},{5... | collective-permute-start | bytes 221192 | tf_op jit(solution)/shard_map/ppermute | solution.py:302
  32.5 1.3 %collective-permute-start.12 = (f32[48,384]{1,0:T(8,128)S(1)}, f32[48,384]{1,0:T(8,128)S(1)}, u32[]{:S(2)}, u32[]{:S(2)}) collective-permute-start(f32[48,384]{1,0:T(8,128)S(1)} %get-tuple-element.51), channel_id=1, source_target_pairs={{0,4},{4,0},{8,12},{12,8},{16,20},{20,16},{24,28},{28,24},{1,5},{5... | collective-permute-start | bytes 221192 | tf_op jit(solution)/shard_map/ppermute | solution.py:302
  32.6 5.2 %collective-permute-start.14 = (f32[48,384]{1,0:T(8,128)S(1)}, f32[48,384]{1,0:T(8,128)S(1)}, u32[]{:S(2)}, u32[]{:S(2)}) collective-permute-start(f32[48,384]{1,0:T(8,128)S(1)} %get-tuple-element.55.sent), channel_id=1, source_target_pairs={{0,28},{4,8},{8,4},{12,16},{16,12},{20,24},{24,20},{28,0},{1,29},{... | collective-permute-start | bytes 221192 | tf_op jit(solution)/shard_map/ppermute | solution.py:305
  34.3 6.0 %collective-permute-start.13 = (f32[48,512]{1,0:T(8,128)S(1)}, f32[48,512]{1,0:T(8,128)S(1)}, u32[]{:S(2)}, u32[]{:S(2)}) collective-permute-start(f32[48,512]{1,0:T(8,128)S(1)} %get-tuple-element.54), channel_id=1, source_target_pairs={{0,28},{4,8},{8,4},{12,16},{16,12},{20,24},{24,20},{28,0},{1,29},{... | collective-permute-start | bytes 294920 | tf_op jit(solution)/shard_map/ppermute | solution.py:305
  38.3 1.3 %collective-permute-start.15 = (f32[48,384]{1,0:T(8,128)S(1)}, f32[48,384]{1,0:T(8,128)S(1)}, u32[]{:S(2)}, u32[]{:S(2)}) collective-permute-start(f32[48,384]{1,0:T(8,128)S(1)} %get-tuple-element.58), channel_id=1, source_target_pairs={{0,4},{4,0},{8,12},{12,8},{16,20},{20,16},{24,28},{28,24},{1,5},{5... | collective-permute-start | bytes 221192 | tf_op jit(solution)/shard_map/ppermute | solution.py:302
  40.7 5.1 %collective-permute-start.16 = (f32[48,384]{1,0:T(8,128)S(1)}, f32[48,384]{1,0:T(8,128)S(1)}, u32[]{:S(2)}, u32[]{:S(2)}) collective-permute-start(f32[48,384]{1,0:T(8,128)S(1)} %get-tuple-element.60), channel_id=1, source_target_pairs={{0,28},{4,8},{8,4},{12,16},{16,12},{20,24},{24,20},{28,0},{1,29},{... | collective-permute-start | bytes 221192 | tf_op jit(solution)/shard_map/ppermute | solution.py:305
  41.4 4.4 %collective-permute-start.17 = (f32[48,384]{1,0:T(8,128)S(1)}, f32[48,384]{1,0:T(8,128)S(1)}, u32[]{:S(2)}, u32[]{:S(2)}) collective-permute-start(f32[48,384]{1,0:T(8,128)S(1)} %get-tuple-element.62), channel_id=1, source_target_pairs={{0,4},{4,0},{8,12},{12,8},{16,20},{20,16},{24,28},{28,24},{1,5},{5... | collective-permute-start | bytes 221192 | tf_op jit(solution)/shard_map/ppermute | solution.py:302

commit v8 on v7

--- a/solution.py
+++ b/solution.py
@@ -71,7 +71,7 @@
     return jax.ShapeDtypeStruct(dims, dtype)
 
 
-def lists_kernel(m, up, dn, column, pick, put_near, put_far):
+def lists_kernel(m, up, dn, column, pick, put_near, put_far, far_is_near, near_is_far, scales):
     owned = m.shape[1]
     column[...] = jnp.broadcast_to(as_column(m[...]), column.shape)
     even = lax.rem(lax.axis_index("dom"), 2) == 0
@@ -81,6 +81,10 @@
     pick[...] = jnp.concatenate([rows.astype(f32)] * 3, axis=1).astype(bf16)
     put_near[...] = jnp.concatenate([put_rows(near, owned).astype(f32)] * 3, axis=1).astype(bf16)
     put_far[...] = jnp.concatenate([put_rows(far, owned).astype(f32)] * 3, axis=1).astype(bf16)
+    for out, these, those in ((far_is_near, far, near), (near_is_far, near, far)):
+        same = as_column(these.astype(f32)) == those.astype(f32)
+        out[...] = jnp.concatenate([same.astype(f32)] * 3, axis=1).astype(bf16)
+    scales[...] = picked(column[...], pick[...])
 
 
 def split_three(x):
@@ -178,50 +182,94 @@
     out[...] = mm(ham[...], jnp.concatenate([hi, hi, lo], axis=0))
 
 
-def add_halo(partial, near, far, ham, to_near, to_far):
+def halo_part(near, far, ham):
+    hi, lo = split(jnp.concatenate([near, far], axis=0))
+    return mm(ham, jnp.concatenate([hi, hi, lo], axis=0))
+
+
+def completed(far, sent):
+    cols = sent.shape[1]
+    scale = far[:, cols : cols + 1]
+    return far[:, :cols] + (sigma_one / filter_half) * scale * scale * sent[...]
+
+
+def send_ham_kernel(ham, pick, out):
+    halo, owned = out.shape[0] * 2 // 3, pick.shape[1] // 3
+    ghost = halo // 2
+    out[:halo, :] = ham[owned:, :]
+    out[halo:, :] = mm(pick[ghost:, :owned], ham[:owned, :]).astype(bf16)
+
+
+def first_partial_kernel(v, column, ham, pick, out, far_out):
+    own_kernel(v, column, ham, out)
+    ghost = far_out.shape[0]
+    far_out[...] = picked(out[: v.shape[0], :], pick[ghost:, :])
+
+
+def first_sums_kernel(
+    far, near, partial, far_partial, far_sent, ham, scales, to_near, to_far, far_rows
+):
     ghost = near.shape[0]
     owned = partial.shape[0] - 2 * ghost
-    hi, lo = split(jnp.concatenate([near, far], axis=0))
-    z = partial[...] + mm(ham[...], jnp.concatenate([hi, hi, lo], axis=0))
-    to_near[...] = z[owned : owned + ghost]
-    to_far[...] = z[owned + ghost :]
-    return z[:owned]
-
-
-def first_kernel(far, partial, near, ham, column, s, base, to_near, to_far):
-    z = add_halo(partial, near[...], far[...], ham, to_near, to_far)
+    z = halo_part(near[...], far[...], ham[...])
+    to_near[...] = partial[owned : owned + ghost, :] + z[:ghost]
+    to_far[...] = partial[owned + ghost :, :] + z[ghost : 2 * ghost]
+    scale = scales[ghost:, :1]
+    rows = scale * scale * (far_partial[...] + z[2 * ghost :])
+    far_rows[...] = (sigma_one / filter_half) * (rows - filter_center * far_sent[...])
+
+
+def first_own_kernel(far, near, partial, ham, column, s, base):
+    owned = s.shape[0]
+    z = partial[:owned, :] + halo_part(near[...], far[...], ham[:owned, :])
     base[...] = (sigma_one / filter_half) * (z * column[:, :1] - filter_center * s[...])
 
 
-def near_sums_kernel(from_near, base, column, put_near, pick, out, to_far):
+def far_rows_kernel(from_near, far_rows, far_is_near, scales, out):
+    ghost, cols = far_rows.shape
+    scale = scales[ghost:, :]
+    added = (sigma_one / filter_half) * scale[:, :1] * scale[:, :1] * placed(from_near, far_is_near)
+    out[...] = jnp.concatenate([far_rows[...] + added, scale], axis=1)
+
+
+def near_sums_kernel(from_near, base, column, put_near, pick, out, near_rows):
     scale = column[:, :1]
     rows = base[...] + (sigma_one / filter_half) * scale * placed(from_near, put_near)
     out[...] = rows
-    wide = jnp.concatenate([rows * scale, column[...]], axis=1)
-    to_far[...] = picked(wide, pick[to_far.shape[0] :, :])
-
-
-def far_sums_kernel(from_far, base, column, put_far, pick, one, to_near):
-    scale = column[:, :1]
-    rows = base[...] + (sigma_one / filter_half) * scale * placed(from_far, put_far)
-    one[...] = rows
-    to_near[...] = picked(rows * scale, pick[: to_near.shape[0], :])
-
-
-def second_kernel(far, near, sent, partial, ham, column, one, s, base, to_near, to_far):
-    cols = sent.shape[1]
-    scale = far[:, cols : cols + 1]
-    whole = far[:, :cols] + (sigma_one / filter_half) * scale * scale * sent[...]
-    z = add_halo(partial, near[...], whole, ham, to_near, to_far)
+    near_rows[...] = picked(rows * scale, pick[: near_rows.shape[0], :])
+
+
+def near_rows_kernel(from_far, near_rows, near_is_far, scales, out):
+    scale = scales[: out.shape[0], :1]
+    added = (sigma_one / filter_half) * scale * scale * placed(from_far, near_is_far)
+    out[...] = near_rows[...] + added
+
+
+def far_sums_kernel(from_far, base, column, put_far, one):
+    scale = (sigma_one / filter_half) * column[:, :1]
+    one[...] = base[...] + scale * placed(from_far, put_far)
+
+
+def second_sums_kernel(far, near, sent, partial, ham, to_near, to_far):
+    ghost = near.shape[0]
+    owned = partial.shape[0] - 2 * ghost
+    z = partial[owned:, :] + halo_part(near[...], completed(far, sent), ham[owned:, :])
+    to_near[...] = z[:ghost]
+    to_far[...] = z[ghost:]
+
+
+def second_own_kernel(far, near, sent, partial, ham, column, one, s, base):
+    owned = s.shape[0]
+    z = partial[:owned, :] + halo_part(near[...], completed(far, sent), ham[:owned, :])
     base[...] = (
         2.0 * sigma_two / filter_half * (z * column[:, :1] - filter_center * one[...])
         - sigma_one * sigma_two * s[...]
     )
 
 
-def last_kernel(from_far, base, from_near, column, put_near, put_far, two):
+def last_kernel(from_far, base, from_near, column, put_near, put_far, out):
     sums = placed(from_near, put_near) + placed(from_far, put_far)
-    two[...] = base[...] + 2.0 * sigma_two / filter_half * column[:, :1] * sums
+    out[...] = base[...] + 2.0 * sigma_two / filter_half * column[:, :1] * sums
 
 
 def order_kernel(owner, *refs):
@@ -306,11 +354,23 @@
 
     ham_own, ham_halo = assemble(cell_nodes, cell_ham, ext, ghost)
     put = shape(owned, 3 * ghost, dtype=bf16)
-    column, pick, put_near, put_far = call(
+    cross = shape(ghost, 3 * ghost, dtype=bf16)
+    column, pick, put_near, put_far, far_is_near, near_is_far, scales = call(
         lists_kernel,
-        (shape(owned, 128), shape(2 * ghost, 3 * owned, dtype=bf16), put, put),
+        (
+            shape(owned, 128),
+            shape(2 * ghost, 3 * owned, dtype=bf16),
+            put,
+            put,
+            cross,
+            cross,
+            shape(2 * ghost, 128),
+        ),
         [m, up, dn],
         owned * owned,
+    )
+    ham_send = call(
+        send_ham_kernel, shape(3 * ghost, 6 * ghost, dtype=bf16), [ham_halo, pick], 0
     )
     band = lax.axis_index("band")
     own_columns = lax.dynamic_slice_in_dim(rotation_store, band * cols, cols, 1)
@@ -343,31 +403,47 @@
     wide = shape(ext, cols)
     work = 6 * ext * ext * cols
     far, near = to_other(to_far), to_pair(to_near)
-    partial = call(own_kernel, wide, [turned, column, ham_own], work)
-    base, to_near, sent = call(
-        first_kernel,
-        (block, halo, halo),
-        [far, partial, near, ham_halo, column, turned],
-        work,
+    partial, far_partial = call(
+        first_partial_kernel, (wide, halo), [turned, column, ham_own, pick], work
+    )
+    to_near, sent, far_rows = call(
+        first_sums_kernel,
+        (halo, halo, halo),
+        [far, near, partial, far_partial, to_far, ham_send, scales],
+        0,
     )
     from_far, from_near = to_other(sent), to_pair(to_near)
-    base, to_far = call(
-        near_sums_kernel, (block, shape(ghost, cols + 128)), [from_near, base, column, put_near, pick], 0
-    )
-    far = to_other(to_far)
-    filtered, to_near = call(
-        far_sums_kernel, (block, halo), [from_far, base, column, put_far, pick], 0
-    )
-    near = to_pair(to_near)
+    base = call(
+        first_own_kernel, block, [far, near, partial, ham_halo, column, turned], 0
+    )
+    far = to_other(
+        call(
+            far_rows_kernel,
+            shape(ghost, cols + 128),
+            [from_near, far_rows, far_is_near, scales],
+            0,
+        )
+    )
+    base, near_rows = call(
+        near_sums_kernel, (block, halo), [from_near, base, column, put_near, pick], 0
+    )
+    near = to_pair(
+        call(near_rows_kernel, halo, [from_far, near_rows, near_is_far, scales], 0)
+    )
+    filtered = call(far_sums_kernel, block, [from_far, base, column, put_far], 0)
     partial = call(own_kernel, wide, [filtered, column, ham_own], work)
-    base, to_near, to_far = call(
-        second_kernel,
-        (block, halo, halo),
+    to_near, to_far = call(
+        second_sums_kernel, (halo, halo), [far, near, sent, partial, ham_halo], 0
+    )
+    from_far, from_near = to_other(to_far), to_pair(to_near)
+    base = call(
+        second_own_kernel,
+        block,
         [far, near, sent, partial, ham_halo, column, filtered, turned],
         work,
     )
-    far, near = to_other(to_far), to_pair(to_near)
-    return call(last_kernel, block, [far, base, near, column, put_near, put_far], small)
+    operands = [from_far, base, from_near, column, put_near, put_far]
+    return call(last_kernel, block, operands, small)
 
 
 def solution(mesh):

time: 46.9 us -> 46.5 us (level)
  waiting for transfers between devices: 18.8 us -> 17.2 us
  Pallas kernels: 12 us -> 12.9 us
    ppermute x4, waiting for transfers between devices: 10.6 us -> 9.37 us  [to_other(): return lax.ppermute(rows, 'dom', far_pairs)]
    pallas_call x12 -> x17, Pallas kernels: 6.21 us -> 7.12 us  [call(): pl.pallas_call(kernel, out_shape=out_shape, in_specs=specs, out_specs=jax...]
  transfers between devices with their start and end apart: 18 -> 18, of which waited for: 12 -> 12; matrix products, arithmetic and copies ran while one was open for 0% -> 0% of each run, Pallas kernels for 21% -> 23%
where the time goes in v8:
time: 46.5 us; the launch traced here: 46.4 us
  waiting for transfers between devices  17.2 us (37%)
  starting transfers between devices  15.9 us (34%)
  Pallas kernels  12.9 us (28%)
    ppermute x4, waiting for transfers between devices, to_other(): return lax.ppermute(rows, 'dom', far_pairs)  9.37 us
    pallas_call x17, Pallas kernels, call(): pl.pallas_call(kernel, out_shape=out_shape, in_specs=specs, out_specs=jax...  7.12 us
    pallas_call x1, Pallas kernels, assemble(): pl.pallas_call(functools.partial(assemble_kernel, ghost), out_shape=(shap...  5.79 us
    ppermute x4, starting transfers between devices, to_other(): return lax.ppermute(rows, 'dom', far_pairs)  4.87 us
    ppermute x3, starting transfers between devices, shards(): lax.ppermute(own_columns, 'dom', flip(doms, b))  3.55 us
    ppermute x1, starting transfers between devices, shards(): one = lax.ppermute(states, 'band', flip(4, 1))  3.02 us
    ppermute x1, starting transfers between devices, shards(): two = lax.ppermute(states, 'band', flip(4, 2))  2.59 us
    ppermute x1, waiting for transfers between devices, shards(): two = lax.ppermute(states, 'band', flip(4, 2))  2.56 us
  transfers between devices with their start and end apart: 18, of which 12 were waited for; matrix products, arithmetic and copies ran while one was open for 0% of the time, Pallas kernels for 23%

profile of v8, /device:TPU:0, one launch (start us, length us, event | category | flops | bytes accessed | tf_op | source)
XLA Modules:
  0.0 46.4 jit_solution(5496807016599280108)
XLA Ops:
  0.0 0.0 copy-start
  0.0 3.0 %collective-permute-start = (f32[192,384]{1,0:T(8,128)}, f32[192,384]{1,0:T(8,128)S(1)}, u32[]{:S(2)}, u32[]{:S(2)}) collective-permute-start(f32[192,384]{1,0:T(8,128)} %own.1), channel_id=1, source_target_pairs={{0,1},{1,0},{2,3},{3,2},{4,5},{5,4},{6,7},{7,6},{8,9},{9,8},{10,11... | collective-permute-start | bytes 884744 | tf_op jit(solution)/shard_map/ppermute | solution.py:377
  3.0 2.6 %collective-permute-start.1 = (f32[192,384]{1,0:T(8,128)}, f32[192,384]{1,0:T(8,128)S(1)}, u32[]{:S(2)}, u32[]{:S(2)}) collective-permute-start(f32[192,384]{1,0:T(8,128)} %own.1), channel_id=1, source_target_pairs={{0,2},{1,3},{2,0},{3,1},{4,6},{5,7},{6,4},{7,5},{8,10},{9,11},{10,... | collective-permute-start | bytes 884744 | tf_op jit(solution)/shard_map/ppermute | solution.py:378
  5.6 0.0 copy-done
  5.6 0.0 copy-start.4
  5.7 0.0 copy-start.6
  5.7 0.0 copy-start.7
  5.7 0.0 copy-start.5
  5.7 1.6 %collective-permute-start.2 = (f32[192,384]{1,0:T(8,128)S(1)}, f32[192,384]{1,0:T(8,128)S(1)}, u32[]{:S(2)}, u32[]{:S(2)}) collective-permute-start(f32[192,384]{1,0:T(8,128)S(1)} %constant_dynamic-slice_fusion.refs_0_), channel_id=1, source_target_pairs={{0,8},{4,12},{8,0},{12,4},{16,24},{20,28},{24,16},{28,20},{1,9},{5... | collective-permute-start | bytes 884744 | tf_op jit(solution)/shard_map/ppermute | solution.py:382
  7.3 1.5 %collective-permute-start.3 = (f32[192,384]{1,0:T(8,128)S(1)}, f32[192,384]{1,0:T(8,128)S(1)}, u32[]{:S(2)}, u32[]{:S(2)}) collective-permute-start(f32[192,384]{1,0:T(8,128)S(1)} %constant_dynamic-slice_fusion.refs_0_), channel_id=1, source_target_pairs={{0,16},{4,20},{8,24},{12,28},{16,0},{20,4},{24,8},{28,12},{1,17},{... | collective-permute-start | bytes 884744 | tf_op jit(solution)/shard_map/ppermute | solution.py:382
  8.8 0.5 %collective-permute-start.4 = (f32[192,384]{1,0:T(8,128)S(1)}, f32[192,384]{1,0:T(8,128)S(1)}, u32[]{:S(2)}, u32[]{:S(2)}) collective-permute-start(f32[192,384]{1,0:T(8,128)S(1)} %constant_dynamic-slice_fusion.refs_0_), channel_id=1, source_target_pairs={{0,24},{4,28},{8,16},{12,20},{16,8},{20,12},{24,0},{28,4},{1,25},{... | collective-permute-start | bytes 884744 | tf_op jit(solution)/shard_map/ppermute | solution.py:382
  9.3 5.8 %shard_map.82 = (bf16[288,576]{1,0:T(8,128)(2,1)}, bf16[288,288]{1,0:T(8,128)(2,1)}) custom-call(s32[5,343]{1,0:T(8,128)} %nodes_any.1, f32[5,343,343]{2,1,0:T(8,128)} %ham_any.1), custom_call_target="tpu_custom_call" | custom-call | flops 1355316480 | bytes 2352980 | tf_op jit(solution)/shard_map/pallas_call | solution.py:158
  15.0 1.4 %collective-permute-done.one = f32[192,384]{1,0:T(8,128)S(1)} collective-permute-done((f32[192,384]{1,0:T(8,128)}, f32[192,384]{1,0:T(8,128)S(1)}, u32[]{:S(2)}, u32[]{:S(2)}) %collective-permute-start) | collective-permute-done | bytes 294944 | tf_op jit(solution)/shard_map/ppermute | solution.py:377
  16.4 2.6 %collective-permute-done.1.two.block = f32[192,384]{1,0:T(8,128)S(1)} collective-permute-done((f32[192,384]{1,0:T(8,128)}, f32[192,384]{1,0:T(8,128)S(1)}, u32[]{:S(2)}, u32[]{:S(2)}) %collective-permute-start.1) | collective-permute-done | bytes 294944 | tf_op jit(solution)/shard_map/ppermute | solution.py:378
  19.0 0.5 %collective-permute-start.9 = (f32[200,384]{1,0:T(8,128)S(1)}, f32[200,384]{1,0:T(8,128)S(1)}, u32[]{:S(2)}, u32[]{:S(2)}) collective-permute-start(f32[200,384]{1,0:T(8,128)S(1)} %shard_map.85), channel_id=1, source_target_pairs={{0,1},{1,0},{2,3},{3,2},{4,5},{5,4},{6,7},{7,6},{8,9},{9,8},{10,11... | collective-permute-start | bytes 921608 | tf_op jit(solution)/shard_map/ppermute | solution.py:385
  19.5 0.0 collective-permute-done.2.refs_2_
  19.5 2.0 %collective-permute-done.3.refs_4_ = f32[192,384]{1,0:T(8,128)S(1)} collective-permute-done((f32[192,384]{1,0:T(8,128)S(1)}, f32[192,384]{1,0:T(8,128)S(1)}, u32[]{:S(2)}, u32[]{:S(2)}) %collective-permute-start.3) | collective-permute-done | bytes 294944 | tf_op jit(solution)/shard_map/ppermute | solution.py:382
  21.5 0.0 collective-permute-done.4.refs_6_
  21.5 0.0 collective-permute-start.5
  21.5 0.5 %collective-permute-start.6 = (f32[192,384]{1,0:T(8,128)S(1)}, f32[192,384]{1,0:T(8,128)S(1)}, u32[]{:S(2)}, u32[]{:S(2)}) collective-permute-start(f32[192,384]{1,0:T(8,128)S(1)} %collective-permute-done.2.refs_2_), channel_id=1, source_target_pairs={{0,4},{4,0},{8,12},{12,8},{16,20},{20,16},{24,28},{28,24},{1,5},{5... | collective-permute-start | bytes 884744 | tf_op jit(solution)/shard_map/ppermute | solution.py:388
  22.0 0.0 collective-permute-start.7
  22.0 0.5 %collective-permute-start.8 = (f32[192,384]{1,0:T(8,128)S(1)}, f32[192,384]{1,0:T(8,128)S(1)}, u32[]{:S(2)}, u32[]{:S(2)}) collective-permute-start(f32[192,384]{1,0:T(8,128)S(1)} %collective-permute-done.4.refs_6_), channel_id=1, source_target_pairs={{0,4},{4,0},{8,12},{12,8},{16,20},{20,16},{24,28},{28,24},{1,5},{5... | collective-permute-start | bytes 884744 | tf_op jit(solution)/shard_map/ppermute | solution.py:388
  22.5 0.0 copy-done.4
  22.5 0.3 shard_map.86
  22.9 0.0 copy-start.3
  22.9 0.2 collective-permute-done.5.refs_1_
  23.1 0.4 collective-permute-done.6.refs_3_
  23.5 0.4 collective-permute-done.7.refs_5_
  23.9 0.4 collective-permute-done.8.refs_7_
  24.3 0.0 copy-done.5
  24.3 1.0 %shard_map.83 = (bf16[8,192,384]{2,1,0:T(8,128)(2,1)S(1)}, bf16[8,192,384]{2,1,0:T(8,128)(2,1)S(1)}) custom-call(s32[8]{0:T(128)S(1)} %copy-done.5, f32[192,384]{1,0:T(8,128)S(1)} %constant_dynamic-slice_fusion.refs_0_, f32[192,384]{1,0:T(8,128)S(1)} %collective-permute-done.5.refs_1_, f32[192,384]{1,0:T(8,128)S(1)} %collective-permute-done.2.refs_2_, ...), custom_call_target="tpu_custom_call" | custom-call | tf_op jit(solution)/shard_map/pallas_call | solution.py:59
  25.3 0.9 %shard_map.84.total = f32[192,384]{1,0:T(8,128)S(1)} custom-call(bf16[4,384,384]{2,1,0:T(8,128)(2,1)S(1)} %bitcast.5, bf16[4,384,384]{2,1,0:T(8,128)(2,1)S(1)} %bitcast.7, f32[192,384]{1,0:T(8,128)S(1)} %copy-done.3, f32[192,384]{1,0:T(8,128)S(1)} %collective-permute-done.one, f32[192,384]{1,0:T(8,128)S(1)} %collective-permute-done.1.two.block), custom_call_target="tpu_custom_call" | custom-call | tf_op jit(solution)/shard_map/pallas_call | solution.py:59
  26.3 0.0 collective-permute-done.9.three
  26.3 0.0 copy-start.1
  26.3 0.7 %shard_map.87 = (f32[192,384]{1,0:T(8,128)S(1)}, f32[48,384]{1,0:T(8,128)S(1)}, f32[48,384]{1,0:T(8,128)S(1)}) custom-call(bf16[4,384,384]{2,1,0:T(8,128)(2,1)S(1)} %bitcast.6, bf16[4,384,384]{2,1,0:T(8,128)(2,1)S(1)} %bitcast.8, f32[192,384]{1,0:T(8,128)S(1)} %shard_map.84.total, f32[200,384]{1,0:T(8,128)S(1)} %collective-permute-done.9.three, ...), custom_call_target="tpu_custom_call" | custom-call | flops 169869312 | bytes 1048576 | tf_op jit(solution)/shard_map/pallas_call | solution.py:59
  27.0 1.3 %collective-permute-start.10 = (f32[48,384]{1,0:T(8,128)S(1)}, f32[48,384]{1,0:T(8,128)S(1)}, u32[]{:S(2)}, u32[]{:S(2)}) collective-permute-start(f32[48,384]{1,0:T(8,128)S(1)} %get-tuple-element.48.far_sent), channel_id=1, source_target_pairs={{0,28},{4,8},{8,4},{12,16},{16,12},{20,24},{24,20},{28,0},{1,29},{... | collective-permute-start | bytes 221192 | tf_op jit(solution)/shard_map/ppermute | solution.py:353
  28.3 0.1 collective-permute-start.11
  28.4 0.0 copy-done.1
  28.4 0.1 shard_map.89.ham
  28.5 0.6 %shard_map.88 = (f32[288,384]{1,0:T(8,128)S(1)}, f32[48,384]{1,0:T(8,128)S(1)}) custom-call(f32[192,384]{1,0:T(8,128)S(1)} %get-tuple-element.50.v.s, f32[192,128]{1,0:T(8,128)S(1)} %get-tuple-element.46.column, bf16[288,576]{1,0:T(8,128)(2,1)S(1)} %copy-done.2, bf16[96,576]{1,0:T(8,128)(2,1)S(1)} %get-tuple-element.47.pick), custom_call_target="tpu_custom_call" | custom-call | flops 191102976 | bytes 1048576 | tf_op jit(solution)/shard_map/pallas_call | solution.py:59
  29.2 3.0 %collective-permute-done.10.far = f32[48,384]{1,0:T(8,128)S(1)} collective-permute-done((f32[48,384]{1,0:T(8,128)S(1)}, f32[48,384]{1,0:T(8,128)S(1)}, u32[]{:S(2)}, u32[]{:S(2)}) %collective-permute-start.10) | collective-permute-done | bytes 73760 | tf_op jit(solution)/shard_map/ppermute | solution.py:353
  32.2 0.0 collective-permute-done.11.near
  32.2 0.2 shard_map.90
  32.5 0.1 collective-permute-start.12
  32.5 1.3 %collective-permute-start.14 = (f32[48,384]{1,0:T(8,128)S(1)}, f32[48,384]{1,0:T(8,128)S(1)}, u32[]{:S(2)}, u32[]{:S(2)}) collective-permute-start(f32[48,384]{1,0:T(8,128)S(1)} %get-tuple-element.59.sent), channel_id=1, source_target_pairs={{0,28},{4,8},{8,4},{12,16},{16,12},{20,24},{24,20},{28,0},{1,29},{... | collective-permute-start | bytes 221192 | tf_op jit(solution)/shard_map/ppermute | solution.py:353
  33.9 0.0 collective-permute-done.12.from_near
  33.9 0.1 shard_map.91
  34.0 1.5 %collective-permute-start.13 = (f32[48,512]{1,0:T(8,128)S(1)}, f32[48,512]{1,0:T(8,128)S(1)}, u32[]{:S(2)}, u32[]{:S(2)}) collective-permute-start(f32[48,512]{1,0:T(8,128)S(1)} %shard_map.91), channel_id=1, source_target_pairs={{0,28},{4,8},{8,4},{12,16},{16,12},{20,24},{24,20},{28,0},{1,29},{... | collective-permute-start | bytes 294920 | tf_op jit(solution)/shard_map/ppermute | solution.py:353
  35.5 0.3 shard_map.92.base
  35.7 0.4 shard_map.93
  36.1 1.6 %collective-permute-done.14.from_far = f32[48,384]{1,0:T(8,128)S(1)} collective-permute-done((f32[48,384]{1,0:T(8,128)S(1)}, f32[48,384]{1,0:T(8,128)S(1)}, u32[]{:S(2)}, u32[]{:S(2)}) %collective-permute-start.14) | collective-permute-done | bytes 73760 | tf_op jit(solution)/shard_map/ppermute | solution.py:353
  37.8 0.1 shard_map.94
  37.9 0.2 collective-permute-start.15
  38.1 0.2 shard_map.95.v.one
  38.3 0.5 %shard_map.96.partial = f32[288,384]{1,0:T(8,128)S(1)} custom-call(f32[192,384]{1,0:T(8,128)S(1)} %shard_map.95.v.one, f32[192,128]{1,0:T(8,128)S(1)} %get-tuple-element.46.column, bf16[288,576]{1,0:T(8,128)(2,1)S(1)} %copy-done.2), custom_call_target="tpu_custom_call" | custom-call | flops 191102976 | bytes 1048576 | tf_op jit(solution)/shard_map/pallas_call | solution.py:59
  38.8 0.5 %collective-permute-done.15.near = f32[48,384]{1,0:T(8,128)S(1)} collective-permute-done((f32[48,384]{1,0:T(8,128)S(1)}, f32[48,384]{1,0:T(8,128)S(1)}, u32[]{:S(2)}, u32[]{:S(2)}) %collective-permute-start.15) | collective-permute-done | bytes 73760 | tf_op jit(solution)/shard_map/ppermute | solution.py:350
  39.3 0.8 %collective-permute-done.13.far = f32[48,512]{1,0:T(8,128)S(1)} collective-permute-done((f32[48,512]{1,0:T(8,128)S(1)}, f32[48,512]{1,0:T(8,128)S(1)}, u32[]{:S(2)}, u32[]{:S(2)}) %collective-permute-start.13) | collective-permute-done | bytes 98336 | tf_op jit(solution)/shard_map/ppermute | solution.py:353
  40.1 0.3 shard_map.97
  40.4 0.8 %collective-permute-start.16 = (f32[48,384]{1,0:T(8,128)S(1)}, f32[48,384]{1,0:T(8,128)S(1)}, u32[]{:S(2)}, u32[]{:S(2)}) collective-permute-start(f32[48,384]{1,0:T(8,128)S(1)} %get-tuple-element.65), channel_id=1, source_target_pairs={{0,28},{4,8},{8,4},{12,16},{16,12},{20,24},{24,20},{28,0},{1,29},{... | collective-permute-start | bytes 221192 | tf_op jit(solution)/shard_map/ppermute | solution.py:353
  41.2 0.0 collective-permute-start.17
  41.2 0.4 shard_map.98.base
  41.5 3.9 %collective-permute-done.16.from_far = f32[48,384]{1,0:T(8,128)S(1)} collective-permute-done((f32[48,384]{1,0:T(8,128)S(1)}, f32[48,384]{1,0:T(8,128)S(1)}, u32[]{:S(2)}, u32[]{:S(2)}) %collective-permute-start.16) | collective-permute-done | bytes 73760 | tf_op jit(solution)/shard_map/ppermute | solution.py:353
  45.4 0.0 collective-permute-done.17.from_near
  45.4 1.0 %shard_map.99 = f32[192,384]{1,0:T(8,128)} custom-call(f32[48,384]{1,0:T(8,128)S(1)} %collective-permute-done.16.from_far, f32[192,384]{1,0:T(8,128)S(1)} %shard_map.98.base, f32[48,384]{1,0:T(8,128)S(1)} %collective-permute-done.17.from_near, f32[192,128]{1,0:T(8,128)S(1)} %get-tuple-element.46.column, bf16[192,144]{1,0:T(8,128)(2,1)S(1)} %get-tuple-element.60.put_near, ...), custom_call_target="tpu_custom_call" | custom-call | flops 42467328 | bytes 1048576 | tf_op jit(solution)/shard_map/pallas_call | solution.py:59
  (7 shorter events, 0.1 us)
Async XLA Ops:
  0.0 5.6 %copy-start = (f32[192,1536]{1,0:T(8,128)S(1)}, f32[192,1536]{1,0:T(8,128)}, u32[]{:S(2)}) copy-start(f32[192,1536]{1,0:T(8,128)} %param.15) | copy-start | bytes 3538948
  0.0 16.4 %collective-permute-start = (f32[192,384]{1,0:T(8,128)}, f32[192,384]{1,0:T(8,128)S(1)}, u32[]{:S(2)}, u32[]{:S(2)}) collective-permute-start(f32[192,384]{1,0:T(8,128)} %own.1), channel_id=1, source_target_pairs={{0,1},{1,0},{2,3},{3,2},{4,5},{5,4},{6,7},{7,6},{8,9},{9,8},{10,11... | collective-permute-start | bytes 884744 | tf_op jit(solution)/shard_map/ppermute | solution.py:377
  3.0 16.0 %collective-permute-start.1 = (f32[192,384]{1,0:T(8,128)}, f32[192,384]{1,0:T(8,128)S(1)}, u32[]{:S(2)}, u32[]{:S(2)}) collective-permute-start(f32[192,384]{1,0:T(8,128)} %own.1), channel_id=1, source_target_pairs={{0,2},{1,3},{2,0},{3,1},{4,6},{5,7},{6,4},{7,5},{8,10},{9,11},{10,... | collective-permute-start | bytes 884744 | tf_op jit(solution)/shard_map/ppermute | solution.py:378
  5.6 16.9 %copy-start.4 = (f32[192]{0:T(256)S(1)}, f32[192]{0:T(256)}, u32[]{:S(2)}) copy-start(f32[192]{0:T(256)} %param.9) | copy-start | bytes 2308
  5.7 16.9 %copy-start.6 = (s32[48]{0:T(128)S(1)}, s32[48]{0:T(128)}, u32[]{:S(2)}) copy-start(s32[48]{0:T(128)} %param.12) | copy-start | bytes 580
  5.7 16.8 %copy-start.7 = (s32[48]{0:T(128)S(1)}, s32[48]{0:T(128)}, u32[]{:S(2)}) copy-start(s32[48]{0:T(128)} %param.13) | copy-start | bytes 580
  5.7 18.7 %copy-start.5 = (s32[8]{0:T(128)S(1)}, s32[8]{0:T(128)}, u32[]{:S(2)}) copy-start(s32[8]{0:T(128)} %owner.1) | copy-start | bytes 100
  5.7 13.8 %collective-permute-start.2 = (f32[192,384]{1,0:T(8,128)S(1)}, f32[192,384]{1,0:T(8,128)S(1)}, u32[]{:S(2)}, u32[]{:S(2)}) collective-permute-start(f32[192,384]{1,0:T(8,128)S(1)} %constant_dynamic-slice_fusion.refs_0_), channel_id=1, source_target_pairs={{0,8},{4,12},{8,0},{12,4},{16,24},{20,28},{24,16},{28,20},{1,9},{5... | collective-permute-start | bytes 884744 | tf_op jit(solution)/shard_map/ppermute | solution.py:382
  7.3 14.2 %collective-permute-start.3 = (f32[192,384]{1,0:T(8,128)S(1)}, f32[192,384]{1,0:T(8,128)S(1)}, u32[]{:S(2)}, u32[]{:S(2)}) collective-permute-start(f32[192,384]{1,0:T(8,128)S(1)} %constant_dynamic-slice_fusion.refs_0_), channel_id=1, source_target_pairs={{0,16},{4,20},{8,24},{12,28},{16,0},{20,4},{24,8},{28,12},{1,17},{... | collective-permute-start | bytes 884744 | tf_op jit(solution)/shard_map/ppermute | solution.py:382
  8.8 12.7 %collective-permute-start.4 = (f32[192,384]{1,0:T(8,128)S(1)}, f32[192,384]{1,0:T(8,128)S(1)}, u32[]{:S(2)}, u32[]{:S(2)}) collective-permute-start(f32[192,384]{1,0:T(8,128)S(1)} %constant_dynamic-slice_fusion.refs_0_), channel_id=1, source_target_pairs={{0,24},{4,28},{8,16},{12,20},{16,8},{20,12},{24,0},{28,4},{1,25},{... | collective-permute-start | bytes 884744 | tf_op jit(solution)/shard_map/ppermute | solution.py:382
  19.0 7.2 %collective-permute-start.9 = (f32[200,384]{1,0:T(8,128)S(1)}, f32[200,384]{1,0:T(8,128)S(1)}, u32[]{:S(2)}, u32[]{:S(2)}) collective-permute-start(f32[200,384]{1,0:T(8,128)S(1)} %shard_map.85), channel_id=1, source_target_pairs={{0,1},{1,0},{2,3},{3,2},{4,5},{5,4},{6,7},{7,6},{8,9},{9,8},{10,11... | collective-permute-start | bytes 921608 | tf_op jit(solution)/shard_map/ppermute | solution.py:385
  21.5 1.6 %collective-permute-start.5 = (f32[192,384]{1,0:T(8,128)S(1)}, f32[192,384]{1,0:T(8,128)S(1)}, u32[]{:S(2)}, u32[]{:S(2)}) collective-permute-start(f32[192,384]{1,0:T(8,128)S(1)} %constant_dynamic-slice_fusion.refs_0_), channel_id=1, source_target_pairs={{0,4},{4,0},{8,12},{12,8},{16,20},{20,16},{24,28},{28,24},{1,5},{5... | collective-permute-start | bytes 884744 | tf_op jit(solution)/shard_map/ppermute | solution.py:388
  21.5 2.0 %collective-permute-start.6 = (f32[192,384]{1,0:T(8,128)S(1)}, f32[192,384]{1,0:T(8,128)S(1)}, u32[]{:S(2)}, u32[]{:S(2)}) collective-permute-start(f32[192,384]{1,0:T(8,128)S(1)} %collective-permute-done.2.refs_2_), channel_id=1, source_target_pairs={{0,4},{4,0},{8,12},{12,8},{16,20},{20,16},{24,28},{28,24},{1,5},{5... | collective-permute-start | bytes 884744 | tf_op jit(solution)/shard_map/ppermute | solution.py:388
  22.0 1.9 %collective-permute-start.7 = (f32[192,384]{1,0:T(8,128)S(1)}, f32[192,384]{1,0:T(8,128)S(1)}, u32[]{:S(2)}, u32[]{:S(2)}) collective-permute-start(f32[192,384]{1,0:T(8,128)S(1)} %collective-permute-done.3.refs_4_), channel_id=1, source_target_pairs={{0,4},{4,0},{8,12},{12,8},{16,20},{20,16},{24,28},{28,24},{1,5},{5... | collective-permute-start | bytes 884744 | tf_op jit(solution)/shard_map/ppermute | solution.py:388
  22.0 2.3 %collective-permute-start.8 = (f32[192,384]{1,0:T(8,128)S(1)}, f32[192,384]{1,0:T(8,128)S(1)}, u32[]{:S(2)}, u32[]{:S(2)}) collective-permute-start(f32[192,384]{1,0:T(8,128)S(1)} %collective-permute-done.4.refs_6_), channel_id=1, source_target_pairs={{0,4},{4,0},{8,12},{12,8},{16,20},{20,16},{24,28},{28,24},{1,5},{5... | collective-permute-start | bytes 884744 | tf_op jit(solution)/shard_map/ppermute | solution.py:388
  22.9 2.5 %copy-start.3 = (f32[192,384]{1,0:T(8,128)S(1)}, f32[192,384]{1,0:T(8,128)}, u32[]{:S(2)}) copy-start(f32[192,384]{1,0:T(8,128)} %own.1) | copy-start | bytes 884740
  26.3 2.1 %copy-start.1 = (bf16[288,288]{1,0:T(8,128)(2,1)S(1)}, bf16[288,288]{1,0:T(8,128)(2,1)}, u32[]{:S(2)}) copy-start(bf16[288,288]{1,0:T(8,128)(2,1)} %get-tuple-element.54.ham) | copy-start | bytes 497668
  26.3 2.3 %copy-start.2 = (bf16[288,576]{1,0:T(8,128)(2,1)S(1)}, bf16[288,576]{1,0:T(8,128)(2,1)}, u32[]{:S(2)}) copy-start(bf16[288,576]{1,0:T(8,128)(2,1)} %get-tuple-element.51.ham) | copy-start | bytes 995332
  27.0 5.3 %collective-permute-start.10 = (f32[48,384]{1,0:T(8,128)S(1)}, f32[48,384]{1,0:T(8,128)S(1)}, u32[]{:S(2)}, u32[]{:S(2)}) collective-permute-start(f32[48,384]{1,0:T(8,128)S(1)} %get-tuple-element.48.far_sent), channel_id=1, source_target_pairs={{0,28},{4,8},{8,4},{12,16},{16,12},{20,24},{24,20},{28,0},{1,29},{... | collective-permute-start | bytes 221192 | tf_op jit(solution)/shard_map/ppermute | solution.py:353
  28.3 4.0 %collective-permute-start.11 = (f32[48,384]{1,0:T(8,128)S(1)}, f32[48,384]{1,0:T(8,128)S(1)}, u32[]{:S(2)}, u32[]{:S(2)}) collective-permute-start(f32[48,384]{1,0:T(8,128)S(1)} %get-tuple-element.49), channel_id=1, source_target_pairs={{0,4},{4,0},{8,12},{12,8},{16,20},{20,16},{24,28},{28,24},{1,5},{5... | collective-permute-start | bytes 221192 | tf_op jit(solution)/shard_map/ppermute | solution.py:350
  32.5 1.4 %collective-permute-start.12 = (f32[48,384]{1,0:T(8,128)S(1)}, f32[48,384]{1,0:T(8,128)S(1)}, u32[]{:S(2)}, u32[]{:S(2)}) collective-permute-start(f32[48,384]{1,0:T(8,128)S(1)} %get-tuple-element.56), channel_id=1, source_target_pairs={{0,4},{4,0},{8,12},{12,8},{16,20},{20,16},{24,28},{28,24},{1,5},{5... | collective-permute-start | bytes 221192 | tf_op jit(solution)/shard_map/ppermute | solution.py:350
  32.5 5.2 %collective-permute-start.14 = (f32[48,384]{1,0:T(8,128)S(1)}, f32[48,384]{1,0:T(8,128)S(1)}, u32[]{:S(2)}, u32[]{:S(2)}) collective-permute-start(f32[48,384]{1,0:T(8,128)S(1)} %get-tuple-element.59.sent), channel_id=1, source_target_pairs={{0,28},{4,8},{8,4},{12,16},{16,12},{20,24},{24,20},{28,0},{1,29},{... | collective-permute-start | bytes 221192 | tf_op jit(solution)/shard_map/ppermute | solution.py:353
  34.0 6.1 %collective-permute-start.13 = (f32[48,512]{1,0:T(8,128)S(1)}, f32[48,512]{1,0:T(8,128)S(1)}, u32[]{:S(2)}, u32[]{:S(2)}) collective-permute-start(f32[48,512]{1,0:T(8,128)S(1)} %shard_map.91), channel_id=1, source_target_pairs={{0,28},{4,8},{8,4},{12,16},{16,12},{20,24},{24,20},{28,0},{1,29},{... | collective-permute-start | bytes 294920 | tf_op jit(solution)/shard_map/ppermute | solution.py:353
  37.9 1.3 %collective-permute-start.15 = (f32[48,384]{1,0:T(8,128)S(1)}, f32[48,384]{1,0:T(8,128)S(1)}, u32[]{:S(2)}, u32[]{:S(2)}) collective-permute-start(f32[48,384]{1,0:T(8,128)S(1)} %shard_map.94), channel_id=1, source_target_pairs={{0,4},{4,0},{8,12},{12,8},{16,20},{20,16},{24,28},{28,24},{1,5},{5... | collective-permute-start | bytes 221192 | tf_op jit(solution)/shard_map/ppermute | solution.py:350
  40.4 5.0 %collective-permute-start.16 = (f32[48,384]{1,0:T(8,128)S(1)}, f32[48,384]{1,0:T(8,128)S(1)}, u32[]{:S(2)}, u32[]{:S(2)}) collective-permute-start(f32[48,384]{1,0:T(8,128)S(1)} %get-tuple-element.65), channel_id=1, source_target_pairs={{0,28},{4,8},{8,4},{12,16},{16,12},{20,24},{24,20},{28,0},{1,29},{... | collective-permute-start | bytes 221192 | tf_op jit(solution)/shard_map/ppermute | solution.py:353
  41.2 4.2 %collective-permute-start.17 = (f32[48,384]{1,0:T(8,128)S(1)}, f32[48,384]{1,0:T(8,128)S(1)}, u32[]{:S(2)}, u32[]{:S(2)}) collective-permute-start(f32[48,384]{1,0:T(8,128)S(1)} %get-tuple-element.66), channel_id=1, source_target_pairs={{0,4},{4,0},{8,12},{12,8},{16,20},{20,16},{24,28},{28,24},{1,5},{5... | collective-permute-start | bytes 221192 | tf_op jit(solution)/shard_map/ppermute | solution.py:350

commit v9 on v8

--- a/solution.py
+++ b/solution.py
@@ -52,14 +52,12 @@
     return (lax.broadcasted_iota(jnp.int32, shape, 0) == list_row).astype(f32).astype(bf16)
 
 
-def call(kernel, out_shape, args, cost, scalars=(), **kwargs):
+def call(kernel, out_shape, args, cost, **kwargs):
     vmem = pl.BlockSpec(memory_space=pltpu.VMEM)
-    smem = pl.BlockSpec(memory_space=pltpu.SMEM)
-    specs = [smem if i in scalars else vmem for i in range(len(args))]
     return pl.pallas_call(
         kernel,
         out_shape=out_shape,
-        in_specs=specs,
+        in_specs=[vmem] * len(args),
         out_specs=jax.tree.map(lambda _: vmem, out_shape),
         compiler_params=pltpu.CompilerParams(vmem_limit_bytes=VMEM_LIMIT),
         cost_estimate=pl.CostEstimate(flops=cost, bytes_accessed=min(cost, 1 << 20), transcendentals=0),
@@ -275,28 +273,28 @@
 def order_kernel(owner, *refs):
     parts, (hi_out, lo_out) = refs[:-2], refs[-2:]
     here = lax.axis_index("dom")
+    panel = lax.broadcasted_iota(jnp.int32, owner.shape, 1).astype(f32)
     for b, part in enumerate(parts):
-        slot = here ^ b
-        place = jnp.int32(0)
-        for p in range(len(parts)):
-            place = place + jnp.where(owner[p] == slot, p, 0)
+        place = jnp.sum(jnp.where(owner[...] == (here ^ b), panel, 0.0)).astype(jnp.int32)
         hi, lo = split(part[...])
         hi_out[place] = hi
         lo_out[place] = lo
 
 
-def rotated_rows(hi_ref, lo_ref, parts):
-    here = lax.axis_index("band")
-    total = None
-    for r, part in parts:
-        k = here ^ r
-        hi, lo = split(part)
-        rhi, rlo = hi_ref[k], lo_ref[k]
-        term = mm(
-            jnp.concatenate([hi, lo, hi], axis=1), jnp.concatenate([rhi, rhi, rlo], axis=0)
-        )
-        total = term if total is None else total + term
-    return total
+def left_side(rows):
+    hi, lo = split(rows)
+    return jnp.concatenate([hi, lo, hi], axis=1)
+
+
+def rotated(left, hi_ref, lo_ref, distance):
+    k = lax.axis_index("band") ^ distance
+    rhi, rlo = hi_ref[k], lo_ref[k]
+    return mm(left, jnp.concatenate([rhi, rhi, rlo], axis=0))
+
+
+def left_kernel(own, one, two, out):
+    for r, block in enumerate((own, one, two)):
+        out[r] = left_side(block[...])
 
 
 def longer_kernel(block, out):
@@ -305,12 +303,13 @@
     out[rows:, :] = block[: out.shape[0] - rows, :]
 
 
-def rotate_kernel(hi_ref, lo_ref, own, one, two, out):
-    out[...] = rotated_rows(hi_ref, lo_ref, [(0, own[...]), (1, one[...]), (2, two[...])])
+def rotate_kernel(hi_ref, lo_ref, left, out):
+    out[...] = sum(rotated(left[r], hi_ref, lo_ref, r) for r in range(left.shape[0]))
 
 
 def rotate_last_kernel(hi_ref, lo_ref, total, three, column, pick, out, near_out, far_out):
-    rows = total[...] + rotated_rows(hi_ref, lo_ref, [(3, three[: total.shape[0], :])])
+    left = left_side(three[: total.shape[0], :])
+    rows = total[...] + rotated(left, hi_ref, lo_ref, 3)
     out[...] = rows
     send_rows(rows * column[:, :1], pick, near_out, far_out)
 
@@ -325,9 +324,8 @@
     hi, lo = call(
         order_kernel,
         (shape(len(slots), rows, cols, dtype=bf16),) * 2,
-        [owner, *slots],
+        [owner[None, :], *slots],
         0,
-        scalars=(0,),
     )
     return hi.reshape(bands, total // bands, cols), lo.reshape(bands, total // bands, cols)
 
@@ -383,7 +381,8 @@
     one, two, ham_own = lax.optimization_barrier((one, two, ham_own))
     longer = call(longer_kernel, shape(owned + 8, cols), [two], 0)
     three = lax.ppermute(longer, "band", flip(4, 1))
-    two, *parts = lax.optimization_barrier((two, *parts))
+    left = call(left_kernel, shape(3, owned, 3 * cols, dtype=bf16), [states, one, two], 0)
+    left, *parts = lax.optimization_barrier((left, *parts))
     if paired:
         other = [lax.ppermute(part, "dom", near_pairs) for part in parts]
         slots = [part for pair in zip(parts, other) for part in pair]
@@ -393,7 +392,7 @@
         columns = columns.reshape(doms, -1, cols)[owner].reshape(bands, -1, cols)
         rotation = split(columns)
     work = 6 * owned * cols * cols
-    total = call(rotate_kernel, block, [*rotation, states, one, two], 0)
+    total = call(rotate_kernel, block, [*rotation, left], 0)
     turned, to_near, to_far = call(
         rotate_last_kernel,
         (block, halo, halo),

time: 46.5 us -> 46 us (0.989)
  waiting for transfers between devices: 17.2 us -> 16.7 us
    ppermute x4, waiting for transfers between devices: 9.37 us -> 8.72 us  [to_other(): return lax.ppermute(rows, 'dom', far_pairs)]
    pallas_call x17 -> x18, Pallas kernels: 7.12 us -> 6.88 us  [call(): pl.pallas_call(kernel, out_shape=out_shape, in_specs=[vmem] * len(args),...]
  transfers between devices with their start and end apart: 18 -> 18, of which waited for: 12 -> 13; matrix products, arithmetic and copies ran while one was open for 0% -> 0% of each run, Pallas kernels for 23% -> 23%
where the time goes in v9:
time: 46 us; the launch traced here: 45.9 us
  waiting for transfers between devices  16.7 us (36%)
  starting transfers between devices  16.3 us (35%)
  Pallas kernels  12.7 us (28%)
    ppermute x4, waiting for transfers between devices, to_other(): return lax.ppermute(rows, 'dom', far_pairs)  8.72 us
    pallas_call x18, Pallas kernels, call(): pl.pallas_call(kernel, out_shape=out_shape, in_specs=[vmem] * len(args),...  6.88 us
    pallas_call x1, Pallas kernels, assemble(): pl.pallas_call(functools.partial(assemble_kernel, ghost), out_shape=(shap...  5.79 us
    ppermute x4, starting transfers between devices, to_other(): return lax.ppermute(rows, 'dom', far_pairs)  4.97 us
    ppermute x3, starting transfers between devices, shards(): lax.ppermute(own_columns, 'dom', flip(doms, b))  3.55 us
    ppermute x1, starting transfers between devices, shards(): one = lax.ppermute(states, 'band', flip(4, 1))  3.02 us
    ppermute x1, starting transfers between devices, shards(): two = lax.ppermute(states, 'band', flip(4, 2))  2.59 us
    ppermute x1, waiting for transfers between devices, shards(): two = lax.ppermute(states, 'band', flip(4, 2))  2.56 us
  transfers between devices with their start and end apart: 18, of which 13 were waited for; matrix products, arithmetic and copies ran while one was open for 0% of the time, Pallas kernels for 23%

profile of v9, /device:TPU:0, one launch (start us, length us, event | category | flops | bytes accessed | tf_op | source)
XLA Modules:
  0.0 45.9 jit_solution(6596341625890942920)
XLA Ops:
  0.0 0.0 copy-start
  0.0 3.0 %collective-permute-start = (f32[192,384]{1,0:T(8,128)}, f32[192,384]{1,0:T(8,128)S(1)}, u32[]{:S(2)}, u32[]{:S(2)}) collective-permute-start(f32[192,384]{1,0:T(8,128)} %own.1), channel_id=1, source_target_pairs={{0,1},{1,0},{2,3},{3,2},{4,5},{5,4},{6,7},{7,6},{8,9},{9,8},{10,11... | collective-permute-start | bytes 884744 | tf_op jit(solution)/shard_map/ppermute | solution.py:375
  3.0 2.6 %collective-permute-start.1 = (f32[192,384]{1,0:T(8,128)}, f32[192,384]{1,0:T(8,128)S(1)}, u32[]{:S(2)}, u32[]{:S(2)}) collective-permute-start(f32[192,384]{1,0:T(8,128)} %own.1), channel_id=1, source_target_pairs={{0,2},{1,3},{2,0},{3,1},{4,6},{5,7},{6,4},{7,5},{8,10},{9,11},{10,... | collective-permute-start | bytes 884744 | tf_op jit(solution)/shard_map/ppermute | solution.py:376
  5.6 0.0 copy-start.3
  5.7 1.6 %collective-permute-start.2 = (f32[192,384]{1,0:T(8,128)S(1)}, f32[192,384]{1,0:T(8,128)S(1)}, u32[]{:S(2)}, u32[]{:S(2)}) collective-permute-start(f32[192,384]{1,0:T(8,128)S(1)} %constant_dynamic-slice_fusion.refs_0_), channel_id=1, source_target_pairs={{0,8},{4,12},{8,0},{12,4},{16,24},{20,28},{24,16},{28,20},{1,9},{5... | collective-permute-start | bytes 884744 | tf_op jit(solution)/shard_map/ppermute | solution.py:380
  7.2 1.5 %collective-permute-start.3 = (f32[192,384]{1,0:T(8,128)S(1)}, f32[192,384]{1,0:T(8,128)S(1)}, u32[]{:S(2)}, u32[]{:S(2)}) collective-permute-start(f32[192,384]{1,0:T(8,128)S(1)} %constant_dynamic-slice_fusion.refs_0_), channel_id=1, source_target_pairs={{0,16},{4,20},{8,24},{12,28},{16,0},{20,4},{24,8},{28,12},{1,17},{... | collective-permute-start | bytes 884744 | tf_op jit(solution)/shard_map/ppermute | solution.py:380
  8.7 0.5 %collective-permute-start.4 = (f32[192,384]{1,0:T(8,128)S(1)}, f32[192,384]{1,0:T(8,128)S(1)}, u32[]{:S(2)}, u32[]{:S(2)}) collective-permute-start(f32[192,384]{1,0:T(8,128)S(1)} %constant_dynamic-slice_fusion.refs_0_), channel_id=1, source_target_pairs={{0,24},{4,28},{8,16},{12,20},{16,8},{20,12},{24,0},{28,4},{1,25},{... | collective-permute-start | bytes 884744 | tf_op jit(solution)/shard_map/ppermute | solution.py:380
  9.2 5.8 %shard_map.82 = (bf16[288,576]{1,0:T(8,128)(2,1)}, bf16[288,288]{1,0:T(8,128)(2,1)}) custom-call(s32[5,343]{1,0:T(8,128)} %nodes_any.1, f32[5,343,343]{2,1,0:T(8,128)} %ham_any.1), custom_call_target="tpu_custom_call" | custom-call | flops 1355316480 | bytes 2352980 | tf_op jit(solution)/shard_map/pallas_call | solution.py:156
  15.0 1.4 %collective-permute-done.one = f32[192,384]{1,0:T(8,128)S(1)} collective-permute-done((f32[192,384]{1,0:T(8,128)}, f32[192,384]{1,0:T(8,128)S(1)}, u32[]{:S(2)}, u32[]{:S(2)}) %collective-permute-start) | collective-permute-done | bytes 294944 | tf_op jit(solution)/shard_map/ppermute | solution.py:375
  16.4 2.6 %collective-permute-done.1.two.block = f32[192,384]{1,0:T(8,128)S(1)} collective-permute-done((f32[192,384]{1,0:T(8,128)}, f32[192,384]{1,0:T(8,128)S(1)}, u32[]{:S(2)}, u32[]{:S(2)}) %collective-permute-start.1) | collective-permute-done | bytes 294944 | tf_op jit(solution)/shard_map/ppermute | solution.py:376
  19.0 0.0 copy-start.4
  19.0 0.0 copy-start.6
  19.0 0.0 copy-start.7
  19.0 0.0 copy-start.5
  19.1 0.5 %collective-permute-start.9 = (f32[200,384]{1,0:T(8,128)S(1)}, f32[200,384]{1,0:T(8,128)S(1)}, u32[]{:S(2)}, u32[]{:S(2)}) collective-permute-start(f32[200,384]{1,0:T(8,128)S(1)} %shard_map.86), channel_id=1, source_target_pairs={{0,1},{1,0},{2,3},{3,2},{4,5},{5,4},{6,7},{7,6},{8,9},{9,8},{10,11... | collective-permute-start | bytes 921608 | tf_op jit(solution)/shard_map/ppermute | solution.py:383
  19.6 0.0 copy-done.3
  19.6 0.1 shard_map.83.left
  19.7 0.0 collective-permute-done.2.refs_2_
  19.7 1.8 %collective-permute-done.3.refs_4_ = f32[192,384]{1,0:T(8,128)S(1)} collective-permute-done((f32[192,384]{1,0:T(8,128)S(1)}, f32[192,384]{1,0:T(8,128)S(1)}, u32[]{:S(2)}, u32[]{:S(2)}) %collective-permute-start.3) | collective-permute-done | bytes 294944 | tf_op jit(solution)/shard_map/ppermute | solution.py:380
  21.4 0.0 collective-permute-done.4.refs_6_
  21.4 0.0 collective-permute-start.5
  21.5 0.5 %collective-permute-start.6 = (f32[192,384]{1,0:T(8,128)S(1)}, f32[192,384]{1,0:T(8,128)S(1)}, u32[]{:S(2)}, u32[]{:S(2)}) collective-permute-start(f32[192,384]{1,0:T(8,128)S(1)} %collective-permute-done.2.refs_2_), channel_id=1, source_target_pairs={{0,4},{4,0},{8,12},{12,8},{16,20},{20,16},{24,28},{28,24},{1,5},{5... | collective-permute-start | bytes 884744 | tf_op jit(solution)/shard_map/ppermute | solution.py:387
  22.0 0.0 collective-permute-start.7
  22.0 0.5 %collective-permute-start.8 = (f32[192,384]{1,0:T(8,128)S(1)}, f32[192,384]{1,0:T(8,128)S(1)}, u32[]{:S(2)}, u32[]{:S(2)}) collective-permute-start(f32[192,384]{1,0:T(8,128)S(1)} %collective-permute-done.4.refs_6_), channel_id=1, source_target_pairs={{0,4},{4,0},{8,12},{12,8},{16,20},{20,16},{24,28},{28,24},{1,5},{5... | collective-permute-start | bytes 884744 | tf_op jit(solution)/shard_map/ppermute | solution.py:387
  22.5 0.0 copy-done.4
  22.5 0.0 copy-done.7
  22.5 0.3 shard_map.87
  22.8 0.2 collective-permute-done.5.refs_1_
  23.0 0.4 collective-permute-done.6.refs_3_
  23.5 0.4 collective-permute-done.7.refs_5_
  23.9 0.4 collective-permute-done.8.refs_7_
  24.3 0.6 %shard_map.84 = (bf16[8,192,384]{2,1,0:T(8,128)(2,1)S(1)}, bf16[8,192,384]{2,1,0:T(8,128)(2,1)S(1)}) custom-call(s32[1,8]{1,0:T(1,128)S(1)} %bitcast.11, f32[192,384]{1,0:T(8,128)S(1)} %constant_dynamic-slice_fusion.refs_0_, f32[192,384]{1,0:T(8,128)S(1)} %collective-permute-done.5.refs_1_, f32[192,384]{1,0:T(8,128)S(1)} %collective-permute-done.2.refs_2_, ...), custom_call_target="tpu_custom_call" | custom-call | tf_op jit(solution)/shard_map/pallas_call | solution.py:57
  24.9 0.9 %shard_map.85.total = f32[192,384]{1,0:T(8,128)S(1)} custom-call(bf16[4,384,384]{2,1,0:T(8,128)(2,1)S(1)} %bitcast.6, bf16[4,384,384]{2,1,0:T(8,128)(2,1)S(1)} %bitcast.8, bf16[3,192,1152]{2,1,0:T(8,128)(2,1)S(1)} %shard_map.83.left), custom_call_target="tpu_custom_call" | custom-call | tf_op jit(solution)/shard_map/pallas_call | solution.py:57
  25.8 0.1 collective-permute-done.9.three
  26.0 0.7 %shard_map.88 = (f32[192,384]{1,0:T(8,128)S(1)}, f32[48,384]{1,0:T(8,128)S(1)}, f32[48,384]{1,0:T(8,128)S(1)}) custom-call(bf16[4,384,384]{2,1,0:T(8,128)(2,1)S(1)} %bitcast.7, bf16[4,384,384]{2,1,0:T(8,128)(2,1)S(1)} %bitcast.9, f32[192,384]{1,0:T(8,128)S(1)} %shard_map.85.total, f32[200,384]{1,0:T(8,128)S(1)} %collective-permute-done.9.three, ...), custom_call_target="tpu_custom_call" | custom-call | flops 169869312 | bytes 1048576 | tf_op jit(solution)/shard_map/pallas_call | solution.py:57
  26.7 1.2 %collective-permute-start.10 = (f32[48,384]{1,0:T(8,128)S(1)}, f32[48,384]{1,0:T(8,128)S(1)}, u32[]{:S(2)}, u32[]{:S(2)}) collective-permute-start(f32[48,384]{1,0:T(8,128)S(1)} %get-tuple-element.48.far_sent), channel_id=1, source_target_pairs={{0,28},{4,8},{8,4},{12,16},{16,12},{20,24},{24,20},{28,0},{1,29},{... | collective-permute-start | bytes 221192 | tf_op jit(solution)/shard_map/ppermute | solution.py:351
  27.8 0.5 %collective-permute-start.11 = (f32[48,384]{1,0:T(8,128)S(1)}, f32[48,384]{1,0:T(8,128)S(1)}, u32[]{:S(2)}, u32[]{:S(2)}) collective-permute-start(f32[48,384]{1,0:T(8,128)S(1)} %get-tuple-element.49), channel_id=1, source_target_pairs={{0,4},{4,0},{8,12},{12,8},{16,20},{20,16},{24,28},{28,24},{1,5},{5... | collective-permute-start | bytes 221192 | tf_op jit(solution)/shard_map/ppermute | solution.py:348
  28.3 0.1 shard_map.90.ham
  28.5 0.0 copy-done.2
  28.5 0.6 %shard_map.89 = (f32[288,384]{1,0:T(8,128)S(1)}, f32[48,384]{1,0:T(8,128)S(1)}) custom-call(f32[192,384]{1,0:T(8,128)S(1)} %get-tuple-element.50.v.s, f32[192,128]{1,0:T(8,128)S(1)} %get-tuple-element.46.column, bf16[288,576]{1,0:T(8,128)(2,1)S(1)} %copy-done.2, bf16[96,576]{1,0:T(8,128)(2,1)S(1)} %get-tuple-element.47.pick), custom_call_target="tpu_custom_call" | custom-call | flops 191102976 | bytes 1048576 | tf_op jit(solution)/shard_map/pallas_call | solution.py:57
  29.1 2.8 %collective-permute-done.10.far = f32[48,384]{1,0:T(8,128)S(1)} collective-permute-done((f32[48,384]{1,0:T(8,128)S(1)}, f32[48,384]{1,0:T(8,128)S(1)}, u32[]{:S(2)}, u32[]{:S(2)}) %collective-permute-start.10) | collective-permute-done | bytes 73760 | tf_op jit(solution)/shard_map/ppermute | solution.py:351
  31.9 0.0 collective-permute-done.11.near
  31.9 0.2 shard_map.91
  32.2 0.1 collective-permute-start.12
  32.3 1.8 %collective-permute-start.14 = (f32[48,384]{1,0:T(8,128)S(1)}, f32[48,384]{1,0:T(8,128)S(1)}, u32[]{:S(2)}, u32[]{:S(2)}) collective-permute-start(f32[48,384]{1,0:T(8,128)S(1)} %get-tuple-element.59.sent), channel_id=1, source_target_pairs={{0,28},{4,8},{8,4},{12,16},{16,12},{20,24},{24,20},{28,0},{1,29},{... | collective-permute-start | bytes 221192 | tf_op jit(solution)/shard_map/ppermute | solution.py:351
  34.1 0.0 collective-permute-done.12.from_near
  34.1 0.1 shard_map.92
  34.2 1.0 %collective-permute-start.13 = (f32[48,512]{1,0:T(8,128)S(1)}, f32[48,512]{1,0:T(8,128)S(1)}, u32[]{:S(2)}, u32[]{:S(2)}) collective-permute-start(f32[48,512]{1,0:T(8,128)S(1)} %shard_map.92), channel_id=1, source_target_pairs={{0,28},{4,8},{8,4},{12,16},{16,12},{20,24},{24,20},{28,0},{1,29},{... | collective-permute-start | bytes 294920 | tf_op jit(solution)/shard_map/ppermute | solution.py:351
  35.2 0.3 shard_map.93.base
  35.5 0.4 shard_map.94
  35.9 1.8 %collective-permute-done.14.from_far = f32[48,384]{1,0:T(8,128)S(1)} collective-permute-done((f32[48,384]{1,0:T(8,128)S(1)}, f32[48,384]{1,0:T(8,128)S(1)}, u32[]{:S(2)}, u32[]{:S(2)}) %collective-permute-start.14) | collective-permute-done | bytes 73760 | tf_op jit(solution)/shard_map/ppermute | solution.py:351
  37.6 0.1 shard_map.95
  37.8 0.1 collective-permute-start.15
  37.9 0.2 shard_map.96.v.one
  38.1 0.5 %shard_map.97.partial = f32[288,384]{1,0:T(8,128)S(1)} custom-call(f32[192,384]{1,0:T(8,128)S(1)} %shard_map.96.v.one, f32[192,128]{1,0:T(8,128)S(1)} %get-tuple-element.46.column, bf16[288,576]{1,0:T(8,128)(2,1)S(1)} %copy-done.2), custom_call_target="tpu_custom_call" | custom-call | flops 191102976 | bytes 1048576 | tf_op jit(solution)/shard_map/pallas_call | solution.py:57
  38.5 0.6 %collective-permute-done.15.near = f32[48,384]{1,0:T(8,128)S(1)} collective-permute-done((f32[48,384]{1,0:T(8,128)S(1)}, f32[48,384]{1,0:T(8,128)S(1)}, u32[]{:S(2)}, u32[]{:S(2)}) %collective-permute-start.15) | collective-permute-done | bytes 73760 | tf_op jit(solution)/shard_map/ppermute | solution.py:348
  39.1 0.8 %collective-permute-done.13.far = f32[48,512]{1,0:T(8,128)S(1)} collective-permute-done((f32[48,512]{1,0:T(8,128)S(1)}, f32[48,512]{1,0:T(8,128)S(1)}, u32[]{:S(2)}, u32[]{:S(2)}) %collective-permute-start.13) | collective-permute-done | bytes 98336 | tf_op jit(solution)/shard_map/ppermute | solution.py:351
  39.9 0.3 shard_map.98
  40.2 1.0 %collective-permute-start.16 = (f32[48,384]{1,0:T(8,128)S(1)}, f32[48,384]{1,0:T(8,128)S(1)}, u32[]{:S(2)}, u32[]{:S(2)}) collective-permute-start(f32[48,384]{1,0:T(8,128)S(1)} %get-tuple-element.65), channel_id=1, source_target_pairs={{0,28},{4,8},{8,4},{12,16},{16,12},{20,24},{24,20},{28,0},{1,29},{... | collective-permute-start | bytes 221192 | tf_op jit(solution)/shard_map/ppermute | solution.py:351
  41.2 0.0 collective-permute-start.17
  41.2 0.4 shard_map.99.base
  41.6 3.4 %collective-permute-done.16.from_far = f32[48,384]{1,0:T(8,128)S(1)} collective-permute-done((f32[48,384]{1,0:T(8,128)S(1)}, f32[48,384]{1,0:T(8,128)S(1)}, u32[]{:S(2)}, u32[]{:S(2)}) %collective-permute-start.16) | collective-permute-done | bytes 73760 | tf_op jit(solution)/shard_map/ppermute | solution.py:351
  44.9 0.0 collective-permute-done.17.from_near
  44.9 1.0 %shard_map.100 = f32[192,384]{1,0:T(8,128)} custom-call(f32[48,384]{1,0:T(8,128)S(1)} %collective-permute-done.16.from_far, f32[192,384]{1,0:T(8,128)S(1)} %shard_map.99.base, f32[48,384]{1,0:T(8,128)S(1)} %collective-permute-done.17.from_near, f32[192,128]{1,0:T(8,128)S(1)} %get-tuple-element.46.column, bf16[192,144]{1,0:T(8,128)(2,1)S(1)} %get-tuple-element.60.put_near, ...), custom_call_target="tpu_custom_call" | custom-call | flops 42467328 | bytes 1048576 | tf_op jit(solution)/shard_map/pallas_call | solution.py:57
  (8 shorter events, 0.1 us)
Async XLA Ops:
  0.0 5.6 %copy-start = (f32[192,1536]{1,0:T(8,128)S(1)}, f32[192,1536]{1,0:T(8,128)}, u32[]{:S(2)}) copy-start(f32[192,1536]{1,0:T(8,128)} %param.15) | copy-start | bytes 3538948
  0.0 16.4 %collective-permute-start = (f32[192,384]{1,0:T(8,128)}, f32[192,384]{1,0:T(8,128)S(1)}, u32[]{:S(2)}, u32[]{:S(2)}) collective-permute-start(f32[192,384]{1,0:T(8,128)} %own.1), channel_id=1, source_target_pairs={{0,1},{1,0},{2,3},{3,2},{4,5},{5,4},{6,7},{7,6},{8,9},{9,8},{10,11... | collective-permute-start | bytes 884744 | tf_op jit(solution)/shard_map/ppermute | solution.py:375
  3.0 16.0 %collective-permute-start.1 = (f32[192,384]{1,0:T(8,128)}, f32[192,384]{1,0:T(8,128)S(1)}, u32[]{:S(2)}, u32[]{:S(2)}) collective-permute-start(f32[192,384]{1,0:T(8,128)} %own.1), channel_id=1, source_target_pairs={{0,2},{1,3},{2,0},{3,1},{4,6},{5,7},{6,4},{7,5},{8,10},{9,11},{10,... | collective-permute-start | bytes 884744 | tf_op jit(solution)/shard_map/ppermute | solution.py:376
  5.6 13.9 %copy-start.3 = (f32[192,384]{1,0:T(8,128)S(1)}, f32[192,384]{1,0:T(8,128)}, u32[]{:S(2)}) copy-start(f32[192,384]{1,0:T(8,128)} %own.1) | copy-start | bytes 884740
  5.7 14.0 %collective-permute-start.2 = (f32[192,384]{1,0:T(8,128)S(1)}, f32[192,384]{1,0:T(8,128)S(1)}, u32[]{:S(2)}, u32[]{:S(2)}) collective-permute-start(f32[192,384]{1,0:T(8,128)S(1)} %constant_dynamic-slice_fusion.refs_0_), channel_id=1, source_target_pairs={{0,8},{4,12},{8,0},{12,4},{16,24},{20,28},{24,16},{28,20},{1,9},{5... | collective-permute-start | bytes 884744 | tf_op jit(solution)/shard_map/ppermute | solution.py:380
  7.2 14.2 %collective-permute-start.3 = (f32[192,384]{1,0:T(8,128)S(1)}, f32[192,384]{1,0:T(8,128)S(1)}, u32[]{:S(2)}, u32[]{:S(2)}) collective-permute-start(f32[192,384]{1,0:T(8,128)S(1)} %constant_dynamic-slice_fusion.refs_0_), channel_id=1, source_target_pairs={{0,16},{4,20},{8,24},{12,28},{16,0},{20,4},{24,8},{28,12},{1,17},{... | collective-permute-start | bytes 884744 | tf_op jit(solution)/shard_map/ppermute | solution.py:380
  8.7 12.7 %collective-permute-start.4 = (f32[192,384]{1,0:T(8,128)S(1)}, f32[192,384]{1,0:T(8,128)S(1)}, u32[]{:S(2)}, u32[]{:S(2)}) collective-permute-start(f32[192,384]{1,0:T(8,128)S(1)} %constant_dynamic-slice_fusion.refs_0_), channel_id=1, source_target_pairs={{0,24},{4,28},{8,16},{12,20},{16,8},{20,12},{24,0},{28,4},{1,25},{... | collective-permute-start | bytes 884744 | tf_op jit(solution)/shard_map/ppermute | solution.py:380
  19.0 3.5 %copy-start.4 = (f32[192]{0:T(256)S(1)}, f32[192]{0:T(256)}, u32[]{:S(2)}) copy-start(f32[192]{0:T(256)} %param.9) | copy-start | bytes 2308
  19.0 3.5 %copy-start.6 = (s32[48]{0:T(128)S(1)}, s32[48]{0:T(128)}, u32[]{:S(2)}) copy-start(s32[48]{0:T(128)} %param.12) | copy-start | bytes 580
  19.0 3.4 %copy-start.7 = (s32[48]{0:T(128)S(1)}, s32[48]{0:T(128)}, u32[]{:S(2)}) copy-start(s32[48]{0:T(128)} %param.13) | copy-start | bytes 580
  19.0 5.3 %copy-start.5 = (s32[8]{0:T(128)S(1)}, s32[8]{0:T(128)}, u32[]{:S(2)}) copy-start(s32[8]{0:T(128)} %param.14) | copy-start | bytes 100
  19.1 6.9 %collective-permute-start.9 = (f32[200,384]{1,0:T(8,128)S(1)}, f32[200,384]{1,0:T(8,128)S(1)}, u32[]{:S(2)}, u32[]{:S(2)}) collective-permute-start(f32[200,384]{1,0:T(8,128)S(1)} %shard_map.86), channel_id=1, source_target_pairs={{0,1},{1,0},{2,3},{3,2},{4,5},{5,4},{6,7},{7,6},{8,9},{9,8},{10,11... | collective-permute-start | bytes 921608 | tf_op jit(solution)/shard_map/ppermute | solution.py:383
  21.4 1.6 %collective-permute-start.5 = (f32[192,384]{1,0:T(8,128)S(1)}, f32[192,384]{1,0:T(8,128)S(1)}, u32[]{:S(2)}, u32[]{:S(2)}) collective-permute-start(f32[192,384]{1,0:T(8,128)S(1)} %constant_dynamic-slice_fusion.refs_0_), channel_id=1, source_target_pairs={{0,4},{4,0},{8,12},{12,8},{16,20},{20,16},{24,28},{28,24},{1,5},{5... | collective-permute-start | bytes 884744 | tf_op jit(solution)/shard_map/ppermute | solution.py:387
  21.5 2.0 %collective-permute-start.6 = (f32[192,384]{1,0:T(8,128)S(1)}, f32[192,384]{1,0:T(8,128)S(1)}, u32[]{:S(2)}, u32[]{:S(2)}) collective-permute-start(f32[192,384]{1,0:T(8,128)S(1)} %collective-permute-done.2.refs_2_), channel_id=1, source_target_pairs={{0,4},{4,0},{8,12},{12,8},{16,20},{20,16},{24,28},{28,24},{1,5},{5... | collective-permute-start | bytes 884744 | tf_op jit(solution)/shard_map/ppermute | solution.py:387
  22.0 1.9 %collective-permute-start.7 = (f32[192,384]{1,0:T(8,128)S(1)}, f32[192,384]{1,0:T(8,128)S(1)}, u32[]{:S(2)}, u32[]{:S(2)}) collective-permute-start(f32[192,384]{1,0:T(8,128)S(1)} %collective-permute-done.3.refs_4_), channel_id=1, source_target_pairs={{0,4},{4,0},{8,12},{12,8},{16,20},{20,16},{24,28},{28,24},{1,5},{5... | collective-permute-start | bytes 884744 | tf_op jit(solution)/shard_map/ppermute | solution.py:387
  22.0 2.3 %collective-permute-start.8 = (f32[192,384]{1,0:T(8,128)S(1)}, f32[192,384]{1,0:T(8,128)S(1)}, u32[]{:S(2)}, u32[]{:S(2)}) collective-permute-start(f32[192,384]{1,0:T(8,128)S(1)} %collective-permute-done.4.refs_6_), channel_id=1, source_target_pairs={{0,4},{4,0},{8,12},{12,8},{16,20},{20,16},{24,28},{28,24},{1,5},{5... | collective-permute-start | bytes 884744 | tf_op jit(solution)/shard_map/ppermute | solution.py:387
  26.0 2.4 %copy-start.1 = (bf16[288,288]{1,0:T(8,128)(2,1)S(1)}, bf16[288,288]{1,0:T(8,128)(2,1)}, u32[]{:S(2)}) copy-start(bf16[288,288]{1,0:T(8,128)(2,1)} %get-tuple-element.54.ham) | copy-start | bytes 497668
  26.0 2.5 %copy-start.2 = (bf16[288,576]{1,0:T(8,128)(2,1)S(1)}, bf16[288,576]{1,0:T(8,128)(2,1)}, u32[]{:S(2)}) copy-start(bf16[288,576]{1,0:T(8,128)(2,1)} %get-tuple-element.51.ham) | copy-start | bytes 995332
  26.7 5.3 %collective-permute-start.10 = (f32[48,384]{1,0:T(8,128)S(1)}, f32[48,384]{1,0:T(8,128)S(1)}, u32[]{:S(2)}, u32[]{:S(2)}) collective-permute-start(f32[48,384]{1,0:T(8,128)S(1)} %get-tuple-element.48.far_sent), channel_id=1, source_target_pairs={{0,28},{4,8},{8,4},{12,16},{16,12},{20,24},{24,20},{28,0},{1,29},{... | collective-permute-start | bytes 221192 | tf_op jit(solution)/shard_map/ppermute | solution.py:351
  27.8 4.1 %collective-permute-start.11 = (f32[48,384]{1,0:T(8,128)S(1)}, f32[48,384]{1,0:T(8,128)S(1)}, u32[]{:S(2)}, u32[]{:S(2)}) collective-permute-start(f32[48,384]{1,0:T(8,128)S(1)} %get-tuple-element.49), channel_id=1, source_target_pairs={{0,4},{4,0},{8,12},{12,8},{16,20},{20,16},{24,28},{28,24},{1,5},{5... | collective-permute-start | bytes 221192 | tf_op jit(solution)/shard_map/ppermute | solution.py:348
  32.2 1.9 %collective-permute-start.12 = (f32[48,384]{1,0:T(8,128)S(1)}, f32[48,384]{1,0:T(8,128)S(1)}, u32[]{:S(2)}, u32[]{:S(2)}) collective-permute-start(f32[48,384]{1,0:T(8,128)S(1)} %get-tuple-element.56), channel_id=1, source_target_pairs={{0,4},{4,0},{8,12},{12,8},{16,20},{20,16},{24,28},{28,24},{1,5},{5... | collective-permute-start | bytes 221192 | tf_op jit(solution)/shard_map/ppermute | solution.py:348
  32.3 5.4 %collective-permute-start.14 = (f32[48,384]{1,0:T(8,128)S(1)}, f32[48,384]{1,0:T(8,128)S(1)}, u32[]{:S(2)}, u32[]{:S(2)}) collective-permute-start(f32[48,384]{1,0:T(8,128)S(1)} %get-tuple-element.59.sent), channel_id=1, source_target_pairs={{0,28},{4,8},{8,4},{12,16},{16,12},{20,24},{24,20},{28,0},{1,29},{... | collective-permute-start | bytes 221192 | tf_op jit(solution)/shard_map/ppermute | solution.py:351
  34.2 5.7 %collective-permute-start.13 = (f32[48,512]{1,0:T(8,128)S(1)}, f32[48,512]{1,0:T(8,128)S(1)}, u32[]{:S(2)}, u32[]{:S(2)}) collective-permute-start(f32[48,512]{1,0:T(8,128)S(1)} %shard_map.92), channel_id=1, source_target_pairs={{0,28},{4,8},{8,4},{12,16},{16,12},{20,24},{24,20},{28,0},{1,29},{... | collective-permute-start | bytes 294920 | tf_op jit(solution)/shard_map/ppermute | solution.py:351
  37.8 1.3 %collective-permute-start.15 = (f32[48,384]{1,0:T(8,128)S(1)}, f32[48,384]{1,0:T(8,128)S(1)}, u32[]{:S(2)}, u32[]{:S(2)}) collective-permute-start(f32[48,384]{1,0:T(8,128)S(1)} %shard_map.95), channel_id=1, source_target_pairs={{0,4},{4,0},{8,12},{12,8},{16,20},{20,16},{24,28},{28,24},{1,5},{5... | collective-permute-start | bytes 221192 | tf_op jit(solution)/shard_map/ppermute | solution.py:348
  40.2 4.7 %collective-permute-start.16 = (f32[48,384]{1,0:T(8,128)S(1)}, f32[48,384]{1,0:T(8,128)S(1)}, u32[]{:S(2)}, u32[]{:S(2)}) collective-permute-start(f32[48,384]{1,0:T(8,128)S(1)} %get-tuple-element.65), channel_id=1, source_target_pairs={{0,28},{4,8},{8,4},{12,16},{16,12},{20,24},{24,20},{28,0},{1,29},{... | collective-permute-start | bytes 221192 | tf_op jit(solution)/shard_map/ppermute | solution.py:351
  41.2 3.7 %collective-permute-start.17 = (f32[48,384]{1,0:T(8,128)S(1)}, f32[48,384]{1,0:T(8,128)S(1)}, u32[]{:S(2)}, u32[]{:S(2)}) collective-permute-start(f32[48,384]{1,0:T(8,128)S(1)} %get-tuple-element.66), channel_id=1, source_target_pairs={{0,4},{4,0},{8,12},{12,8},{16,20},{20,16},{24,28},{28,24},{1,5},{5... | collective-permute-start | bytes 221192 | tf_op jit(solution)/shard_map/ppermute | solution.py:348

commit v10 on v9

--- a/solution.py
+++ b/solution.py
@@ -27,12 +27,6 @@
 
 def mm(a, b, dims=((1,), (0,))):
     return lax.dot_general(a, b, (dims, ((), ())), preferred_element_type=f32)
-
-
-def select(onehot, x):
-    hi, lo = split(x)
-    rest = (x - hi.astype(f32) - lo.astype(f32)).astype(bf16)
-    return mm(onehot, hi) + mm(onehot, lo) + mm(onehot, rest)
 
 
 def as_column(row):
@@ -76,22 +70,17 @@
     up, dn = up[...], dn[...]
     near, far = jnp.where(even, up, dn), jnp.where(even, dn, up)
     rows = jnp.concatenate([pick_rows(near, owned), pick_rows(far, owned)], axis=0)
-    pick[...] = jnp.concatenate([rows.astype(f32)] * 3, axis=1).astype(bf16)
-    put_near[...] = jnp.concatenate([put_rows(near, owned).astype(f32)] * 3, axis=1).astype(bf16)
-    put_far[...] = jnp.concatenate([put_rows(far, owned).astype(f32)] * 3, axis=1).astype(bf16)
+    pick[...] = jnp.concatenate([rows.astype(f32)] * 2, axis=1).astype(bf16)
+    put_near[...] = jnp.concatenate([put_rows(near, owned).astype(f32)] * 2, axis=1).astype(bf16)
+    put_far[...] = jnp.concatenate([put_rows(far, owned).astype(f32)] * 2, axis=1).astype(bf16)
     for out, these, those in ((far_is_near, far, near), (near_is_far, near, far)):
         same = as_column(these.astype(f32)) == those.astype(f32)
-        out[...] = jnp.concatenate([same.astype(f32)] * 3, axis=1).astype(bf16)
+        out[...] = jnp.concatenate([same.astype(f32)] * 2, axis=1).astype(bf16)
     scales[...] = picked(column[...], pick[...])
 
 
-def split_three(x):
-    hi, lo = split(x)
-    return hi, lo, (x - hi.astype(f32) - lo.astype(f32)).astype(bf16)
-
-
 def picked(x, pick):
-    return mm(pick, jnp.concatenate(split_three(x), axis=0))
+    return mm(pick, jnp.concatenate(split(x), axis=0))
 
 
 def send_rows(x, pick, near_out, far_out):
@@ -102,7 +91,7 @@
 
 
 def placed(rows, put):
-    return mm(put[...], jnp.concatenate(split_three(rows[...]), axis=0))
+    return mm(put[...], jnp.concatenate(split(rows[...]), axis=0))
 
 
 def cell_term(ham, row, ext):
@@ -192,7 +181,7 @@
 
 
 def send_ham_kernel(ham, pick, out):
-    halo, owned = out.shape[0] * 2 // 3, pick.shape[1] // 3
+    halo, owned = out.shape[0] * 2 // 3, pick.shape[1] // 2
     ghost = halo // 2
     out[:halo, :] = ham[owned:, :]
     out[halo:, :] = mm(pick[ghost:, :owned], ham[:owned, :]).astype(bf16)
@@ -351,13 +340,13 @@
         return lax.ppermute(rows, "dom", far_pairs)
 
     ham_own, ham_halo = assemble(cell_nodes, cell_ham, ext, ghost)
-    put = shape(owned, 3 * ghost, dtype=bf16)
-    cross = shape(ghost, 3 * ghost, dtype=bf16)
+    put = shape(owned, 2 * ghost, dtype=bf16)
+    cross = shape(ghost, 2 * ghost, dtype=bf16)
     column, pick, put_near, put_far, far_is_near, near_is_far, scales = call(
         lists_kernel,
         (
             shape(owned, 128),
-            shape(2 * ghost, 3 * owned, dtype=bf16),
+            shape(2 * ghost, 2 * owned, dtype=bf16),
             put,
             put,
             cross,

time: 46 us -> 46 us (level)
  no operation moved by 1% of the time
where the time goes in v10:
time: 46 us; the launch traced here: 45.8 us
  waiting for transfers between devices  16.7 us (36%)
  starting transfers between devices  16.3 us (35%)
  Pallas kernels  12.5 us (27%)
    ppermute x4, waiting for transfers between devices, to_other(): return lax.ppermute(rows, 'dom', far_pairs)  8.76 us
    pallas_call x18, Pallas kernels, call(): pl.pallas_call(kernel, out_shape=out_shape, in_specs=[vmem] * len(args),...  6.68 us
    pallas_call x1, Pallas kernels, assemble(): pl.pallas_call(functools.partial(assemble_kernel, ghost), out_shape=(shap...  5.79 us
    ppermute x4, starting transfers between devices, to_other(): return lax.ppermute(rows, 'dom', far_pairs)  5.01 us
    ppermute x3, starting transfers between devices, shards(): lax.ppermute(own_columns, 'dom', flip(doms, b))  3.55 us
    ppermute x1, starting transfers between devices, shards(): one = lax.ppermute(states, 'band', flip(4, 1))  3.02 us
    ppermute x1, starting transfers between devices, shards(): two = lax.ppermute(states, 'band', flip(4, 2))  2.59 us
    ppermute x1, waiting for transfers between devices, shards(): two = lax.ppermute(states, 'band', flip(4, 2))  2.56 us
  transfers between devices with their start and end apart: 18, of which 13 were waited for; matrix products, arithmetic and copies ran while one was open for 0% of the time, Pallas kernels for 23%

profile of v10, /device:TPU:0, one launch (start us, length us, event | category | flops | bytes accessed | tf_op | source)
XLA Modules:
  0.0 45.8 jit_solution(12478251256298618045)
XLA Ops:
  0.0 0.0 copy-start
  0.0 3.0 %collective-permute-start = (f32[192,384]{1,0:T(8,128)}, f32[192,384]{1,0:T(8,128)S(1)}, u32[]{:S(2)}, u32[]{:S(2)}) collective-permute-start(f32[192,384]{1,0:T(8,128)} %own.1), channel_id=1, source_target_pairs={{0,1},{1,0},{2,3},{3,2},{4,5},{5,4},{6,7},{7,6},{8,9},{9,8},{10,11... | collective-permute-start | bytes 884744 | tf_op jit(solution)/shard_map/ppermute | solution.py:364
  3.0 2.6 %collective-permute-start.1 = (f32[192,384]{1,0:T(8,128)}, f32[192,384]{1,0:T(8,128)S(1)}, u32[]{:S(2)}, u32[]{:S(2)}) collective-permute-start(f32[192,384]{1,0:T(8,128)} %own.1), channel_id=1, source_target_pairs={{0,2},{1,3},{2,0},{3,1},{4,6},{5,7},{6,4},{7,5},{8,10},{9,11},{10,... | collective-permute-start | bytes 884744 | tf_op jit(solution)/shard_map/ppermute | solution.py:365
  5.6 0.0 copy-done
  5.6 0.0 copy-start.3
  5.7 1.6 %collective-permute-start.2 = (f32[192,384]{1,0:T(8,128)S(1)}, f32[192,384]{1,0:T(8,128)S(1)}, u32[]{:S(2)}, u32[]{:S(2)}) collective-permute-start(f32[192,384]{1,0:T(8,128)S(1)} %constant_dynamic-slice_fusion.refs_0_), channel_id=1, source_target_pairs={{0,8},{4,12},{8,0},{12,4},{16,24},{20,28},{24,16},{28,20},{1,9},{5... | collective-permute-start | bytes 884744 | tf_op jit(solution)/shard_map/ppermute | solution.py:369
  7.2 1.5 %collective-permute-start.3 = (f32[192,384]{1,0:T(8,128)S(1)}, f32[192,384]{1,0:T(8,128)S(1)}, u32[]{:S(2)}, u32[]{:S(2)}) collective-permute-start(f32[192,384]{1,0:T(8,128)S(1)} %constant_dynamic-slice_fusion.refs_0_), channel_id=1, source_target_pairs={{0,16},{4,20},{8,24},{12,28},{16,0},{20,4},{24,8},{28,12},{1,17},{... | collective-permute-start | bytes 884744 | tf_op jit(solution)/shard_map/ppermute | solution.py:369
  8.7 0.5 %collective-permute-start.4 = (f32[192,384]{1,0:T(8,128)S(1)}, f32[192,384]{1,0:T(8,128)S(1)}, u32[]{:S(2)}, u32[]{:S(2)}) collective-permute-start(f32[192,384]{1,0:T(8,128)S(1)} %constant_dynamic-slice_fusion.refs_0_), channel_id=1, source_target_pairs={{0,24},{4,28},{8,16},{12,20},{16,8},{20,12},{24,0},{28,4},{1,25},{... | collective-permute-start | bytes 884744 | tf_op jit(solution)/shard_map/ppermute | solution.py:369
  9.2 5.8 %shard_map.82 = (bf16[288,576]{1,0:T(8,128)(2,1)}, bf16[288,288]{1,0:T(8,128)(2,1)}) custom-call(s32[5,343]{1,0:T(8,128)} %nodes_any.1, f32[5,343,343]{2,1,0:T(8,128)} %ham_any.1), custom_call_target="tpu_custom_call" | custom-call | flops 1355316480 | bytes 2352980 | tf_op jit(solution)/shard_map/pallas_call | solution.py:145
  15.0 1.4 %collective-permute-done.one = f32[192,384]{1,0:T(8,128)S(1)} collective-permute-done((f32[192,384]{1,0:T(8,128)}, f32[192,384]{1,0:T(8,128)S(1)}, u32[]{:S(2)}, u32[]{:S(2)}) %collective-permute-start) | collective-permute-done | bytes 294944 | tf_op jit(solution)/shard_map/ppermute | solution.py:364
  16.4 2.6 %collective-permute-done.1.two.block = f32[192,384]{1,0:T(8,128)S(1)} collective-permute-done((f32[192,384]{1,0:T(8,128)}, f32[192,384]{1,0:T(8,128)S(1)}, u32[]{:S(2)}, u32[]{:S(2)}) %collective-permute-start.1) | collective-permute-done | bytes 294944 | tf_op jit(solution)/shard_map/ppermute | solution.py:365
  19.0 0.0 copy-start.4
  19.0 0.0 copy-start.6
  19.0 0.0 copy-start.7
  19.0 0.0 copy-start.5
  19.1 0.5 %collective-permute-start.9 = (f32[200,384]{1,0:T(8,128)S(1)}, f32[200,384]{1,0:T(8,128)S(1)}, u32[]{:S(2)}, u32[]{:S(2)}) collective-permute-start(f32[200,384]{1,0:T(8,128)S(1)} %shard_map.86), channel_id=1, source_target_pairs={{0,1},{1,0},{2,3},{3,2},{4,5},{5,4},{6,7},{7,6},{8,9},{9,8},{10,11... | collective-permute-start | bytes 921608 | tf_op jit(solution)/shard_map/ppermute | solution.py:372
  19.6 0.0 copy-done.3
  19.6 0.1 shard_map.83.left
  19.7 0.0 collective-permute-done.2.refs_2_
  19.7 1.8 %collective-permute-done.3.refs_4_ = f32[192,384]{1,0:T(8,128)S(1)} collective-permute-done((f32[192,384]{1,0:T(8,128)S(1)}, f32[192,384]{1,0:T(8,128)S(1)}, u32[]{:S(2)}, u32[]{:S(2)}) %collective-permute-start.3) | collective-permute-done | bytes 294944 | tf_op jit(solution)/shard_map/ppermute | solution.py:369
  21.4 0.0 collective-permute-done.4.refs_6_
  21.4 0.0 collective-permute-start.5
  21.5 0.5 %collective-permute-start.6 = (f32[192,384]{1,0:T(8,128)S(1)}, f32[192,384]{1,0:T(8,128)S(1)}, u32[]{:S(2)}, u32[]{:S(2)}) collective-permute-start(f32[192,384]{1,0:T(8,128)S(1)} %collective-permute-done.2.refs_2_), channel_id=1, source_target_pairs={{0,4},{4,0},{8,12},{12,8},{16,20},{20,16},{24,28},{28,24},{1,5},{5... | collective-permute-start | bytes 884744 | tf_op jit(solution)/shard_map/ppermute | solution.py:376
  22.0 0.0 collective-permute-start.7
  22.0 0.5 %collective-permute-start.8 = (f32[192,384]{1,0:T(8,128)S(1)}, f32[192,384]{1,0:T(8,128)S(1)}, u32[]{:S(2)}, u32[]{:S(2)}) collective-permute-start(f32[192,384]{1,0:T(8,128)S(1)} %collective-permute-done.4.refs_6_), channel_id=1, source_target_pairs={{0,4},{4,0},{8,12},{12,8},{16,20},{20,16},{24,28},{28,24},{1,5},{5... | collective-permute-start | bytes 884744 | tf_op jit(solution)/shard_map/ppermute | solution.py:376
  22.5 0.3 shard_map.87
  22.8 0.2 collective-permute-done.5.refs_1_
  23.0 0.4 collective-permute-done.6.refs_3_
  23.5 0.4 collective-permute-done.7.refs_5_
  23.9 0.4 collective-permute-done.8.refs_7_
  24.3 0.0 copy-done.5
  24.3 0.6 %shard_map.84 = (bf16[8,192,384]{2,1,0:T(8,128)(2,1)S(1)}, bf16[8,192,384]{2,1,0:T(8,128)(2,1)S(1)}) custom-call(s32[1,8]{1,0:T(1,128)S(1)} %bitcast.11, f32[192,384]{1,0:T(8,128)S(1)} %constant_dynamic-slice_fusion.refs_0_, f32[192,384]{1,0:T(8,128)S(1)} %collective-permute-done.5.refs_1_, f32[192,384]{1,0:T(8,128)S(1)} %collective-permute-done.2.refs_2_, ...), custom_call_target="tpu_custom_call" | custom-call | tf_op jit(solution)/shard_map/pallas_call | solution.py:51
  24.9 0.9 %shard_map.85.total = f32[192,384]{1,0:T(8,128)S(1)} custom-call(bf16[4,384,384]{2,1,0:T(8,128)(2,1)S(1)} %bitcast.6, bf16[4,384,384]{2,1,0:T(8,128)(2,1)S(1)} %bitcast.8, bf16[3,192,1152]{2,1,0:T(8,128)(2,1)S(1)} %shard_map.83.left), custom_call_target="tpu_custom_call" | custom-call | tf_op jit(solution)/shard_map/pallas_call | solution.py:51
  25.8 0.1 collective-permute-done.9.three
  26.0 0.6 %shard_map.88 = (f32[192,384]{1,0:T(8,128)S(1)}, f32[48,384]{1,0:T(8,128)S(1)}, f32[48,384]{1,0:T(8,128)S(1)}) custom-call(bf16[4,384,384]{2,1,0:T(8,128)(2,1)S(1)} %bitcast.7, bf16[4,384,384]{2,1,0:T(8,128)(2,1)S(1)} %bitcast.9, f32[192,384]{1,0:T(8,128)S(1)} %shard_map.85.total, f32[200,384]{1,0:T(8,128)S(1)} %collective-permute-done.9.three, ...), custom_call_target="tpu_custom_call" | custom-call | flops 169869312 | bytes 1048576 | tf_op jit(solution)/shard_map/pallas_call | solution.py:51
  26.6 1.2 %collective-permute-start.10 = (f32[48,384]{1,0:T(8,128)S(1)}, f32[48,384]{1,0:T(8,128)S(1)}, u32[]{:S(2)}, u32[]{:S(2)}) collective-permute-start(f32[48,384]{1,0:T(8,128)S(1)} %get-tuple-element.48.far_sent), channel_id=1, source_target_pairs={{0,28},{4,8},{8,4},{12,16},{16,12},{20,24},{24,20},{28,0},{1,29},{... | collective-permute-start | bytes 221192 | tf_op jit(solution)/shard_map/ppermute | solution.py:340
  27.8 0.5 %collective-permute-start.11 = (f32[48,384]{1,0:T(8,128)S(1)}, f32[48,384]{1,0:T(8,128)S(1)}, u32[]{:S(2)}, u32[]{:S(2)}) collective-permute-start(f32[48,384]{1,0:T(8,128)S(1)} %get-tuple-element.49), channel_id=1, source_target_pairs={{0,4},{4,0},{8,12},{12,8},{16,20},{20,16},{24,28},{28,24},{1,5},{5... | collective-permute-start | bytes 221192 | tf_op jit(solution)/shard_map/ppermute | solution.py:337
  28.3 0.1 shard_map.90.ham
  28.4 0.0 copy-done.2
  28.5 0.6 %shard_map.89 = (f32[288,384]{1,0:T(8,128)S(1)}, f32[48,384]{1,0:T(8,128)S(1)}) custom-call(f32[192,384]{1,0:T(8,128)S(1)} %get-tuple-element.50.v.s, f32[192,128]{1,0:T(8,128)S(1)} %get-tuple-element.46.column, bf16[288,576]{1,0:T(8,128)(2,1)S(1)} %copy-done.2, bf16[96,384]{1,0:T(8,128)(2,1)S(1)} %get-tuple-element.47.pick), custom_call_target="tpu_custom_call" | custom-call | flops 191102976 | bytes 1048576 | tf_op jit(solution)/shard_map/pallas_call | solution.py:51
  29.1 2.8 %collective-permute-done.10.far = f32[48,384]{1,0:T(8,128)S(1)} collective-permute-done((f32[48,384]{1,0:T(8,128)S(1)}, f32[48,384]{1,0:T(8,128)S(1)}, u32[]{:S(2)}, u32[]{:S(2)}) %collective-permute-start.10) | collective-permute-done | bytes 73760 | tf_op jit(solution)/shard_map/ppermute | solution.py:340
  31.9 0.0 collective-permute-done.11.near
  31.9 0.2 shard_map.91
  32.1 0.1 collective-permute-start.12
  32.2 1.8 %collective-permute-start.14 = (f32[48,384]{1,0:T(8,128)S(1)}, f32[48,384]{1,0:T(8,128)S(1)}, u32[]{:S(2)}, u32[]{:S(2)}) collective-permute-start(f32[48,384]{1,0:T(8,128)S(1)} %get-tuple-element.59.sent), channel_id=1, source_target_pairs={{0,28},{4,8},{8,4},{12,16},{16,12},{20,24},{24,20},{28,0},{1,29},{... | collective-permute-start | bytes 221192 | tf_op jit(solution)/shard_map/ppermute | solution.py:340
  34.0 0.0 collective-permute-done.12.from_near
  34.0 0.1 shard_map.92
  34.2 1.0 %collective-permute-start.13 = (f32[48,512]{1,0:T(8,128)S(1)}, f32[48,512]{1,0:T(8,128)S(1)}, u32[]{:S(2)}, u32[]{:S(2)}) collective-permute-start(f32[48,512]{1,0:T(8,128)S(1)} %shard_map.92), channel_id=1, source_target_pairs={{0,28},{4,8},{8,4},{12,16},{16,12},{20,24},{24,20},{28,0},{1,29},{... | collective-permute-start | bytes 294920 | tf_op jit(solution)/shard_map/ppermute | solution.py:340
  35.1 0.3 shard_map.93.base
  35.4 0.4 shard_map.94
  35.8 1.8 %collective-permute-done.14.from_far = f32[48,384]{1,0:T(8,128)S(1)} collective-permute-done((f32[48,384]{1,0:T(8,128)S(1)}, f32[48,384]{1,0:T(8,128)S(1)}, u32[]{:S(2)}, u32[]{:S(2)}) %collective-permute-start.14) | collective-permute-done | bytes 73760 | tf_op jit(solution)/shard_map/ppermute | solution.py:340
  37.6 0.1 shard_map.95
  37.7 0.1 collective-permute-start.15
  37.8 0.2 shard_map.96.v.one
  38.0 0.5 %shard_map.97.partial = f32[288,384]{1,0:T(8,128)S(1)} custom-call(f32[192,384]{1,0:T(8,128)S(1)} %shard_map.96.v.one, f32[192,128]{1,0:T(8,128)S(1)} %get-tuple-element.46.column, bf16[288,576]{1,0:T(8,128)(2,1)S(1)} %copy-done.2), custom_call_target="tpu_custom_call" | custom-call | flops 191102976 | bytes 1048576 | tf_op jit(solution)/shard_map/pallas_call | solution.py:51
  38.4 0.6 %collective-permute-done.15.near = f32[48,384]{1,0:T(8,128)S(1)} collective-permute-done((f32[48,384]{1,0:T(8,128)S(1)}, f32[48,384]{1,0:T(8,128)S(1)}, u32[]{:S(2)}, u32[]{:S(2)}) %collective-permute-start.15) | collective-permute-done | bytes 73760 | tf_op jit(solution)/shard_map/ppermute | solution.py:337
  39.0 0.8 %collective-permute-done.13.far = f32[48,512]{1,0:T(8,128)S(1)} collective-permute-done((f32[48,512]{1,0:T(8,128)S(1)}, f32[48,512]{1,0:T(8,128)S(1)}, u32[]{:S(2)}, u32[]{:S(2)}) %collective-permute-start.13) | collective-permute-done | bytes 98336 | tf_op jit(solution)/shard_map/ppermute | solution.py:340
  39.9 0.3 shard_map.98
  40.1 1.0 %collective-permute-start.16 = (f32[48,384]{1,0:T(8,128)S(1)}, f32[48,384]{1,0:T(8,128)S(1)}, u32[]{:S(2)}, u32[]{:S(2)}) collective-permute-start(f32[48,384]{1,0:T(8,128)S(1)} %get-tuple-element.65), channel_id=1, source_target_pairs={{0,28},{4,8},{8,4},{12,16},{16,12},{20,24},{24,20},{28,0},{1,29},{... | collective-permute-start | bytes 221192 | tf_op jit(solution)/shard_map/ppermute | solution.py:340
  41.2 0.0 collective-permute-start.17
  41.2 0.4 shard_map.99.base
  41.5 3.3 %collective-permute-done.16.from_far = f32[48,384]{1,0:T(8,128)S(1)} collective-permute-done((f32[48,384]{1,0:T(8,128)S(1)}, f32[48,384]{1,0:T(8,128)S(1)}, u32[]{:S(2)}, u32[]{:S(2)}) %collective-permute-start.16) | collective-permute-done | bytes 73760 | tf_op jit(solution)/shard_map/ppermute | solution.py:340
  44.9 0.0 collective-permute-done.17.from_near
  44.9 0.9 %shard_map.100 = f32[192,384]{1,0:T(8,128)} custom-call(f32[48,384]{1,0:T(8,128)S(1)} %collective-permute-done.16.from_far, f32[192,384]{1,0:T(8,128)S(1)} %shard_map.99.base, f32[48,384]{1,0:T(8,128)S(1)} %collective-permute-done.17.from_near, f32[192,128]{1,0:T(8,128)S(1)} %get-tuple-element.46.column, bf16[192,96]{1,0:T(8,128)(2,1)S(1)} %get-tuple-element.60.put_near, ...), custom_call_target="tpu_custom_call" | custom-call | flops 42467328 | bytes 1048576 | tf_op jit(solution)/shard_map/pallas_call | solution.py:51
  (8 shorter events, 0.1 us)
Async XLA Ops:
  0.0 5.6 %copy-start = (f32[192,1536]{1,0:T(8,128)S(1)}, f32[192,1536]{1,0:T(8,128)}, u32[]{:S(2)}) copy-start(f32[192,1536]{1,0:T(8,128)} %param.15) | copy-start | bytes 3538948
  0.0 16.4 %collective-permute-start = (f32[192,384]{1,0:T(8,128)}, f32[192,384]{1,0:T(8,128)S(1)}, u32[]{:S(2)}, u32[]{:S(2)}) collective-permute-start(f32[192,384]{1,0:T(8,128)} %own.1), channel_id=1, source_target_pairs={{0,1},{1,0},{2,3},{3,2},{4,5},{5,4},{6,7},{7,6},{8,9},{9,8},{10,11... | collective-permute-start | bytes 884744 | tf_op jit(solution)/shard_map/ppermute | solution.py:364
  3.0 16.0 %collective-permute-start.1 = (f32[192,384]{1,0:T(8,128)}, f32[192,384]{1,0:T(8,128)S(1)}, u32[]{:S(2)}, u32[]{:S(2)}) collective-permute-start(f32[192,384]{1,0:T(8,128)} %own.1), channel_id=1, source_target_pairs={{0,2},{1,3},{2,0},{3,1},{4,6},{5,7},{6,4},{7,5},{8,10},{9,11},{10,... | collective-permute-start | bytes 884744 | tf_op jit(solution)/shard_map/ppermute | solution.py:365
  5.6 13.9 %copy-start.3 = (f32[192,384]{1,0:T(8,128)S(1)}, f32[192,384]{1,0:T(8,128)}, u32[]{:S(2)}) copy-start(f32[192,384]{1,0:T(8,128)} %own.1) | copy-start | bytes 884740
  5.7 14.0 %collective-permute-start.2 = (f32[192,384]{1,0:T(8,128)S(1)}, f32[192,384]{1,0:T(8,128)S(1)}, u32[]{:S(2)}, u32[]{:S(2)}) collective-permute-start(f32[192,384]{1,0:T(8,128)S(1)} %constant_dynamic-slice_fusion.refs_0_), channel_id=1, source_target_pairs={{0,8},{4,12},{8,0},{12,4},{16,24},{20,28},{24,16},{28,20},{1,9},{5... | collective-permute-start | bytes 884744 | tf_op jit(solution)/shard_map/ppermute | solution.py:369
  7.2 14.2 %collective-permute-start.3 = (f32[192,384]{1,0:T(8,128)S(1)}, f32[192,384]{1,0:T(8,128)S(1)}, u32[]{:S(2)}, u32[]{:S(2)}) collective-permute-start(f32[192,384]{1,0:T(8,128)S(1)} %constant_dynamic-slice_fusion.refs_0_), channel_id=1, source_target_pairs={{0,16},{4,20},{8,24},{12,28},{16,0},{20,4},{24,8},{28,12},{1,17},{... | collective-permute-start | bytes 884744 | tf_op jit(solution)/shard_map/ppermute | solution.py:369
  8.7 12.7 %collective-permute-start.4 = (f32[192,384]{1,0:T(8,128)S(1)}, f32[192,384]{1,0:T(8,128)S(1)}, u32[]{:S(2)}, u32[]{:S(2)}) collective-permute-start(f32[192,384]{1,0:T(8,128)S(1)} %constant_dynamic-slice_fusion.refs_0_), channel_id=1, source_target_pairs={{0,24},{4,28},{8,16},{12,20},{16,8},{20,12},{24,0},{28,4},{1,25},{... | collective-permute-start | bytes 884744 | tf_op jit(solution)/shard_map/ppermute | solution.py:369
  19.0 3.5 %copy-start.4 = (f32[192]{0:T(256)S(1)}, f32[192]{0:T(256)}, u32[]{:S(2)}) copy-start(f32[192]{0:T(256)} %param.9) | copy-start | bytes 2308
  19.0 3.5 %copy-start.6 = (s32[48]{0:T(128)S(1)}, s32[48]{0:T(128)}, u32[]{:S(2)}) copy-start(s32[48]{0:T(128)} %param.12) | copy-start | bytes 580
  19.0 3.4 %copy-start.7 = (s32[48]{0:T(128)S(1)}, s32[48]{0:T(128)}, u32[]{:S(2)}) copy-start(s32[48]{0:T(128)} %param.13) | copy-start | bytes 580
  19.0 5.3 %copy-start.5 = (s32[8]{0:T(128)S(1)}, s32[8]{0:T(128)}, u32[]{:S(2)}) copy-start(s32[8]{0:T(128)} %param.14) | copy-start | bytes 100
  19.1 6.9 %collective-permute-start.9 = (f32[200,384]{1,0:T(8,128)S(1)}, f32[200,384]{1,0:T(8,128)S(1)}, u32[]{:S(2)}, u32[]{:S(2)}) collective-permute-start(f32[200,384]{1,0:T(8,128)S(1)} %shard_map.86), channel_id=1, source_target_pairs={{0,1},{1,0},{2,3},{3,2},{4,5},{5,4},{6,7},{7,6},{8,9},{9,8},{10,11... | collective-permute-start | bytes 921608 | tf_op jit(solution)/shard_map/ppermute | solution.py:372
  21.4 1.6 %collective-permute-start.5 = (f32[192,384]{1,0:T(8,128)S(1)}, f32[192,384]{1,0:T(8,128)S(1)}, u32[]{:S(2)}, u32[]{:S(2)}) collective-permute-start(f32[192,384]{1,0:T(8,128)S(1)} %constant_dynamic-slice_fusion.refs_0_), channel_id=1, source_target_pairs={{0,4},{4,0},{8,12},{12,8},{16,20},{20,16},{24,28},{28,24},{1,5},{5... | collective-permute-start | bytes 884744 | tf_op jit(solution)/shard_map/ppermute | solution.py:376
  21.5 2.0 %collective-permute-start.6 = (f32[192,384]{1,0:T(8,128)S(1)}, f32[192,384]{1,0:T(8,128)S(1)}, u32[]{:S(2)}, u32[]{:S(2)}) collective-permute-start(f32[192,384]{1,0:T(8,128)S(1)} %collective-permute-done.2.refs_2_), channel_id=1, source_target_pairs={{0,4},{4,0},{8,12},{12,8},{16,20},{20,16},{24,28},{28,24},{1,5},{5... | collective-permute-start | bytes 884744 | tf_op jit(solution)/shard_map/ppermute | solution.py:376
  22.0 1.9 %collective-permute-start.7 = (f32[192,384]{1,0:T(8,128)S(1)}, f32[192,384]{1,0:T(8,128)S(1)}, u32[]{:S(2)}, u32[]{:S(2)}) collective-permute-start(f32[192,384]{1,0:T(8,128)S(1)} %collective-permute-done.3.refs_4_), channel_id=1, source_target_pairs={{0,4},{4,0},{8,12},{12,8},{16,20},{20,16},{24,28},{28,24},{1,5},{5... | collective-permute-start | bytes 884744 | tf_op jit(solution)/shard_map/ppermute | solution.py:376
  22.0 2.3 %collective-permute-start.8 = (f32[192,384]{1,0:T(8,128)S(1)}, f32[192,384]{1,0:T(8,128)S(1)}, u32[]{:S(2)}, u32[]{:S(2)}) collective-permute-start(f32[192,384]{1,0:T(8,128)S(1)} %collective-permute-done.4.refs_6_), channel_id=1, source_target_pairs={{0,4},{4,0},{8,12},{12,8},{16,20},{20,16},{24,28},{28,24},{1,5},{5... | collective-permute-start | bytes 884744 | tf_op jit(solution)/shard_map/ppermute | solution.py:376
  26.0 2.3 %copy-start.1 = (bf16[288,288]{1,0:T(8,128)(2,1)S(1)}, bf16[288,288]{1,0:T(8,128)(2,1)}, u32[]{:S(2)}) copy-start(bf16[288,288]{1,0:T(8,128)(2,1)} %get-tuple-element.54.ham) | copy-start | bytes 497668
  26.0 2.5 %copy-start.2 = (bf16[288,576]{1,0:T(8,128)(2,1)S(1)}, bf16[288,576]{1,0:T(8,128)(2,1)}, u32[]{:S(2)}) copy-start(bf16[288,576]{1,0:T(8,128)(2,1)} %get-tuple-element.51.ham) | copy-start | bytes 995332
  26.6 5.3 %collective-permute-start.10 = (f32[48,384]{1,0:T(8,128)S(1)}, f32[48,384]{1,0:T(8,128)S(1)}, u32[]{:S(2)}, u32[]{:S(2)}) collective-permute-start(f32[48,384]{1,0:T(8,128)S(1)} %get-tuple-element.48.far_sent), channel_id=1, source_target_pairs={{0,28},{4,8},{8,4},{12,16},{16,12},{20,24},{24,20},{28,0},{1,29},{... | collective-permute-start | bytes 221192 | tf_op jit(solution)/shard_map/ppermute | solution.py:340
  27.8 4.1 %collective-permute-start.11 = (f32[48,384]{1,0:T(8,128)S(1)}, f32[48,384]{1,0:T(8,128)S(1)}, u32[]{:S(2)}, u32[]{:S(2)}) collective-permute-start(f32[48,384]{1,0:T(8,128)S(1)} %get-tuple-element.49), channel_id=1, source_target_pairs={{0,4},{4,0},{8,12},{12,8},{16,20},{20,16},{24,28},{28,24},{1,5},{5... | collective-permute-start | bytes 221192 | tf_op jit(solution)/shard_map/ppermute | solution.py:337
  32.1 1.9 %collective-permute-start.12 = (f32[48,384]{1,0:T(8,128)S(1)}, f32[48,384]{1,0:T(8,128)S(1)}, u32[]{:S(2)}, u32[]{:S(2)}) collective-permute-start(f32[48,384]{1,0:T(8,128)S(1)} %get-tuple-element.56), channel_id=1, source_target_pairs={{0,4},{4,0},{8,12},{12,8},{16,20},{20,16},{24,28},{28,24},{1,5},{5... | collective-permute-start | bytes 221192 | tf_op jit(solution)/shard_map/ppermute | solution.py:337
  32.2 5.3 %collective-permute-start.14 = (f32[48,384]{1,0:T(8,128)S(1)}, f32[48,384]{1,0:T(8,128)S(1)}, u32[]{:S(2)}, u32[]{:S(2)}) collective-permute-start(f32[48,384]{1,0:T(8,128)S(1)} %get-tuple-element.59.sent), channel_id=1, source_target_pairs={{0,28},{4,8},{8,4},{12,16},{16,12},{20,24},{24,20},{28,0},{1,29},{... | collective-permute-start | bytes 221192 | tf_op jit(solution)/shard_map/ppermute | solution.py:340
  34.2 5.7 %collective-permute-start.13 = (f32[48,512]{1,0:T(8,128)S(1)}, f32[48,512]{1,0:T(8,128)S(1)}, u32[]{:S(2)}, u32[]{:S(2)}) collective-permute-start(f32[48,512]{1,0:T(8,128)S(1)} %shard_map.92), channel_id=1, source_target_pairs={{0,28},{4,8},{8,4},{12,16},{16,12},{20,24},{24,20},{28,0},{1,29},{... | collective-permute-start | bytes 294920 | tf_op jit(solution)/shard_map/ppermute | solution.py:340
  37.7 1.3 %collective-permute-start.15 = (f32[48,384]{1,0:T(8,128)S(1)}, f32[48,384]{1,0:T(8,128)S(1)}, u32[]{:S(2)}, u32[]{:S(2)}) collective-permute-start(f32[48,384]{1,0:T(8,128)S(1)} %shard_map.95), channel_id=1, source_target_pairs={{0,4},{4,0},{8,12},{12,8},{16,20},{20,16},{24,28},{28,24},{1,5},{5... | collective-permute-start | bytes 221192 | tf_op jit(solution)/shard_map/ppermute | solution.py:337
  40.1 4.7 %collective-permute-start.16 = (f32[48,384]{1,0:T(8,128)S(1)}, f32[48,384]{1,0:T(8,128)S(1)}, u32[]{:S(2)}, u32[]{:S(2)}) collective-permute-start(f32[48,384]{1,0:T(8,128)S(1)} %get-tuple-element.65), channel_id=1, source_target_pairs={{0,28},{4,8},{8,4},{12,16},{16,12},{20,24},{24,20},{28,0},{1,29},{... | collective-permute-start | bytes 221192 | tf_op jit(solution)/shard_map/ppermute | solution.py:340
  41.2 3.7 %collective-permute-start.17 = (f32[48,384]{1,0:T(8,128)S(1)}, f32[48,384]{1,0:T(8,128)S(1)}, u32[]{:S(2)}, u32[]{:S(2)}) collective-permute-start(f32[48,384]{1,0:T(8,128)S(1)} %get-tuple-element.66), channel_id=1, source_target_pairs={{0,4},{4,0},{8,12},{12,8},{16,20},{20,16},{24,28},{28,24},{1,5},{5... | collective-permute-start | bytes 221192 | tf_op jit(solution)/shard_map/ppermute | solution.py:337

commit v11 on v10

--- a/solution.py
+++ b/solution.py
@@ -368,7 +368,7 @@
     if paired:
         parts += [lax.ppermute(own_columns, "dom", flip(doms, b)) for b in (2, 4, 6)]
     one, two, ham_own = lax.optimization_barrier((one, two, ham_own))
-    longer = call(longer_kernel, shape(owned + 8, cols), [two], 0)
+    longer = call(longer_kernel, shape(owned + 1, cols), [two], 0)
     three = lax.ppermute(longer, "band", flip(4, 1))
     left = call(left_kernel, shape(3, owned, 3 * cols, dtype=bf16), [states, one, two], 0)
     left, *parts = lax.optimization_barrier((left, *parts))

time: 46 us -> 46 us (level)
  no operation moved by 1% of the time
where the time goes in v11:
time: 46 us; the launch traced here: 45.8 us
  waiting for transfers between devices  16.7 us (36%)
  starting transfers between devices  16.3 us (35%)
  Pallas kernels  12.5 us (27%)
    ppermute x4, waiting for transfers between devices, to_other(): return lax.ppermute(rows, 'dom', far_pairs)  8.76 us
    pallas_call x18, Pallas kernels, call(): pl.pallas_call(kernel, out_shape=out_shape, in_specs=[vmem] * len(args),...  6.68 us
    pallas_call x1, Pallas kernels, assemble(): pl.pallas_call(functools.partial(assemble_kernel, ghost), out_shape=(shap...  5.79 us
    ppermute x4, starting transfers between devices, to_other(): return lax.ppermute(rows, 'dom', far_pairs)  5.01 us
    ppermute x3, starting transfers between devices, shards(): lax.ppermute(own_columns, 'dom', flip(doms, b))  3.55 us
    ppermute x1, starting transfers between devices, shards(): one = lax.ppermute(states, 'band', flip(4, 1))  3.02 us
    ppermute x1, starting transfers between devices, shards(): two = lax.ppermute(states, 'band', flip(4, 2))  2.59 us
    ppermute x1, waiting for transfers between devices, shards(): two = lax.ppermute(states, 'band', flip(4, 2))  2.56 us
  transfers between devices with their start and end apart: 18, of which 13 were waited for; matrix products, arithmetic and copies ran while one was open for 0% of the time, Pallas kernels for 23%

profile of v11, /device:TPU:0, one launch (start us, length us, event | category | flops | bytes accessed | tf_op | source)
XLA Modules:
  0.0 45.8 jit_solution(2510713697147234182)
XLA Ops:
  0.0 0.0 copy-start
  0.0 3.0 %collective-permute-start = (f32[192,384]{1,0:T(8,128)}, f32[192,384]{1,0:T(8,128)S(1)}, u32[]{:S(2)}, u32[]{:S(2)}) collective-permute-start(f32[192,384]{1,0:T(8,128)} %own.1), channel_id=1, source_target_pairs={{0,1},{1,0},{2,3},{3,2},{4,5},{5,4},{6,7},{7,6},{8,9},{9,8},{10,11... | collective-permute-start | bytes 884744 | tf_op jit(solution)/shard_map/ppermute | solution.py:364
  3.0 2.6 %collective-permute-start.1 = (f32[192,384]{1,0:T(8,128)}, f32[192,384]{1,0:T(8,128)S(1)}, u32[]{:S(2)}, u32[]{:S(2)}) collective-permute-start(f32[192,384]{1,0:T(8,128)} %own.1), channel_id=1, source_target_pairs={{0,2},{1,3},{2,0},{3,1},{4,6},{5,7},{6,4},{7,5},{8,10},{9,11},{10,... | collective-permute-start | bytes 884744 | tf_op jit(solution)/shard_map/ppermute | solution.py:365
  5.6 0.0 copy-done
  5.6 0.0 copy-start.3
  5.7 1.6 %collective-permute-start.2 = (f32[192,384]{1,0:T(8,128)S(1)}, f32[192,384]{1,0:T(8,128)S(1)}, u32[]{:S(2)}, u32[]{:S(2)}) collective-permute-start(f32[192,384]{1,0:T(8,128)S(1)} %constant_dynamic-slice_fusion.refs_0_), channel_id=1, source_target_pairs={{0,8},{4,12},{8,0},{12,4},{16,24},{20,28},{24,16},{28,20},{1,9},{5... | collective-permute-start | bytes 884744 | tf_op jit(solution)/shard_map/ppermute | solution.py:369
  7.2 1.5 %collective-permute-start.3 = (f32[192,384]{1,0:T(8,128)S(1)}, f32[192,384]{1,0:T(8,128)S(1)}, u32[]{:S(2)}, u32[]{:S(2)}) collective-permute-start(f32[192,384]{1,0:T(8,128)S(1)} %constant_dynamic-slice_fusion.refs_0_), channel_id=1, source_target_pairs={{0,16},{4,20},{8,24},{12,28},{16,0},{20,4},{24,8},{28,12},{1,17},{... | collective-permute-start | bytes 884744 | tf_op jit(solution)/shard_map/ppermute | solution.py:369
  8.7 0.5 %collective-permute-start.4 = (f32[192,384]{1,0:T(8,128)S(1)}, f32[192,384]{1,0:T(8,128)S(1)}, u32[]{:S(2)}, u32[]{:S(2)}) collective-permute-start(f32[192,384]{1,0:T(8,128)S(1)} %constant_dynamic-slice_fusion.refs_0_), channel_id=1, source_target_pairs={{0,24},{4,28},{8,16},{12,20},{16,8},{20,12},{24,0},{28,4},{1,25},{... | collective-permute-start | bytes 884744 | tf_op jit(solution)/shard_map/ppermute | solution.py:369
  9.2 5.8 %shard_map.82 = (bf16[288,576]{1,0:T(8,128)(2,1)}, bf16[288,288]{1,0:T(8,128)(2,1)}) custom-call(s32[5,343]{1,0:T(8,128)} %nodes_any.1, f32[5,343,343]{2,1,0:T(8,128)} %ham_any.1), custom_call_target="tpu_custom_call" | custom-call | flops 1355316480 | bytes 2352980 | tf_op jit(solution)/shard_map/pallas_call | solution.py:145
  15.0 1.4 %collective-permute-done.one = f32[192,384]{1,0:T(8,128)S(1)} collective-permute-done((f32[192,384]{1,0:T(8,128)}, f32[192,384]{1,0:T(8,128)S(1)}, u32[]{:S(2)}, u32[]{:S(2)}) %collective-permute-start) | collective-permute-done | bytes 294944 | tf_op jit(solution)/shard_map/ppermute | solution.py:364
  16.4 2.6 %collective-permute-done.1.two.block = f32[192,384]{1,0:T(8,128)S(1)} collective-permute-done((f32[192,384]{1,0:T(8,128)}, f32[192,384]{1,0:T(8,128)S(1)}, u32[]{:S(2)}, u32[]{:S(2)}) %collective-permute-start.1) | collective-permute-done | bytes 294944 | tf_op jit(solution)/shard_map/ppermute | solution.py:365
  19.0 0.0 copy-start.4
  19.0 0.0 copy-start.6
  19.0 0.0 copy-start.7
  19.0 0.0 copy-start.5
  19.1 0.5 %collective-permute-start.9 = (f32[193,384]{1,0:T(8,128)S(1)}, f32[193,384]{1,0:T(8,128)S(1)}, u32[]{:S(2)}, u32[]{:S(2)}) collective-permute-start(f32[193,384]{1,0:T(8,128)S(1)} %shard_map.86), channel_id=1, source_target_pairs={{0,1},{1,0},{2,3},{3,2},{4,5},{5,4},{6,7},{7,6},{8,9},{9,8},{10,11... | collective-permute-start | bytes 889352 | tf_op jit(solution)/shard_map/ppermute | solution.py:372
  19.6 0.0 copy-done.3
  19.6 0.1 shard_map.83.left
  19.7 0.0 collective-permute-done.2.refs_2_
  19.7 1.8 %collective-permute-done.3.refs_4_ = f32[192,384]{1,0:T(8,128)S(1)} collective-permute-done((f32[192,384]{1,0:T(8,128)S(1)}, f32[192,384]{1,0:T(8,128)S(1)}, u32[]{:S(2)}, u32[]{:S(2)}) %collective-permute-start.3) | collective-permute-done | bytes 294944 | tf_op jit(solution)/shard_map/ppermute | solution.py:369
  21.4 0.0 collective-permute-done.4.refs_6_
  21.4 0.0 collective-permute-start.5
  21.5 0.5 %collective-permute-start.6 = (f32[192,384]{1,0:T(8,128)S(1)}, f32[192,384]{1,0:T(8,128)S(1)}, u32[]{:S(2)}, u32[]{:S(2)}) collective-permute-start(f32[192,384]{1,0:T(8,128)S(1)} %collective-permute-done.2.refs_2_), channel_id=1, source_target_pairs={{0,4},{4,0},{8,12},{12,8},{16,20},{20,16},{24,28},{28,24},{1,5},{5... | collective-permute-start | bytes 884744 | tf_op jit(solution)/shard_map/ppermute | solution.py:376
  22.0 0.0 collective-permute-start.7
  22.0 0.5 %collective-permute-start.8 = (f32[192,384]{1,0:T(8,128)S(1)}, f32[192,384]{1,0:T(8,128)S(1)}, u32[]{:S(2)}, u32[]{:S(2)}) collective-permute-start(f32[192,384]{1,0:T(8,128)S(1)} %collective-permute-done.4.refs_6_), channel_id=1, source_target_pairs={{0,4},{4,0},{8,12},{12,8},{16,20},{20,16},{24,28},{28,24},{1,5},{5... | collective-permute-start | bytes 884744 | tf_op jit(solution)/shard_map/ppermute | solution.py:376
  22.5 0.3 shard_map.87
  22.8 0.2 collective-permute-done.5.refs_1_
  23.0 0.4 collective-permute-done.6.refs_3_
  23.5 0.4 collective-permute-done.7.refs_5_
  23.9 0.4 collective-permute-done.8.refs_7_
  24.3 0.0 copy-done.5
  24.3 0.6 %shard_map.84 = (bf16[8,192,384]{2,1,0:T(8,128)(2,1)S(1)}, bf16[8,192,384]{2,1,0:T(8,128)(2,1)S(1)}) custom-call(s32[1,8]{1,0:T(1,128)S(1)} %bitcast.11, f32[192,384]{1,0:T(8,128)S(1)} %constant_dynamic-slice_fusion.refs_0_, f32[192,384]{1,0:T(8,128)S(1)} %collective-permute-done.5.refs_1_, f32[192,384]{1,0:T(8,128)S(1)} %collective-permute-done.2.refs_2_, ...), custom_call_target="tpu_custom_call" | custom-call | tf_op jit(solution)/shard_map/pallas_call | solution.py:51
  24.9 0.9 %shard_map.85.total = f32[192,384]{1,0:T(8,128)S(1)} custom-call(bf16[4,384,384]{2,1,0:T(8,128)(2,1)S(1)} %bitcast.6, bf16[4,384,384]{2,1,0:T(8,128)(2,1)S(1)} %bitcast.8, bf16[3,192,1152]{2,1,0:T(8,128)(2,1)S(1)} %shard_map.83.left), custom_call_target="tpu_custom_call" | custom-call | tf_op jit(solution)/shard_map/pallas_call | solution.py:51
  25.8 0.1 collective-permute-done.9.three
  26.0 0.6 %shard_map.88 = (f32[192,384]{1,0:T(8,128)S(1)}, f32[48,384]{1,0:T(8,128)S(1)}, f32[48,384]{1,0:T(8,128)S(1)}) custom-call(bf16[4,384,384]{2,1,0:T(8,128)(2,1)S(1)} %bitcast.7, bf16[4,384,384]{2,1,0:T(8,128)(2,1)S(1)} %bitcast.9, f32[192,384]{1,0:T(8,128)S(1)} %shard_map.85.total, f32[193,384]{1,0:T(8,128)S(1)} %collective-permute-done.9.three, ...), custom_call_target="tpu_custom_call" | custom-call | flops 169869312 | bytes 1048576 | tf_op jit(solution)/shard_map/pallas_call | solution.py:51
  26.6 1.2 %collective-permute-start.10 = (f32[48,384]{1,0:T(8,128)S(1)}, f32[48,384]{1,0:T(8,128)S(1)}, u32[]{:S(2)}, u32[]{:S(2)}) collective-permute-start(f32[48,384]{1,0:T(8,128)S(1)} %get-tuple-element.48.far_sent), channel_id=1, source_target_pairs={{0,28},{4,8},{8,4},{12,16},{16,12},{20,24},{24,20},{28,0},{1,29},{... | collective-permute-start | bytes 221192 | tf_op jit(solution)/shard_map/ppermute | solution.py:340
  27.8 0.5 %collective-permute-start.11 = (f32[48,384]{1,0:T(8,128)S(1)}, f32[48,384]{1,0:T(8,128)S(1)}, u32[]{:S(2)}, u32[]{:S(2)}) collective-permute-start(f32[48,384]{1,0:T(8,128)S(1)} %get-tuple-element.49), channel_id=1, source_target_pairs={{0,4},{4,0},{8,12},{12,8},{16,20},{20,16},{24,28},{28,24},{1,5},{5... | collective-permute-start | bytes 221192 | tf_op jit(solution)/shard_map/ppermute | solution.py:337
  28.3 0.1 shard_map.90.ham
  28.4 0.0 copy-done.2
  28.5 0.6 %shard_map.89 = (f32[288,384]{1,0:T(8,128)S(1)}, f32[48,384]{1,0:T(8,128)S(1)}) custom-call(f32[192,384]{1,0:T(8,128)S(1)} %get-tuple-element.50.v.s, f32[192,128]{1,0:T(8,128)S(1)} %get-tuple-element.46.column, bf16[288,576]{1,0:T(8,128)(2,1)S(1)} %copy-done.2, bf16[96,384]{1,0:T(8,128)(2,1)S(1)} %get-tuple-element.47.pick), custom_call_target="tpu_custom_call" | custom-call | flops 191102976 | bytes 1048576 | tf_op jit(solution)/shard_map/pallas_call | solution.py:51
  29.1 2.8 %collective-permute-done.10.far = f32[48,384]{1,0:T(8,128)S(1)} collective-permute-done((f32[48,384]{1,0:T(8,128)S(1)}, f32[48,384]{1,0:T(8,128)S(1)}, u32[]{:S(2)}, u32[]{:S(2)}) %collective-permute-start.10) | collective-permute-done | bytes 73760 | tf_op jit(solution)/shard_map/ppermute | solution.py:340
  31.9 0.0 collective-permute-done.11.near
  31.9 0.2 shard_map.91
  32.1 0.1 collective-permute-start.12
  32.2 1.8 %collective-permute-start.14 = (f32[48,384]{1,0:T(8,128)S(1)}, f32[48,384]{1,0:T(8,128)S(1)}, u32[]{:S(2)}, u32[]{:S(2)}) collective-permute-start(f32[48,384]{1,0:T(8,128)S(1)} %get-tuple-element.59.sent), channel_id=1, source_target_pairs={{0,28},{4,8},{8,4},{12,16},{16,12},{20,24},{24,20},{28,0},{1,29},{... | collective-permute-start | bytes 221192 | tf_op jit(solution)/shard_map/ppermute | solution.py:340
  34.0 0.0 collective-permute-done.12.from_near
  34.0 0.1 shard_map.92
  34.2 1.0 %collective-permute-start.13 = (f32[48,512]{1,0:T(8,128)S(1)}, f32[48,512]{1,0:T(8,128)S(1)}, u32[]{:S(2)}, u32[]{:S(2)}) collective-permute-start(f32[48,512]{1,0:T(8,128)S(1)} %shard_map.92), channel_id=1, source_target_pairs={{0,28},{4,8},{8,4},{12,16},{16,12},{20,24},{24,20},{28,0},{1,29},{... | collective-permute-start | bytes 294920 | tf_op jit(solution)/shard_map/ppermute | solution.py:340
  35.1 0.3 shard_map.93.base
  35.4 0.4 shard_map.94
  35.8 1.8 %collective-permute-done.14.from_far = f32[48,384]{1,0:T(8,128)S(1)} collective-permute-done((f32[48,384]{1,0:T(8,128)S(1)}, f32[48,384]{1,0:T(8,128)S(1)}, u32[]{:S(2)}, u32[]{:S(2)}) %collective-permute-start.14) | collective-permute-done | bytes 73760 | tf_op jit(solution)/shard_map/ppermute | solution.py:340
  37.6 0.1 shard_map.95
  37.7 0.1 collective-permute-start.15
  37.8 0.2 shard_map.96.v.one
  38.0 0.5 %shard_map.97.partial = f32[288,384]{1,0:T(8,128)S(1)} custom-call(f32[192,384]{1,0:T(8,128)S(1)} %shard_map.96.v.one, f32[192,128]{1,0:T(8,128)S(1)} %get-tuple-element.46.column, bf16[288,576]{1,0:T(8,128)(2,1)S(1)} %copy-done.2), custom_call_target="tpu_custom_call" | custom-call | flops 191102976 | bytes 1048576 | tf_op jit(solution)/shard_map/pallas_call | solution.py:51
  38.4 0.6 %collective-permute-done.15.near = f32[48,384]{1,0:T(8,128)S(1)} collective-permute-done((f32[48,384]{1,0:T(8,128)S(1)}, f32[48,384]{1,0:T(8,128)S(1)}, u32[]{:S(2)}, u32[]{:S(2)}) %collective-permute-start.15) | collective-permute-done | bytes 73760 | tf_op jit(solution)/shard_map/ppermute | solution.py:337
  39.0 0.8 %collective-permute-done.13.far = f32[48,512]{1,0:T(8,128)S(1)} collective-permute-done((f32[48,512]{1,0:T(8,128)S(1)}, f32[48,512]{1,0:T(8,128)S(1)}, u32[]{:S(2)}, u32[]{:S(2)}) %collective-permute-start.13) | collective-permute-done | bytes 98336 | tf_op jit(solution)/shard_map/ppermute | solution.py:340
  39.9 0.3 shard_map.98
  40.1 1.0 %collective-permute-start.16 = (f32[48,384]{1,0:T(8,128)S(1)}, f32[48,384]{1,0:T(8,128)S(1)}, u32[]{:S(2)}, u32[]{:S(2)}) collective-permute-start(f32[48,384]{1,0:T(8,128)S(1)} %get-tuple-element.65), channel_id=1, source_target_pairs={{0,28},{4,8},{8,4},{12,16},{16,12},{20,24},{24,20},{28,0},{1,29},{... | collective-permute-start | bytes 221192 | tf_op jit(solution)/shard_map/ppermute | solution.py:340
  41.2 0.0 collective-permute-start.17
  41.2 0.4 shard_map.99.base
  41.5 3.3 %collective-permute-done.16.from_far = f32[48,384]{1,0:T(8,128)S(1)} collective-permute-done((f32[48,384]{1,0:T(8,128)S(1)}, f32[48,384]{1,0:T(8,128)S(1)}, u32[]{:S(2)}, u32[]{:S(2)}) %collective-permute-start.16) | collective-permute-done | bytes 73760 | tf_op jit(solution)/shard_map/ppermute | solution.py:340
  44.9 0.0 collective-permute-done.17.from_near
  44.9 0.9 %shard_map.100 = f32[192,384]{1,0:T(8,128)} custom-call(f32[48,384]{1,0:T(8,128)S(1)} %collective-permute-done.16.from_far, f32[192,384]{1,0:T(8,128)S(1)} %shard_map.99.base, f32[48,384]{1,0:T(8,128)S(1)} %collective-permute-done.17.from_near, f32[192,128]{1,0:T(8,128)S(1)} %get-tuple-element.46.column, bf16[192,96]{1,0:T(8,128)(2,1)S(1)} %get-tuple-element.60.put_near, ...), custom_call_target="tpu_custom_call" | custom-call | flops 42467328 | bytes 1048576 | tf_op jit(solution)/shard_map/pallas_call | solution.py:51
  (8 shorter events, 0.1 us)
Async XLA Ops:
  0.0 5.6 %copy-start = (f32[192,1536]{1,0:T(8,128)S(1)}, f32[192,1536]{1,0:T(8,128)}, u32[]{:S(2)}) copy-start(f32[192,1536]{1,0:T(8,128)} %param.15) | copy-start | bytes 3538948
  0.0 16.4 %collective-permute-start = (f32[192,384]{1,0:T(8,128)}, f32[192,384]{1,0:T(8,128)S(1)}, u32[]{:S(2)}, u32[]{:S(2)}) collective-permute-start(f32[192,384]{1,0:T(8,128)} %own.1), channel_id=1, source_target_pairs={{0,1},{1,0},{2,3},{3,2},{4,5},{5,4},{6,7},{7,6},{8,9},{9,8},{10,11... | collective-permute-start | bytes 884744 | tf_op jit(solution)/shard_map/ppermute | solution.py:364
  3.0 16.0 %collective-permute-start.1 = (f32[192,384]{1,0:T(8,128)}, f32[192,384]{1,0:T(8,128)S(1)}, u32[]{:S(2)}, u32[]{:S(2)}) collective-permute-start(f32[192,384]{1,0:T(8,128)} %own.1), channel_id=1, source_target_pairs={{0,2},{1,3},{2,0},{3,1},{4,6},{5,7},{6,4},{7,5},{8,10},{9,11},{10,... | collective-permute-start | bytes 884744 | tf_op jit(solution)/shard_map/ppermute | solution.py:365
  5.6 13.9 %copy-start.3 = (f32[192,384]{1,0:T(8,128)S(1)}, f32[192,384]{1,0:T(8,128)}, u32[]{:S(2)}) copy-start(f32[192,384]{1,0:T(8,128)} %own.1) | copy-start | bytes 884740
  5.7 14.0 %collective-permute-start.2 = (f32[192,384]{1,0:T(8,128)S(1)}, f32[192,384]{1,0:T(8,128)S(1)}, u32[]{:S(2)}, u32[]{:S(2)}) collective-permute-start(f32[192,384]{1,0:T(8,128)S(1)} %constant_dynamic-slice_fusion.refs_0_), channel_id=1, source_target_pairs={{0,8},{4,12},{8,0},{12,4},{16,24},{20,28},{24,16},{28,20},{1,9},{5... | collective-permute-start | bytes 884744 | tf_op jit(solution)/shard_map/ppermute | solution.py:369
  7.2 14.2 %collective-permute-start.3 = (f32[192,384]{1,0:T(8,128)S(1)}, f32[192,384]{1,0:T(8,128)S(1)}, u32[]{:S(2)}, u32[]{:S(2)}) collective-permute-start(f32[192,384]{1,0:T(8,128)S(1)} %constant_dynamic-slice_fusion.refs_0_), channel_id=1, source_target_pairs={{0,16},{4,20},{8,24},{12,28},{16,0},{20,4},{24,8},{28,12},{1,17},{... | collective-permute-start | bytes 884744 | tf_op jit(solution)/shard_map/ppermute | solution.py:369
  8.7 12.7 %collective-permute-start.4 = (f32[192,384]{1,0:T(8,128)S(1)}, f32[192,384]{1,0:T(8,128)S(1)}, u32[]{:S(2)}, u32[]{:S(2)}) collective-permute-start(f32[192,384]{1,0:T(8,128)S(1)} %constant_dynamic-slice_fusion.refs_0_), channel_id=1, source_target_pairs={{0,24},{4,28},{8,16},{12,20},{16,8},{20,12},{24,0},{28,4},{1,25},{... | collective-permute-start | bytes 884744 | tf_op jit(solution)/shard_map/ppermute | solution.py:369
  19.0 3.5 %copy-start.4 = (f32[192]{0:T(256)S(1)}, f32[192]{0:T(256)}, u32[]{:S(2)}) copy-start(f32[192]{0:T(256)} %param.9) | copy-start | bytes 2308
  19.0 3.5 %copy-start.6 = (s32[48]{0:T(128)S(1)}, s32[48]{0:T(128)}, u32[]{:S(2)}) copy-start(s32[48]{0:T(128)} %param.12) | copy-start | bytes 580
  19.0 3.4 %copy-start.7 = (s32[48]{0:T(128)S(1)}, s32[48]{0:T(128)}, u32[]{:S(2)}) copy-start(s32[48]{0:T(128)} %param.13) | copy-start | bytes 580
  19.0 5.3 %copy-start.5 = (s32[8]{0:T(128)S(1)}, s32[8]{0:T(128)}, u32[]{:S(2)}) copy-start(s32[8]{0:T(128)} %param.14) | copy-start | bytes 100
  19.1 6.9 %collective-permute-start.9 = (f32[193,384]{1,0:T(8,128)S(1)}, f32[193,384]{1,0:T(8,128)S(1)}, u32[]{:S(2)}, u32[]{:S(2)}) collective-permute-start(f32[193,384]{1,0:T(8,128)S(1)} %shard_map.86), channel_id=1, source_target_pairs={{0,1},{1,0},{2,3},{3,2},{4,5},{5,4},{6,7},{7,6},{8,9},{9,8},{10,11... | collective-permute-start | bytes 889352 | tf_op jit(solution)/shard_map/ppermute | solution.py:372
  21.4 1.6 %collective-permute-start.5 = (f32[192,384]{1,0:T(8,128)S(1)}, f32[192,384]{1,0:T(8,128)S(1)}, u32[]{:S(2)}, u32[]{:S(2)}) collective-permute-start(f32[192,384]{1,0:T(8,128)S(1)} %constant_dynamic-slice_fusion.refs_0_), channel_id=1, source_target_pairs={{0,4},{4,0},{8,12},{12,8},{16,20},{20,16},{24,28},{28,24},{1,5},{5... | collective-permute-start | bytes 884744 | tf_op jit(solution)/shard_map/ppermute | solution.py:376
  21.5 2.0 %collective-permute-start.6 = (f32[192,384]{1,0:T(8,128)S(1)}, f32[192,384]{1,0:T(8,128)S(1)}, u32[]{:S(2)}, u32[]{:S(2)}) collective-permute-start(f32[192,384]{1,0:T(8,128)S(1)} %collective-permute-done.2.refs_2_), channel_id=1, source_target_pairs={{0,4},{4,0},{8,12},{12,8},{16,20},{20,16},{24,28},{28,24},{1,5},{5... | collective-permute-start | bytes 884744 | tf_op jit(solution)/shard_map/ppermute | solution.py:376
  22.0 1.9 %collective-permute-start.7 = (f32[192,384]{1,0:T(8,128)S(1)}, f32[192,384]{1,0:T(8,128)S(1)}, u32[]{:S(2)}, u32[]{:S(2)}) collective-permute-start(f32[192,384]{1,0:T(8,128)S(1)} %collective-permute-done.3.refs_4_), channel_id=1, source_target_pairs={{0,4},{4,0},{8,12},{12,8},{16,20},{20,16},{24,28},{28,24},{1,5},{5... | collective-permute-start | bytes 884744 | tf_op jit(solution)/shard_map/ppermute | solution.py:376
  22.0 2.3 %collective-permute-start.8 = (f32[192,384]{1,0:T(8,128)S(1)}, f32[192,384]{1,0:T(8,128)S(1)}, u32[]{:S(2)}, u32[]{:S(2)}) collective-permute-start(f32[192,384]{1,0:T(8,128)S(1)} %collective-permute-done.4.refs_6_), channel_id=1, source_target_pairs={{0,4},{4,0},{8,12},{12,8},{16,20},{20,16},{24,28},{28,24},{1,5},{5... | collective-permute-start | bytes 884744 | tf_op jit(solution)/shard_map/ppermute | solution.py:376
  26.0 2.3 %copy-start.1 = (bf16[288,288]{1,0:T(8,128)(2,1)S(1)}, bf16[288,288]{1,0:T(8,128)(2,1)}, u32[]{:S(2)}) copy-start(bf16[288,288]{1,0:T(8,128)(2,1)} %get-tuple-element.54.ham) | copy-start | bytes 497668
  26.0 2.5 %copy-start.2 = (bf16[288,576]{1,0:T(8,128)(2,1)S(1)}, bf16[288,576]{1,0:T(8,128)(2,1)}, u32[]{:S(2)}) copy-start(bf16[288,576]{1,0:T(8,128)(2,1)} %get-tuple-element.51.ham) | copy-start | bytes 995332
  26.6 5.3 %collective-permute-start.10 = (f32[48,384]{1,0:T(8,128)S(1)}, f32[48,384]{1,0:T(8,128)S(1)}, u32[]{:S(2)}, u32[]{:S(2)}) collective-permute-start(f32[48,384]{1,0:T(8,128)S(1)} %get-tuple-element.48.far_sent), channel_id=1, source_target_pairs={{0,28},{4,8},{8,4},{12,16},{16,12},{20,24},{24,20},{28,0},{1,29},{... | collective-permute-start | bytes 221192 | tf_op jit(solution)/shard_map/ppermute | solution.py:340
  27.8 4.1 %collective-permute-start.11 = (f32[48,384]{1,0:T(8,128)S(1)}, f32[48,384]{1,0:T(8,128)S(1)}, u32[]{:S(2)}, u32[]{:S(2)}) collective-permute-start(f32[48,384]{1,0:T(8,128)S(1)} %get-tuple-element.49), channel_id=1, source_target_pairs={{0,4},{4,0},{8,12},{12,8},{16,20},{20,16},{24,28},{28,24},{1,5},{5... | collective-permute-start | bytes 221192 | tf_op jit(solution)/shard_map/ppermute | solution.py:337
  32.1 1.9 %collective-permute-start.12 = (f32[48,384]{1,0:T(8,128)S(1)}, f32[48,384]{1,0:T(8,128)S(1)}, u32[]{:S(2)}, u32[]{:S(2)}) collective-permute-start(f32[48,384]{1,0:T(8,128)S(1)} %get-tuple-element.56), channel_id=1, source_target_pairs={{0,4},{4,0},{8,12},{12,8},{16,20},{20,16},{24,28},{28,24},{1,5},{5... | collective-permute-start | bytes 221192 | tf_op jit(solution)/shard_map/ppermute | solution.py:337
  32.2 5.3 %collective-permute-start.14 = (f32[48,384]{1,0:T(8,128)S(1)}, f32[48,384]{1,0:T(8,128)S(1)}, u32[]{:S(2)}, u32[]{:S(2)}) collective-permute-start(f32[48,384]{1,0:T(8,128)S(1)} %get-tuple-element.59.sent), channel_id=1, source_target_pairs={{0,28},{4,8},{8,4},{12,16},{16,12},{20,24},{24,20},{28,0},{1,29},{... | collective-permute-start | bytes 221192 | tf_op jit(solution)/shard_map/ppermute | solution.py:340
  34.2 5.7 %collective-permute-start.13 = (f32[48,512]{1,0:T(8,128)S(1)}, f32[48,512]{1,0:T(8,128)S(1)}, u32[]{:S(2)}, u32[]{:S(2)}) collective-permute-start(f32[48,512]{1,0:T(8,128)S(1)} %shard_map.92), channel_id=1, source_target_pairs={{0,28},{4,8},{8,4},{12,16},{16,12},{20,24},{24,20},{28,0},{1,29},{... | collective-permute-start | bytes 294920 | tf_op jit(solution)/shard_map/ppermute | solution.py:340
  37.7 1.3 %collective-permute-start.15 = (f32[48,384]{1,0:T(8,128)S(1)}, f32[48,384]{1,0:T(8,128)S(1)}, u32[]{:S(2)}, u32[]{:S(2)}) collective-permute-start(f32[48,384]{1,0:T(8,128)S(1)} %shard_map.95), channel_id=1, source_target_pairs={{0,4},{4,0},{8,12},{12,8},{16,20},{20,16},{24,28},{28,24},{1,5},{5... | collective-permute-start | bytes 221192 | tf_op jit(solution)/shard_map/ppermute | solution.py:337
  40.1 4.7 %collective-permute-start.16 = (f32[48,384]{1,0:T(8,128)S(1)}, f32[48,384]{1,0:T(8,128)S(1)}, u32[]{:S(2)}, u32[]{:S(2)}) collective-permute-start(f32[48,384]{1,0:T(8,128)S(1)} %get-tuple-element.65), channel_id=1, source_target_pairs={{0,28},{4,8},{8,4},{12,16},{16,12},{20,24},{24,20},{28,0},{1,29},{... | collective-permute-start | bytes 221192 | tf_op jit(solution)/shard_map/ppermute | solution.py:340
  41.2 3.7 %collective-permute-start.17 = (f32[48,384]{1,0:T(8,128)S(1)}, f32[48,384]{1,0:T(8,128)S(1)}, u32[]{:S(2)}, u32[]{:S(2)}) collective-permute-start(f32[48,384]{1,0:T(8,128)S(1)} %get-tuple-element.66), channel_id=1, source_target_pairs={{0,4},{4,0},{8,12},{12,8},{16,20},{20,16},{24,28},{28,24},{1,5},{5... | collective-permute-start | bytes 221192 | tf_op jit(solution)/shard_map/ppermute | solution.py:337
